TPU v7x, 32 devices: a whole 2x2x4 slice. The times are simulated.
32 devices in a mesh: ctx: 16 (over z, x, core), head: 2 (over y).
Axes of the slice: x: 2, y: 2, z: 4, core: 2. Of those that a mesh axis runs over, the one named last changes fastest.
Arguments:
- queries: bfloat16 [2, 4096, 1024], P(None, 'ctx', 'head'), may hold values from -64 to 64
- keys: bfloat16 [2, 4096, 1024], P(None, 'ctx', 'head'), may hold values from -4 to 4
- values: bfloat16 [2, 4096, 1024], P(None, 'ctx', 'head'), may hold values from -5 to 5
- gates: bfloat16 [2, 4096, 1024], P(None, 'ctx', 'head'), may hold values from -4 to 4
- token_rates: float32 [4096, 2], P('ctx', 'head'), may hold values from 0.05 to 1
- fast_init: bfloat16 [2, 512, 768], P('head', 'ctx'), may hold values from -0.25 to 0.25
- fast_rate: float32 [2], P('head'), may hold values from 0.3 to 1
- norm_gain: float32 [1024], replicated, may hold values from 0.5 to 1.5
Outputs:
- normed: bfloat16 [2, 4096, 1024], P(None, ('ctx', 'head'))
All inputs are finite; a program needn't handle non-finite values.
Results may differ from a plain program's by a relative error of at most 0.02.
Values may be sent and summed in bfloat16 or wider, within the bound.
No kernel may reach another device: no remote copies, remote signals or barrier semaphores. Data moves between devices by JAX's collectives and lax.ppermute only.
A program may use at most 64 MiB of HBM per device.

v0:
```python
import jax
import jax.numpy as jnp
from jax import lax
from jax.sharding import PartitionSpec as P

WIN = 1024


A_COEF = 3.4445
B_COEF = -4.775
C_COEF = 2.0315


def passed_along(value, axis, steps):
    count = lax.axis_size(axis)
    pairs = [(source, (source + steps) % count) for source in range(count)]
    return lax.ppermute(value, axis, pairs)


def fast_hidden(inputs, weights):
    block_width = weights.shape[1] // 3
    gate_up = jnp.dot(inputs, weights[:, : 2 * block_width], preferred_element_type=jnp.float32)
    gate_part = gate_up[:, :block_width]
    up_part = gate_up[:, block_width:]
    hidden = (jax.nn.silu(gate_part) * up_part).astype(jnp.bfloat16)
    return (gate_part, up_part, hidden)


def fast_apply(inputs, weights):
    block_width = weights.shape[1] // 3
    gate_part, up_part, hidden = fast_hidden(inputs, weights)
    return lax.dot_general(
        hidden,
        weights[:, 2 * block_width :],
        (((1,), (1,)), ((), ())),
        preferred_element_type=jnp.float32,
    )


def fast_gradient(key_rows, value_rows, rate_rows, weights):
    block_width = weights.shape[1] // 3
    gate_part, up_part, hidden = fast_hidden(key_rows, weights)
    target = (-rate_rows * value_rows.astype(jnp.float32)).astype(jnp.bfloat16)
    out_grad = lax.dot_general(
        target, hidden, (((0,), (0,)), ((), ())), preferred_element_type=jnp.float32
    )
    hidden_grad = jnp.dot(target, weights[:, 2 * block_width :], preferred_element_type=jnp.float32)
    sigmoid_g = jax.nn.sigmoid(gate_part)
    gate_grad = hidden_grad * up_part * sigmoid_g * (1.0 + gate_part * (1.0 - sigmoid_g))
    up_grad = hidden_grad * jax.nn.silu(gate_part)
    joined = jnp.concatenate([gate_grad, up_grad], 1).astype(jnp.bfloat16)
    in_grad = lax.dot_general(
        key_rows, joined, (((0,), (0,)), ((), ())), preferred_element_type=jnp.float32
    )
    return jnp.concatenate([in_grad, out_grad], 1)


def newton_turn(ortho, gram_mat):
    gram_low = gram_mat.astype(jnp.bfloat16)
    square = jnp.einsum("mfg,mgh->mfh", gram_low, gram_low, preferred_element_type=jnp.float32)
    mixer_mat = (B_COEF * gram_mat + C_COEF * square).astype(jnp.bfloat16)
    product = jnp.einsum("rmf,mfg->rmg", ortho, mixer_mat, preferred_element_type=jnp.float32)
    return (A_COEF * ortho.astype(jnp.float32) + product).astype(jnp.bfloat16)


def renew(initial, ortho, rate_value):
    anchor = initial.astype(jnp.float32)
    updated = anchor - rate_value * ortho.astype(jnp.float32)
    first_norm = jnp.sqrt(jnp.sum(anchor * anchor, 0))
    updated_norm = jnp.sqrt(jnp.sum(updated * updated, 0))
    return (updated * (first_norm / (updated_norm + 1e-06))).astype(jnp.bfloat16)


def shards(queries, keys, values, gates, token_rates, fast_init, fast_rate, norm_gain):
    position = lax.axis_index("ctx")
    block_rows = queries.shape[1]
    head_dim = queries.shape[2]
    reach = (WIN - 1) // block_rows + 1
    received = []
    carried = (keys, values)
    for hop_index in range(1, reach + 1):
        carried = passed_along((carried[0], carried[1]), "ctx", 1)
        received.append(carried)
    earlier_keys = []
    earlier_values = []
    earlier_live = []
    for hop_index in range(reach, 0, -1):
        recv_keys, recv_values = received[hop_index - 1]
        wrapped = position < hop_index
        earlier_keys.append(
            jnp.stack([recv_keys[0], jnp.where(wrapped, recv_keys[0], recv_keys[1])])
        )
        earlier_values.append(
            jnp.stack([recv_values[0], jnp.where(wrapped, recv_values[0], recv_values[1])])
        )
        earlier_live.append(jnp.stack([jnp.logical_not(wrapped), jnp.asarray(True)]))
    prev_keys = jnp.concatenate(earlier_keys, 1)
    prev_values = jnp.concatenate(earlier_values, 1)
    prev_live = jnp.repeat(jnp.stack(earlier_live, 1), block_rows, axis=1)
    row_pos = jnp.arange(block_rows)[:, None]
    prev_rel = (jnp.arange(reach * block_rows) - reach * block_rows)[None, :]
    own_rel = jnp.arange(block_rows)[None, :]
    prev_allowed = (prev_rel > row_pos - WIN)[None] & prev_live[:, None, :]
    own_allowed = jnp.broadcast_to(
        ((own_rel <= row_pos) & (own_rel > row_pos - WIN))[None], (2, block_rows, block_rows)
    )
    score_scale = head_dim ** (-0.5)
    initial = lax.all_gather(fast_init, "ctx", axis=1, tiled=True)[0]
    block_width = initial.shape[1] // 3
    own_scores = (
        jnp.einsum("cqd,ckd->cqk", queries, keys, preferred_element_type=jnp.float32) * score_scale
    )
    own_scores = jnp.where(own_allowed, own_scores, -1e30)
    prev_scores = (
        jnp.einsum("cqd,ckd->cqk", queries, prev_keys, preferred_element_type=jnp.float32)
        * score_scale
    )
    prev_scores = jnp.where(prev_allowed, prev_scores, -1e30)
    row_max = jnp.maximum(
        jnp.max(own_scores, -1, keepdims=True), jnp.max(prev_scores, -1, keepdims=True)
    )
    own_exp = jnp.where(own_allowed, jnp.exp(own_scores - row_max), 0.0)
    prev_exp = jnp.where(prev_allowed, jnp.exp(prev_scores - row_max), 0.0)
    row_total = jnp.sum(own_exp, -1, keepdims=True) + jnp.sum(prev_exp, -1, keepdims=True)
    own_part = jnp.einsum(
        "cqk,ckd->cqd", own_exp.astype(jnp.bfloat16), values, preferred_element_type=jnp.float32
    )
    prev_part = jnp.einsum(
        "cqk,ckd->cqd",
        prev_exp.astype(jnp.bfloat16),
        prev_values,
        preferred_element_type=jnp.float32,
    )
    window_out = (own_part + prev_part) / row_total
    gradient = fast_gradient(keys[0], values[0], token_rates, initial)
    total_grad = lax.psum(gradient, "ctx")
    blocks = total_grad.reshape(total_grad.shape[0], 3, block_width)
    block_norms = jnp.sqrt(jnp.sum(blocks * blocks, axis=(0, 2)))
    ortho = (blocks / (block_norms[None, :, None] + 1e-06)).astype(jnp.bfloat16)
    for turn_index in range(3):
        gram_mat = jnp.einsum("rmf,rmg->mfg", ortho, ortho, preferred_element_type=jnp.float32)
        ortho = newton_turn(ortho, gram_mat)
    ortho_full = ortho.reshape(ortho.shape[0], 3 * block_width)
    renewed = renew(initial, ortho_full, fast_rate[0])
    fast_out = jnp.stack([fast_apply(queries[0], initial), fast_apply(queries[1], renewed)])
    combined = window_out + fast_out
    gated_out = (combined * jax.nn.silu(gates.astype(jnp.float32))).astype(jnp.bfloat16)
    wide_vals = lax.all_to_all(gated_out, "head", split_axis=1, concat_axis=2, tiled=True).astype(
        jnp.float32
    )
    inv_rms = lax.rsqrt(jnp.mean(wide_vals * wide_vals, -1, keepdims=True) + 1e-06)
    return (wide_vals * inv_rms * norm_gain).astype(jnp.bfloat16)


def solution(mesh):
    placed = (
        P(None, "ctx", "head"),
        P(None, "ctx", "head"),
        P(None, "ctx", "head"),
        P(None, "ctx", "head"),
        P("ctx", "head"),
        P("head", "ctx", None),
        P("head"),
        P(),
    )
    return jax.shard_map(
        shards,
        mesh=mesh,
        in_specs=placed,
        out_specs=P(None, ("ctx", "head"), None),
        check_vma=False,
    )
```

profile of v0, /device:TPU:0, one launch (start us, length us, event | category | flops | bytes accessed | tf_op | source)
XLA Modules:
  0.0 200.5 jit_solution(6698294185047462078)
XLA Ops:
  6.5 0.5 collective-permute-start
  7.0 2.6 %collective-permute-start.4 = (bf16[2,256,512]{2,1,0:T(8,128)(2,1)}, bf16[2,256,512]{2,1,0:T(8,128)(2,1)}, u32[]{:S(2)}, u32[]{:S(2)}) collective-permute-start(bf16[2,256,512]{2,1,0:T(8,128)(2,1)} %param.10), channel_id=1, source_target_pairs={{0,2},{2,4},{4,6},{6,8},{8,10},{10,12},{12,14},{14,16},{16,18},{18... | collective-permute-start | bytes 1572872 | tf_op jit(solution)/shard_map/ppermute | solution.py:17
  9.6 29.3 %all_gather.3 = bf16[1,512,768]{2,1,0:T(8,128)(2,1)S(1)} all-gather(bf16[1,32,768]{2,1,0:T(8,128)(2,1)} %param.13), channel_id=1, replica_groups=mesh['ctx'=16,'head'=2] {'ctx'}, dimensions={1}, use_global_device_ids=true | all-gather | bytes 835584 | tf_op jit(solution)/shard_map/all_gather | solution.py:108
  38.9 1.2 fusion.84
  40.2 0.3 multiply_convert_fusion.4
  40.4 0.3 fusion.126
  40.8 0.4 copy-done.6
  41.2 0.3 convolution_bitcast_fusion
  41.5 0.0 copy-start.2
  41.5 1.3 pad_maximum_fusion
  42.8 0.0 all-reduce.2.cloned.1.call-update
  42.9 0.1 fusion.134
  42.9 0.1 fusion.136
  43.0 0.1 copy.100
  43.2 0.2 broadcast_compare_fusion
  43.4 0.3 fusion.86
  43.7 0.1 broadcast_bitcast_fusion
  43.8 1.1 convolution_bitcast_fusion.3
  45.5 1.1 fusion.162
  46.7 0.3 collective-permute-start.1
  47.0 2.2 %collective-permute-start.5 = (bf16[2,256,512]{2,1,0:T(8,128)(2,1)}, bf16[2,256,512]{2,1,0:T(8,128)(2,1)}, u32[]{:S(2)}, u32[]{:S(2)}) collective-permute-start(bf16[2,256,512]{2,1,0:T(8,128)(2,1)} %collective-permute-done.4), channel_id=1, source_target_pairs={{0,2},{2,4},{4,6},{6,8},{8,10},{10,12},{12,14},{14,16},{16,18},{18... | collective-permute-start | bytes 1572872 | tf_op jit(solution)/shard_map/ppermute | solution.py:17
  49.3 1.9 fusion.161
  51.1 1.9 fusion.157
  53.0 88.3 %all-reduce.2.cloned.1.call-done = f32[512,768]{0,1:T(8,128)} async-done(((f32[512,768]{0,1:T(8,128)}), f32[512,768]{0,1:T(8,128)}) %all-reduce.2.cloned.1.call-update) | async-done | bytes 1572880 | tf_op jit(solution)/shard_map/psum | solution.py:136
  141.3 1.7 multiply_reduce_fusion.1
  143.0 0.1 reduce_sum.72
  143.1 0.0 copy-done
  143.1 0.2 divide_convert_fusion
  143.4 0.4 fusion.163
  143.8 0.6 fusion.36
  144.4 0.4 fusion.164
  144.8 0.6 fusion.35
  145.4 0.4 fusion.165
  145.8 1.8 convert_multiply_fusion.1
  147.6 1.9 copy.114
  149.4 0.3 fusion.33
  149.8 0.2 multiply_convert_fusion
  150.0 0.1 collective-permute-start.2
  150.1 0.7 copy-done.3
  150.8 0.3 convolution_bitcast_fusion.1
  151.1 0.8 collective-permute-start.6
  151.9 0.3 convolution_bitcast_fusion.2
  152.2 1.1 fusion.160
  153.3 8.3 %collective-permute-done.2 = bf16[2,256,512]{2,1,0:T(8,128)(2,1)S(1)} collective-permute-done((bf16[2,256,512]{2,1,0:T(8,128)(2,1)}, bf16[2,256,512]{2,1,0:T(8,128)(2,1)S(1)}, u32[]{:S(2)}, u32[]{:S(2)}) %collective-permute-start.2) | collective-permute-done | bytes 524320 | tf_op jit(solution)/shard_map/ppermute | solution.py:17
  161.6 1.1 fusion.156
  162.6 4.5 %collective-permute-done.6 = bf16[2,256,512]{2,1,0:T(8,128)(2,1)S(1)} collective-permute-done((bf16[2,256,512]{2,1,0:T(8,128)(2,1)}, bf16[2,256,512]{2,1,0:T(8,128)(2,1)S(1)}, u32[]{:S(2)}, u32[]{:S(2)}) %collective-permute-start.6) | collective-permute-done | bytes 524320 | tf_op jit(solution)/shard_map/ppermute | solution.py:17
  167.3 5.6 %collective-permute-done.3 = bf16[2,256,512]{2,1,0:T(8,128)(2,1)S(1)} collective-permute-done((bf16[2,256,512]{2,1,0:T(8,128)(2,1)S(1)}, bf16[2,256,512]{2,1,0:T(8,128)(2,1)S(1)}, u32[]{:S(2)}, u32[]{:S(2)}) %collective-permute-start.3) | collective-permute-done | bytes 524320 | tf_op jit(solution)/shard_map/ppermute | solution.py:17
  172.9 0.0 copy-start.1
  172.9 0.9 fusion.32
  173.8 0.1 copy-done.1
  174.0 0.1 fusion.88
  174.1 0.8 fusion.47
  175.0 0.4 fusion.102
  175.4 3.1 %collective-permute-done.7 = bf16[2,256,512]{2,1,0:T(8,128)(2,1)S(1)} collective-permute-done((bf16[2,256,512]{2,1,0:T(8,128)(2,1)S(1)}, bf16[2,256,512]{2,1,0:T(8,128)(2,1)S(1)}, u32[]{:S(2)}, u32[]{:S(2)}) %collective-permute-start.7) | collective-permute-done | bytes 524320 | tf_op jit(solution)/shard_map/ppermute | solution.py:17
  178.6 1.6 fusion.65
  180.2 0.5 copy.116
  180.7 9.1 %all_to_all.4 = bf16[2,256,512]{2,0,1:T(2,128)(2,1)S(1)} all-to-all(bf16[2,256,512]{2,0,1:T(2,128)(2,1)S(1)} %copy.116), channel_id=1, replica_groups=mesh['ctx'=16,'head'=2] {'head'}, dimensions={1} | all-to-all | bytes 1048576 | tf_op jit(solution)/shard_map/all_to_all | solution.py:148
  189.9 0.4 convert_element_type.135
  190.2 0.8 copy.117
  191.1 0.9 reshape.122
  192.0 0.6 multiply_reduce_fusion.2
  192.6 0.1 copy.118
  192.7 0.0 copy-done.11
  192.7 1.0 multiply_convert_fusion.1
  (47 shorter events, 0.4 us)
Async XLA Ops:
  6.5 33.6 %copy-start.4 = (bf16[2,256,512]{2,1,0:T(8,128)(2,1)S(1)}, bf16[2,256,512]{2,1,0:T(8,128)(2,1)}, u32[]{:S(2)}) copy-start(bf16[2,256,512]{2,1,0:T(8,128)(2,1)} %param.10) | copy-start | bytes 1572868
  6.5 33.6 %copy-start.12 = (f32[256,1]{0,1:T(1,128)S(1)}, f32[256,1]{0,1:T(1,128)}, u32[]{:S(2)}) copy-start(f32[256,1]{0,1:T(1,128)} %param.12) | copy-start | bytes 3076
  6.5 134.7 %all-reduce.2.cloned.1.call-start = ((), (), s32[]{:S(2)}) async-start(), calls=%async_computation.1 | async-start | bytes 3145728 | tf_op jit(solution)/shard_map/psum | solution.py:136
  6.5 40.1 %collective-permute-start = (bf16[2,256,512]{2,1,0:T(8,128)(2,1)}, bf16[2,256,512]{2,1,0:T(8,128)(2,1)}, u32[]{:S(2)}, u32[]{:S(2)}) collective-permute-start(bf16[2,256,512]{2,1,0:T(8,128)(2,1)} %param.9), channel_id=1, source_target_pairs={{0,2},{2,4},{4,6},{6,8},{8,10},{10,12},{12,14},{14,16},{16,18},{18... | collective-permute-start | bytes 1572872 | tf_op jit(solution)/shard_map/ppermute | solution.py:17
  7.0 40.0 %collective-permute-start.4 = (bf16[2,256,512]{2,1,0:T(8,128)(2,1)}, bf16[2,256,512]{2,1,0:T(8,128)(2,1)}, u32[]{:S(2)}, u32[]{:S(2)}) collective-permute-start(bf16[2,256,512]{2,1,0:T(8,128)(2,1)} %param.10), channel_id=1, source_target_pairs={{0,2},{2,4},{4,6},{6,8},{8,10},{10,12},{12,14},{14,16},{16,18},{18... | collective-permute-start | bytes 1572872 | tf_op jit(solution)/shard_map/ppermute | solution.py:17
  40.1 1.0 copy-start.6
  41.5 1.9 copy-start.2
  46.7 103.3 %collective-permute-start.1 = (bf16[2,256,512]{2,1,0:T(8,128)(2,1)}, bf16[2,256,512]{2,1,0:T(8,128)(2,1)}, u32[]{:S(2)}, u32[]{:S(2)}) collective-permute-start(bf16[2,256,512]{2,1,0:T(8,128)(2,1)} %collective-permute-done), channel_id=1, source_target_pairs={{0,2},{2,4},{4,6},{6,8},{8,10},{10,12},{12,14},{14,16},{16,18},{18... | collective-permute-start | bytes 1572872 | tf_op jit(solution)/shard_map/ppermute | solution.py:17
  47.0 104.1 %collective-permute-start.5 = (bf16[2,256,512]{2,1,0:T(8,128)(2,1)}, bf16[2,256,512]{2,1,0:T(8,128)(2,1)}, u32[]{:S(2)}, u32[]{:S(2)}) collective-permute-start(bf16[2,256,512]{2,1,0:T(8,128)(2,1)} %collective-permute-done.4), channel_id=1, source_target_pairs={{0,2},{2,4},{4,6},{6,8},{8,10},{10,12},{12,14},{14,16},{16,18},{18... | collective-permute-start | bytes 1572872 | tf_op jit(solution)/shard_map/ppermute | solution.py:17
  141.3 1.9 copy-start
  149.8 1.0 copy-start.3
  150.0 11.6 %collective-permute-start.2 = (bf16[2,256,512]{2,1,0:T(8,128)(2,1)}, bf16[2,256,512]{2,1,0:T(8,128)(2,1)S(1)}, u32[]{:S(2)}, u32[]{:S(2)}) collective-permute-start(bf16[2,256,512]{2,1,0:T(8,128)(2,1)} %collective-permute-done.1), channel_id=1, source_target_pairs={{0,2},{2,4},{4,6},{6,8},{8,10},{10,12},{12,14},{14,16},{16,18},{18... | collective-permute-start | bytes 1572872 | tf_op jit(solution)/shard_map/ppermute | solution.py:17
  151.1 16.1 %collective-permute-start.6 = (bf16[2,256,512]{2,1,0:T(8,128)(2,1)}, bf16[2,256,512]{2,1,0:T(8,128)(2,1)S(1)}, u32[]{:S(2)}, u32[]{:S(2)}) collective-permute-start(bf16[2,256,512]{2,1,0:T(8,128)(2,1)} %collective-permute-done.5), channel_id=1, source_target_pairs={{0,2},{2,4},{4,6},{6,8},{8,10},{10,12},{12,14},{14,16},{16,18},{18... | collective-permute-start | bytes 1572872 | tf_op jit(solution)/shard_map/ppermute | solution.py:17
  153.2 19.7 %copy-start.9 = (bf16[1,256,512]{2,1,0:T(8,128)(2,1)S(1)}, bf16[1,256,512]{2,1,0:T(8,128)(2,1)}, u32[]{:S(2)}) copy-start(bf16[1,256,512]{2,1,0:T(8,128)(2,1)} %get-tuple-element.23) | copy-start | bytes 786436
  153.2 19.7 %copy-start.10 = (bf16[1,256,512]{2,1,0:T(8,128)(2,1)S(1)}, bf16[1,256,512]{2,1,0:T(8,128)(2,1)}, u32[]{:S(2)}) copy-start(bf16[1,256,512]{2,1,0:T(8,128)(2,1)} %get-tuple-element.24) | copy-start | bytes 786436
  161.6 11.3 %collective-permute-start.3 = (bf16[2,256,512]{2,1,0:T(8,128)(2,1)S(1)}, bf16[2,256,512]{2,1,0:T(8,128)(2,1)S(1)}, u32[]{:S(2)}, u32[]{:S(2)}) collective-permute-start(bf16[2,256,512]{2,1,0:T(8,128)(2,1)S(1)} %collective-permute-done.2), channel_id=1, source_target_pairs={{0,2},{2,4},{4,6},{6,8},{8,10},{10,12},{12,14},{14,16},{16,18},{18... | collective-permute-start | bytes 1572872 | tf_op jit(solution)/shard_map/ppermute | solution.py:17
  167.2 11.3 %collective-permute-start.7 = (bf16[2,256,512]{2,1,0:T(8,128)(2,1)S(1)}, bf16[2,256,512]{2,1,0:T(8,128)(2,1)S(1)}, u32[]{:S(2)}, u32[]{:S(2)}) collective-permute-start(bf16[2,256,512]{2,1,0:T(8,128)(2,1)S(1)} %collective-permute-done.6), channel_id=1, source_target_pairs={{0,2},{2,4},{4,6},{6,8},{8,10},{10,12},{12,14},{14,16},{16,18},{18... | collective-permute-start | bytes 1572872 | tf_op jit(solution)/shard_map/ppermute | solution.py:17
  172.9 1.0 copy-start.1
  173.8 1.2 copy-start.5
  174.9 3.6 %copy-start.7 = (bf16[1,256,512]{2,1,0:T(8,128)(2,1)S(1)}, bf16[1,256,512]{2,1,0:T(8,128)(2,1)}, u32[]{:S(2)}) copy-start(bf16[1,256,512]{2,1,0:T(8,128)(2,1)} %get-tuple-element.15) | copy-start | bytes 786436
  174.9 3.6 %copy-start.8 = (bf16[1,256,512]{2,1,0:T(8,128)(2,1)S(1)}, bf16[1,256,512]{2,1,0:T(8,128)(2,1)}, u32[]{:S(2)}) copy-start(bf16[1,256,512]{2,1,0:T(8,128)(2,1)} %get-tuple-element.16) | copy-start | bytes 786436
  175.0 3.6 %copy-start.13 = (bf16[2,256,512]{2,1,0:T(8,128)(2,1)S(1)}, bf16[2,256,512]{2,1,0:T(8,128)(2,1)}, u32[]{:S(2)}) copy-start(bf16[2,256,512]{2,1,0:T(8,128)(2,1)} %param.11) | copy-start | bytes 1572868
  175.0 3.6 %copy-start.14 = (f32[1,256,512]{2,1,0:T(8,128)S(1)}, f32[1,256,512]{2,1,0:T(8,128)}, u32[]{:S(2)}) copy-start(f32[1,256,512]{2,1,0:T(8,128)} %convolution_bitcast_fusion.3) | copy-start | bytes 1572868
  190.2 2.4 %copy-start.11 = (f32[1024]{0:T(1024)S(1)}, f32[1024]{0:T(1024)}, u32[]{:S(2)}) copy-start(f32[1024]{0:T(1024)} %param.15) | copy-start | bytes 12292
Sparse Core Ops, SparseCore 0:
  42.9 98.2 all-reduce.1
where the time goes:
time: 201 us; the launch traced here: 200 us
  waiting for transfers between devices  110 us (55%)
  blocking collectives  38.4 us (19%)
  between operations  14.5 us (7%)
  other arithmetic  13.3 us (7%)
  matrix products  12.3 us (6%)
  starting transfers between devices  6.47 us (3%)
  local copies, waits for them, and re-layouts  5.77 us (3%)
    psum x1, waiting for transfers between devices, shards(): total_grad = lax.psum(gradient, 'ctx')  88.3 us
    all_gather x1, blocking collectives, shards(): initial = lax.all_gather(fast_init, 'ctx', axis=1, tiled=True)[0]  29.3 us
    ppermute x8, waiting for transfers between devices, passed_along(): return lax.ppermute(value, axis, pairs)  21.6 us
    all_to_all x1, blocking collectives, shards(): lax.all_to_all(gated_out, 'head', split_axis=1, concat_axis=2, tiled=True)  9.12 us
    ppermute x8, starting transfers between devices, passed_along(): return lax.ppermute(value, axis, pairs)  6.47 us
  transfers between devices with their start and end apart: 9, of which 5 were waited for; matrix products, arithmetic and copies ran while one was open for 12% of the time, Pallas kernels for 0%

commit v1 on v0

v1 whole, which is shorter than its diff:
```python
import functools

import jax
import jax.numpy as jnp
from jax import lax
from jax.experimental import pallas as pl
from jax.experimental.pallas import tpu as pltpu
from jax.sharding import PartitionSpec as P

WIN = 1024
A_COEF = 3.4445
B_COEF = -4.775
C_COEF = 2.0315
BF = jnp.bfloat16
F32 = jnp.float32
VMEM_LIMIT = 48 * 1024 * 1024


def dot_nn(a, b):
    return lax.dot_general(a, b, (((1,), (0,)), ((), ())), preferred_element_type=F32)


def dot_nt(a, b):
    return lax.dot_general(a, b, (((1,), (1,)), ((), ())), preferred_element_type=F32)


def dot_tn(a, b):
    return lax.dot_general(a, b, (((0,), (0,)), ((), ())), preferred_element_type=F32)


def swapped(value, mask, axis="ctx"):
    count = lax.axis_size(axis)
    return lax.ppermute(value, axis, [(i, i ^ mask) for i in range(count)])


def vmem_spec():
    return pl.BlockSpec(memory_space=pltpu.VMEM)


def call(body, args, outs, scratch=(), cost=None):
    return pl.pallas_call(
        body,
        out_shape=outs,
        in_specs=[pl.BlockSpec(memory_space=pltpu.SMEM)] + [vmem_spec()] * (len(args) - 1),
        out_specs=jax.tree.map(lambda _: vmem_spec(), outs),
        scratch_shapes=list(scratch),
        compiler_params=pltpu.CompilerParams(vmem_limit_bytes=VMEM_LIMIT),
        cost_estimate=cost,
    )(*args)


def cost_of(flops, moved):
    return pl.CostEstimate(flops=int(flops), bytes_accessed=int(moved), transcendentals=0)


def silu(v):
    return v / (1.0 + jnp.exp(-v))


def gradient_body(planes, ids, mine, other, pair_a, pair_b, send, keep, weights, total):
    plane, side = ids[0], ids[1]
    rows = mine.shape[1]
    for m in range(planes):
        base = ((plane ^ m) * 2) * rows
        weights[pl.ds(pl.multiple_of(base + side * rows, rows), rows), :] = mine[m]
        weights[pl.ds(pl.multiple_of(base + (1 - side) * rows, rows), rows), :] = other[m]
    half = weights.shape[1] // 3
    gate_up_w = weights[:, : 2 * half]
    out_w = weights[:, 2 * half :]
    first = None
    for pair in (pair_a, pair_b):
        key_rows, target = pair[0], pair[1]
        gate_up = dot_nn(key_rows, gate_up_w)
        g, u = gate_up[:, :half], gate_up[:, half:]
        dh = dot_nn(target, out_w)
        s = 1.0 / (1.0 + jnp.exp(-g))
        gs = g * s
        hidden = (gs * u).astype(BF)
        dg = dh * u * s * (1.0 + g * (1.0 - s))
        du = dh * gs
        joined = jnp.concatenate([dg, du], 1).astype(BF)
        in_grad = dot_tn(joined, key_rows)
        out_grad = dot_tn(hidden, target)
        first = (in_grad, out_grad) if first is None else (first[0] + in_grad, first[1] + out_grad)
    total[: 2 * half, :] = first[0]
    total[2 * half : 3 * half, :] = first[1]
    if total.shape[0] > 3 * half:
        total[3 * half :, :] = jnp.zeros((total.shape[0] - 3 * half, total.shape[1]), F32)
    part = send.shape[0]
    send[...] = total[pl.ds(pl.multiple_of((1 - side) * part, part), part), :].astype(BF)
    keep[...] = total[pl.ds(pl.multiple_of(side * part, part), part), :]


def side_sum_body(planes, ids, keep, got, *refs):
    outs, total = refs[:planes], refs[planes]
    plane = ids[0]
    total[...] = keep[...] + got[...].astype(F32)
    part = outs[0].shape[0]
    for m in range(planes):
        rows = total[pl.ds(pl.multiple_of((plane ^ m) * part, part), part), :]
        outs[m][...] = rows.astype(outs[m].dtype)


def plane_sum_body(ids, own, *refs):
    total = own[...]
    for ref in refs[:-1]:
        total = total + ref[...].astype(F32)
    refs[-1][...] = total.astype(BF)


def weights_body(planes, ids, mine, other, beside, whole, flipped, norms):
    plane, side, core = ids[0], ids[1], ids[2]
    rows = mine.shape[1]
    half = mine.shape[2] // 3
    for m in range(planes):
        for far in range(2):
            base = ((plane ^ m) * 2 + (side if far == 0 else 1 - side)) * rows
            block_k = (mine, other)[far][m]
            block_c = beside[far * planes + m]
            low = jnp.where(core == 0, block_k, block_c)
            high = jnp.where(core == 0, block_c, block_k)
            where = pl.ds(pl.multiple_of(base, rows), rows)
            for b in range(3):
                whole[where, 2 * b * half : (2 * b + 1) * half] = low[:, b * half : (b + 1) * half]
                whole[where, (2 * b + 1) * half : (2 * b + 2) * half] = high[
                    :, b * half : (b + 1) * half
                ]
    width = whole.shape[1]
    for b in range(3):
        cols = slice(b * width // 3, (b + 1) * width // 3)
        turned = whole[:, cols].astype(F32).T
        flipped[cols, :] = turned
        norms[cols, :] = jnp.sqrt(jnp.sum(turned * turned, 1, keepdims=True))


def window(ids, q, k_own, v_own, first_group, far_pair, full_pairs):
    rows, depth = q.shape
    scale = depth**-0.5
    row = lax.broadcasted_iota(jnp.int32, (rows, rows), 0)
    col = lax.broadcasted_iota(jnp.int32, (rows, rows), 1)
    blocks = [(k_own, v_own, col <= row)]
    far_ok = col > row
    for keys, values, live in [far_pair] + full_pairs:
        allowed = far_ok if keys is far_pair[0] else None
        if first_group:
            alive = jnp.full((rows, rows), live, jnp.int32) != 0
            allowed = alive if allowed is None else allowed & alive
        blocks.append((keys, values, allowed))
    scores = []
    for keys, values, allowed in blocks:
        s = dot_nt(q, keys) * scale
        scores.append(s if allowed is None else jnp.where(allowed, s, -1e30))
    top = jnp.max(scores[0], -1, keepdims=True)
    for s in scores[1:]:
        top = jnp.maximum(top, jnp.max(s, -1, keepdims=True))
    total = None
    out = None
    for s, (keys, values, allowed) in zip(scores, blocks):
        e = jnp.exp(s - top)
        t = jnp.sum(e, -1, keepdims=True)
        o = dot_nn(e.astype(BF), values)
        total = t if total is None else total + t
        out = o if out is None else out + o
    return out / total


def live_flags(ids):
    plane, side, core = ids[0], ids[1], ids[2]
    later = (plane > 0).astype(jnp.int32)
    side_live = jnp.maximum(later, side)
    core_live = jnp.maximum(later, core)
    return later, side_live, core_live


def first_group_body(ids, q, k_own, v_own, far, near, core, gates, whole, out):
    later, side_live, core_live = live_flags(ids)
    pairs = [
        (near[0], near[1], side_live),
        (core[0], core[1], core_live),
        (core[2], core[3], side_live),
    ]
    win = window(ids, q[0], k_own[0], v_own[0], True, (far[0], far[1], later), pairs)
    width = whole.shape[1] // 3
    gate_up = dot_nn(q[0], whole[:, : 2 * width])
    hidden = (silu(gate_up[:, :width]) * gate_up[:, width:]).astype(BF)
    fast = dot_nt(hidden, whole[:, 2 * width :])
    gate = gates[0].astype(F32)
    out[...] = ((win + fast) * silu(gate)).astype(BF)


def second_group_body(ids, q, k_own, v_own, far, near, core, out):
    pairs = [(near[0], near[1], 1), (core[0], core[1], 1), (core[2], core[3], 1)]
    out[...] = window(ids, q[0], k_own[0], v_own[0], False, (far[0], far[1], 1), pairs)


def group_call(body, index, ids, grouped, others, outs, cost):
    def spec(a):
        tail = (0,) * (a.ndim - 1)
        return pl.BlockSpec((1,) + a.shape[1:], lambda i: (index,) + tail)

    def full(a):
        return pl.BlockSpec(a.shape, lambda i, nd=a.ndim: (0,) * nd)

    specs, args = [], []
    for a, is_grouped in grouped:
        specs.append(spec(a) if is_grouped else full(a))
        args.append(a)
    for a in others:
        specs.append(full(a))
        args.append(a)
    return pl.pallas_call(
        body,
        grid=(1,),
        out_shape=outs,
        in_specs=[pl.BlockSpec(memory_space=pltpu.SMEM)] + specs,
        out_specs=pl.BlockSpec(outs.shape, lambda i: (0,) * len(outs.shape)),
        compiler_params=pltpu.CompilerParams(vmem_limit_bytes=VMEM_LIMIT),
        cost_estimate=cost,
    )(ids, *args)


def update_body(planes, ids, rate, mine, other, flipped, norms, q, win, gates, out, grads):
    plane, side, core = ids[0], ids[1], ids[2]
    part = mine.shape[1]
    for m in range(planes):
        for far in range(2):
            base = ((side if far == 0 else 1 - side) * planes + (plane ^ m)) * part
            where = pl.ds(pl.multiple_of(base, part), part)
            grads[core, where, :] = mine[far * planes + m]
            grads[1 - core, where, :] = other[far * planes + m]
    width = flipped.shape[0] // 3
    half = width // 2
    turned = []
    for b in range(3):
        block = jnp.concatenate(
            [grads[0, b * half : (b + 1) * half, :], grads[1, b * half : (b + 1) * half, :]], 0
        ).astype(F32)
        length = jnp.sqrt(jnp.sum(block * block, keepdims=True))
        turned.append((block / (length + 1e-06)).astype(BF))
    for _ in range(3):
        grams = [dot_nt(y, y) for y in turned]
        lows = [a.astype(BF) for a in grams]
        squares = [dot_nn(a, a) for a in lows]
        mixers = [(B_COEF * a + C_COEF * s).astype(BF) for a, s in zip(grams, squares)]
        turned = [
            (A_COEF * y.astype(F32) + dot_nn(b, y)).astype(BF) for b, y in zip(mixers, turned)
        ]
    fresh = []
    for b in range(3):
        cols = slice(b * width, (b + 1) * width)
        moved = flipped[cols, :] - rate[0] * turned[b].astype(F32)
        length = jnp.sqrt(jnp.sum(moved * moved, 1, keepdims=True))
        fresh.append((moved * (norms[cols, :] / (length + 1e-06))).astype(BF))
    x = q[...]
    g = dot_nt(x, fresh[0])
    u = dot_nt(x, fresh[1])
    hidden = (silu(g) * u).astype(BF)
    fast = dot_nn(hidden, fresh[2])
    gate = gates[...].astype(F32)
    out[...] = ((win[...] + fast) * silu(gate)).astype(BF)


def norm_body(ids, own, got, gain, out):
    head = ids[3]
    rows, depth = own.shape
    a = own[...].astype(F32)
    b = got[...].astype(F32)
    low = jnp.where(head == 0, a, b)
    high = jnp.where(head == 0, b, a)
    square = jnp.sum(a * a, -1, keepdims=True) + jnp.sum(b * b, -1, keepdims=True)
    inv = lax.rsqrt(square / (2 * depth) + 1e-06)
    out[:, :depth] = (low * inv * gain[:, :depth]).astype(BF)
    out[:, depth:] = (high * inv * gain[:, depth:]).astype(BF)


def finished(ids, gated, norm_gain):
    heads = lax.axis_size("head")
    rows = gated.shape[0] // heads
    if heads == 2:
        own_head = lax.axis_index("head")
        low, high = gated[:rows], gated[rows:]
        own = jnp.where(own_head == 0, low, high)
        got = swapped(jnp.where(own_head == 0, high, low), 1, "head")
        return call(
            norm_body,
            (ids, own, got, norm_gain[None, :]),
            jax.ShapeDtypeStruct((rows, norm_gain.shape[0]), BF),
            cost=cost_of(0, 4 * rows * norm_gain.shape[0]),
        )
    wide = lax.all_to_all(gated, "head", split_axis=0, concat_axis=1, tiled=True).astype(F32)
    inv = lax.rsqrt(jnp.mean(wide * wide, -1, keepdims=True) + 1e-06)
    return (wide * inv * norm_gain).astype(BF)


def shards(queries, keys, values, gates, token_rates, fast_init, fast_rate, norm_gain):
    count = lax.axis_size("ctx")
    rows, depth = queries.shape[1], queries.shape[2]
    reach = (WIN - 1) // rows + 1
    planes = count // reach
    if reach != 4 or WIN % rows or planes * reach != count or planes & (planes - 1):
        raise ValueError("unsupported shapes")
    position = lax.axis_index("ctx")
    plane, side, core = position // 4, (position // 2) % 2, position % 2
    ids = jnp.stack([plane, side, core, lax.axis_index("head")]).astype(jnp.int32)
    width = fast_init.shape[2] // 3
    half = width // 2

    local = fast_init[0]
    fast_rows = local.shape[0]
    split = local.reshape(fast_rows, 3, 2, half)
    low, high = split[:, :, 0].reshape(fast_rows, -1), split[:, :, 1].reshape(fast_rows, -1)
    mine = jnp.where(core == 0, low, high)
    theirs = swapped(jnp.where(core == 0, high, low), 1)
    pair = jnp.concatenate(
        [jnp.where(core == 0, mine, theirs), jnp.where(core == 0, theirs, mine)], 0
    )
    target = (-token_rates * values[0].astype(F32)).astype(BF)
    grad_pair = jnp.stack([keys[0], target])
    grad_other = swapped(grad_pair, 1)
    mine_w = jnp.stack([pair] + [swapped(pair, 4 * m) for m in range(1, planes)])
    other_w = swapped(mine_w, 2)

    pieces = 2 * planes
    part = -(-3 * half // (16 * pieces)) * 16
    send, keep = call(
        functools.partial(gradient_body, planes),
        (ids, mine_w, other_w, grad_pair, grad_other),
        (
            jax.ShapeDtypeStruct((planes * part, depth), BF),
            jax.ShapeDtypeStruct((planes * part, depth), F32),
        ),
        scratch=(pltpu.VMEM((depth, 3 * half), BF), pltpu.VMEM((pieces * part, depth), F32)),
        cost=cost_of(2 * 2 * rows * depth * half * 6, 4 * rows * depth * 4),
    )
    got = swapped(send, 2)
    parts = call(
        functools.partial(side_sum_body, planes),
        (ids, keep, got),
        tuple(jax.ShapeDtypeStruct((part, depth), F32 if m == 0 else BF) for m in range(planes)),
        scratch=(pltpu.VMEM((planes * part, depth), F32),),
        cost=cost_of(0, planes * part * depth * 8),
    )
    arrived = [swapped(parts[m], 4 * m) for m in range(1, planes)]
    total = call(
        plane_sum_body,
        (ids, parts[0], *arrived),
        jax.ShapeDtypeStruct((part, depth), BF),
        cost=cost_of(0, planes * part * depth * 3),
    )
    stacked = jnp.stack([total] + [swapped(total, 4 * m) for m in range(1, planes)])
    side_grad = jnp.concatenate([stacked, swapped(stacked, 2)], 0)
    core_grad = swapped(side_grad, 1)

    last = plane == planes - 1
    windows = []
    for g in range(2):
        own = jnp.stack([keys[g], values[g]])
        if g == 0:
            pairs = [(i, i + reach) for i in range(count - reach)]
            far = lax.ppermute(own, "ctx", pairs)
        else:
            first = jnp.stack([keys[0], values[0]])
            pairs = [(i, (i + reach) % count) for i in range(count)]
            far = lax.ppermute(jnp.where(last, first, own), "ctx", pairs)
        near = swapped(jnp.where(side == 0, own, far), 2)
        beside = swapped(jnp.concatenate([jnp.where(core == 0, own, far), near], 0), 1)
        windows.append((far, near, beside))

    half_w = jnp.concatenate([mine_w, other_w], 0)
    beside_w = swapped(half_w, 1)
    whole, flipped, norms = call(
        functools.partial(weights_body, planes),
        (ids, mine_w, other_w, beside_w),
        (
            jax.ShapeDtypeStruct((depth, 3 * width), BF),
            jax.ShapeDtypeStruct((3 * width, depth), F32),
            jax.ShapeDtypeStruct((3 * width, 1), F32),
        ),
        cost=cost_of(0, depth * width * 3 * 8),
    )
    attn_flops = 4 * rows * depth * 5 * rows
    far, near, beside = windows[0]
    gated_first = group_call(
        first_group_body,
        0,
        ids,
        [(queries, True), (keys, True), (values, True)]
        + [(far, False), (near, False), (beside, False)]
        + [(gates, True)],
        [whole],
        jax.ShapeDtypeStruct((rows, depth), BF),
        cost_of(attn_flops * 2, rows * depth * 30),
    )
    far, near, beside = windows[1]
    window_second = group_call(
        second_group_body,
        1,
        ids,
        [(queries, True), (keys, True), (values, True)]
        + [(far, False), (near, False), (beside, False)],
        [],
        jax.ShapeDtypeStruct((rows, depth), F32),
        cost_of(attn_flops * 2, rows * depth * 30),
    )
    done_first = finished(ids, gated_first, norm_gain)

    gated_second = pl.pallas_call(
        functools.partial(update_body, planes),
        grid=(1,),
        out_shape=jax.ShapeDtypeStruct((rows, depth), BF),
        in_specs=[
            pl.BlockSpec(memory_space=pltpu.SMEM),
            pl.BlockSpec(memory_space=pltpu.SMEM),
            pl.BlockSpec(side_grad.shape, lambda i: (0, 0, 0)),
            pl.BlockSpec(core_grad.shape, lambda i: (0, 0, 0)),
            pl.BlockSpec(flipped.shape, lambda i: (0, 0)),
            pl.BlockSpec(norms.shape, lambda i: (0, 0)),
            pl.BlockSpec((None, rows, depth), lambda i: (1, 0, 0)),
            pl.BlockSpec((rows, depth), lambda i: (0, 0)),
            pl.BlockSpec((None, rows, depth), lambda i: (1, 0, 0)),
        ],
        out_specs=pl.BlockSpec((rows, depth), lambda i: (0, 0)),
        scratch_shapes=[pltpu.VMEM((2, pieces * part, depth), BF)],
        compiler_params=pltpu.CompilerParams(vmem_limit_bytes=VMEM_LIMIT),
        cost_estimate=cost_of(3e9, 4e6),
    )(ids, fast_rate, side_grad, core_grad, flipped, norms, queries, window_second, gates)
    done_second = finished(ids, gated_second, norm_gain)
    return jnp.stack([done_first, done_second])


def solution(mesh):
    placed = (
        P(None, "ctx", "head"),
        P(None, "ctx", "head"),
        P(None, "ctx", "head"),
        P(None, "ctx", "head"),
        P("ctx", "head"),
        P("head", "ctx", None),
        P("head"),
        P(),
    )
    return jax.shard_map(
        shards,
        mesh=mesh,
        in_specs=placed,
        out_specs=P(None, ("ctx", "head"), None),
        check_vma=False,
    )
```

time: 201 us -> 89.8 us (0.45)
  waiting for transfers between devices: 110 us -> 35.5 us
  blocking collectives: 38.4 us -> 0 us
  starting transfers between devices: 6.47 us -> 29 us
  Pallas kernels: 0 us -> 14.9 us
  between operations: 14.5 us -> 1.13 us
  matrix products: 12.3 us -> 0 us
  other arithmetic: 13.3 us -> 4.24 us
    psum x1 -> x0, waiting for transfers between devices: 88.3 us -> none  [shards(): total_grad = lax.psum(gradient, 'ctx')]
    all_gather x1 -> x0, blocking collectives: 29.3 us -> none  [shards(): initial = lax.all_gather(fast_init, 'ctx', axis=1, tiled=True)[0]]
    ppermute x8 -> x24, starting transfers between devices: 6.47 us -> 29 us  [the longest x22 21.7 us: swapped(): return lax.ppermute(value, axis, [(i, i ^ mask) for i in range(count)])]
    pallas_call x0 -> x9, Pallas kernels: none -> 14.9 us  [the longest x6 6.71 us: call(): pl.pallas_call(body, out_shape=outs, in_specs=[pl.BlockSpec(memory_space=...]
    ppermute x8 -> x24, waiting for transfers between devices: 21.6 us -> 35.5 us  [the longest x22 28.8 us: swapped(): return lax.ppermute(value, axis, [(i, i ^ mask) for i in range(count)])]
    dot_general x18 -> x0, matrix products: 12.3 us -> none  [the longest x3 2.95 us: newton_turn(): jnp.einsum('rmf,mfg->rmg', ortho, mixer_mat, preferred_element_type=jnp.f...]
    all_to_all x1 -> x0, blocking collectives: 9.12 us -> none  [shards(): lax.all_to_all(gated_out, 'head', split_axis=1, concat_axis=2, tiled=True)]
    slice x8 -> x0, other arithmetic: 6.02 us -> none  [the longest x4 3.02 us: shards(): recv_values[0]]
  transfers between devices with their start and end apart: 9 -> 24, of which waited for: 5 -> 11; matrix products, arithmetic and copies ran while one was open for 12% -> 8% of each run, Pallas kernels for 0% -> 16%
where the time goes in v1:
time: 89.8 us; the launch traced here: 89.5 us
  waiting for transfers between devices  35.5 us (40%)
  starting transfers between devices  29 us (32%)
  Pallas kernels  14.9 us (17%)
  local copies, waits for them, and re-layouts  4.8 us (5%)
  other arithmetic  4.24 us (5%)
  between operations  1.13 us (1%)
    ppermute x22, waiting for transfers between devices, swapped(): return lax.ppermute(value, axis, [(i, i ^ mask) for i in range(count)])  28.8 us
    ppermute x22, starting transfers between devices, swapped(): return lax.ppermute(value, axis, [(i, i ^ mask) for i in range(count)])  21.7 us
    pallas_call x6, Pallas kernels, call(): pl.pallas_call(body, out_shape=outs, in_specs=[pl.BlockSpec(memory_space=...  6.71 us
    ppermute x1, waiting for transfers between devices, shards(): far = lax.ppermute(jnp.where(last, first, own), 'ctx', pairs)  6.66 us
    ppermute x1, starting transfers between devices, shards(): far = lax.ppermute(own, 'ctx', pairs)  4.58 us
    pallas_call x2, Pallas kernels, group_call(): pl.pallas_call(body, grid=(1,), out_shape=outs, in_specs=[pl.BlockSpec(me...  4.4 us
    pallas_call x1, Pallas kernels, shards(): pl.pallas_call(functools.partial(update_body, planes), grid=(1,), out_sha...  3.81 us
    ppermute x1, starting transfers between devices, shards(): far = lax.ppermute(jnp.where(last, first, own), 'ctx', pairs)  2.68 us
  transfers between devices with their start and end apart: 24, of which 11 were waited for; matrix products, arithmetic and copies ran while one was open for 8% of the time, Pallas kernels for 16%

profile of v1, /device:TPU:0, one launch (start us, length us, event | category | flops | bytes accessed | tf_op | source)
XLA Modules:
  0.0 89.5 jit_solution(12439498472629811929)
XLA Ops:
  0.0 0.8 reshape_squeeze.2
  0.8 0.1 fusion.3
  1.0 0.0 copy-start.11
  1.0 0.0 copy-start
  1.0 0.5 collective-permute-start.3
  1.5 1.3 %fusion.1 = (bf16[1,256,512]{2,1,0:T(8,128)(2,1)S(1)}, bf16[1,256,512]{2,1,0:T(8,128)(2,1)S(1)}, bf16[1,256,512]{2,1,0:T(8,128)(2,1)S(1)}, bf16[1,256,512]{2,1,0:T(8,128)(2,1)S(1)}) fusion(bf16[2,256,512]{2,1,0:T(8,128)(2,1)} %v_own.3, bf16[2,256,512]{2,1,0:T(8,128)(2,1)} %k_own.3), kind=kLoop, calls=%fused_computation.36 | loop fusion | bytes 2097152 | tf_op jit(solution)/shard_map/slice | solution.py:357
  2.8 0.1 pad_maximum_fusion.3
  2.8 4.6 %collective-permute-start = (bf16[2,256,512]{2,1,0:T(8,128)(2,1)S(1)}, bf16[2,256,512]{2,1,0:T(8,128)(2,1)S(1)}, u32[]{:S(2)}, u32[]{:S(2)}) collective-permute-start(bf16[2,256,512]{2,1,0:T(8,128)(2,1)S(1)} %pad_maximum_fusion.3), channel_id=1, source_target_pairs={{0,8},{2,10},{4,12},{6,14},{8,16},{10,18},{12,20},{14,22},{16,24},... | collective-permute-start | bytes 1572872 | tf_op jit(solution)/shard_map/ppermute | solution.py:360
  7.5 0.1 multiply_convert_fusion
  7.6 0.0 collective-permute-done.3
  7.7 2.6 %collective-permute-start.5 = (bf16[64,384]{1,0:T(8,128)(2,1)S(1)}, bf16[64,384]{1,0:T(8,128)(2,1)S(1)}, u32[]{:S(2)}, u32[]{:S(2)}) collective-permute-start(bf16[64,384]{1,0:T(8,128)(2,1)S(1)} %get-tuple-element.42), channel_id=1, source_target_pairs={{0,16},{2,18},{4,20},{6,22},{8,24},{10,26},{12,28},{14,30},{16,0},... | collective-permute-start | bytes 147464 | tf_op jit(solution)/shard_map/ppermute | solution.py:33
  10.3 1.8 %collective-permute-start.6 = (bf16[64,384]{1,0:T(8,128)(2,1)S(1)}, bf16[64,384]{1,0:T(8,128)(2,1)S(1)}, u32[]{:S(2)}, u32[]{:S(2)}) collective-permute-start(bf16[64,384]{1,0:T(8,128)(2,1)S(1)} %get-tuple-element.42), channel_id=1, source_target_pairs={{0,24},{2,26},{4,28},{6,30},{8,16},{10,18},{12,20},{14,22},{16,8},... | collective-permute-start | bytes 147464 | tf_op jit(solution)/shard_map/ppermute | solution.py:33
  12.1 0.6 constant_dynamic-update-slice_fusion.4
  12.7 7.9 %collective-permute-done.5 = bf16[64,384]{1,0:T(8,128)(2,1)S(1)} collective-permute-done((bf16[64,384]{1,0:T(8,128)(2,1)S(1)}, bf16[64,384]{1,0:T(8,128)(2,1)S(1)}, u32[]{:S(2)}, u32[]{:S(2)}) %collective-permute-start.5) | collective-permute-done | bytes 49184 | tf_op jit(solution)/shard_map/ppermute | solution.py:33
  20.7 1.1 %collective-permute-done.4 = bf16[64,384]{1,0:T(8,128)(2,1)S(1)} collective-permute-done((bf16[64,384]{1,0:T(8,128)(2,1)S(1)}, bf16[64,384]{1,0:T(8,128)(2,1)S(1)}, u32[]{:S(2)}, u32[]{:S(2)}) %collective-permute-start.4) | collective-permute-done | bytes 49184 | tf_op jit(solution)/shard_map/ppermute | solution.py:33
  21.7 0.6 collective-permute-done.6
  22.4 1.6 %collective-permute-start.7 = (bf16[4,64,384]{2,1,0:T(8,128)(2,1)S(1)}, bf16[4,64,384]{2,1,0:T(8,128)(2,1)S(1)}, u32[]{:S(2)}, u32[]{:S(2)}) collective-permute-start(bf16[4,64,384]{2,1,0:T(8,128)(2,1)S(1)} %pad_maximum_fusion.6.mine), channel_id=1, source_target_pairs={{0,4},{2,6},{4,0},{6,2},{8,12},{10,14},{12,8},{14,10},{16,20},{18,... | collective-permute-start | bytes 589832 | tf_op jit(solution)/shard_map/ppermute | solution.py:33
  23.9 0.6 constant_dynamic-update-slice_fusion.3
  24.5 0.0 collective-permute-done.far
  24.5 1.1 %broadcast_select_fusion.2 = (bf16[2,256,512]{2,1,0:T(8,128)(2,1)}, bf16[2,256,512]{2,1,0:T(8,128)(2,1)}, bf16[2,256,512]{2,1,0:T(8,128)(2,1)S(1)}, bf16[2,256,512]{2,1,0:T(8,128)(2,1)S(1)}) fusion(bf16[2,256,512]{2,1,0:T(8,128)(2,1)S(1)} %collective-permute-done.far, pred[]{:T(512)S(6)} %eq.13, bf16[1,256,512]{2,1,0:T(8,128)(2,1)S(1)} %get-tuple-element.28, ...), kind=kLoop, calls=%fused_computation.9 | loop fusion | flops 1572864 | bytes 3932163 | tf_op jit(solution)/shard_map/jit(_where)/select_n | solution.py:366
  25.7 2.7 %collective-permute-start.20 = (bf16[2,256,512]{2,1,0:T(8,128)(2,1)S(1)}, bf16[2,256,512]{2,1,0:T(8,128)(2,1)S(1)}, u32[]{:S(2)}, u32[]{:S(2)}) collective-permute-start(bf16[2,256,512]{2,1,0:T(8,128)(2,1)S(1)} %get-tuple-element.27), channel_id=1, source_target_pairs={{0,8},{2,10},{4,12},{6,14},{8,16},{10,18},{12,20},{14,22},{16,24},... | collective-permute-start | bytes 1572872 | tf_op jit(solution)/shard_map/ppermute | solution.py:364
  28.4 0.6 constant_dynamic-update-slice_fusion.2
  29.0 0.6 constant_dynamic-update-slice_fusion.1
  29.6 0.5 collective-permute-start.1
  30.1 0.0 collective-permute-done.7.other
  30.1 0.7 constant_dynamic-update-slice_fusion
  30.8 0.2 collective-permute-start.8
  31.1 0.1 pad_add_fusion.ids
  31.1 2.2 %shard_map.85 = (bf16[192,512]{1,0:T(8,128)(2,1)}, f32[192,512]{1,0:T(8,128)S(1)}) custom-call(s32[4]{0:T(128)S(1)} %pad_add_fusion.ids, bf16[4,64,384]{2,1,0:T(8,128)(2,1)S(1)} %pad_maximum_fusion.6.mine, bf16[4,64,384]{2,1,0:T(8,128)(2,1)S(1)} %collective-permute-done.7.other, bf16[2,256,512]{2,1,0:T(8,128)(2,1)S(1)} %get-tuple-element.34.pair_a, ...), custom_call_target="tpu_custom_call" | custom-call | flops 402653184 | bytes 2097152 | tf_op jit(solution)/shard_map/pallas_call | solution.py:41
  33.3 1.5 %collective-permute-start.11 = (bf16[192,512]{1,0:T(8,128)(2,1)}, bf16[192,512]{1,0:T(8,128)(2,1)}, u32[]{:S(2)}, u32[]{:S(2)}) collective-permute-start(bf16[192,512]{1,0:T(8,128)(2,1)} %get-tuple-element.16), channel_id=1, source_target_pairs={{0,4},{2,6},{4,0},{6,2},{8,12},{10,14},{12,8},{14,10},{16,20},{18,... | collective-permute-start | bytes 589832 | tf_op jit(solution)/shard_map/ppermute | solution.py:33
  34.8 6.7 %collective-permute-done.20.far = bf16[2,256,512]{2,1,0:T(8,128)(2,1)S(1)} collective-permute-done((bf16[2,256,512]{2,1,0:T(8,128)(2,1)S(1)}, bf16[2,256,512]{2,1,0:T(8,128)(2,1)S(1)}, u32[]{:S(2)}, u32[]{:S(2)}) %collective-permute-start.20) | collective-permute-done | bytes 524320 | tf_op jit(solution)/shard_map/ppermute | solution.py:364
  41.5 1.1 %broadcast_select_fusion.1 = (bf16[2,256,512]{2,1,0:T(8,128)(2,1)}, bf16[2,256,512]{2,1,0:T(8,128)(2,1)}) fusion(bf16[2,256,512]{2,1,0:T(8,128)(2,1)S(1)} %collective-permute-done.20.far, pred[]{:T(512)S(6)} %eq.13, bf16[1,256,512]{2,1,0:T(8,128)(2,1)S(1)} %copy-done.6, bf16[1,256,512]{2,1,0:T(8,128)(2,1)S(1)} %copy-done.8, pred[]{:T(512)S(6)} %eq.12), kind=kLoop, calls=%fused_computation.8 | loop fusion | flops 786432 | bytes 2097154 | tf_op jit(solution)/shard_map/jit(_where)/select_n | solution.py:366
  42.5 0.5 collective-permute-start.21
  43.8 1.5 %shard_map.82 = (bf16[512,768]{1,0:T(8,128)(2,1)S(1)}, f32[768,512]{1,0:T(8,128)S(1)}, f32[768,1]{1,0:T(8,128)S(1)}) custom-call(s32[4]{0:T(128)S(1)} %pad_add_fusion.ids, bf16[4,64,384]{2,1,0:T(8,128)(2,1)S(1)} %pad_maximum_fusion.6.mine, bf16[4,64,384]{2,1,0:T(8,128)(2,1)S(1)} %collective-permute-done.7.other, ...), custom_call_target="tpu_custom_call" | custom-call | bytes 3145728 | tf_op jit(solution)/shard_map/pallas_call | solution.py:41
  45.3 3.5 %collective-permute-done.11.got = bf16[192,512]{1,0:T(8,128)(2,1)} collective-permute-done((bf16[192,512]{1,0:T(8,128)(2,1)}, bf16[192,512]{1,0:T(8,128)(2,1)}, u32[]{:S(2)}, u32[]{:S(2)}) %collective-permute-start.11) | collective-permute-done | bytes 196640 | tf_op jit(solution)/shard_map/ppermute | solution.py:33
  48.8 1.0 %shard_map.86 = (f32[48,512]{1,0:T(8,128)S(1)}, bf16[48,512]{1,0:T(8,128)(2,1)S(1)}, bf16[48,512]{1,0:T(8,128)(2,1)S(1)}, bf16[48,512]{1,0:T(8,128)(2,1)S(1)}) custom-call(s32[4]{0:T(128)S(1)} %pad_add_fusion.ids, f32[192,512]{1,0:T(8,128)S(1)} %get-tuple-element.15.keep, bf16[192,512]{1,0:T(8,128)(2,1)} %collective-permute-done.11.got), custom_call_target="tpu_custom_call" | custom-call | bytes 786432 | tf_op jit(solution)/shard_map/pallas_call | solution.py:41
  49.9 2.5 %collective-permute-start.12 = (bf16[48,512]{1,0:T(8,128)(2,1)S(1)}, bf16[48,512]{1,0:T(8,128)(2,1)S(1)}, u32[]{:S(2)}, u32[]{:S(2)}) collective-permute-start(bf16[48,512]{1,0:T(8,128)(2,1)S(1)} %get-tuple-element.18), channel_id=1, source_target_pairs={{0,8},{2,10},{4,12},{6,14},{8,0},{10,2},{12,4},{14,6},{16,24},{18,... | collective-permute-start | bytes 147464 | tf_op jit(solution)/shard_map/ppermute | solution.py:33
  52.4 0.4 collective-permute-start.13
  52.8 2.0 %collective-permute-start.14 = (bf16[48,512]{1,0:T(8,128)(2,1)S(1)}, bf16[48,512]{1,0:T(8,128)(2,1)S(1)}, u32[]{:S(2)}, u32[]{:S(2)}) collective-permute-start(bf16[48,512]{1,0:T(8,128)(2,1)S(1)} %get-tuple-element.20), channel_id=1, source_target_pairs={{0,24},{2,26},{4,28},{6,30},{8,16},{10,18},{12,20},{14,22},{16,8},... | collective-permute-start | bytes 147464 | tf_op jit(solution)/shard_map/ppermute | solution.py:33
  54.9 0.1 pad_maximum_fusion
  54.9 0.1 collective-permute-start.2
  55.0 2.9 %collective-permute-done.13.refs_1_ = bf16[48,512]{1,0:T(8,128)(2,1)S(1)} collective-permute-done((bf16[48,512]{1,0:T(8,128)(2,1)S(1)}, bf16[48,512]{1,0:T(8,128)(2,1)S(1)}, u32[]{:S(2)}, u32[]{:S(2)}) %collective-permute-start.13) | collective-permute-done | bytes 49184 | tf_op jit(solution)/shard_map/ppermute | solution.py:33
  57.9 0.9 collective-permute-done.14.refs_2_
  58.8 0.6 shard_map.87
  59.4 2.1 %collective-permute-start.17 = (bf16[48,512]{1,0:T(8,128)(2,1)S(1)}, bf16[48,512]{1,0:T(8,128)(2,1)S(1)}, u32[]{:S(2)}, u32[]{:S(2)}) collective-permute-start(bf16[48,512]{1,0:T(8,128)(2,1)S(1)} %shard_map.87), channel_id=1, source_target_pairs={{0,24},{2,26},{4,28},{6,30},{8,16},{10,18},{12,20},{14,22},{16,8},... | collective-permute-start | bytes 147464 | tf_op jit(solution)/shard_map/ppermute | solution.py:33
  61.5 0.2 collective-permute-start.16
  61.6 2.2 %collective-permute-start.15 = (bf16[48,512]{1,0:T(8,128)(2,1)S(1)}, bf16[48,512]{1,0:T(8,128)(2,1)S(1)}, u32[]{:S(2)}, u32[]{:S(2)}) collective-permute-start(bf16[48,512]{1,0:T(8,128)(2,1)S(1)} %shard_map.87), channel_id=1, source_target_pairs={{0,8},{2,10},{4,12},{6,14},{8,0},{10,2},{12,4},{14,6},{16,24},{18,... | collective-permute-start | bytes 147464 | tf_op jit(solution)/shard_map/ppermute | solution.py:33
  63.8 1.5 %collective-permute-done.17 = bf16[48,512]{1,0:T(8,128)(2,1)S(1)} collective-permute-done((bf16[48,512]{1,0:T(8,128)(2,1)S(1)}, bf16[48,512]{1,0:T(8,128)(2,1)S(1)}, u32[]{:S(2)}, u32[]{:S(2)}) %collective-permute-start.17) | collective-permute-done | bytes 49184 | tf_op jit(solution)/shard_map/ppermute | solution.py:33
  65.3 1.1 %collective-permute-done.16 = bf16[48,512]{1,0:T(8,128)(2,1)S(1)} collective-permute-done((bf16[48,512]{1,0:T(8,128)(2,1)S(1)}, bf16[48,512]{1,0:T(8,128)(2,1)S(1)}, u32[]{:S(2)}, u32[]{:S(2)}) %collective-permute-start.16) | collective-permute-done | bytes 49184 | tf_op jit(solution)/shard_map/ppermute | solution.py:33
  66.5 0.6 collective-permute-start.18
  67.1 0.1 pad_maximum_fusion.1
  67.2 0.1 collective-permute-start.22
  67.3 4.9 %collective-permute-done.18 = bf16[4,48,512]{2,1,0:T(8,128)(2,1)S(1)} collective-permute-done((bf16[4,48,512]{2,1,0:T(8,128)(2,1)S(1)}, bf16[4,48,512]{2,1,0:T(8,128)(2,1)S(1)}, u32[]{:S(2)}, u32[]{:S(2)}) %collective-permute-start.18) | collective-permute-done | bytes 196640 | tf_op jit(solution)/shard_map/ppermute | solution.py:33
  72.3 0.1 collective-permute-start.19
  72.4 2.1 %shard_map.83 = bf16[256,512]{1,0:T(8,128)(2,1)S(1)} custom-call(s32[4]{0:T(128)S(1)} %pad_add_fusion.ids, bf16[2,256,512]{2,1,0:T(8,128)(2,1)S(1)} %copy-done.2, bf16[2,256,512]{2,1,0:T(8,128)(2,1)S(1)} %copy-done.1, bf16[2,256,512]{2,1,0:T(8,128)(2,1)S(1)} %copy-done, bf16[2,256,512]{2,1,0:T(8,128)(2,1)S(1)} %collective-permute-done.far, ...), custom_call_target="tpu_custom_call" | custom-call | flops 1342177280 | bytes 3932160 | tf_op jit(solution)/shard_map/pallas_call | solution.py:211
  74.6 1.6 %collective-permute-start.9 = (bf16[128,512]{1,0:T(8,128)(2,1)S(1)}, bf16[128,512]{1,0:T(8,128)(2,1)S(1)}, u32[]{:S(2)}, u32[]{:S(2)}) collective-permute-start(bf16[128,512]{1,0:T(8,128)(2,1)S(1)} %get-tuple-element.32), channel_id=1, source_target_pairs={{0,1},{1,0},{2,3},{3,2},{4,5},{5,4},{6,7},{7,6},{8,9},{9,8},{10,11... | collective-permute-start | bytes 393224 | tf_op jit(solution)/shard_map/ppermute | solution.py:33
  76.2 2.3 %shard_map.88.win = f32[256,512]{1,0:T(8,128)S(1)} custom-call(s32[4]{0:T(128)S(1)} %pad_add_fusion.ids, bf16[2,256,512]{2,1,0:T(8,128)(2,1)S(1)} %copy-done.2, bf16[2,256,512]{2,1,0:T(8,128)(2,1)S(1)} %copy-done.1, bf16[2,256,512]{2,1,0:T(8,128)(2,1)S(1)} %copy-done, bf16[2,256,512]{2,1,0:T(8,128)(2,1)S(1)} %collective-permute-done.20.far, ...), custom_call_target="tpu_custom_call" | custom-call | flops 1342177280 | bytes 3932160 | tf_op jit(solution)/shard_map/pallas_call | solution.py:211
  78.4 0.0 copy-start.4
  78.5 3.8 %shard_map.89 = bf16[256,512]{1,0:T(8,128)(2,1)S(1)} custom-call(s32[4]{0:T(128)S(1)} %pad_add_fusion.ids, f32[1]{0:T(128)S(6)} %copy.33.rate, bf16[8,48,512]{2,1,0:T(8,128)(2,1)S(1)} %constant_dynamic-update-slice_fusion.5.mine, bf16[8,48,512]{2,1,0:T(8,128)(2,1)S(1)} %collective-permute-done.19.other, f32[768,512]{1,0:T(8,128)S(1)} %get-tuple-element.21.flipped, ...), custom_call_target="tpu_custom_call" | custom-call | flops 3000000000 | bytes 4000000 | tf_op jit(solution)/shard_map/pallas_call | solution.py:407
  82.3 0.6 collective-permute-start.23
  82.9 0.7 shard_map.84
  83.6 4.4 %collective-permute-done.23.got = bf16[128,512]{1,0:T(8,128)(2,1)S(1)} collective-permute-done((bf16[128,512]{1,0:T(8,128)(2,1)S(1)}, bf16[128,512]{1,0:T(8,128)(2,1)S(1)}, u32[]{:S(2)}, u32[]{:S(2)}) %collective-permute-start.23) | collective-permute-done | bytes 131104 | tf_op jit(solution)/shard_map/ppermute | solution.py:33
  88.0 0.7 shard_map.90
  88.7 0.8 pad_maximum_fusion.5
  (47 shorter events, 0.3 us)
Async XLA Ops:
  1.0 6.5 %copy-start.11 = (f32[256,1]{0,1:T(1,128)S(1)}, f32[256,1]{0,1:T(1,128)}, u32[]{:S(2)}) copy-start(f32[256,1]{0,1:T(1,128)} %param.12) | copy-start | bytes 3076
  1.0 6.5 %copy-start = (bf16[2,256,512]{2,1,0:T(8,128)(2,1)S(1)}, bf16[2,256,512]{2,1,0:T(8,128)(2,1)}, u32[]{:S(2)}) copy-start(bf16[2,256,512]{2,1,0:T(8,128)(2,1)} %v_own.3) | copy-start | bytes 1572868
  1.0 6.6 %collective-permute-start.3 = (bf16[32,384]{1,0:T(8,128)(2,1)S(1)}, bf16[32,384]{1,0:T(8,128)(2,1)S(1)}, u32[]{:S(2)}, u32[]{:S(2)}) collective-permute-start(bf16[32,384]{1,0:T(8,128)(2,1)S(1)} %bitcast.50), channel_id=1, source_target_pairs={{0,2},{2,0},{4,6},{6,4},{8,10},{10,8},{12,14},{14,12},{16,18},{18,... | collective-permute-start | bytes 73736 | tf_op jit(solution)/shard_map/ppermute | solution.py:33
  2.8 22.9 %copy-start.5 = (bf16[1,256,512]{2,1,0:T(8,128)(2,1)}, bf16[1,256,512]{2,1,0:T(8,128)(2,1)S(1)}, u32[]{:S(2)}) copy-start(bf16[1,256,512]{2,1,0:T(8,128)(2,1)S(1)} %get-tuple-element.29) | copy-start | bytes 786436
  2.8 22.9 %copy-start.7 = (bf16[1,256,512]{2,1,0:T(8,128)(2,1)}, bf16[1,256,512]{2,1,0:T(8,128)(2,1)S(1)}, u32[]{:S(2)}) copy-start(bf16[1,256,512]{2,1,0:T(8,128)(2,1)S(1)} %get-tuple-element.46) | copy-start | bytes 786436
  2.8 21.7 %collective-permute-start = (bf16[2,256,512]{2,1,0:T(8,128)(2,1)S(1)}, bf16[2,256,512]{2,1,0:T(8,128)(2,1)S(1)}, u32[]{:S(2)}, u32[]{:S(2)}) collective-permute-start(bf16[2,256,512]{2,1,0:T(8,128)(2,1)S(1)} %pad_maximum_fusion.3), channel_id=1, source_target_pairs={{0,8},{2,10},{4,12},{6,14},{8,16},{10,18},{12,20},{14,22},{16,24},... | collective-permute-start | bytes 1572872 | tf_op jit(solution)/shard_map/ppermute | solution.py:360
  7.7 13.0 %collective-permute-start.5 = (bf16[64,384]{1,0:T(8,128)(2,1)S(1)}, bf16[64,384]{1,0:T(8,128)(2,1)S(1)}, u32[]{:S(2)}, u32[]{:S(2)}) collective-permute-start(bf16[64,384]{1,0:T(8,128)(2,1)S(1)} %get-tuple-element.42), channel_id=1, source_target_pairs={{0,16},{2,18},{4,20},{6,22},{8,24},{10,26},{12,28},{14,30},{16,0},... | collective-permute-start | bytes 147464 | tf_op jit(solution)/shard_map/ppermute | solution.py:33
  10.3 11.4 %collective-permute-start.4 = (bf16[64,384]{1,0:T(8,128)(2,1)S(1)}, bf16[64,384]{1,0:T(8,128)(2,1)S(1)}, u32[]{:S(2)}, u32[]{:S(2)}) collective-permute-start(bf16[64,384]{1,0:T(8,128)(2,1)S(1)} %get-tuple-element.42), channel_id=1, source_target_pairs={{0,8},{2,10},{4,12},{6,14},{8,0},{10,2},{12,4},{14,6},{16,24},{18,... | collective-permute-start | bytes 147464 | tf_op jit(solution)/shard_map/ppermute | solution.py:33
  10.3 12.0 %collective-permute-start.6 = (bf16[64,384]{1,0:T(8,128)(2,1)S(1)}, bf16[64,384]{1,0:T(8,128)(2,1)S(1)}, u32[]{:S(2)}, u32[]{:S(2)}) collective-permute-start(bf16[64,384]{1,0:T(8,128)(2,1)S(1)} %get-tuple-element.42), channel_id=1, source_target_pairs={{0,24},{2,26},{4,28},{6,30},{8,16},{10,18},{12,20},{14,22},{16,8},... | collective-permute-start | bytes 147464 | tf_op jit(solution)/shard_map/ppermute | solution.py:33
  22.4 7.8 %collective-permute-start.7 = (bf16[4,64,384]{2,1,0:T(8,128)(2,1)S(1)}, bf16[4,64,384]{2,1,0:T(8,128)(2,1)S(1)}, u32[]{:S(2)}, u32[]{:S(2)}) collective-permute-start(bf16[4,64,384]{2,1,0:T(8,128)(2,1)S(1)} %pad_maximum_fusion.6.mine), channel_id=1, source_target_pairs={{0,4},{2,6},{4,0},{6,2},{8,12},{10,14},{12,8},{14,10},{16,20},{18,... | collective-permute-start | bytes 589832 | tf_op jit(solution)/shard_map/ppermute | solution.py:33
  25.7 15.8 %copy-start.6 = (bf16[1,256,512]{2,1,0:T(8,128)(2,1)S(1)}, bf16[1,256,512]{2,1,0:T(8,128)(2,1)}, u32[]{:S(2)}) copy-start(bf16[1,256,512]{2,1,0:T(8,128)(2,1)} %copy-done.5) | copy-start | bytes 786436
  25.7 15.8 %copy-start.8 = (bf16[1,256,512]{2,1,0:T(8,128)(2,1)S(1)}, bf16[1,256,512]{2,1,0:T(8,128)(2,1)}, u32[]{:S(2)}) copy-start(bf16[1,256,512]{2,1,0:T(8,128)(2,1)} %copy-done.7) | copy-start | bytes 786436
  25.7 15.8 %collective-permute-start.20 = (bf16[2,256,512]{2,1,0:T(8,128)(2,1)S(1)}, bf16[2,256,512]{2,1,0:T(8,128)(2,1)S(1)}, u32[]{:S(2)}, u32[]{:S(2)}) collective-permute-start(bf16[2,256,512]{2,1,0:T(8,128)(2,1)S(1)} %get-tuple-element.27), channel_id=1, source_target_pairs={{0,8},{2,10},{4,12},{6,14},{8,16},{10,18},{12,20},{14,22},{16,24},... | collective-permute-start | bytes 1572872 | tf_op jit(solution)/shard_map/ppermute | solution.py:364
  28.4 2.8 %collective-permute-start.10 = (bf16[2,256,512]{2,1,0:T(8,128)(2,1)S(1)}, bf16[2,256,512]{2,1,0:T(8,128)(2,1)S(1)}, u32[]{:S(2)}, u32[]{:S(2)}) collective-permute-start(bf16[2,256,512]{2,1,0:T(8,128)(2,1)S(1)} %get-tuple-element.34.pair_a), channel_id=1, source_target_pairs={{0,2},{2,0},{4,6},{6,4},{8,10},{10,8},{12,14},{14,12},{16,18},{18,... | collective-permute-start | bytes 1572872 | tf_op jit(solution)/shard_map/ppermute | solution.py:33
  29.6 25.3 %collective-permute-start.1 = (bf16[2,256,512]{2,1,0:T(8,128)(2,1)}, bf16[2,256,512]{2,1,0:T(8,128)(2,1)S(1)}, u32[]{:S(2)}, u32[]{:S(2)}) collective-permute-start(bf16[2,256,512]{2,1,0:T(8,128)(2,1)} %get-tuple-element.24), channel_id=1, source_target_pairs={{0,4},{2,6},{4,0},{6,2},{8,12},{10,14},{12,8},{14,10},{16,20},{18,... | collective-permute-start | bytes 1572872 | tf_op jit(solution)/shard_map/ppermute | solution.py:33
  30.8 12.9 %collective-permute-start.8 = (bf16[8,64,384]{2,1,0:T(8,128)(2,1)}, bf16[8,64,384]{2,1,0:T(8,128)(2,1)}, u32[]{:S(2)}, u32[]{:S(2)}) collective-permute-start(bf16[8,64,384]{2,1,0:T(8,128)(2,1)} %constant_dynamic-update-slice_fusion), channel_id=1, source_target_pairs={{0,2},{2,0},{4,6},{6,4},{8,10},{10,8},{12,14},{14,12},{16,18},{18,... | collective-permute-start | bytes 1179656 | tf_op jit(solution)/shard_map/ppermute | solution.py:33
  33.3 15.5 %collective-permute-start.11 = (bf16[192,512]{1,0:T(8,128)(2,1)}, bf16[192,512]{1,0:T(8,128)(2,1)}, u32[]{:S(2)}, u32[]{:S(2)}) collective-permute-start(bf16[192,512]{1,0:T(8,128)(2,1)} %get-tuple-element.16), channel_id=1, source_target_pairs={{0,4},{2,6},{4,0},{6,2},{8,12},{10,14},{12,8},{14,10},{16,20},{18,... | collective-permute-start | bytes 589832 | tf_op jit(solution)/shard_map/ppermute | solution.py:33
  42.5 24.6 %collective-permute-start.21 = (bf16[2,256,512]{2,1,0:T(8,128)(2,1)}, bf16[2,256,512]{2,1,0:T(8,128)(2,1)S(1)}, u32[]{:S(2)}, u32[]{:S(2)}) collective-permute-start(bf16[2,256,512]{2,1,0:T(8,128)(2,1)} %get-tuple-element.26), channel_id=1, source_target_pairs={{0,4},{2,6},{4,0},{6,2},{8,12},{10,14},{12,8},{14,10},{16,20},{18,... | collective-permute-start | bytes 1572872 | tf_op jit(solution)/shard_map/ppermute | solution.py:33
  43.1 11.8 %copy-start.9 = (bf16[2,256,512]{2,1,0:T(8,128)(2,1)S(1)}, bf16[2,256,512]{2,1,0:T(8,128)(2,1)}, u32[]{:S(2)}) copy-start(bf16[2,256,512]{2,1,0:T(8,128)(2,1)} %get-tuple-element.23) | copy-start | bytes 1572868
  49.8 17.3 %copy-start.10 = (bf16[2,256,512]{2,1,0:T(8,128)(2,1)S(1)}, bf16[2,256,512]{2,1,0:T(8,128)(2,1)}, u32[]{:S(2)}) copy-start(bf16[2,256,512]{2,1,0:T(8,128)(2,1)} %get-tuple-element.25) | copy-start | bytes 1572868
  49.9 5.2 %collective-permute-start.12 = (bf16[48,512]{1,0:T(8,128)(2,1)S(1)}, bf16[48,512]{1,0:T(8,128)(2,1)S(1)}, u32[]{:S(2)}, u32[]{:S(2)}) collective-permute-start(bf16[48,512]{1,0:T(8,128)(2,1)S(1)} %get-tuple-element.18), channel_id=1, source_target_pairs={{0,8},{2,10},{4,12},{6,14},{8,0},{10,2},{12,4},{14,6},{16,24},{18,... | collective-permute-start | bytes 147464 | tf_op jit(solution)/shard_map/ppermute | solution.py:33
  52.4 5.5 %collective-permute-start.13 = (bf16[48,512]{1,0:T(8,128)(2,1)S(1)}, bf16[48,512]{1,0:T(8,128)(2,1)S(1)}, u32[]{:S(2)}, u32[]{:S(2)}) collective-permute-start(bf16[48,512]{1,0:T(8,128)(2,1)S(1)} %get-tuple-element.19), channel_id=1, source_target_pairs={{0,16},{2,18},{4,20},{6,22},{8,24},{10,26},{12,28},{14,30},{16,0},... | collective-permute-start | bytes 147464 | tf_op jit(solution)/shard_map/ppermute | solution.py:33
  52.8 6.0 %collective-permute-start.14 = (bf16[48,512]{1,0:T(8,128)(2,1)S(1)}, bf16[48,512]{1,0:T(8,128)(2,1)S(1)}, u32[]{:S(2)}, u32[]{:S(2)}) collective-permute-start(bf16[48,512]{1,0:T(8,128)(2,1)S(1)} %get-tuple-element.20), channel_id=1, source_target_pairs={{0,24},{2,26},{4,28},{6,30},{8,16},{10,18},{12,20},{14,22},{16,8},... | collective-permute-start | bytes 147464 | tf_op jit(solution)/shard_map/ppermute | solution.py:33
  54.9 17.4 %collective-permute-start.2 = (bf16[4,256,512]{2,1,0:T(8,128)(2,1)S(1)}, bf16[4,256,512]{2,1,0:T(8,128)(2,1)S(1)}, u32[]{:S(2)}, u32[]{:S(2)}) collective-permute-start(bf16[4,256,512]{2,1,0:T(8,128)(2,1)S(1)} %pad_maximum_fusion), channel_id=1, source_target_pairs={{0,2},{2,0},{4,6},{6,4},{8,10},{10,8},{12,14},{14,12},{16,18},{18,... | collective-permute-start | bytes 3145736 | tf_op jit(solution)/shard_map/ppermute | solution.py:33
  59.4 6.0 %collective-permute-start.17 = (bf16[48,512]{1,0:T(8,128)(2,1)S(1)}, bf16[48,512]{1,0:T(8,128)(2,1)S(1)}, u32[]{:S(2)}, u32[]{:S(2)}) collective-permute-start(bf16[48,512]{1,0:T(8,128)(2,1)S(1)} %shard_map.87), channel_id=1, source_target_pairs={{0,24},{2,26},{4,28},{6,30},{8,16},{10,18},{12,20},{14,22},{16,8},... | collective-permute-start | bytes 147464 | tf_op jit(solution)/shard_map/ppermute | solution.py:33
  61.5 5.0 %collective-permute-start.16 = (bf16[48,512]{1,0:T(8,128)(2,1)S(1)}, bf16[48,512]{1,0:T(8,128)(2,1)S(1)}, u32[]{:S(2)}, u32[]{:S(2)}) collective-permute-start(bf16[48,512]{1,0:T(8,128)(2,1)S(1)} %shard_map.87), channel_id=1, source_target_pairs={{0,16},{2,18},{4,20},{6,22},{8,24},{10,26},{12,28},{14,30},{16,0},... | collective-permute-start | bytes 147464 | tf_op jit(solution)/shard_map/ppermute | solution.py:33
  61.6 4.8 %collective-permute-start.15 = (bf16[48,512]{1,0:T(8,128)(2,1)S(1)}, bf16[48,512]{1,0:T(8,128)(2,1)S(1)}, u32[]{:S(2)}, u32[]{:S(2)}) collective-permute-start(bf16[48,512]{1,0:T(8,128)(2,1)S(1)} %shard_map.87), channel_id=1, source_target_pairs={{0,8},{2,10},{4,12},{6,14},{8,0},{10,2},{12,4},{14,6},{16,24},{18,... | collective-permute-start | bytes 147464 | tf_op jit(solution)/shard_map/ppermute | solution.py:33
  66.5 5.9 %copy-start.1 = (bf16[2,256,512]{2,1,0:T(8,128)(2,1)S(1)}, bf16[2,256,512]{2,1,0:T(8,128)(2,1)}, u32[]{:S(2)}) copy-start(bf16[2,256,512]{2,1,0:T(8,128)(2,1)} %k_own.3) | copy-start | bytes 1572868
  66.5 5.9 %copy-start.2 = (bf16[2,256,512]{2,1,0:T(8,128)(2,1)S(1)}, bf16[2,256,512]{2,1,0:T(8,128)(2,1)}, u32[]{:S(2)}) copy-start(bf16[2,256,512]{2,1,0:T(8,128)(2,1)} %q.5) | copy-start | bytes 1572868
  66.5 5.9 %copy-start.3 = (bf16[2,256,512]{2,1,0:T(8,128)(2,1)S(1)}, bf16[2,256,512]{2,1,0:T(8,128)(2,1)}, u32[]{:S(2)}) copy-start(bf16[2,256,512]{2,1,0:T(8,128)(2,1)} %gates.3) | copy-start | bytes 1572868
  66.5 5.7 %collective-permute-start.18 = (bf16[4,48,512]{2,1,0:T(8,128)(2,1)S(1)}, bf16[4,48,512]{2,1,0:T(8,128)(2,1)S(1)}, u32[]{:S(2)}, u32[]{:S(2)}) collective-permute-start(bf16[4,48,512]{2,1,0:T(8,128)(2,1)S(1)} %pad_maximum_fusion.7), channel_id=1, source_target_pairs={{0,4},{2,6},{4,0},{6,2},{8,12},{10,14},{12,8},{14,10},{16,20},{18,... | collective-permute-start | bytes 589832 | tf_op jit(solution)/shard_map/ppermute | solution.py:33
  67.2 8.9 %collective-permute-start.22 = (bf16[4,256,512]{2,1,0:T(8,128)(2,1)S(1)}, bf16[4,256,512]{2,1,0:T(8,128)(2,1)S(1)}, u32[]{:S(2)}, u32[]{:S(2)}) collective-permute-start(bf16[4,256,512]{2,1,0:T(8,128)(2,1)S(1)} %pad_maximum_fusion.1), channel_id=1, source_target_pairs={{0,2},{2,0},{4,6},{6,4},{8,10},{10,8},{12,14},{14,12},{16,18},{18,... | collective-permute-start | bytes 3145736 | tf_op jit(solution)/shard_map/ppermute | solution.py:33
  72.3 6.2 %collective-permute-start.19 = (bf16[8,48,512]{2,1,0:T(8,128)(2,1)S(1)}, bf16[8,48,512]{2,1,0:T(8,128)(2,1)S(1)}, u32[]{:S(2)}, u32[]{:S(2)}) collective-permute-start(bf16[8,48,512]{2,1,0:T(8,128)(2,1)S(1)} %constant_dynamic-update-slice_fusion.5.mine), channel_id=1, source_target_pairs={{0,2},{2,0},{4,6},{6,4},{8,10},{10,8},{12,14},{14,12},{16,18},{18,... | collective-permute-start | bytes 1179656 | tf_op jit(solution)/shard_map/ppermute | solution.py:33
  74.6 8.3 %collective-permute-start.9 = (bf16[128,512]{1,0:T(8,128)(2,1)S(1)}, bf16[128,512]{1,0:T(8,128)(2,1)S(1)}, u32[]{:S(2)}, u32[]{:S(2)}) collective-permute-start(bf16[128,512]{1,0:T(8,128)(2,1)S(1)} %get-tuple-element.32), channel_id=1, source_target_pairs={{0,1},{1,0},{2,3},{3,2},{4,5},{5,4},{6,7},{7,6},{8,9},{9,8},{10,11... | collective-permute-start | bytes 393224 | tf_op jit(solution)/shard_map/ppermute | solution.py:33
  78.4 4.4 %copy-start.4 = (f32[1024]{0:T(1024)S(1)}, f32[1024]{0:T(1024)}, u32[]{:S(2)}) copy-start(f32[1024]{0:T(1024)} %param.15) | copy-start | bytes 12292
  82.3 5.7 %collective-permute-start.23 = (bf16[128,512]{1,0:T(8,128)(2,1)S(1)}, bf16[128,512]{1,0:T(8,128)(2,1)S(1)}, u32[]{:S(2)}, u32[]{:S(2)}) collective-permute-start(bf16[128,512]{1,0:T(8,128)(2,1)S(1)} %get-tuple-element.35), channel_id=1, source_target_pairs={{0,1},{1,0},{2,3},{3,2},{4,5},{5,4},{6,7},{7,6},{8,9},{9,8},{10,11... | collective-permute-start | bytes 393224 | tf_op jit(solution)/shard_map/ppermute | solution.py:33

commit v2 on v1

v2 whole, which is shorter than its diff:
```python
import functools

import jax
import jax.numpy as jnp
from jax import lax
from jax.experimental import pallas as pl
from jax.experimental.pallas import tpu as pltpu
from jax.sharding import PartitionSpec as P

WIN = 1024
A_COEF = 3.4445
B_COEF = -4.775
C_COEF = 2.0315
BF = jnp.bfloat16
F32 = jnp.float32
VMEM_LIMIT = 48 * 1024 * 1024


def dot_nn(a, b):
    return lax.dot_general(a, b, (((1,), (0,)), ((), ())), preferred_element_type=F32)


def dot_nt(a, b):
    return lax.dot_general(a, b, (((1,), (1,)), ((), ())), preferred_element_type=F32)


def dot_tn(a, b):
    return lax.dot_general(a, b, (((0,), (0,)), ((), ())), preferred_element_type=F32)


def swapped(value, mask, axis="ctx"):
    count = lax.axis_size(axis)
    return lax.ppermute(value, axis, [(i, i ^ mask) for i in range(count)])


def vmem_spec():
    return pl.BlockSpec(memory_space=pltpu.VMEM)


def call(body, args, outs, scratch=(), cost=None):
    return pl.pallas_call(
        body,
        out_shape=outs,
        in_specs=[pl.BlockSpec(memory_space=pltpu.SMEM)] + [vmem_spec()] * (len(args) - 1),
        out_specs=jax.tree.map(lambda _: vmem_spec(), outs),
        scratch_shapes=list(scratch),
        compiler_params=pltpu.CompilerParams(vmem_limit_bytes=VMEM_LIMIT),
        cost_estimate=cost,
    )(*args)


def cost_of(flops, moved):
    return pl.CostEstimate(flops=int(flops), bytes_accessed=int(moved), transcendentals=0)


def silu(v):
    return v / (1.0 + jnp.exp(-v))


def gradient_body(planes, ids, mine, other, beside, pair_a, pair_b, rate_a, rate_b, *refs):
    send, keep, whole, total = refs[:4]
    plane, side, core = ids[0], ids[1], ids[2]
    rows = mine.shape[1]
    target_ref = refs[4] if len(refs) > 4 else whole
    for m in range(planes):
        for far in range(2):
            block = ((plane ^ m) * 2 + (side if far == 0 else 1 - side)) * 2
            own_at = pl.multiple_of((block + core) * rows, rows)
            other_at = pl.multiple_of((block + 1 - core) * rows, rows)
            source = (mine, other)[far]
            target_ref[pl.ds(own_at, rows), :] = source[m].astype(target_ref.dtype)
            target_ref[pl.ds(other_at, rows), :] = beside[far * planes + m].astype(target_ref.dtype)
    if target_ref is not whole:
        whole[...] = target_ref[...].astype(BF)
    width = whole.shape[1] // 3
    half = width // 2
    parts = [
        whole[:, pl.ds(pl.multiple_of(b * width + core * half, half), half)] for b in range(3)
    ]
    gate_up_w = jnp.concatenate(parts[:2], 1)
    out_w = parts[2]
    first = None
    for pair, rate in ((pair_a, rate_a), (pair_b, rate_b)):
        key_rows = pair[0]
        target = (-rate[...] * pair[1].astype(F32)).astype(BF)
        gate_up = dot_nn(key_rows, gate_up_w)
        g, u = gate_up[:, :half], gate_up[:, half:]
        dh = dot_nn(target, out_w)
        s = 1.0 / (1.0 + jnp.exp(-g))
        gs = g * s
        hidden = (gs * u).astype(BF)
        dg = dh * u * s * (1.0 + g * (1.0 - s))
        du = dh * gs
        joined = jnp.concatenate([dg, du], 1).astype(BF)
        in_grad = dot_tn(joined, key_rows)
        out_grad = dot_tn(hidden, target)
        first = (in_grad, out_grad) if first is None else (first[0] + in_grad, first[1] + out_grad)
    total[: 2 * half, :] = first[0]
    total[2 * half : 3 * half, :] = first[1]
    if total.shape[0] > 3 * half:
        total[3 * half :, :] = jnp.zeros((total.shape[0] - 3 * half, total.shape[1]), F32)
    part = send.shape[0]
    send[...] = total[pl.ds(pl.multiple_of((1 - side) * part, part), part), :].astype(BF)
    keep[...] = total[pl.ds(pl.multiple_of(side * part, part), part), :]


def side_sum_body(planes, ids, keep, got, *refs):
    outs, total = refs[:planes], refs[planes]
    plane = ids[0]
    total[...] = keep[...] + got[...].astype(F32)
    part = outs[0].shape[0]
    for m in range(planes):
        rows = total[pl.ds(pl.multiple_of((plane ^ m) * part, part), part), :]
        outs[m][...] = rows.astype(outs[m].dtype)


def plane_sum_body(ids, own, *refs):
    total = own[...]
    for ref in refs[:-1]:
        total = total + ref[...].astype(F32)
    refs[-1][...] = total.astype(BF)


def weights_body(ids, whole, flipped, norms):
    width = whole.shape[1] // 3
    for b in range(3):
        cols = slice(b * width, (b + 1) * width)
        turned = whole[:, cols].astype(F32).T
        flipped[cols, :] = turned
        norms[cols, :] = jnp.sqrt(jnp.sum(turned * turned, 1, keepdims=True))


def fetch(slots, options):
    held, sems = slots
    for slot, choices in enumerate(options):
        for condition, source in choices:
            for which in range(2):
                part = source[which] if isinstance(source, tuple) else source.at[which]
                copy = pltpu.make_async_copy(part, held.at[slot, which], sems.at[slot, which])
                if condition is None:
                    copy.start()
                else:
                    pl.when(condition)(copy.start)

    def wait(slot, which):
        part = held.at[slot, which]
        pltpu.make_async_copy(part, part, sems.at[slot, which]).wait()

    return wait


def window(q, k_own, v_own, held, wait, lives):
    rows, depth = q.shape
    scale = depth**-0.5
    row = lax.broadcasted_iota(jnp.int32, (rows, rows), 0)
    col = lax.broadcasted_iota(jnp.int32, (rows, rows), 1)
    scores = [jnp.where(col <= row, dot_nt(q, k_own) * scale, -1e30)]
    for slot in range(4):
        wait(slot, 0)
        s = dot_nt(q, held[slot, 0]) * scale
        allowed = col > row if slot == 0 else None
        if lives is not None:
            alive = jnp.full((rows, rows), lives[slot], jnp.int32) != 0
            allowed = alive if allowed is None else allowed & alive
        scores.append(s if allowed is None else jnp.where(allowed, s, -1e30))
    top = jnp.max(scores[0], -1, keepdims=True)
    for s in scores[1:]:
        top = jnp.maximum(top, jnp.max(s, -1, keepdims=True))
    total = None
    out = None
    for slot, s in enumerate(scores):
        e = jnp.exp(s - top)
        t = jnp.sum(e, -1, keepdims=True)
        if slot:
            wait(slot - 1, 1)
        o = dot_nn(e.astype(BF), v_own if slot == 0 else held[slot - 1, 1])
        total = t if total is None else total + t
        out = o if out is None else out + o
    return out / total


def first_group_body(ids, q, k_own, v_own, gates, whole, *refs):
    far, near_k, near_v, near, own_beside, far_beside, diag_k, diag_v, diag = refs[:9]
    outs, (held, sems, gated) = refs[9:-3], refs[-3:]
    plane, side, core = ids[0], ids[1], ids[2]
    wait = fetch(
        (held, sems),
        [
            [(None, far)],
            [(side == 1, (near_k, near_v)), (side == 0, near)],
            [(core == 1, own_beside), (core == 0, far_beside)],
            [(side == 1, (diag_k, diag_v)), (side == 0, diag)],
        ],
    )
    later = (plane > 0).astype(jnp.int32)
    side_live = jnp.maximum(later, side)
    core_live = jnp.maximum(later, core)
    lives = [later, side_live, core_live, side_live]
    width = whole.shape[1] // 3
    gate_up = dot_nn(q[0], whole[:, : 2 * width])
    hidden = (silu(gate_up[:, :width]) * gate_up[:, width:]).astype(BF)
    fast = dot_nt(hidden, whole[:, 2 * width :])
    win = window(q[0], k_own[0], v_own[0], held, wait, lives)
    gate = gates[0].astype(F32)
    spread(ids, ((win + fast) * silu(gate)).astype(BF), outs, gated)


def spread(ids, value, outs, held):
    if len(outs) == 1:
        outs[0][...] = value
        return
    held[...] = value
    rows = outs[0].shape[0]
    outs[0][...] = held[pl.ds(pl.multiple_of(ids[3] * rows, rows), rows), :]
    outs[1][...] = held[pl.ds(pl.multiple_of((1 - ids[3]) * rows, rows), rows), :]


def second_group_body(ids, q, k_own, v_own, *refs):
    far_0, far_1, near_own, near_0, near_1, own_beside, far_beside_0, far_beside_1 = refs[:8]
    diag_own, diag_0, diag_1, out, held, sems = refs[8:]
    plane, side, core = ids[0], ids[1], ids[2]
    begin, after = plane == 0, plane > 0
    wait = fetch(
        (held, sems),
        [
            [(begin, far_0), (after, far_1)],
            [
                (side == 1, near_own),
                ((side == 0) & begin, near_0),
                ((side == 0) & after, near_1),
            ],
            [
                (core == 1, own_beside),
                ((core == 0) & begin, far_beside_0),
                ((core == 0) & after, far_beside_1),
            ],
            [
                (side == 1, diag_own),
                ((side == 0) & begin, diag_0),
                ((side == 0) & after, diag_1),
            ],
        ],
    )
    out[...] = window(q[0], k_own[0], v_own[0], held, wait, None)


def group_call(body, index, ids, grouped, whole, raw, outs, rows, depth, scratch, cost):
    def full(a):
        return pl.BlockSpec(a.shape, lambda i, nd=len(a.shape): (0,) * nd)

    specs = [pl.BlockSpec((1,) + a.shape[1:], lambda i: (index, 0, 0)) for a in grouped]
    specs += [full(a) for a in whole]
    specs += [pl.BlockSpec(memory_space=pl.ANY)] * len(raw)
    return pl.pallas_call(
        body,
        grid=(1,),
        out_shape=outs,
        in_specs=[pl.BlockSpec(memory_space=pltpu.SMEM)] + specs,
        out_specs=jax.tree.map(full, outs),
        scratch_shapes=[
            pltpu.VMEM((4, 2, rows, depth), BF),
            pltpu.SemaphoreType.DMA((4, 2)),
            *scratch,
        ],
        compiler_params=pltpu.CompilerParams(vmem_limit_bytes=VMEM_LIMIT),
        cost_estimate=cost,
    )(ids, *grouped, *whole, *raw)


def update_body(planes, ids, rate, mine, other, flipped, norms, q, win, gates, *refs):
    outs, (grads, gated) = refs[:-2], refs[-2:]
    plane, side, core = ids[0], ids[1], ids[2]
    part = mine.shape[1]
    for m in range(planes):
        for far in range(2):
            base = ((side if far == 0 else 1 - side) * planes + (plane ^ m)) * part
            where = pl.ds(pl.multiple_of(base, part), part)
            grads[core, where, :] = mine[far * planes + m]
            grads[1 - core, where, :] = other[far * planes + m]
    width = flipped.shape[0] // 3
    half = width // 2
    turned = []
    for b in range(3):
        block = jnp.concatenate(
            [grads[0, b * half : (b + 1) * half, :], grads[1, b * half : (b + 1) * half, :]], 0
        ).astype(F32)
        length = jnp.sqrt(jnp.sum(block * block, keepdims=True))
        turned.append((block / (length + 1e-06)).astype(BF))
    for _ in range(3):
        grams = [dot_nt(y, y) for y in turned]
        lows = [a.astype(BF) for a in grams]
        squares = [dot_nn(a, a) for a in lows]
        mixers = [(B_COEF * a + C_COEF * s).astype(BF) for a, s in zip(grams, squares)]
        turned = [
            (A_COEF * y.astype(F32) + dot_nn(b, y)).astype(BF) for b, y in zip(mixers, turned)
        ]
    fresh = []
    for b in range(3):
        cols = slice(b * width, (b + 1) * width)
        moved = flipped[cols, :] - rate[0] * turned[b].astype(F32)
        length = jnp.sqrt(jnp.sum(moved * moved, 1, keepdims=True))
        fresh.append((moved * (norms[cols, :] / (length + 1e-06))).astype(BF))
    x = q[...]
    g = dot_nt(x, fresh[0])
    u = dot_nt(x, fresh[1])
    hidden = (silu(g) * u).astype(BF)
    fast = dot_nn(hidden, fresh[2])
    gate = gates[...].astype(F32)
    spread(ids, ((win[...] + fast) * silu(gate)).astype(BF), outs, gated)


def norm_body(ids, own, got, gain, *refs):
    out = refs[-1]
    head = ids[3]
    rows, depth = own.shape
    a = own[...].astype(F32)
    b = got[...].astype(F32)
    low = jnp.where(head == 0, a, b)
    high = jnp.where(head == 0, b, a)
    square = jnp.sum(a * a, -1, keepdims=True) + jnp.sum(b * b, -1, keepdims=True)
    inv = lax.rsqrt(square / (2 * depth) + 1e-06)
    out[0, :, :depth] = (low * inv * gain[:, :depth]).astype(BF)
    out[0, :, depth:] = (high * inv * gain[:, depth:]).astype(BF)


def finished(ids, group, gated, norm_gain, before):
    total = norm_gain.shape[0]
    if len(gated) == 2:
        own, away = gated
        got = swapped(away, 1, "head")
        rows, depth = own.shape
        earlier = () if before is None else (before,)
        return pl.pallas_call(
            norm_body,
            grid=(1,),
            out_shape=jax.ShapeDtypeStruct((2, rows, total), BF),
            in_specs=[
                pl.BlockSpec(memory_space=pltpu.SMEM),
                pl.BlockSpec((rows, depth), lambda i: (0, 0)),
                pl.BlockSpec((rows, depth), lambda i: (0, 0)),
                pl.BlockSpec((1, total), lambda i: (0, 0)),
                *([pl.BlockSpec(memory_space=pl.ANY)] * len(earlier)),
            ],
            out_specs=pl.BlockSpec((1, rows, total), lambda i: (group, 0, 0)),
            input_output_aliases={4: 0} if earlier else {},
            compiler_params=pltpu.CompilerParams(vmem_limit_bytes=VMEM_LIMIT),
            cost_estimate=cost_of(0, 4 * rows * total),
        )(ids, own, got, norm_gain[None, :], *earlier)
    wide = lax.all_to_all(gated[0], "head", split_axis=0, concat_axis=1, tiled=True).astype(F32)
    inv = lax.rsqrt(jnp.mean(wide * wide, -1, keepdims=True) + 1e-06)
    done = (wide * inv * norm_gain).astype(BF)[None]
    return done if before is None else jnp.concatenate([before, done], 0)


def after(value, *needed):
    return lax.optimization_barrier((value,) + needed)[0]


def sent(value, pairs, axis="ctx"):
    return lax.ppermute(value, axis, pairs)


def shards(queries, keys, values, gates, token_rates, fast_init, fast_rate, norm_gain):
    count = lax.axis_size("ctx")
    heads = lax.axis_size("head")
    rows, depth = queries.shape[1], queries.shape[2]
    reach = (WIN - 1) // rows + 1
    planes = count // reach
    if reach != 4 or WIN % rows or planes * reach != count or planes & (planes - 1):
        raise ValueError("unsupported shapes")
    position = lax.axis_index("ctx")
    plane, side, core = position // 4, (position // 2) % 2, position % 2
    ids = jnp.stack([plane, side, core, lax.axis_index("head")]).astype(jnp.int32)
    width = fast_init.shape[2] // 3
    half = width // 2
    everyone = range(count)
    side_up = [(i, i ^ 2) for i in everyone if i & 2 == 0]
    side_down = [(i, i ^ 2) for i in everyone if i & 2]
    core_up = [(i, i ^ 1) for i in everyone if i & 1 == 0]
    core_down = [(i, i ^ 1) for i in everyone if i & 1]
    high_cores = [(i, i ^ 1) for i in everyone if i & 2]
    low_cores = [(i, i ^ 1) for i in everyone if i & 2 == 0]

    local = fast_init[0]
    arrived = [swapped(local, 4 * m) for m in range(1, planes)]
    mine_w = jnp.stack([local] + arrived)
    other_w = swapped(mine_w, 2)
    beside_w = swapped(jnp.concatenate([mine_w, other_w], 0), 1)

    pair_0 = jnp.stack([keys[0], values[0]])
    pair_1 = jnp.stack([keys[1], values[1]])
    beside_0 = swapped(pair_0, 1)
    beside_1 = sent(pair_1, core_up)
    rates_beside = swapped(token_rates, 1)
    near_k = sent(keys[0], side_up)
    near_v = sent(after(values[0], other_w), side_up)
    diag_k = sent(near_k, high_cores)
    diag_v = sent(near_v, high_cores)

    pieces = 2 * planes
    part = -(-3 * half // (16 * pieces)) * 16
    scratch = [pltpu.VMEM((pieces * part, depth), F32)]
    if local.shape[0] % 16:
        scratch.append(pltpu.VMEM((depth, 3 * width), F32))
    send, keep, whole = call(
        functools.partial(gradient_body, planes),
        (ids, mine_w, other_w, beside_w, pair_0, beside_0, token_rates, rates_beside),
        (
            jax.ShapeDtypeStruct((planes * part, depth), BF),
            jax.ShapeDtypeStruct((planes * part, depth), F32),
            jax.ShapeDtypeStruct((depth, 3 * width), BF),
        ),
        scratch=scratch,
        cost=cost_of(2 * 2 * rows * depth * half * 6, 4 * rows * depth * 4),
    )
    got = swapped(send, 2)
    parts = call(
        functools.partial(side_sum_body, planes),
        (ids, keep, got),
        tuple(jax.ShapeDtypeStruct((part, depth), F32 if m == 0 else BF) for m in range(planes)),
        scratch=(pltpu.VMEM((planes * part, depth), F32),),
        cost=cost_of(0, planes * part * depth * 8),
    )
    partial = [swapped(parts[m], 4 * m) for m in range(1, planes)]
    total = call(
        plane_sum_body,
        (ids, parts[0], *partial),
        jax.ShapeDtypeStruct((part, depth), BF),
        cost=cost_of(0, planes * part * depth * 3),
    )
    stacked = jnp.stack([total] + [swapped(total, 4 * m) for m in range(1, planes)])
    side_grad = jnp.concatenate([stacked, swapped(stacked, 2)], 0)
    core_grad = swapped(side_grad, 1)

    ring = [(i, (i + reach) % count) for i in everyone]
    line = [(i, i + reach) for i in range(count - reach)]
    far_0 = sent(after(pair_0, mine_w), ring)
    far_1 = sent(after(pair_1, send), line)
    far_beside_0 = sent(far_0, core_down)
    far_beside_1 = sent(far_1, core_down)
    near_0 = sent(after(far_0, got), side_down)
    diag_0 = sent(near_0, low_cores)
    near_own = sent(after(pair_1, got), side_up)
    diag_own = sent(near_own, high_cores)
    near_1 = sent(after(far_1, total), side_down)
    diag_1 = sent(near_1, low_cores)

    flipped, norms = call(
        weights_body,
        (ids, whole),
        (
            jax.ShapeDtypeStruct((3 * width, depth), F32),
            jax.ShapeDtypeStruct((3 * width, 1), F32),
        ),
        cost=cost_of(0, depth * width * 3 * 8),
    )
    attn_cost = cost_of(8 * rows * depth * 5 * rows, rows * depth * 30)
    if heads == 2:
        split = (jax.ShapeDtypeStruct((rows // 2, depth), BF),) * 2
    else:
        split = (jax.ShapeDtypeStruct((rows, depth), BF),)
    gated_first = group_call(
        first_group_body,
        0,
        ids,
        [queries, keys, values, gates],
        [whole],
        [far_0, near_k, near_v, near_0, beside_0, far_beside_0, diag_k, diag_v, diag_0],
        split,
        rows,
        depth,
        [pltpu.VMEM((rows, depth), BF)],
        attn_cost,
    )
    window_second = group_call(
        second_group_body,
        1,
        ids,
        [queries, keys, values],
        [],
        [far_0, far_1, near_own, near_0, near_1, beside_1, far_beside_0, far_beside_1]
        + [diag_own, diag_0, diag_1],
        jax.ShapeDtypeStruct((rows, depth), F32),
        rows,
        depth,
        [],
        attn_cost,
    )
    done = finished(ids, 0, gated_first, norm_gain, None)

    def full(shape):
        return pl.BlockSpec(shape, lambda i, nd=len(shape): (0,) * nd)

    gated_second = pl.pallas_call(
        functools.partial(update_body, planes),
        grid=(1,),
        out_shape=split,
        in_specs=[
            pl.BlockSpec(memory_space=pltpu.SMEM),
            pl.BlockSpec(memory_space=pltpu.SMEM),
            full(side_grad.shape),
            full(core_grad.shape),
            full(flipped.shape),
            full(norms.shape),
            pl.BlockSpec((None, rows, depth), lambda i: (1, 0, 0)),
            full((rows, depth)),
            pl.BlockSpec((None, rows, depth), lambda i: (1, 0, 0)),
        ],
        out_specs=tuple(full(s.shape) for s in split),
        scratch_shapes=[
            pltpu.VMEM((2, pieces * part, depth), BF),
            pltpu.VMEM((rows, depth), BF),
        ],
        compiler_params=pltpu.CompilerParams(vmem_limit_bytes=VMEM_LIMIT),
        cost_estimate=cost_of(3e9, 4e6),
    )(ids, fast_rate, side_grad, core_grad, flipped, norms, queries, window_second, gates)
    return finished(ids, 1, gated_second, norm_gain, done)


def solution(mesh):
    placed = (
        P(None, "ctx", "head"),
        P(None, "ctx", "head"),
        P(None, "ctx", "head"),
        P(None, "ctx", "head"),
        P("ctx", "head"),
        P("head", "ctx", None),
        P("head"),
        P(),
    )
    return jax.shard_map(
        shards,
        mesh=mesh,
        in_specs=placed,
        out_specs=P(None, ("ctx", "head"), None),
        check_vma=False,
    )
```

time: 89.8 us -> 111 us (1.24)
  starting transfers between devices: 29 us -> 50.1 us
  other arithmetic: 4.24 us -> 0.24 us
  Pallas kernels: 14.9 us -> 18.5 us
  local copies, waits for them, and re-layouts: 4.8 us -> 7.05 us
  waiting for transfers between devices: 35.5 us -> 34 us
    ppermute x2 -> x15, starting transfers between devices: 7.26 us -> 29.2 us  [sent(): return lax.ppermute(value, axis, pairs)]
    ppermute x2 -> x15, waiting for transfers between devices: 6.66 us -> 0.04 us  [sent(): return lax.ppermute(value, axis, pairs)]
    ppermute x22 -> x18, waiting for transfers between devices: 28.8 us -> 33.9 us  [swapped(): return lax.ppermute(value, axis, [(i, i ^ mask) for i in range(count)])]
    pallas_call x2, Pallas kernels: 4.4 us -> 8.16 us  [group_call(): pl.pallas_call(body, grid=(1,), out_shape=outs, in_specs=[pl.BlockSpec(me...]
    pallas_call x6 -> x4, Pallas kernels: 6.71 us -> 3.64 us  [call(): pl.pallas_call(body, out_shape=outs, in_specs=[pl.BlockSpec(memory_space=...]
    pallas_call x0 -> x2, Pallas kernels: none -> 2.85 us  [finished(): pl.pallas_call(norm_body, grid=(1,), out_shape=jax.ShapeDtypeStruct((2, r...]
    unnamed x32 -> x35, local copies, waits for them, and re-layouts: 1.94 us -> 4.48 us
    select_n x6 -> x0, other arithmetic: 2.28 us -> none  [the longest x2 2.18 us: shards(): jnp.where(core == 0, own, far)]
  transfers between devices with their start and end apart: 24 -> 33, of which waited for: 11 -> 11; matrix products, arithmetic and copies ran while one was open for 8% -> 5% of each run, Pallas kernels for 16% -> 15%
where the time goes in v2:
time: 111 us
  starting transfers between devices  50.1 us (45%)
  waiting for transfers between devices  34 us (31%)
  Pallas kernels  18.5 us (17%)
  local copies, waits for them, and re-layouts  7.05 us (6%)
  between operations  1.17 us (1%)
    ppermute x18, waiting for transfers between devices, swapped(): return lax.ppermute(value, axis, [(i, i ^ mask) for i in range(count)])  33.9 us
    ppermute x15, starting transfers between devices, sent(): return lax.ppermute(value, axis, pairs)  29.2 us
    ppermute x18, starting transfers between devices, swapped(): return lax.ppermute(value, axis, [(i, i ^ mask) for i in range(count)])  20.9 us
    pallas_call x2, Pallas kernels, group_call(): pl.pallas_call(body, grid=(1,), out_shape=outs, in_specs=[pl.BlockSpec(me...  8.16 us
    unnamed x35, local copies, waits for them, and re-layouts  4.48 us
    pallas_call x1, Pallas kernels, shards(): pl.pallas_call(functools.partial(update_body, planes), grid=(1,), out_sha...  3.83 us
    pallas_call x4, Pallas kernels, call(): pl.pallas_call(body, out_shape=outs, in_specs=[pl.BlockSpec(memory_space=...  3.64 us
    pallas_call x2, Pallas kernels, finished(): pl.pallas_call(norm_body, grid=(1,), out_shape=jax.ShapeDtypeStruct((2, r...  2.85 us
  transfers between devices with their start and end apart: 33, of which 11 were waited for; matrix products, arithmetic and copies ran while one was open for 5% of the time, Pallas kernels for 15%

profile of v2, /device:TPU:0, one launch (start us, length us, event | category | flops | bytes accessed | tf_op | source)
XLA Modules:
  0.0 111.0 jit_solution(744550620342098607)
XLA Ops:
  0.0 3.0 %collective-permute-start = (bf16[32,768]{1,0:T(8,128)(2,1)}, bf16[32,768]{1,0:T(8,128)(2,1)S(1)}, u32[]{:S(2)}, u32[]{:S(2)}) collective-permute-start(bf16[32,768]{1,0:T(8,128)(2,1)} %bitcast.27), channel_id=1, source_target_pairs={{0,8},{2,10},{4,12},{6,14},{8,0},{10,2},{12,4},{14,6},{16,24},{18,... | collective-permute-start | bytes 147464 | tf_op jit(solution)/shard_map/ppermute | solution.py:33
  3.0 2.6 %collective-permute-start.1 = (bf16[32,768]{1,0:T(8,128)(2,1)}, bf16[32,768]{1,0:T(8,128)(2,1)S(1)}, u32[]{:S(2)}, u32[]{:S(2)}) collective-permute-start(bf16[32,768]{1,0:T(8,128)(2,1)} %bitcast.28), channel_id=1, source_target_pairs={{0,16},{2,18},{4,20},{6,22},{8,24},{10,26},{12,28},{14,30},{16,0},... | collective-permute-start | bytes 147464 | tf_op jit(solution)/shard_map/ppermute | solution.py:33
  5.6 1.1 slice_bitcast_fusion
  6.7 0.8 slice_bitcast_fusion.1
  7.5 0.1 pad_maximum_fusion.pair_a
  7.6 0.1 collective-permute-start.5
  7.7 0.6 constant_dynamic-update-slice_fusion.4
  8.3 0.9 collective-permute-done.1
  9.2 2.6 %collective-permute-done.2 = bf16[32,768]{1,0:T(8,128)(2,1)S(1)} collective-permute-done((bf16[32,768]{1,0:T(8,128)(2,1)}, bf16[32,768]{1,0:T(8,128)(2,1)S(1)}, u32[]{:S(2)}, u32[]{:S(2)}) %collective-permute-start.2) | collective-permute-done | bytes 49184 | tf_op jit(solution)/shard_map/ppermute | solution.py:33
  11.7 1.6 %collective-permute-start.3 = (bf16[4,32,768]{2,1,0:T(8,128)(2,1)S(1)}, bf16[4,32,768]{2,1,0:T(8,128)(2,1)S(1)}, u32[]{:S(2)}, u32[]{:S(2)}) collective-permute-start(bf16[4,32,768]{2,1,0:T(8,128)(2,1)S(1)} %pad_maximum_fusion.2.mine), channel_id=1, source_target_pairs={{0,4},{2,6},{4,0},{6,2},{8,12},{10,14},{12,8},{14,10},{16,20},{18,... | collective-permute-start | bytes 589832 | tf_op jit(solution)/shard_map/ppermute | solution.py:33
  13.3 0.6 constant_dynamic-update-slice_fusion.3
  13.9 0.6 constant_dynamic-update-slice_fusion.2
  14.6 0.6 constant_dynamic-update-slice_fusion.1
  15.2 2.3 %collective-permute-done.3.other = bf16[4,32,768]{2,1,0:T(8,128)(2,1)S(1)} collective-permute-done((bf16[4,32,768]{2,1,0:T(8,128)(2,1)S(1)}, bf16[4,32,768]{2,1,0:T(8,128)(2,1)S(1)}, u32[]{:S(2)}, u32[]{:S(2)}) %collective-permute-start.3) | collective-permute-done | bytes 196640 | tf_op jit(solution)/shard_map/ppermute | solution.py:33
  17.5 0.7 constant_dynamic-update-slice_fusion
  18.2 0.1 copy.11.rate_a
  18.3 0.6 collective-permute-start.6
  18.9 0.1 collective-permute-start.16
  19.0 0.1 pad_add_fusion.ids
  19.1 1.0 collective-permute-done.6.rate_b
  20.1 1.5 %shard_map.82 = (bf16[192,512]{1,0:T(8,128)(2,1)S(1)}, f32[192,512]{1,0:T(8,128)S(1)}, bf16[512,768]{1,0:T(8,128)(2,1)S(1)}) custom-call(s32[4]{0:T(128)S(1)} %pad_add_fusion.ids, bf16[4,32,768]{2,1,0:T(8,128)(2,1)S(1)} %pad_maximum_fusion.2.mine, bf16[4,32,768]{2,1,0:T(8,128)(2,1)S(1)} %collective-permute-done.3.other, ...), custom_call_target="tpu_custom_call" | custom-call | flops 402653184 | bytes 2097152 | tf_op jit(solution)/shard_map/pallas_call | solution.py:41
  21.7 2.0 %collective-permute-start.17 = (bf16[2,256,512]{2,1,0:T(8,128)(2,1)S(1)}, bf16[2,256,512]{2,1,0:T(8,128)(2,1)S(1)}, u32[]{:S(2)}, u32[]{:S(2)}) collective-permute-start(bf16[2,256,512]{2,1,0:T(8,128)(2,1)S(1)} %pad_maximum_fusion.1), channel_id=1, source_target_pairs={{0,8},{2,10},{4,12},{6,14},{8,16},{10,18},{12,20},{14,22},{16,24},... | collective-permute-start | bytes 1572872 | tf_op jit(solution)/shard_map/ppermute | solution.py:360
  23.7 3.4 %collective-permute-start.28 = (bf16[256,512]{1,0:T(8,128)(2,1)S(1)}, bf16[256,512]{1,0:T(8,128)(2,1)S(1)}, u32[]{:S(2)}, u32[]{:S(2)}) collective-permute-start(bf16[256,512]{1,0:T(8,128)(2,1)S(1)} %copy-done.10), channel_id=1, source_target_pairs={{0,4},{2,6},{8,12},{10,14},{16,20},{18,22},{24,28},{26,30},{1,5},{... | collective-permute-start | bytes 786440 | tf_op jit(solution)/shard_map/ppermute | solution.py:360
  27.1 0.1 collective-permute-start.7
  27.2 3.9 %collective-permute-start.29 = (bf16[256,512]{1,0:T(8,128)(2,1)S(1)}, bf16[256,512]{1,0:T(8,128)(2,1)S(1)}, u32[]{:S(2)}, u32[]{:S(2)}) collective-permute-start(bf16[256,512]{1,0:T(8,128)(2,1)S(1)} %get-tuple-element.40), channel_id=1, source_target_pairs={{0,4},{2,6},{8,12},{10,14},{16,20},{18,22},{24,28},{26,30},{1,5},{... | collective-permute-start | bytes 786440 | tf_op jit(solution)/shard_map/ppermute | solution.py:360
  31.1 6.9 %collective-permute-done.7.got = bf16[192,512]{1,0:T(8,128)(2,1)S(1)} collective-permute-done((bf16[192,512]{1,0:T(8,128)(2,1)S(1)}, bf16[192,512]{1,0:T(8,128)(2,1)S(1)}, u32[]{:S(2)}, u32[]{:S(2)}) %collective-permute-start.7) | collective-permute-done | bytes 196640 | tf_op jit(solution)/shard_map/ppermute | solution.py:33
  38.0 0.6 shard_map.83
  38.6 2.3 %collective-permute-start.10 = (bf16[48,512]{1,0:T(8,128)(2,1)S(1)}, bf16[48,512]{1,0:T(8,128)(2,1)S(1)}, u32[]{:S(2)}, u32[]{:S(2)}) collective-permute-start(bf16[48,512]{1,0:T(8,128)(2,1)S(1)} %get-tuple-element.29), channel_id=1, source_target_pairs={{0,24},{2,26},{4,28},{6,30},{8,16},{10,18},{12,20},{14,22},{16,8},... | collective-permute-start | bytes 147464 | tf_op jit(solution)/shard_map/ppermute | solution.py:33
  40.9 1.8 %collective-permute-start.8 = (bf16[48,512]{1,0:T(8,128)(2,1)S(1)}, bf16[48,512]{1,0:T(8,128)(2,1)S(1)}, u32[]{:S(2)}, u32[]{:S(2)}) collective-permute-start(bf16[48,512]{1,0:T(8,128)(2,1)S(1)} %get-tuple-element.27), channel_id=1, source_target_pairs={{0,8},{2,10},{4,12},{6,14},{8,0},{10,2},{12,4},{14,6},{16,24},{18,... | collective-permute-start | bytes 147464 | tf_op jit(solution)/shard_map/ppermute | solution.py:33
  42.7 0.4 collective-permute-start.9
  43.1 1.5 %collective-permute-done.10.refs_2_ = bf16[48,512]{1,0:T(8,128)(2,1)S(1)} collective-permute-done((bf16[48,512]{1,0:T(8,128)(2,1)S(1)}, bf16[48,512]{1,0:T(8,128)(2,1)S(1)}, u32[]{:S(2)}, u32[]{:S(2)}) %collective-permute-start.10) | collective-permute-done | bytes 49184 | tf_op jit(solution)/shard_map/ppermute | solution.py:33
  44.6 0.7 collective-permute-start.30
  45.3 1.3 %collective-permute-start.19 = (bf16[2,256,512]{2,1,0:T(8,128)(2,1)S(1)}, bf16[2,256,512]{2,1,0:T(8,128)(2,1)S(1)}, u32[]{:S(2)}, u32[]{:S(2)}) collective-permute-start(bf16[2,256,512]{2,1,0:T(8,128)(2,1)S(1)} %collective-permute-done.16.refs_0_), channel_id=1, source_target_pairs={{4,0},{6,2},{12,8},{14,10},{20,16},{22,18},{28,24},{30,26},{5,1},{... | collective-permute-start | bytes 1572872 | tf_op jit(solution)/shard_map/ppermute | solution.py:360
  46.6 1.3 %collective-permute-done.9.refs_1_ = bf16[48,512]{1,0:T(8,128)(2,1)S(1)} collective-permute-done((bf16[48,512]{1,0:T(8,128)(2,1)S(1)}, bf16[48,512]{1,0:T(8,128)(2,1)S(1)}, u32[]{:S(2)}, u32[]{:S(2)}) %collective-permute-start.9) | collective-permute-done | bytes 49184 | tf_op jit(solution)/shard_map/ppermute | solution.py:33
  47.9 0.6 shard_map.84
  48.5 1.8 %collective-permute-start.12 = (bf16[48,512]{1,0:T(8,128)(2,1)S(1)}, bf16[48,512]{1,0:T(8,128)(2,1)S(1)}, u32[]{:S(2)}, u32[]{:S(2)}) collective-permute-start(bf16[48,512]{1,0:T(8,128)(2,1)S(1)} %shard_map.84), channel_id=1, source_target_pairs={{0,16},{2,18},{4,20},{6,22},{8,24},{10,26},{12,28},{14,30},{16,0},... | collective-permute-start | bytes 147464 | tf_op jit(solution)/shard_map/ppermute | solution.py:33
  50.3 1.1 collective-permute-start.13
  51.4 0.7 collective-permute-start.11
  52.1 0.7 collective-permute-start.31
  52.7 1.5 %collective-permute-done.12 = bf16[48,512]{1,0:T(8,128)(2,1)S(1)} collective-permute-done((bf16[48,512]{1,0:T(8,128)(2,1)S(1)}, bf16[48,512]{1,0:T(8,128)(2,1)S(1)}, u32[]{:S(2)}, u32[]{:S(2)}) %collective-permute-start.12) | collective-permute-done | bytes 49184 | tf_op jit(solution)/shard_map/ppermute | solution.py:33
  54.3 1.3 %collective-permute-start.22 = (bf16[2,256,512]{2,1,0:T(8,128)(2,1)S(1)}, bf16[2,256,512]{2,1,0:T(8,128)(2,1)S(1)}, u32[]{:S(2)}, u32[]{:S(2)}) collective-permute-start(bf16[2,256,512]{2,1,0:T(8,128)(2,1)S(1)} %collective-permute-done.16.refs_0_), channel_id=1, source_target_pairs={{2,0},{6,4},{10,8},{14,12},{18,16},{22,20},{26,24},{30,28},{3,1},{... | collective-permute-start | bytes 1572872 | tf_op jit(solution)/shard_map/ppermute | solution.py:360
  55.6 0.6 collective-permute-done.13
  56.2 5.3 %collective-permute-start.18 = (bf16[2,256,512]{2,1,0:T(8,128)(2,1)S(1)}, bf16[2,256,512]{2,1,0:T(8,128)(2,1)S(1)}, u32[]{:S(2)}, u32[]{:S(2)}) collective-permute-start(bf16[2,256,512]{2,1,0:T(8,128)(2,1)S(1)} %pad_maximum_fusion.1), channel_id=1, source_target_pairs={{0,4},{2,6},{8,12},{10,14},{16,20},{18,22},{24,28},{26,30},{1,5},{... | collective-permute-start | bytes 1572872 | tf_op jit(solution)/shard_map/ppermute | solution.py:360
  61.5 1.3 %collective-permute-start.20 = (bf16[2,256,512]{2,1,0:T(8,128)(2,1)S(1)}, bf16[2,256,512]{2,1,0:T(8,128)(2,1)S(1)}, u32[]{:S(2)}, u32[]{:S(2)}) collective-permute-start(bf16[2,256,512]{2,1,0:T(8,128)(2,1)S(1)} %collective-permute-done.17.refs_1_), channel_id=1, source_target_pairs={{4,0},{6,2},{12,8},{14,10},{20,16},{22,18},{28,24},{30,26},{5,1},{... | collective-permute-start | bytes 1572872 | tf_op jit(solution)/shard_map/ppermute | solution.py:360
  62.9 2.7 %collective-permute-start.14 = (bf16[4,48,512]{2,1,0:T(8,128)(2,1)S(1)}, bf16[4,48,512]{2,1,0:T(8,128)(2,1)S(1)}, u32[]{:S(2)}, u32[]{:S(2)}) collective-permute-start(bf16[4,48,512]{2,1,0:T(8,128)(2,1)S(1)} %pad_maximum_fusion.3), channel_id=1, source_target_pairs={{0,4},{2,6},{4,0},{6,2},{8,12},{10,14},{12,8},{14,10},{16,20},{18,... | collective-permute-start | bytes 589832 | tf_op jit(solution)/shard_map/ppermute | solution.py:33
  65.6 1.9 %collective-permute-start.25 = (bf16[2,256,512]{2,1,0:T(8,128)(2,1)S(1)}, bf16[2,256,512]{2,1,0:T(8,128)(2,1)S(1)}, u32[]{:S(2)}, u32[]{:S(2)}) collective-permute-start(bf16[2,256,512]{2,1,0:T(8,128)(2,1)S(1)} %collective-permute-done.19.refs_3_), channel_id=1, source_target_pairs={{0,2},{2,0},{8,10},{10,8},{16,18},{18,16},{24,26},{26,24},{1,3},{3... | collective-permute-start | bytes 1572872 | tf_op jit(solution)/shard_map/ppermute | solution.py:360
  67.5 2.4 %collective-permute-start.21 = (bf16[2,256,512]{2,1,0:T(8,128)(2,1)S(1)}, bf16[2,256,512]{2,1,0:T(8,128)(2,1)S(1)}, u32[]{:S(2)}, u32[]{:S(2)}) collective-permute-start(bf16[2,256,512]{2,1,0:T(8,128)(2,1)S(1)} %pad_maximum_fusion.1), channel_id=1, source_target_pairs={{0,2},{4,6},{8,10},{12,14},{16,18},{20,22},{24,26},{28,30},{1,3},{... | collective-permute-start | bytes 1572872 | tf_op jit(solution)/shard_map/ppermute | solution.py:360
  70.0 11.6 %collective-permute-done.14 = bf16[4,48,512]{2,1,0:T(8,128)(2,1)S(1)} collective-permute-done((bf16[4,48,512]{2,1,0:T(8,128)(2,1)S(1)}, bf16[4,48,512]{2,1,0:T(8,128)(2,1)S(1)}, u32[]{:S(2)}, u32[]{:S(2)}) %collective-permute-start.14) | collective-permute-done | bytes 196640 | tf_op jit(solution)/shard_map/ppermute | solution.py:33
  81.6 1.3 %collective-permute-start.23 = (bf16[2,256,512]{2,1,0:T(8,128)(2,1)S(1)}, bf16[2,256,512]{2,1,0:T(8,128)(2,1)S(1)}, u32[]{:S(2)}, u32[]{:S(2)}) collective-permute-start(bf16[2,256,512]{2,1,0:T(8,128)(2,1)S(1)} %collective-permute-done.17.refs_1_), channel_id=1, source_target_pairs={{2,0},{6,4},{10,8},{14,12},{18,16},{22,20},{26,24},{30,28},{3,1},{... | collective-permute-start | bytes 1572872 | tf_op jit(solution)/shard_map/ppermute | solution.py:360
  82.9 0.7 collective-permute-start.24
  83.6 3.1 %collective-permute-start.26 = (bf16[2,256,512]{2,1,0:T(8,128)(2,1)S(1)}, bf16[2,256,512]{2,1,0:T(8,128)(2,1)S(1)}, u32[]{:S(2)}, u32[]{:S(2)}) collective-permute-start(bf16[2,256,512]{2,1,0:T(8,128)(2,1)S(1)} %collective-permute-done.20.refs_4_), channel_id=1, source_target_pairs={{0,2},{2,0},{8,10},{10,8},{16,18},{18,16},{24,26},{26,24},{1,3},{3... | collective-permute-start | bytes 1572872 | tf_op jit(solution)/shard_map/ppermute | solution.py:360
  86.7 0.1 collective-permute-start.15
  87.5 1.0 shard_map.85
  88.5 4.5 %shard_map.88 = (bf16[128,512]{1,0:T(8,128)(2,1)S(1)}, bf16[128,512]{1,0:T(8,128)(2,1)S(1)}) custom-call(s32[4]{0:T(128)S(1)} %pad_add_fusion.ids, bf16[2,256,512]{2,1,0:T(8,128)(2,1)S(1)} %copy-done.3, bf16[2,256,512]{2,1,0:T(8,128)(2,1)S(1)} %copy-done.1, bf16[2,256,512]{2,1,0:T(8,128)(2,1)S(1)} %copy-done, bf16[2,256,512]{2,1,0:T(8,128)(2,1)S(1)} %copy-done.5, ...), custom_call_target="tpu_custom_call" | custom-call | flops 1342177280 | bytes 3932160 | tf_op jit(solution)/shard_map/pallas_call | solution.py:254
  93.0 1.6 %collective-permute-start.32 = (bf16[128,512]{1,0:T(8,128)(2,1)S(1)}, bf16[128,512]{1,0:T(8,128)(2,1)S(1)}, u32[]{:S(2)}, u32[]{:S(2)}) collective-permute-start(bf16[128,512]{1,0:T(8,128)(2,1)S(1)} %get-tuple-element.42), channel_id=1, source_target_pairs={{0,1},{1,0},{2,3},{3,2},{4,5},{5,4},{6,7},{7,6},{8,9},{9,8},{10,11... | collective-permute-start | bytes 393224 | tf_op jit(solution)/shard_map/ppermute | solution.py:33
  94.6 0.8 copy-done.7
  95.4 0.2 copy-done.8
  95.6 0.8 copy-done.9
  96.4 3.7 %shard_map.86.win = f32[256,512]{1,0:T(8,128)S(1)} custom-call(s32[4]{0:T(128)S(1)} %pad_add_fusion.ids, bf16[2,256,512]{2,1,0:T(8,128)(2,1)S(1)} %copy-done.3, bf16[2,256,512]{2,1,0:T(8,128)(2,1)S(1)} %copy-done.1, bf16[2,256,512]{2,1,0:T(8,128)(2,1)S(1)} %copy-done, bf16[2,256,512]{2,1,0:T(8,128)(2,1)S(1)} %collective-permute-done.16.refs_0_, ...), custom_call_target="tpu_custom_call" | custom-call | flops 1342177280 | bytes 3932160 | tf_op jit(solution)/shard_map/pallas_call | solution.py:254
  100.1 3.8 %shard_map.87 = (bf16[128,512]{1,0:T(8,128)(2,1)S(1)}, bf16[128,512]{1,0:T(8,128)(2,1)S(1)}) custom-call(s32[4]{0:T(128)S(1)} %pad_add_fusion.ids, f32[1]{0:T(128)S(6)} %copy.21.rate, bf16[8,48,512]{2,1,0:T(8,128)(2,1)S(1)} %constant_dynamic-update-slice_fusion.5.mine, bf16[8,48,512]{2,1,0:T(8,128)(2,1)S(1)} %collective-permute-done.15.other, ...), custom_call_target="tpu_custom_call" | custom-call | flops 3000000000 | bytes 4000000 | tf_op jit(solution)/shard_map/pallas_call | solution.py:494
  103.9 0.6 collective-permute-start.27
  104.5 1.4 %shard_map.89.refs_0_ = bf16[2,128,1024]{2,1,0:T(8,128)(2,1)} custom-call(s32[4]{0:T(128)S(1)} %pad_add_fusion.ids, bf16[128,512]{1,0:T(8,128)(2,1)S(1)} %get-tuple-element.41.own, bf16[128,512]{1,0:T(8,128)(2,1)S(1)} %collective-permute-done.32.got, f32[1,1024]{1,0:T(1,128)S(1)} %bitcast.25), custom_call_target="tpu_custom_call" | custom-call | bytes 524288 | tf_op jit(solution)/shard_map/pallas_call | solution.py:333
  105.9 3.7 %collective-permute-done.27.got = bf16[128,512]{1,0:T(8,128)(2,1)S(1)} collective-permute-done((bf16[128,512]{1,0:T(8,128)(2,1)S(1)}, bf16[128,512]{1,0:T(8,128)(2,1)S(1)}, u32[]{:S(2)}, u32[]{:S(2)}) %collective-permute-start.27) | collective-permute-done | bytes 131104 | tf_op jit(solution)/shard_map/ppermute | solution.py:33
  109.6 1.4 %shard_map.90 = bf16[2,128,1024]{2,1,0:T(8,128)(2,1)} custom-call(s32[4]{0:T(128)S(1)} %pad_add_fusion.ids, bf16[128,512]{1,0:T(8,128)(2,1)S(1)} %get-tuple-element.38.own, bf16[128,512]{1,0:T(8,128)(2,1)S(1)} %collective-permute-done.27.got, f32[1,1024]{1,0:T(1,128)S(1)} %bitcast.26, ...), custom_call_target="tpu_custom_call", output_to_operand_aliasing={{}: (4, {})} | custom-call | bytes 524288 | tf_op jit(solution)/shard_map/pallas_call | solution.py:333
  (55 shorter events, 0.3 us)
Async XLA Ops:
  0.0 6.7 %copy-start.1 = (bf16[2,256,512]{2,1,0:T(8,128)(2,1)S(1)}, bf16[2,256,512]{2,1,0:T(8,128)(2,1)}, u32[]{:S(2)}) copy-start(bf16[2,256,512]{2,1,0:T(8,128)(2,1)} %k_own.3) | copy-start | bytes 1572868
  0.0 7.6 %copy-start.11 = (bf16[1,32,768]{2,1,0:T(8,128)(2,1)S(1)}, bf16[1,32,768]{2,1,0:T(8,128)(2,1)}, u32[]{:S(2)}) copy-start(bf16[1,32,768]{2,1,0:T(8,128)(2,1)} %param.13) | copy-start | bytes 147460
  0.0 8.3 %collective-permute-start = (bf16[32,768]{1,0:T(8,128)(2,1)}, bf16[32,768]{1,0:T(8,128)(2,1)S(1)}, u32[]{:S(2)}, u32[]{:S(2)}) collective-permute-start(bf16[32,768]{1,0:T(8,128)(2,1)} %bitcast.27), channel_id=1, source_target_pairs={{0,8},{2,10},{4,12},{6,14},{8,0},{10,2},{12,4},{14,6},{16,24},{18,... | collective-permute-start | bytes 147464 | tf_op jit(solution)/shard_map/ppermute | solution.py:33
  3.0 6.1 %collective-permute-start.1 = (bf16[32,768]{1,0:T(8,128)(2,1)}, bf16[32,768]{1,0:T(8,128)(2,1)S(1)}, u32[]{:S(2)}, u32[]{:S(2)}) collective-permute-start(bf16[32,768]{1,0:T(8,128)(2,1)} %bitcast.28), channel_id=1, source_target_pairs={{0,16},{2,18},{4,20},{6,22},{8,24},{10,26},{12,28},{14,30},{16,0},... | collective-permute-start | bytes 147464 | tf_op jit(solution)/shard_map/ppermute | solution.py:33
  5.6 6.1 %collective-permute-start.2 = (bf16[32,768]{1,0:T(8,128)(2,1)}, bf16[32,768]{1,0:T(8,128)(2,1)S(1)}, u32[]{:S(2)}, u32[]{:S(2)}) collective-permute-start(bf16[32,768]{1,0:T(8,128)(2,1)} %bitcast.29), channel_id=1, source_target_pairs={{0,24},{2,26},{4,28},{6,30},{8,16},{10,18},{12,20},{14,22},{16,8},... | collective-permute-start | bytes 147464 | tf_op jit(solution)/shard_map/ppermute | solution.py:33
  6.7 11.5 %copy-start.12 = (f32[256,1]{0,1:T(1,128)S(1)}, f32[256,1]{0,1:T(1,128)}, u32[]{:S(2)}) copy-start(f32[256,1]{0,1:T(1,128)} %param.12) | copy-start | bytes 3076
  7.6 12.5 %collective-permute-start.5 = (bf16[2,256,512]{2,1,0:T(8,128)(2,1)S(1)}, bf16[2,256,512]{2,1,0:T(8,128)(2,1)S(1)}, u32[]{:S(2)}, u32[]{:S(2)}) collective-permute-start(bf16[2,256,512]{2,1,0:T(8,128)(2,1)S(1)} %pad_maximum_fusion.pair_a), channel_id=1, source_target_pairs={{0,2},{2,0},{4,6},{6,4},{8,10},{10,8},{12,14},{14,12},{16,18},{18,... | collective-permute-start | bytes 1572872 | tf_op jit(solution)/shard_map/ppermute | solution.py:33
  11.7 5.7 %collective-permute-start.3 = (bf16[4,32,768]{2,1,0:T(8,128)(2,1)S(1)}, bf16[4,32,768]{2,1,0:T(8,128)(2,1)S(1)}, u32[]{:S(2)}, u32[]{:S(2)}) collective-permute-start(bf16[4,32,768]{2,1,0:T(8,128)(2,1)S(1)} %pad_maximum_fusion.2.mine), channel_id=1, source_target_pairs={{0,4},{2,6},{4,0},{6,2},{8,12},{10,14},{12,8},{14,10},{16,20},{18,... | collective-permute-start | bytes 589832 | tf_op jit(solution)/shard_map/ppermute | solution.py:33
  18.2 1.9 %collective-permute-start.4 = (bf16[8,32,768]{2,1,0:T(8,128)(2,1)}, bf16[8,32,768]{2,1,0:T(8,128)(2,1)S(1)}, u32[]{:S(2)}, u32[]{:S(2)}) collective-permute-start(bf16[8,32,768]{2,1,0:T(8,128)(2,1)} %constant_dynamic-update-slice_fusion), channel_id=1, source_target_pairs={{0,2},{2,0},{4,6},{6,4},{8,10},{10,8},{12,14},{14,12},{16,18},{18,... | collective-permute-start | bytes 1179656 | tf_op jit(solution)/shard_map/ppermute | solution.py:33
  18.3 1.8 %collective-permute-start.6 = (f32[256,1]{1,0:T(8,128)S(1)}, f32[256,1]{1,0:T(8,128)S(1)}, u32[]{:S(2)}, u32[]{:S(2)}) collective-permute-start(f32[256,1]{1,0:T(8,128)S(1)} %copy.11.rate_a), channel_id=1, source_target_pairs={{0,2},{2,0},{4,6},{6,4},{8,10},{10,8},{12,14},{14,12},{16,18},{18,... | collective-permute-start | bytes 3080 | tf_op jit(solution)/shard_map/ppermute | solution.py:33
  18.9 4.8 %copy-start.10 = (bf16[256,512]{1,0:T(8,128)(2,1)S(1)}, bf16[256,512]{1,0:T(8,128)(2,1)}, u32[]{:S(2)}) copy-start(bf16[256,512]{1,0:T(8,128)(2,1)} %get-tuple-element.46) | copy-start | bytes 786436
  18.9 23.8 %collective-permute-start.16 = (bf16[2,256,512]{2,1,0:T(8,128)(2,1)S(1)}, bf16[2,256,512]{2,1,0:T(8,128)(2,1)S(1)}, u32[]{:S(2)}, u32[]{:S(2)}) collective-permute-start(bf16[2,256,512]{2,1,0:T(8,128)(2,1)S(1)} %pad_maximum_fusion.pair_a), channel_id=1, source_target_pairs={{0,8},{2,10},{4,12},{6,14},{8,16},{10,18},{12,20},{14,22},{16,24},... | collective-permute-start | bytes 1572872 | tf_op jit(solution)/shard_map/ppermute | solution.py:360
  21.6 66.8 %copy-start.2 = (bf16[512,768]{1,0:T(8,128)(2,1)}, bf16[512,768]{1,0:T(8,128)(2,1)S(1)}, u32[]{:S(2)}) copy-start(bf16[512,768]{1,0:T(8,128)(2,1)S(1)} %get-tuple-element.30.whole) | copy-start | bytes 2359300
  21.6 66.8 %copy-start = (bf16[2,256,512]{2,1,0:T(8,128)(2,1)S(1)}, bf16[2,256,512]{2,1,0:T(8,128)(2,1)}, u32[]{:S(2)}) copy-start(bf16[2,256,512]{2,1,0:T(8,128)(2,1)} %v_own.3) | copy-start | bytes 1572868
  21.7 66.8 %copy-start.3 = (bf16[2,256,512]{2,1,0:T(8,128)(2,1)S(1)}, bf16[2,256,512]{2,1,0:T(8,128)(2,1)}, u32[]{:S(2)}) copy-start(bf16[2,256,512]{2,1,0:T(8,128)(2,1)} %q.5) | copy-start | bytes 1572868
  21.7 66.8 %copy-start.5 = (bf16[2,256,512]{2,1,0:T(8,128)(2,1)S(1)}, bf16[2,256,512]{2,1,0:T(8,128)(2,1)}, u32[]{:S(2)}) copy-start(bf16[2,256,512]{2,1,0:T(8,128)(2,1)} %gates.3) | copy-start | bytes 1572868
  21.7 29.7 %collective-permute-start.17 = (bf16[2,256,512]{2,1,0:T(8,128)(2,1)S(1)}, bf16[2,256,512]{2,1,0:T(8,128)(2,1)S(1)}, u32[]{:S(2)}, u32[]{:S(2)}) collective-permute-start(bf16[2,256,512]{2,1,0:T(8,128)(2,1)S(1)} %pad_maximum_fusion.1), channel_id=1, source_target_pairs={{0,8},{2,10},{4,12},{6,14},{8,16},{10,18},{12,20},{14,22},{16,24},... | collective-permute-start | bytes 1572872 | tf_op jit(solution)/shard_map/ppermute | solution.py:360
  23.7 17.3 %collective-permute-start.28 = (bf16[256,512]{1,0:T(8,128)(2,1)S(1)}, bf16[256,512]{1,0:T(8,128)(2,1)S(1)}, u32[]{:S(2)}, u32[]{:S(2)}) collective-permute-start(bf16[256,512]{1,0:T(8,128)(2,1)S(1)} %copy-done.10), channel_id=1, source_target_pairs={{0,4},{2,6},{8,12},{10,14},{16,20},{18,22},{24,28},{26,30},{1,5},{... | collective-permute-start | bytes 786440 | tf_op jit(solution)/shard_map/ppermute | solution.py:360
  27.1 10.9 %collective-permute-start.7 = (bf16[192,512]{1,0:T(8,128)(2,1)S(1)}, bf16[192,512]{1,0:T(8,128)(2,1)S(1)}, u32[]{:S(2)}, u32[]{:S(2)}) collective-permute-start(bf16[192,512]{1,0:T(8,128)(2,1)S(1)} %get-tuple-element.25), channel_id=1, source_target_pairs={{0,4},{2,6},{4,0},{6,2},{8,12},{10,14},{12,8},{14,10},{16,20},{18,... | collective-permute-start | bytes 589832 | tf_op jit(solution)/shard_map/ppermute | solution.py:33
  27.2 23.1 %collective-permute-start.29 = (bf16[256,512]{1,0:T(8,128)(2,1)S(1)}, bf16[256,512]{1,0:T(8,128)(2,1)S(1)}, u32[]{:S(2)}, u32[]{:S(2)}) collective-permute-start(bf16[256,512]{1,0:T(8,128)(2,1)S(1)} %get-tuple-element.40), channel_id=1, source_target_pairs={{0,4},{2,6},{8,12},{10,14},{16,20},{18,22},{24,28},{26,30},{1,5},{... | collective-permute-start | bytes 786440 | tf_op jit(solution)/shard_map/ppermute | solution.py:360
  38.6 6.0 %collective-permute-start.10 = (bf16[48,512]{1,0:T(8,128)(2,1)S(1)}, bf16[48,512]{1,0:T(8,128)(2,1)S(1)}, u32[]{:S(2)}, u32[]{:S(2)}) collective-permute-start(bf16[48,512]{1,0:T(8,128)(2,1)S(1)} %get-tuple-element.29), channel_id=1, source_target_pairs={{0,24},{2,26},{4,28},{6,30},{8,16},{10,18},{12,20},{14,22},{16,8},... | collective-permute-start | bytes 147464 | tf_op jit(solution)/shard_map/ppermute | solution.py:33
  40.9 4.4 %collective-permute-start.8 = (bf16[48,512]{1,0:T(8,128)(2,1)S(1)}, bf16[48,512]{1,0:T(8,128)(2,1)S(1)}, u32[]{:S(2)}, u32[]{:S(2)}) collective-permute-start(bf16[48,512]{1,0:T(8,128)(2,1)S(1)} %get-tuple-element.27), channel_id=1, source_target_pairs={{0,8},{2,10},{4,12},{6,14},{8,0},{10,2},{12,4},{14,6},{16,24},{18,... | collective-permute-start | bytes 147464 | tf_op jit(solution)/shard_map/ppermute | solution.py:33
  42.7 5.2 %collective-permute-start.9 = (bf16[48,512]{1,0:T(8,128)(2,1)S(1)}, bf16[48,512]{1,0:T(8,128)(2,1)S(1)}, u32[]{:S(2)}, u32[]{:S(2)}) collective-permute-start(bf16[48,512]{1,0:T(8,128)(2,1)S(1)} %get-tuple-element.28), channel_id=1, source_target_pairs={{0,16},{2,18},{4,20},{6,22},{8,24},{10,26},{12,28},{14,30},{16,0},... | collective-permute-start | bytes 147464 | tf_op jit(solution)/shard_map/ppermute | solution.py:33
  44.6 7.4 %collective-permute-start.30 = (bf16[256,512]{1,0:T(8,128)(2,1)S(1)}, bf16[256,512]{1,0:T(8,128)(2,1)S(1)}, u32[]{:S(2)}, u32[]{:S(2)}) collective-permute-start(bf16[256,512]{1,0:T(8,128)(2,1)S(1)} %collective-permute-done.28.refs_1_), channel_id=1, source_target_pairs={{4,6},{6,4},{12,14},{14,12},{20,22},{22,20},{28,30},{30,28},{5,7},... | collective-permute-start | bytes 786440 | tf_op jit(solution)/shard_map/ppermute | solution.py:360
  45.3 20.3 %collective-permute-start.19 = (bf16[2,256,512]{2,1,0:T(8,128)(2,1)S(1)}, bf16[2,256,512]{2,1,0:T(8,128)(2,1)S(1)}, u32[]{:S(2)}, u32[]{:S(2)}) collective-permute-start(bf16[2,256,512]{2,1,0:T(8,128)(2,1)S(1)} %collective-permute-done.16.refs_0_), channel_id=1, source_target_pairs={{4,0},{6,2},{12,8},{14,10},{20,16},{22,18},{28,24},{30,26},{5,1},{... | collective-permute-start | bytes 1572872 | tf_op jit(solution)/shard_map/ppermute | solution.py:360
  48.5 5.8 %collective-permute-start.12 = (bf16[48,512]{1,0:T(8,128)(2,1)S(1)}, bf16[48,512]{1,0:T(8,128)(2,1)S(1)}, u32[]{:S(2)}, u32[]{:S(2)}) collective-permute-start(bf16[48,512]{1,0:T(8,128)(2,1)S(1)} %shard_map.84), channel_id=1, source_target_pairs={{0,16},{2,18},{4,20},{6,22},{8,24},{10,26},{12,28},{14,30},{16,0},... | collective-permute-start | bytes 147464 | tf_op jit(solution)/shard_map/ppermute | solution.py:33
  50.3 5.9 %collective-permute-start.13 = (bf16[48,512]{1,0:T(8,128)(2,1)S(1)}, bf16[48,512]{1,0:T(8,128)(2,1)S(1)}, u32[]{:S(2)}, u32[]{:S(2)}) collective-permute-start(bf16[48,512]{1,0:T(8,128)(2,1)S(1)} %shard_map.84), channel_id=1, source_target_pairs={{0,24},{2,26},{4,28},{6,30},{8,16},{10,18},{12,20},{14,22},{16,8},... | collective-permute-start | bytes 147464 | tf_op jit(solution)/shard_map/ppermute | solution.py:33
  51.4 10.1 %collective-permute-start.11 = (bf16[48,512]{1,0:T(8,128)(2,1)S(1)}, bf16[48,512]{1,0:T(8,128)(2,1)S(1)}, u32[]{:S(2)}, u32[]{:S(2)}) collective-permute-start(bf16[48,512]{1,0:T(8,128)(2,1)S(1)} %shard_map.84), channel_id=1, source_target_pairs={{0,8},{2,10},{4,12},{6,14},{8,0},{10,2},{12,4},{14,6},{16,24},{18,... | collective-permute-start | bytes 147464 | tf_op jit(solution)/shard_map/ppermute | solution.py:33
  52.1 10.8 %collective-permute-start.31 = (bf16[256,512]{1,0:T(8,128)(2,1)S(1)}, bf16[256,512]{1,0:T(8,128)(2,1)S(1)}, u32[]{:S(2)}, u32[]{:S(2)}) collective-permute-start(bf16[256,512]{1,0:T(8,128)(2,1)S(1)} %collective-permute-done.29.refs_2_), channel_id=1, source_target_pairs={{4,6},{6,4},{12,14},{14,12},{20,22},{22,20},{28,30},{30,28},{5,7},... | collective-permute-start | bytes 786440 | tf_op jit(solution)/shard_map/ppermute | solution.py:360
  54.3 13.2 %collective-permute-start.22 = (bf16[2,256,512]{2,1,0:T(8,128)(2,1)S(1)}, bf16[2,256,512]{2,1,0:T(8,128)(2,1)S(1)}, u32[]{:S(2)}, u32[]{:S(2)}) collective-permute-start(bf16[2,256,512]{2,1,0:T(8,128)(2,1)S(1)} %collective-permute-done.16.refs_0_), channel_id=1, source_target_pairs={{2,0},{6,4},{10,8},{14,12},{18,16},{22,20},{26,24},{30,28},{3,1},{... | collective-permute-start | bytes 1572872 | tf_op jit(solution)/shard_map/ppermute | solution.py:360
  56.2 26.7 %collective-permute-start.18 = (bf16[2,256,512]{2,1,0:T(8,128)(2,1)S(1)}, bf16[2,256,512]{2,1,0:T(8,128)(2,1)S(1)}, u32[]{:S(2)}, u32[]{:S(2)}) collective-permute-start(bf16[2,256,512]{2,1,0:T(8,128)(2,1)S(1)} %pad_maximum_fusion.1), channel_id=1, source_target_pairs={{0,4},{2,6},{8,12},{10,14},{16,20},{18,22},{24,28},{26,30},{1,5},{... | collective-permute-start | bytes 1572872 | tf_op jit(solution)/shard_map/ppermute | solution.py:360
  61.5 22.1 %collective-permute-start.20 = (bf16[2,256,512]{2,1,0:T(8,128)(2,1)S(1)}, bf16[2,256,512]{2,1,0:T(8,128)(2,1)S(1)}, u32[]{:S(2)}, u32[]{:S(2)}) collective-permute-start(bf16[2,256,512]{2,1,0:T(8,128)(2,1)S(1)} %collective-permute-done.17.refs_1_), channel_id=1, source_target_pairs={{4,0},{6,2},{12,8},{14,10},{20,16},{22,18},{28,24},{30,26},{5,1},{... | collective-permute-start | bytes 1572872 | tf_op jit(solution)/shard_map/ppermute | solution.py:360
  62.9 18.7 %collective-permute-start.14 = (bf16[4,48,512]{2,1,0:T(8,128)(2,1)S(1)}, bf16[4,48,512]{2,1,0:T(8,128)(2,1)S(1)}, u32[]{:S(2)}, u32[]{:S(2)}) collective-permute-start(bf16[4,48,512]{2,1,0:T(8,128)(2,1)S(1)} %pad_maximum_fusion.3), channel_id=1, source_target_pairs={{0,4},{2,6},{4,0},{6,2},{8,12},{10,14},{12,8},{14,10},{16,20},{18,... | collective-permute-start | bytes 589832 | tf_op jit(solution)/shard_map/ppermute | solution.py:33
  65.6 21.1 %collective-permute-start.25 = (bf16[2,256,512]{2,1,0:T(8,128)(2,1)S(1)}, bf16[2,256,512]{2,1,0:T(8,128)(2,1)S(1)}, u32[]{:S(2)}, u32[]{:S(2)}) collective-permute-start(bf16[2,256,512]{2,1,0:T(8,128)(2,1)S(1)} %collective-permute-done.19.refs_3_), channel_id=1, source_target_pairs={{0,2},{2,0},{8,10},{10,8},{16,18},{18,16},{24,26},{26,24},{1,3},{3... | collective-permute-start | bytes 1572872 | tf_op jit(solution)/shard_map/ppermute | solution.py:360
  67.5 25.5 %collective-permute-start.21 = (bf16[2,256,512]{2,1,0:T(8,128)(2,1)S(1)}, bf16[2,256,512]{2,1,0:T(8,128)(2,1)S(1)}, u32[]{:S(2)}, u32[]{:S(2)}) collective-permute-start(bf16[2,256,512]{2,1,0:T(8,128)(2,1)S(1)} %pad_maximum_fusion.1), channel_id=1, source_target_pairs={{0,2},{4,6},{8,10},{12,14},{16,18},{20,22},{24,26},{28,30},{1,3},{... | collective-permute-start | bytes 1572872 | tf_op jit(solution)/shard_map/ppermute | solution.py:360
  81.6 13.0 %collective-permute-start.23 = (bf16[2,256,512]{2,1,0:T(8,128)(2,1)S(1)}, bf16[2,256,512]{2,1,0:T(8,128)(2,1)S(1)}, u32[]{:S(2)}, u32[]{:S(2)}) collective-permute-start(bf16[2,256,512]{2,1,0:T(8,128)(2,1)S(1)} %collective-permute-done.17.refs_1_), channel_id=1, source_target_pairs={{2,0},{6,4},{10,8},{14,12},{18,16},{22,20},{26,24},{30,28},{3,1},{... | collective-permute-start | bytes 1572872 | tf_op jit(solution)/shard_map/ppermute | solution.py:360
  82.9 11.7 %collective-permute-start.24 = (bf16[2,256,512]{2,1,0:T(8,128)(2,1)S(1)}, bf16[2,256,512]{2,1,0:T(8,128)(2,1)S(1)}, u32[]{:S(2)}, u32[]{:S(2)}) collective-permute-start(bf16[2,256,512]{2,1,0:T(8,128)(2,1)S(1)} %collective-permute-done.18.refs_2_), channel_id=1, source_target_pairs={{4,6},{6,4},{12,14},{14,12},{20,22},{22,20},{28,30},{30,28},{5,7},... | collective-permute-start | bytes 1572872 | tf_op jit(solution)/shard_map/ppermute | solution.py:360
  83.6 11.0 %collective-permute-start.26 = (bf16[2,256,512]{2,1,0:T(8,128)(2,1)S(1)}, bf16[2,256,512]{2,1,0:T(8,128)(2,1)S(1)}, u32[]{:S(2)}, u32[]{:S(2)}) collective-permute-start(bf16[2,256,512]{2,1,0:T(8,128)(2,1)S(1)} %collective-permute-done.20.refs_4_), channel_id=1, source_target_pairs={{0,2},{2,0},{8,10},{10,8},{16,18},{18,16},{24,26},{26,24},{1,3},{3... | collective-permute-start | bytes 1572872 | tf_op jit(solution)/shard_map/ppermute | solution.py:360
  86.7 6.3 %copy-start.4 = (bf16[2,256,512]{2,1,0:T(8,128)(2,1)}, bf16[2,256,512]{2,1,0:T(8,128)(2,1)S(1)}, u32[]{:S(2)}) copy-start(bf16[2,256,512]{2,1,0:T(8,128)(2,1)S(1)} %collective-permute-done.25.refs_9_.refs_8_) | copy-start | bytes 1572868
  86.7 13.3 %collective-permute-start.15 = (bf16[8,48,512]{2,1,0:T(8,128)(2,1)S(1)}, bf16[8,48,512]{2,1,0:T(8,128)(2,1)S(1)}, u32[]{:S(2)}, u32[]{:S(2)}) collective-permute-start(bf16[8,48,512]{2,1,0:T(8,128)(2,1)S(1)} %constant_dynamic-update-slice_fusion.5.mine), channel_id=1, source_target_pairs={{0,2},{2,0},{4,6},{6,4},{8,10},{10,8},{12,14},{14,12},{16,18},{18,... | collective-permute-start | bytes 1179656 | tf_op jit(solution)/shard_map/ppermute | solution.py:33
  93.0 11.5 %collective-permute-start.32 = (bf16[128,512]{1,0:T(8,128)(2,1)S(1)}, bf16[128,512]{1,0:T(8,128)(2,1)S(1)}, u32[]{:S(2)}, u32[]{:S(2)}) collective-permute-start(bf16[128,512]{1,0:T(8,128)(2,1)S(1)} %get-tuple-element.42), channel_id=1, source_target_pairs={{0,1},{1,0},{2,3},{3,2},{4,5},{5,4},{6,7},{7,6},{8,9},{9,8},{10,11... | collective-permute-start | bytes 393224 | tf_op jit(solution)/shard_map/ppermute | solution.py:33
  94.6 0.8 copy-start.7
  94.6 1.0 copy-start.8
  95.6 0.8 copy-start.9
  100.1 4.4 %copy-start.6 = (f32[1024]{0:T(1024)S(1)}, f32[1024]{0:T(1024)}, u32[]{:S(2)}) copy-start(f32[1024]{0:T(1024)} %param.15) | copy-start | bytes 12292
  103.9 5.7 %collective-permute-start.27 = (bf16[128,512]{1,0:T(8,128)(2,1)S(1)}, bf16[128,512]{1,0:T(8,128)(2,1)S(1)}, u32[]{:S(2)}, u32[]{:S(2)}) collective-permute-start(bf16[128,512]{1,0:T(8,128)(2,1)S(1)} %get-tuple-element.39), channel_id=1, source_target_pairs={{0,1},{1,0},{2,3},{3,2},{4,5},{5,4},{6,7},{7,6},{8,9},{9,8},{10,11... | collective-permute-start | bytes 393224 | tf_op jit(solution)/shard_map/ppermute | solution.py:33

commit v3 on v2

--- a/solution.py
+++ b/solution.py
@@ -57,7 +57,69 @@
     return v / (1.0 + jnp.exp(-v))
 
 
-def gradient_body(planes, ids, mine, other, beside, pair_a, pair_b, rate_a, rate_b, *refs):
+def prepare_body(keys, values, rates, pair_0, pair_1, target, held, sems, value_sem):
+    load = pltpu.make_async_copy(values.at[0], held, value_sem)
+    load.start()
+    copies = []
+    for g, pair in enumerate((pair_0, pair_1)):
+        for which, source in enumerate((keys, values)):
+            copies.append(
+                pltpu.make_async_copy(source.at[g], pair.at[which], sems.at[2 * g + which])
+            )
+    for copy in copies:
+        copy.start()
+    load.wait()
+    target[...] = (-rates[...] * held[...].astype(F32)).astype(BF)
+    for copy in copies:
+        copy.wait()
+
+
+def prepared(keys, values, rates):
+    rows, depth = keys.shape[1:]
+    anywhere = pl.BlockSpec(memory_space=pl.ANY)
+    pair = jax.ShapeDtypeStruct((2, rows, depth), BF)
+    return pl.pallas_call(
+        prepare_body,
+        out_shape=(pair, pair, jax.ShapeDtypeStruct((rows, depth), BF)),
+        in_specs=[anywhere, anywhere, vmem_spec()],
+        out_specs=(anywhere, anywhere, vmem_spec()),
+        scratch_shapes=[
+            pltpu.VMEM((rows, depth), BF),
+            pltpu.SemaphoreType.DMA((4,)),
+            pltpu.SemaphoreType.DMA,
+        ],
+        cost_estimate=cost_of(0, rows * depth * 8),
+    )(keys, values, rates)
+
+
+def pick_body(ids, own, far, out, sems):
+    side = ids[1]
+    for condition, source in ((side == 0, own), (side == 1, far)):
+
+        @pl.when(condition)
+        def _():
+            copies = [
+                pltpu.make_async_copy(source.at[w], out.at[w], sems.at[w]) for w in range(2)
+            ]
+            for copy in copies:
+                copy.start()
+            for copy in copies:
+                copy.wait()
+
+
+def picked(ids, own, far):
+    anywhere = pl.BlockSpec(memory_space=pl.ANY)
+    return pl.pallas_call(
+        pick_body,
+        out_shape=jax.ShapeDtypeStruct(own.shape, own.dtype),
+        in_specs=[pl.BlockSpec(memory_space=pltpu.SMEM), anywhere, anywhere],
+        out_specs=anywhere,
+        scratch_shapes=[pltpu.SemaphoreType.DMA((2,))],
+        cost_estimate=cost_of(0, own.size * 4),
+    )(ids, own, far)
+
+
+def gradient_body(planes, ids, mine, other, beside, pair_a, pair_b, target_a, target_b, *refs):
     send, keep, whole, total = refs[:4]
     plane, side, core = ids[0], ids[1], ids[2]
     rows = mine.shape[1]
@@ -80,9 +142,8 @@
     gate_up_w = jnp.concatenate(parts[:2], 1)
     out_w = parts[2]
     first = None
-    for pair, rate in ((pair_a, rate_a), (pair_b, rate_b)):
-        key_rows = pair[0]
-        target = (-rate[...] * pair[1].astype(F32)).astype(BF)
+    for pair, target_rows in ((pair_a, target_a), (pair_b, target_b)):
+        key_rows, target = pair[0], target_rows[...]
         gate_up = dot_nn(key_rows, gate_up_w)
         g, u = gate_up[:, :half], gate_up[:, half:]
         dh = dot_nn(target, out_w)
@@ -135,8 +196,9 @@
     for slot, choices in enumerate(options):
         for condition, source in choices:
             for which in range(2):
-                part = source[which] if isinstance(source, tuple) else source.at[which]
-                copy = pltpu.make_async_copy(part, held.at[slot, which], sems.at[slot, which])
+                copy = pltpu.make_async_copy(
+                    source.at[which], held.at[slot, which], sems.at[slot, which]
+                )
                 if condition is None:
                     copy.start()
                 else:
@@ -180,16 +242,16 @@
 
 
 def first_group_body(ids, q, k_own, v_own, gates, whole, *refs):
-    far, near_k, near_v, near, own_beside, far_beside, diag_k, diag_v, diag = refs[:9]
-    outs, (held, sems, gated) = refs[9:-3], refs[-3:]
+    far, near, own_beside, far_beside, diag = refs[:5]
+    outs, (held, sems, gated) = refs[5:-3], refs[-3:]
     plane, side, core = ids[0], ids[1], ids[2]
     wait = fetch(
         (held, sems),
         [
             [(None, far)],
-            [(side == 1, (near_k, near_v)), (side == 0, near)],
+            [(None, near)],
             [(core == 1, own_beside), (core == 0, far_beside)],
-            [(side == 1, (diag_k, diag_v)), (side == 0, diag)],
+            [(None, diag)],
         ],
     )
     later = (plane > 0).astype(jnp.int32)
@@ -216,29 +278,22 @@
 
 
 def second_group_body(ids, q, k_own, v_own, *refs):
-    far_0, far_1, near_own, near_0, near_1, own_beside, far_beside_0, far_beside_1 = refs[:8]
-    diag_own, diag_0, diag_1, out, held, sems = refs[8:]
+    far_0, far_1, near_0, near_1, own_beside, far_beside_0, far_beside_1 = refs[:7]
+    diag_0, diag_1, out, held, sems = refs[7:]
     plane, side, core = ids[0], ids[1], ids[2]
-    begin, after = plane == 0, plane > 0
+    begin = plane == 0
+    wrapped = begin & (side == 0)
     wait = fetch(
         (held, sems),
         [
-            [(begin, far_0), (after, far_1)],
-            [
-                (side == 1, near_own),
-                ((side == 0) & begin, near_0),
-                ((side == 0) & after, near_1),
-            ],
+            [(begin, far_0), (plane > 0, far_1)],
+            [(wrapped, near_0), (jnp.logical_not(wrapped), near_1)],
             [
                 (core == 1, own_beside),
                 ((core == 0) & begin, far_beside_0),
-                ((core == 0) & after, far_beside_1),
+                ((core == 0) & (plane > 0), far_beside_1),
             ],
-            [
-                (side == 1, diag_own),
-                ((side == 0) & begin, diag_0),
-                ((side == 0) & after, diag_1),
-            ],
+            [(wrapped, diag_0), (jnp.logical_not(wrapped), diag_1)],
         ],
     )
     out[...] = window(q[0], k_own[0], v_own[0], held, wait, None)
@@ -309,18 +364,26 @@
     spread(ids, ((win[...] + fast) * silu(gate)).astype(BF), outs, gated)
 
 
-def norm_body(ids, own, got, gain, *refs):
-    out = refs[-1]
+def norm_body(group, ids, own, got, gain, *refs):
+    out, held, sems = refs[-3:]
     head = ids[3]
     rows, depth = own.shape
-    a = own[...].astype(F32)
-    b = got[...].astype(F32)
-    low = jnp.where(head == 0, a, b)
-    high = jnp.where(head == 0, b, a)
-    square = jnp.sum(a * a, -1, keepdims=True) + jnp.sum(b * b, -1, keepdims=True)
-    inv = lax.rsqrt(square / (2 * depth) + 1e-06)
-    out[0, :, :depth] = (low * inv * gain[:, :depth]).astype(BF)
-    out[0, :, depth:] = (high * inv * gain[:, depth:]).astype(BF)
+    chunk = rows // 4
+    copies = []
+    for c in range(4):
+        at = slice(c * chunk, (c + 1) * chunk)
+        a = own[at, :].astype(F32)
+        b = got[at, :].astype(F32)
+        low = jnp.where(head == 0, a, b)
+        high = jnp.where(head == 0, b, a)
+        square = jnp.sum(a * a, -1, keepdims=True) + jnp.sum(b * b, -1, keepdims=True)
+        inv = lax.rsqrt(square / (2 * depth) + 1e-06)
+        held[at, :depth] = (low * inv * gain[:, :depth]).astype(BF)
+        held[at, depth:] = (high * inv * gain[:, depth:]).astype(BF)
+        copies.append(pltpu.make_async_copy(held.at[at], out.at[group, at], sems.at[c]))
+        copies[-1].start()
+    for copy in copies:
+        copy.wait()
 
 
 def finished(ids, group, gated, norm_gain, before):
@@ -331,17 +394,17 @@
         rows, depth = own.shape
         earlier = () if before is None else (before,)
         return pl.pallas_call(
-            norm_body,
-            grid=(1,),
+            functools.partial(norm_body, group),
             out_shape=jax.ShapeDtypeStruct((2, rows, total), BF),
             in_specs=[
                 pl.BlockSpec(memory_space=pltpu.SMEM),
-                pl.BlockSpec((rows, depth), lambda i: (0, 0)),
-                pl.BlockSpec((rows, depth), lambda i: (0, 0)),
-                pl.BlockSpec((1, total), lambda i: (0, 0)),
+                vmem_spec(),
+                vmem_spec(),
+                vmem_spec(),
                 *([pl.BlockSpec(memory_space=pl.ANY)] * len(earlier)),
             ],
-            out_specs=pl.BlockSpec((1, rows, total), lambda i: (group, 0, 0)),
+            out_specs=pl.BlockSpec(memory_space=pl.ANY),
+            scratch_shapes=[pltpu.VMEM((rows, total), BF), pltpu.SemaphoreType.DMA((4,))],
             input_output_aliases={4: 0} if earlier else {},
             compiler_params=pltpu.CompilerParams(vmem_limit_bytes=VMEM_LIMIT),
             cost_estimate=cost_of(0, 4 * rows * total),
@@ -374,28 +437,14 @@
     width = fast_init.shape[2] // 3
     half = width // 2
     everyone = range(count)
-    side_up = [(i, i ^ 2) for i in everyone if i & 2 == 0]
-    side_down = [(i, i ^ 2) for i in everyone if i & 2]
-    core_up = [(i, i ^ 1) for i in everyone if i & 1 == 0]
-    core_down = [(i, i ^ 1) for i in everyone if i & 1]
-    high_cores = [(i, i ^ 1) for i in everyone if i & 2]
-    low_cores = [(i, i ^ 1) for i in everyone if i & 2 == 0]
-
     local = fast_init[0]
     arrived = [swapped(local, 4 * m) for m in range(1, planes)]
+    pair_0, pair_1, target = prepared(keys, values, token_rates)
+    beside_0 = swapped(pair_0, 1)
+    target_beside = swapped(target, 1)
     mine_w = jnp.stack([local] + arrived)
-    other_w = swapped(mine_w, 2)
+    other_w = swapped(after(mine_w, beside_0, target_beside), 2)
     beside_w = swapped(jnp.concatenate([mine_w, other_w], 0), 1)
-
-    pair_0 = jnp.stack([keys[0], values[0]])
-    pair_1 = jnp.stack([keys[1], values[1]])
-    beside_0 = swapped(pair_0, 1)
-    beside_1 = sent(pair_1, core_up)
-    rates_beside = swapped(token_rates, 1)
-    near_k = sent(keys[0], side_up)
-    near_v = sent(after(values[0], other_w), side_up)
-    diag_k = sent(near_k, high_cores)
-    diag_v = sent(near_v, high_cores)
 
     pieces = 2 * planes
     part = -(-3 * half // (16 * pieces)) * 16
@@ -404,7 +453,7 @@
         scratch.append(pltpu.VMEM((depth, 3 * width), F32))
     send, keep, whole = call(
         functools.partial(gradient_body, planes),
-        (ids, mine_w, other_w, beside_w, pair_0, beside_0, token_rates, rates_beside),
+        (ids, mine_w, other_w, beside_w, pair_0, beside_0, target, target_beside),
         (
             jax.ShapeDtypeStruct((planes * part, depth), BF),
             jax.ShapeDtypeStruct((planes * part, depth), F32),
@@ -433,17 +482,13 @@
     core_grad = swapped(side_grad, 1)
 
     ring = [(i, (i + reach) % count) for i in everyone]
-    line = [(i, i + reach) for i in range(count - reach)]
     far_0 = sent(after(pair_0, mine_w), ring)
-    far_1 = sent(after(pair_1, send), line)
-    far_beside_0 = sent(far_0, core_down)
-    far_beside_1 = sent(far_1, core_down)
-    near_0 = sent(after(far_0, got), side_down)
-    diag_0 = sent(near_0, low_cores)
-    near_own = sent(after(pair_1, got), side_up)
-    diag_own = sent(near_own, high_cores)
-    near_1 = sent(after(far_1, total), side_down)
-    diag_1 = sent(near_1, low_cores)
+    pair_1, far_0, _ = lax.optimization_barrier((pair_1, far_0, send))
+    far_1 = sent(pair_1, ring)
+    near_0 = swapped(picked(ids, pair_0, far_0), 2)
+    near_1 = swapped(picked(ids, pair_1, far_1), 2)
+    beside_1, far_beside_0, far_beside_1 = (swapped(v, 1) for v in (pair_1, far_0, far_1))
+    diag_0, diag_1 = (swapped(v, 1) for v in (near_0, near_1))
 
     flipped, norms = call(
         weights_body,
@@ -465,7 +510,7 @@
         ids,
         [queries, keys, values, gates],
         [whole],
-        [far_0, near_k, near_v, near_0, beside_0, far_beside_0, diag_k, diag_v, diag_0],
+        [far_0, near_0, beside_0, far_beside_0, diag_0],
         split,
         rows,
         depth,
@@ -478,8 +523,7 @@
         ids,
         [queries, keys, values],
         [],
-        [far_0, far_1, near_own, near_0, near_1, beside_1, far_beside_0, far_beside_1]
-        + [diag_own, diag_0, diag_1],
+        [far_0, far_1, near_0, near_1, beside_1, far_beside_0, far_beside_1, diag_0, diag_1],
         jax.ShapeDtypeStruct((rows, depth), F32),
         rows,
         depth,

time: 111 us -> 159 us (1.43)
  Pallas kernels: 18.5 us -> 87.5 us
  starting transfers between devices: 50.1 us -> 25.2 us
  local copies, waits for them, and re-layouts: 7.05 us -> 10.2 us
    pallas_call x2 -> x5, Pallas kernels: 2.85 us -> 72.6 us  [the longest x2 35.3 us: picked(): pl.pallas_call(pick_body, out_shape=jax.ShapeDtypeStruct(own.shape, own.d...]
    ppermute x15 -> x2, starting transfers between devices: 29.2 us -> 0.95 us  [sent(): return lax.ppermute(value, axis, pairs)]
    ppermute x18 -> x25, waiting for transfers between devices: 33.9 us -> 28.3 us  [swapped(): return lax.ppermute(value, axis, [(i, i ^ mask) for i in range(count)])]
    unnamed x35 -> x43, local copies, waits for them, and re-layouts: 4.48 us -> 9.47 us
    ppermute x15 -> x2, waiting for transfers between devices: 0.04 us -> 4.36 us  [sent(): return lax.ppermute(value, axis, pairs)]
    ppermute x18 -> x25, starting transfers between devices: 20.9 us -> 24.2 us  [swapped(): return lax.ppermute(value, axis, [(i, i ^ mask) for i in range(count)])]
    squeeze x2 -> x0, local copies, waits for them, and re-layouts: 1.86 us -> none  [the longest x1 1.09 us: shards(): near_v = sent(after(values[0], other_w), side_up)]
  transfers between devices with their start and end apart: 33 -> 27, of which waited for: 11 -> 6; matrix products, arithmetic and copies ran while one was open for 5% -> 6% of each run, Pallas kernels for 15% -> 54%
where the time goes in v3:
time: 159 us; the launch traced here: 158 us
  Pallas kernels  87.5 us (55%)
  waiting for transfers between devices  32.6 us (21%)
  starting transfers between devices  25.2 us (16%)
  local copies, waits for them, and re-layouts  10.2 us (6%)
  other arithmetic  1.76 us (1%)
    pallas_call x2, Pallas kernels, picked(): pl.pallas_call(pick_body, out_shape=jax.ShapeDtypeStruct(own.shape, own.d...  35.3 us
    pallas_call x1, Pallas kernels, prepared(): pl.pallas_call(prepare_body, out_shape=(pair, pair, jax.ShapeDtypeStruct(...  34.5 us
    ppermute x25, waiting for transfers between devices, swapped(): return lax.ppermute(value, axis, [(i, i ^ mask) for i in range(count)])  28.3 us
    ppermute x25, starting transfers between devices, swapped(): return lax.ppermute(value, axis, [(i, i ^ mask) for i in range(count)])  24.2 us
    unnamed x43, local copies, waits for them, and re-layouts  9.47 us
    pallas_call x2, Pallas kernels, group_call(): pl.pallas_call(body, grid=(1,), out_shape=outs, in_specs=[pl.BlockSpec(me...  7.48 us
    ppermute x2, waiting for transfers between devices, sent(): return lax.ppermute(value, axis, pairs)  4.36 us
    pallas_call x1, Pallas kernels, shards(): pl.pallas_call(functools.partial(update_body, planes), grid=(1,), out_sha...  3.82 us
  transfers between devices with their start and end apart: 27, of which 6 were waited for; matrix products, arithmetic and copies ran while one was open for 6% of the time, Pallas kernels for 54%

profile of v3, /device:TPU:0, one launch (start us, length us, event | category | flops | bytes accessed | tf_op | source)
XLA Modules:
  0.0 158.3 jit_solution(843805996152629039)
XLA Ops:
  0.0 3.0 %collective-permute-start = (bf16[32,768]{1,0:T(8,128)(2,1)}, bf16[32,768]{1,0:T(8,128)(2,1)S(1)}, u32[]{:S(2)}, u32[]{:S(2)}) collective-permute-start(bf16[32,768]{1,0:T(8,128)(2,1)} %bitcast.23), channel_id=1, source_target_pairs={{0,8},{2,10},{4,12},{6,14},{8,0},{10,2},{12,4},{14,6},{16,24},{18,... | collective-permute-start | bytes 147464 | tf_op jit(solution)/shard_map/ppermute | solution.py:33
  3.0 2.6 %collective-permute-start.1 = (bf16[32,768]{1,0:T(8,128)(2,1)}, bf16[32,768]{1,0:T(8,128)(2,1)S(1)}, u32[]{:S(2)}, u32[]{:S(2)}) collective-permute-start(bf16[32,768]{1,0:T(8,128)(2,1)} %bitcast.24), channel_id=1, source_target_pairs={{0,16},{2,18},{4,20},{6,22},{8,24},{10,26},{12,28},{14,30},{16,0},... | collective-permute-start | bytes 147464 | tf_op jit(solution)/shard_map/ppermute | solution.py:33
  5.6 1.5 copy.10.rates
  7.1 34.5 %shard_map.82 = (bf16[2,256,512]{2,1,0:T(8,128)(2,1)}, bf16[2,256,512]{2,1,0:T(8,128)(2,1)}, bf16[256,512]{1,0:T(8,128)(2,1)}) custom-call(bf16[2,256,512]{2,1,0:T(8,128)(2,1)} %k_own.3, bf16[2,256,512]{2,1,0:T(8,128)(2,1)} %v_own.3, f32[256,1]{1,0:T(8,128)} %copy.10.rates), custom_call_target="tpu_custom_call" | custom-call | bytes 1048576 | tf_op jit(solution)/shard_map/pallas_call | solution.py:81
  41.6 0.0 copy-start.4
  41.6 0.1 collective-permute-start.3
  41.7 0.5 collective-permute-start.4
  42.2 0.8 constant_dynamic-update-slice_fusion.4
  43.0 0.0 collective-permute-done
  43.0 0.0 collective-permute-done.1
  43.0 0.8 pad_maximum_fusion.mine
  43.9 0.9 collective-permute-start.16
  44.8 0.0 collective-permute-done.3.pair_b.refs_2_
  44.8 1.6 collective-permute-start.5
  46.4 5.1 %collective-permute-done.5.other = bf16[4,32,768]{2,1,0:T(8,128)(2,1)S(1)} collective-permute-done((bf16[4,32,768]{2,1,0:T(8,128)(2,1)S(1)}, bf16[4,32,768]{2,1,0:T(8,128)(2,1)S(1)}, u32[]{:S(2)}, u32[]{:S(2)}) %collective-permute-start.5) | collective-permute-done | bytes 196640 | tf_op jit(solution)/shard_map/ppermute | solution.py:33
  51.5 0.1 collective-permute-start.6
  51.7 0.1 pad_add_fusion.ids
  51.7 1.6 %collective-permute-done.6.beside = bf16[8,32,768]{2,1,0:T(8,128)(2,1)S(1)} collective-permute-done((bf16[8,32,768]{2,1,0:T(8,128)(2,1)S(1)}, bf16[8,32,768]{2,1,0:T(8,128)(2,1)S(1)}, u32[]{:S(2)}, u32[]{:S(2)}) %collective-permute-start.6) | collective-permute-done | bytes 393248 | tf_op jit(solution)/shard_map/ppermute | solution.py:33
  53.3 0.9 copy-done.10
  54.3 1.5 shard_map.83
  55.8 4.4 %collective-permute-done.16.far.refs_0_ = bf16[2,256,512]{2,1,0:T(8,128)(2,1)S(1)} collective-permute-done((bf16[2,256,512]{2,1,0:T(8,128)(2,1)}, bf16[2,256,512]{2,1,0:T(8,128)(2,1)S(1)}, u32[]{:S(2)}, u32[]{:S(2)}) %collective-permute-start.16) | collective-permute-done | bytes 524320 | tf_op jit(solution)/shard_map/ppermute | solution.py:423
  60.1 0.0 collective-permute-start.17
  60.1 1.5 collective-permute-start.7
  61.6 4.9 %collective-permute-done.7.got = bf16[192,512]{1,0:T(8,128)(2,1)S(1)} collective-permute-done((bf16[192,512]{1,0:T(8,128)(2,1)S(1)}, bf16[192,512]{1,0:T(8,128)(2,1)S(1)}, u32[]{:S(2)}, u32[]{:S(2)}) %collective-permute-start.7) | collective-permute-done | bytes 196640 | tf_op jit(solution)/shard_map/ppermute | solution.py:33
  66.5 0.6 shard_map.84
  67.1 3.6 %collective-permute-start.10 = (bf16[48,512]{1,0:T(8,128)(2,1)S(1)}, bf16[48,512]{1,0:T(8,128)(2,1)S(1)}, u32[]{:S(2)}, u32[]{:S(2)}) collective-permute-start(bf16[48,512]{1,0:T(8,128)(2,1)S(1)} %get-tuple-element.33), channel_id=1, source_target_pairs={{0,24},{2,26},{4,28},{6,30},{8,16},{10,18},{12,20},{14,22},{16,8},... | collective-permute-start | bytes 147464 | tf_op jit(solution)/shard_map/ppermute | solution.py:33
  70.7 0.8 collective-permute-start.9
  71.6 17.7 %shard_map.87 = bf16[2,256,512]{2,1,0:T(8,128)(2,1)} custom-call(s32[4]{0:T(128)} %copy-done.11, bf16[2,256,512]{2,1,0:T(8,128)(2,1)} %get-tuple-element.38.pair_a.own, bf16[2,256,512]{2,1,0:T(8,128)(2,1)} %copy-done.2), custom_call_target="tpu_custom_call" | custom-call | bytes 1048576 | tf_op jit(solution)/shard_map/pallas_call | solution.py:112
  89.2 1.3 collective-permute-start.18
  90.6 0.6 copy-done.12
  91.2 0.6 shard_map.85
  91.7 2.1 %collective-permute-start.12 = (bf16[48,512]{1,0:T(8,128)(2,1)S(1)}, bf16[48,512]{1,0:T(8,128)(2,1)}, u32[]{:S(2)}, u32[]{:S(2)}) collective-permute-start(bf16[48,512]{1,0:T(8,128)(2,1)S(1)} %shard_map.85), channel_id=1, source_target_pairs={{0,16},{2,18},{4,20},{6,22},{8,24},{10,26},{12,28},{14,30},{16,0},... | collective-permute-start | bytes 147464 | tf_op jit(solution)/shard_map/ppermute | solution.py:33
  93.9 1.5 collective-permute-start.13
  95.4 0.5 collective-permute-start.11
  95.9 0.6 constant_dynamic-update-slice_fusion.9
  96.5 0.0 copy-start.5
  96.6 0.1 collective-permute-start.21
  96.6 0.7 copy-done.5
  97.3 17.7 %shard_map.88 = bf16[2,256,512]{2,1,0:T(8,128)(2,1)} custom-call(s32[4]{0:T(128)} %copy-done.11, bf16[2,256,512]{2,1,0:T(8,128)(2,1)} %get-tuple-element.40.own, bf16[2,256,512]{2,1,0:T(8,128)(2,1)} %copy-done.5), custom_call_target="tpu_custom_call" | custom-call | bytes 1048576 | tf_op jit(solution)/shard_map/pallas_call | solution.py:112
  115.0 0.0 copy-start.7
  115.0 0.0 copy-start.9
  115.0 0.1 collective-permute-start.20
  115.1 0.8 collective-permute-start.19
  116.0 0.8 pad_maximum_fusion.1
  116.8 1.3 collective-permute-start.14
  118.1 1.4 constant_dynamic-update-slice_fusion.8
  119.6 1.4 constant_dynamic-update-slice_fusion.7
  121.0 12.9 %collective-permute-done.14 = bf16[4,48,512]{2,1,0:T(8,128)(2,1)S(1)} collective-permute-done((bf16[4,48,512]{2,1,0:T(8,128)(2,1)S(1)}, bf16[4,48,512]{2,1,0:T(8,128)(2,1)S(1)}, u32[]{:S(2)}, u32[]{:S(2)}) %collective-permute-start.14) | collective-permute-done | bytes 196640 | tf_op jit(solution)/shard_map/ppermute | solution.py:33
  133.9 0.5 collective-permute-start.24
  134.4 0.6 constant_dynamic-update-slice_fusion.6
  135.0 0.7 constant_dynamic-update-slice_fusion.5.mine
  135.7 0.0 collective-permute-start.15
  136.4 1.0 shard_map.86
  137.3 0.0 copy-start.6
  137.4 3.8 %shard_map.91 = (bf16[128,512]{1,0:T(8,128)(2,1)S(1)}, bf16[128,512]{1,0:T(8,128)(2,1)S(1)}) custom-call(s32[4]{0:T(128)S(1)} %copy-done.13, bf16[2,256,512]{2,1,0:T(8,128)(2,1)S(1)} %copy-done.7, bf16[2,256,512]{2,1,0:T(8,128)(2,1)S(1)} %copy-done, bf16[2,256,512]{2,1,0:T(8,128)(2,1)S(1)} %copy-done.1, bf16[2,256,512]{2,1,0:T(8,128)(2,1)S(1)} %copy-done.9, ...), custom_call_target="tpu_custom_call" | custom-call | flops 1342177280 | bytes 3932160 | tf_op jit(solution)/shard_map/pallas_call | solution.py:309
  141.2 1.6 %collective-permute-start.26 = (bf16[128,512]{1,0:T(8,128)(2,1)S(1)}, bf16[128,512]{1,0:T(8,128)(2,1)S(1)}, u32[]{:S(2)}, u32[]{:S(2)}) collective-permute-start(bf16[128,512]{1,0:T(8,128)(2,1)S(1)} %get-tuple-element.44), channel_id=1, source_target_pairs={{0,1},{1,0},{2,3},{3,2},{4,5},{5,4},{6,7},{7,6},{8,9},{9,8},{10,11... | collective-permute-start | bytes 393224 | tf_op jit(solution)/shard_map/ppermute | solution.py:33
  142.9 0.8 copy-done.16
  143.7 3.7 %shard_map.89.win = f32[256,512]{1,0:T(8,128)S(1)} custom-call(s32[4]{0:T(128)S(1)} %copy-done.13, bf16[2,256,512]{2,1,0:T(8,128)(2,1)S(1)} %copy-done.7, bf16[2,256,512]{2,1,0:T(8,128)(2,1)S(1)} %copy-done, bf16[2,256,512]{2,1,0:T(8,128)(2,1)S(1)} %copy-done.1, bf16[2,256,512]{2,1,0:T(8,128)(2,1)S(1)} %copy-done.3, bf16[2,256,512]{2,1,0:T(8,128)(2,1)S(1)} %copy-done.6, ...), custom_call_target="tpu_custom_call" | custom-call | flops 1342177280 | bytes 3932160 | tf_op jit(solution)/shard_map/pallas_call | solution.py:309
  147.4 0.0 copy-start.14
  147.4 3.8 %shard_map.90 = (bf16[128,512]{1,0:T(8,128)(2,1)S(1)}, bf16[128,512]{1,0:T(8,128)(2,1)S(1)}) custom-call(s32[4]{0:T(128)S(1)} %copy-done.13, f32[1]{0:T(128)S(6)} %copy.20.rate, bf16[8,48,512]{2,1,0:T(8,128)(2,1)S(1)} %copy-done.15, bf16[8,48,512]{2,1,0:T(8,128)(2,1)S(1)} %collective-permute-done.15.other, f32[768,512]{1,0:T(8,128)S(1)} %get-tuple-element.35.flipped, ...), custom_call_target="tpu_custom_call" | custom-call | flops 3000000000 | bytes 4000000 | tf_op jit(solution)/shard_map/pallas_call | solution.py:538
  151.2 0.6 collective-permute-start.25
  151.8 1.4 shard_map.92.refs_0_
  153.2 3.8 %collective-permute-done.25.got = bf16[128,512]{1,0:T(8,128)(2,1)S(1)} collective-permute-done((bf16[128,512]{1,0:T(8,128)(2,1)S(1)}, bf16[128,512]{1,0:T(8,128)(2,1)S(1)}, u32[]{:S(2)}, u32[]{:S(2)}) %collective-permute-start.25) | collective-permute-done | bytes 131104 | tf_op jit(solution)/shard_map/ppermute | solution.py:33
  156.9 1.4 shard_map.93
  (50 shorter events, 0.1 us)
Async XLA Ops:
  0.0 43.0 %collective-permute-start = (bf16[32,768]{1,0:T(8,128)(2,1)}, bf16[32,768]{1,0:T(8,128)(2,1)S(1)}, u32[]{:S(2)}, u32[]{:S(2)}) collective-permute-start(bf16[32,768]{1,0:T(8,128)(2,1)} %bitcast.23), channel_id=1, source_target_pairs={{0,8},{2,10},{4,12},{6,14},{8,0},{10,2},{12,4},{14,6},{16,24},{18,... | collective-permute-start | bytes 147464 | tf_op jit(solution)/shard_map/ppermute | solution.py:33
  3.0 40.0 %collective-permute-start.1 = (bf16[32,768]{1,0:T(8,128)(2,1)}, bf16[32,768]{1,0:T(8,128)(2,1)S(1)}, u32[]{:S(2)}, u32[]{:S(2)}) collective-permute-start(bf16[32,768]{1,0:T(8,128)(2,1)} %bitcast.24), channel_id=1, source_target_pairs={{0,16},{2,18},{4,20},{6,22},{8,24},{10,26},{12,28},{14,30},{16,0},... | collective-permute-start | bytes 147464 | tf_op jit(solution)/shard_map/ppermute | solution.py:33
  5.6 37.4 %collective-permute-start.2 = (bf16[32,768]{1,0:T(8,128)(2,1)}, bf16[32,768]{1,0:T(8,128)(2,1)S(1)}, u32[]{:S(2)}, u32[]{:S(2)}) collective-permute-start(bf16[32,768]{1,0:T(8,128)(2,1)} %bitcast.25), channel_id=1, source_target_pairs={{0,24},{2,26},{4,28},{6,30},{8,16},{10,18},{12,20},{14,22},{16,8},... | collective-permute-start | bytes 147464 | tf_op jit(solution)/shard_map/ppermute | solution.py:33
  41.6 11.7 %copy-start.4 = (bf16[2,256,512]{2,1,0:T(8,128)(2,1)S(1)}, bf16[2,256,512]{2,1,0:T(8,128)(2,1)}, u32[]{:S(2)}) copy-start(bf16[2,256,512]{2,1,0:T(8,128)(2,1)} %get-tuple-element.38.pair_a.own) | copy-start | bytes 1572868
  41.6 3.2 %collective-permute-start.3 = (bf16[2,256,512]{2,1,0:T(8,128)(2,1)}, bf16[2,256,512]{2,1,0:T(8,128)(2,1)S(1)}, u32[]{:S(2)}, u32[]{:S(2)}) collective-permute-start(bf16[2,256,512]{2,1,0:T(8,128)(2,1)} %get-tuple-element.38.pair_a.own), channel_id=1, source_target_pairs={{0,2},{2,0},{4,6},{6,4},{8,10},{10,8},{12,14},{14,12},{16,18},{18,... | collective-permute-start | bytes 1572872 | tf_op jit(solution)/shard_map/ppermute | solution.py:33
  41.7 3.1 %collective-permute-start.4 = (bf16[256,512]{1,0:T(8,128)(2,1)}, bf16[256,512]{1,0:T(8,128)(2,1)S(1)}, u32[]{:S(2)}, u32[]{:S(2)}) collective-permute-start(bf16[256,512]{1,0:T(8,128)(2,1)} %get-tuple-element.26.target_a), channel_id=1, source_target_pairs={{0,2},{2,0},{4,6},{6,4},{8,10},{10,8},{12,14},{14,12},{16,18},{18,... | collective-permute-start | bytes 786440 | tf_op jit(solution)/shard_map/ppermute | solution.py:33
  43.9 16.2 %collective-permute-start.16 = (bf16[2,256,512]{2,1,0:T(8,128)(2,1)}, bf16[2,256,512]{2,1,0:T(8,128)(2,1)S(1)}, u32[]{:S(2)}, u32[]{:S(2)}) collective-permute-start(bf16[2,256,512]{2,1,0:T(8,128)(2,1)} %get-tuple-element.38.pair_a.own), channel_id=1, source_target_pairs={{0,8},{2,10},{4,12},{6,14},{8,16},{10,18},{12,20},{14,22},{16,24},... | collective-permute-start | bytes 1572872 | tf_op jit(solution)/shard_map/ppermute | solution.py:423
  44.8 6.7 %collective-permute-start.5 = (bf16[4,32,768]{2,1,0:T(8,128)(2,1)S(1)}, bf16[4,32,768]{2,1,0:T(8,128)(2,1)S(1)}, u32[]{:S(2)}, u32[]{:S(2)}) collective-permute-start(bf16[4,32,768]{2,1,0:T(8,128)(2,1)S(1)} %pad_maximum_fusion.mine), channel_id=1, source_target_pairs={{0,4},{2,6},{4,0},{6,2},{8,12},{10,14},{12,8},{14,10},{16,20},{18,... | collective-permute-start | bytes 589832 | tf_op jit(solution)/shard_map/ppermute | solution.py:33
  51.5 1.8 %collective-permute-start.6 = (bf16[8,32,768]{2,1,0:T(8,128)(2,1)S(1)}, bf16[8,32,768]{2,1,0:T(8,128)(2,1)S(1)}, u32[]{:S(2)}, u32[]{:S(2)}) collective-permute-start(bf16[8,32,768]{2,1,0:T(8,128)(2,1)S(1)} %constant_dynamic-update-slice_fusion), channel_id=1, source_target_pairs={{0,2},{2,0},{4,6},{6,4},{8,10},{10,8},{12,14},{14,12},{16,18},{18,... | collective-permute-start | bytes 1179656 | tf_op jit(solution)/shard_map/ppermute | solution.py:33
  51.7 19.8 %copy-start.11 = (s32[4]{0:T(128)}, s32[4]{0:T(128)S(1)}, u32[]{:S(2)}) copy-start(s32[4]{0:T(128)S(1)} %pad_add_fusion.ids) | copy-start | bytes 52
  53.3 1.0 copy-start.10
  60.1 11.4 %copy-start.2 = (bf16[2,256,512]{2,1,0:T(8,128)(2,1)}, bf16[2,256,512]{2,1,0:T(8,128)(2,1)S(1)}, u32[]{:S(2)}) copy-start(bf16[2,256,512]{2,1,0:T(8,128)(2,1)S(1)} %collective-permute-done.16.far.refs_0_) | copy-start | bytes 1572868
  60.1 36.4 %collective-permute-start.17 = (bf16[2,256,512]{2,1,0:T(8,128)(2,1)}, bf16[2,256,512]{2,1,0:T(8,128)(2,1)S(1)}, u32[]{:S(2)}, u32[]{:S(2)}) collective-permute-start(bf16[2,256,512]{2,1,0:T(8,128)(2,1)} %get-tuple-element.40.own), channel_id=1, source_target_pairs={{0,8},{2,10},{4,12},{6,14},{8,16},{10,18},{12,20},{14,22},{16,24},... | collective-permute-start | bytes 1572872 | tf_op jit(solution)/shard_map/ppermute | solution.py:423
  60.1 6.4 %collective-permute-start.7 = (bf16[192,512]{1,0:T(8,128)(2,1)S(1)}, bf16[192,512]{1,0:T(8,128)(2,1)S(1)}, u32[]{:S(2)}, u32[]{:S(2)}) collective-permute-start(bf16[192,512]{1,0:T(8,128)(2,1)S(1)} %get-tuple-element.29), channel_id=1, source_target_pairs={{0,4},{2,6},{4,0},{6,2},{8,12},{10,14},{12,8},{14,10},{16,20},{18,... | collective-permute-start | bytes 589832 | tf_op jit(solution)/shard_map/ppermute | solution.py:33
  67.1 23.5 %collective-permute-start.10 = (bf16[48,512]{1,0:T(8,128)(2,1)S(1)}, bf16[48,512]{1,0:T(8,128)(2,1)S(1)}, u32[]{:S(2)}, u32[]{:S(2)}) collective-permute-start(bf16[48,512]{1,0:T(8,128)(2,1)S(1)} %get-tuple-element.33), channel_id=1, source_target_pairs={{0,24},{2,26},{4,28},{6,30},{8,16},{10,18},{12,20},{14,22},{16,8},... | collective-permute-start | bytes 147464 | tf_op jit(solution)/shard_map/ppermute | solution.py:33
  70.7 19.9 %collective-permute-start.8 = (bf16[48,512]{1,0:T(8,128)(2,1)S(1)}, bf16[48,512]{1,0:T(8,128)(2,1)S(1)}, u32[]{:S(2)}, u32[]{:S(2)}) collective-permute-start(bf16[48,512]{1,0:T(8,128)(2,1)S(1)} %get-tuple-element.31), channel_id=1, source_target_pairs={{0,8},{2,10},{4,12},{6,14},{8,0},{10,2},{12,4},{14,6},{16,24},{18,... | collective-permute-start | bytes 147464 | tf_op jit(solution)/shard_map/ppermute | solution.py:33
  70.7 19.9 %collective-permute-start.9 = (bf16[48,512]{1,0:T(8,128)(2,1)S(1)}, bf16[48,512]{1,0:T(8,128)(2,1)S(1)}, u32[]{:S(2)}, u32[]{:S(2)}) collective-permute-start(bf16[48,512]{1,0:T(8,128)(2,1)S(1)} %get-tuple-element.32), channel_id=1, source_target_pairs={{0,16},{2,18},{4,20},{6,22},{8,24},{10,26},{12,28},{14,30},{16,0},... | collective-permute-start | bytes 147464 | tf_op jit(solution)/shard_map/ppermute | solution.py:33
  89.2 47.1 %copy-start.13 = (s32[4]{0:T(128)S(1)}, s32[4]{0:T(128)}, u32[]{:S(2)}) copy-start(s32[4]{0:T(128)} %copy-done.11) | copy-start | bytes 52
  89.2 30.3 %collective-permute-start.18 = (bf16[2,256,512]{2,1,0:T(8,128)(2,1)}, bf16[2,256,512]{2,1,0:T(8,128)(2,1)}, u32[]{:S(2)}, u32[]{:S(2)}) collective-permute-start(bf16[2,256,512]{2,1,0:T(8,128)(2,1)} %shard_map.87), channel_id=1, source_target_pairs={{0,4},{2,6},{4,0},{6,2},{8,12},{10,14},{12,8},{14,10},{16,20},{18,... | collective-permute-start | bytes 1572872 | tf_op jit(solution)/shard_map/ppermute | solution.py:33
  90.6 0.6 copy-start.12
  91.7 23.3 %collective-permute-start.12 = (bf16[48,512]{1,0:T(8,128)(2,1)S(1)}, bf16[48,512]{1,0:T(8,128)(2,1)}, u32[]{:S(2)}, u32[]{:S(2)}) collective-permute-start(bf16[48,512]{1,0:T(8,128)(2,1)S(1)} %shard_map.85), channel_id=1, source_target_pairs={{0,16},{2,18},{4,20},{6,22},{8,24},{10,26},{12,28},{14,30},{16,0},... | collective-permute-start | bytes 147464 | tf_op jit(solution)/shard_map/ppermute | solution.py:33
  93.9 21.2 %collective-permute-start.13 = (bf16[48,512]{1,0:T(8,128)(2,1)S(1)}, bf16[48,512]{1,0:T(8,128)(2,1)S(1)}, u32[]{:S(2)}, u32[]{:S(2)}) collective-permute-start(bf16[48,512]{1,0:T(8,128)(2,1)S(1)} %shard_map.85), channel_id=1, source_target_pairs={{0,24},{2,26},{4,28},{6,30},{8,16},{10,18},{12,20},{14,22},{16,8},... | collective-permute-start | bytes 147464 | tf_op jit(solution)/shard_map/ppermute | solution.py:33
  95.4 20.6 %collective-permute-start.11 = (bf16[48,512]{1,0:T(8,128)(2,1)S(1)}, bf16[48,512]{1,0:T(8,128)(2,1)}, u32[]{:S(2)}, u32[]{:S(2)}) collective-permute-start(bf16[48,512]{1,0:T(8,128)(2,1)S(1)} %shard_map.85), channel_id=1, source_target_pairs={{0,8},{2,10},{4,12},{6,14},{8,0},{10,2},{12,4},{14,6},{16,24},{18,... | collective-permute-start | bytes 147464 | tf_op jit(solution)/shard_map/ppermute | solution.py:33
  96.5 40.8 %copy-start = (bf16[2,256,512]{2,1,0:T(8,128)(2,1)S(1)}, bf16[2,256,512]{2,1,0:T(8,128)(2,1)}, u32[]{:S(2)}) copy-start(bf16[2,256,512]{2,1,0:T(8,128)(2,1)} %k_own.3) | copy-start | bytes 1572868
  96.5 40.8 %copy-start.1 = (bf16[2,256,512]{2,1,0:T(8,128)(2,1)S(1)}, bf16[2,256,512]{2,1,0:T(8,128)(2,1)}, u32[]{:S(2)}) copy-start(bf16[2,256,512]{2,1,0:T(8,128)(2,1)} %v_own.3) | copy-start | bytes 1572868
  96.5 40.8 %copy-start.3 = (bf16[2,256,512]{2,1,0:T(8,128)(2,1)S(1)}, bf16[2,256,512]{2,1,0:T(8,128)(2,1)}, u32[]{:S(2)}) copy-start(bf16[2,256,512]{2,1,0:T(8,128)(2,1)} %copy-done.2) | copy-start | bytes 1572868
  96.5 0.8 copy-start.5
  96.6 39.1 %collective-permute-start.21 = (bf16[2,256,512]{2,1,0:T(8,128)(2,1)}, bf16[2,256,512]{2,1,0:T(8,128)(2,1)}, u32[]{:S(2)}, u32[]{:S(2)}) collective-permute-start(bf16[2,256,512]{2,1,0:T(8,128)(2,1)} %copy-done.2), channel_id=1, source_target_pairs={{0,2},{2,0},{4,6},{6,4},{8,10},{10,8},{12,14},{14,12},{16,18},{18,... | collective-permute-start | bytes 1572872 | tf_op jit(solution)/shard_map/ppermute | solution.py:33
  115.0 22.4 %copy-start.7 = (bf16[2,256,512]{2,1,0:T(8,128)(2,1)S(1)}, bf16[2,256,512]{2,1,0:T(8,128)(2,1)}, u32[]{:S(2)}) copy-start(bf16[2,256,512]{2,1,0:T(8,128)(2,1)} %q.5) | copy-start | bytes 1572868
  115.0 22.4 %copy-start.9 = (bf16[2,256,512]{2,1,0:T(8,128)(2,1)S(1)}, bf16[2,256,512]{2,1,0:T(8,128)(2,1)}, u32[]{:S(2)}) copy-start(bf16[2,256,512]{2,1,0:T(8,128)(2,1)} %gates.3) | copy-start | bytes 1572868
  115.0 27.8 %collective-permute-start.20 = (bf16[2,256,512]{2,1,0:T(8,128)(2,1)}, bf16[2,256,512]{2,1,0:T(8,128)(2,1)S(1)}, u32[]{:S(2)}, u32[]{:S(2)}) collective-permute-start(bf16[2,256,512]{2,1,0:T(8,128)(2,1)} %get-tuple-element.40.own), channel_id=1, source_target_pairs={{0,2},{2,0},{4,6},{6,4},{8,10},{10,8},{12,14},{14,12},{16,18},{18,... | collective-permute-start | bytes 1572872 | tf_op jit(solution)/shard_map/ppermute | solution.py:33
  115.1 18.8 %collective-permute-start.19 = (bf16[2,256,512]{2,1,0:T(8,128)(2,1)}, bf16[2,256,512]{2,1,0:T(8,128)(2,1)S(1)}, u32[]{:S(2)}, u32[]{:S(2)}) collective-permute-start(bf16[2,256,512]{2,1,0:T(8,128)(2,1)} %shard_map.88), channel_id=1, source_target_pairs={{0,4},{2,6},{4,0},{6,2},{8,12},{10,14},{12,8},{14,10},{16,20},{18,... | collective-permute-start | bytes 1572872 | tf_op jit(solution)/shard_map/ppermute | solution.py:33
  116.8 17.1 %collective-permute-start.14 = (bf16[4,48,512]{2,1,0:T(8,128)(2,1)S(1)}, bf16[4,48,512]{2,1,0:T(8,128)(2,1)S(1)}, u32[]{:S(2)}, u32[]{:S(2)}) collective-permute-start(bf16[4,48,512]{2,1,0:T(8,128)(2,1)S(1)} %pad_maximum_fusion.1), channel_id=1, source_target_pairs={{0,4},{2,6},{4,0},{6,2},{8,12},{10,14},{12,8},{14,10},{16,20},{18,... | collective-permute-start | bytes 589832 | tf_op jit(solution)/shard_map/ppermute | solution.py:33
  119.6 17.8 %collective-permute-start.23 = (bf16[2,256,512]{2,1,0:T(8,128)(2,1)}, bf16[2,256,512]{2,1,0:T(8,128)(2,1)S(1)}, u32[]{:S(2)}, u32[]{:S(2)}) collective-permute-start(bf16[2,256,512]{2,1,0:T(8,128)(2,1)} %collective-permute-done.18.refs_2_.refs_1_), channel_id=1, source_target_pairs={{0,2},{2,0},{4,6},{6,4},{8,10},{10,8},{12,14},{14,12},{16,18},{18,... | collective-permute-start | bytes 1572872 | tf_op jit(solution)/shard_map/ppermute | solution.py:33
  133.9 8.9 %collective-permute-start.22 = (bf16[2,256,512]{2,1,0:T(8,128)(2,1)}, bf16[2,256,512]{2,1,0:T(8,128)(2,1)S(1)}, u32[]{:S(2)}, u32[]{:S(2)}) collective-permute-start(bf16[2,256,512]{2,1,0:T(8,128)(2,1)} %copy-done.5), channel_id=1, source_target_pairs={{0,2},{2,0},{4,6},{6,4},{8,10},{10,8},{12,14},{14,12},{16,18},{18,... | collective-permute-start | bytes 1572872 | tf_op jit(solution)/shard_map/ppermute | solution.py:33
  133.9 8.9 %collective-permute-start.24 = (bf16[2,256,512]{2,1,0:T(8,128)(2,1)S(1)}, bf16[2,256,512]{2,1,0:T(8,128)(2,1)S(1)}, u32[]{:S(2)}, u32[]{:S(2)}) collective-permute-start(bf16[2,256,512]{2,1,0:T(8,128)(2,1)S(1)} %collective-permute-done.19.refs_3_), channel_id=1, source_target_pairs={{0,2},{2,0},{4,6},{6,4},{8,10},{10,8},{12,14},{14,12},{16,18},{18,... | collective-permute-start | bytes 1572872 | tf_op jit(solution)/shard_map/ppermute | solution.py:33
  135.7 11.6 %collective-permute-start.15 = (bf16[8,48,512]{2,1,0:T(8,128)(2,1)}, bf16[8,48,512]{2,1,0:T(8,128)(2,1)S(1)}, u32[]{:S(2)}, u32[]{:S(2)}) collective-permute-start(bf16[8,48,512]{2,1,0:T(8,128)(2,1)} %constant_dynamic-update-slice_fusion.5.mine), channel_id=1, source_target_pairs={{0,2},{2,0},{4,6},{6,4},{8,10},{10,8},{12,14},{14,12},{16,18},{18,... | collective-permute-start | bytes 1179656 | tf_op jit(solution)/shard_map/ppermute | solution.py:33
  137.3 6.3 %copy-start.6 = (bf16[2,256,512]{2,1,0:T(8,128)(2,1)S(1)}, bf16[2,256,512]{2,1,0:T(8,128)(2,1)}, u32[]{:S(2)}) copy-start(bf16[2,256,512]{2,1,0:T(8,128)(2,1)} %copy-done.5) | copy-start | bytes 1572868
  137.4 3.8 %copy-start.8 = (bf16[2,256,512]{2,1,0:T(8,128)(2,1)}, bf16[2,256,512]{2,1,0:T(8,128)(2,1)S(1)}, u32[]{:S(2)}) copy-start(bf16[2,256,512]{2,1,0:T(8,128)(2,1)S(1)} %collective-permute-done.23.refs_7_.refs_4_) | copy-start | bytes 1572868
  141.2 6.1 %copy-start.15 = (bf16[8,48,512]{2,1,0:T(8,128)(2,1)S(1)}, bf16[8,48,512]{2,1,0:T(8,128)(2,1)}, u32[]{:S(2)}) copy-start(bf16[8,48,512]{2,1,0:T(8,128)(2,1)} %constant_dynamic-update-slice_fusion.5.mine) | copy-start | bytes 1179652
  141.2 10.5 %collective-permute-start.26 = (bf16[128,512]{1,0:T(8,128)(2,1)S(1)}, bf16[128,512]{1,0:T(8,128)(2,1)S(1)}, u32[]{:S(2)}, u32[]{:S(2)}) collective-permute-start(bf16[128,512]{1,0:T(8,128)(2,1)S(1)} %get-tuple-element.44), channel_id=1, source_target_pairs={{0,1},{1,0},{2,3},{3,2},{4,5},{5,4},{6,7},{7,6},{8,9},{9,8},{10,11... | collective-permute-start | bytes 393224 | tf_op jit(solution)/shard_map/ppermute | solution.py:33
  142.8 0.8 copy-start.16
  147.4 4.4 %copy-start.14 = (f32[1024]{0:T(1024)S(1)}, f32[1024]{0:T(1024)}, u32[]{:S(2)}) copy-start(f32[1024]{0:T(1024)} %param.15) | copy-start | bytes 12292
  151.2 5.7 %collective-permute-start.25 = (bf16[128,512]{1,0:T(8,128)(2,1)S(1)}, bf16[128,512]{1,0:T(8,128)(2,1)S(1)}, u32[]{:S(2)}, u32[]{:S(2)}) collective-permute-start(bf16[128,512]{1,0:T(8,128)(2,1)S(1)} %get-tuple-element.42), channel_id=1, source_target_pairs={{0,1},{1,0},{2,3},{3,2},{4,5},{5,4},{6,7},{7,6},{8,9},{9,8},{10,11... | collective-permute-start | bytes 393224 | tf_op jit(solution)/shard_map/ppermute | solution.py:33

commit v4 on v3

--- a/solution.py
+++ b/solution.py
@@ -57,21 +57,29 @@
     return v / (1.0 + jnp.exp(-v))
 
 
-def prepare_body(keys, values, rates, pair_0, pair_1, target, held, sems, value_sem):
-    load = pltpu.make_async_copy(values.at[0], held, value_sem)
-    load.start()
-    copies = []
-    for g, pair in enumerate((pair_0, pair_1)):
-        for which, source in enumerate((keys, values)):
-            copies.append(
-                pltpu.make_async_copy(source.at[g], pair.at[which], sems.at[2 * g + which])
-            )
-    for copy in copies:
-        copy.start()
-    load.wait()
-    target[...] = (-rates[...] * held[...].astype(F32)).astype(BF)
-    for copy in copies:
-        copy.wait()
+def prepare_body(keys, values, rates, pair_0, pair_1, target, held, sems_in, sems_out):
+    loads = [
+        pltpu.make_async_copy(source.at[g], held.at[2 * g + which], sems_in.at[2 * g + which])
+        for g in range(2)
+        for which, source in enumerate((keys, values))
+    ]
+    stores = [
+        pltpu.make_async_copy(
+            held.at[2 * g + which], pair.at[which], sems_out.at[2 * g + which]
+        )
+        for g, pair in enumerate((pair_0, pair_1))
+        for which in range(2)
+    ]
+    for load in loads:
+        load.start()
+    rows = target.shape[0]
+    column = jnp.broadcast_to(rates[...], (128, rows)).T[:, :1]
+    for load, store in zip(loads, stores):
+        load.wait()
+        store.start()
+    target[...] = (-column * held[1].astype(F32)).astype(BF)
+    for store in stores:
+        store.wait()
 
 
 def prepared(keys, values, rates):
@@ -84,27 +92,38 @@
         in_specs=[anywhere, anywhere, vmem_spec()],
         out_specs=(anywhere, anywhere, vmem_spec()),
         scratch_shapes=[
-            pltpu.VMEM((rows, depth), BF),
+            pltpu.VMEM((4, rows, depth), BF),
             pltpu.SemaphoreType.DMA((4,)),
-            pltpu.SemaphoreType.DMA,
+            pltpu.SemaphoreType.DMA((4,)),
         ],
+        compiler_params=pltpu.CompilerParams(vmem_limit_bytes=VMEM_LIMIT),
         cost_estimate=cost_of(0, rows * depth * 8),
-    )(keys, values, rates)
-
-
-def pick_body(ids, own, far, out, sems):
+    )(keys, values, rates.reshape(1, rows))
+
+
+def pick_body(ids, own, far, out, held, sems_in, sems_out):
     side = ids[1]
+    half = held.shape[1] // 2
+    parts = [(w, pl.ds(h * half, half)) for w in range(2) for h in range(2)]
     for condition, source in ((side == 0, own), (side == 1, far)):
 
         @pl.when(condition)
         def _():
-            copies = [
-                pltpu.make_async_copy(source.at[w], out.at[w], sems.at[w]) for w in range(2)
+            loads = [
+                pltpu.make_async_copy(source.at[w, at], held.at[w, at], sems_in.at[i])
+                for i, (w, at) in enumerate(parts)
             ]
-            for copy in copies:
-                copy.start()
-            for copy in copies:
-                copy.wait()
+            stores = [
+                pltpu.make_async_copy(held.at[w, at], out.at[w, at], sems_out.at[i])
+                for i, (w, at) in enumerate(parts)
+            ]
+            for load in loads:
+                load.start()
+            for load, store in zip(loads, stores):
+                load.wait()
+                store.start()
+            for store in stores:
+                store.wait()
 
 
 def picked(ids, own, far):
@@ -114,12 +133,33 @@
         out_shape=jax.ShapeDtypeStruct(own.shape, own.dtype),
         in_specs=[pl.BlockSpec(memory_space=pltpu.SMEM), anywhere, anywhere],
         out_specs=anywhere,
-        scratch_shapes=[pltpu.SemaphoreType.DMA((2,))],
+        scratch_shapes=[
+            pltpu.VMEM(own.shape, own.dtype),
+            pltpu.SemaphoreType.DMA((4,)),
+            pltpu.SemaphoreType.DMA((4,)),
+        ],
+        compiler_params=pltpu.CompilerParams(vmem_limit_bytes=VMEM_LIMIT),
         cost_estimate=cost_of(0, own.size * 4),
     )(ids, own, far)
 
 
-def gradient_body(planes, ids, mine, other, beside, pair_a, pair_b, target_a, target_b, *refs):
+def pack_body(*refs):
+    for m, ref in enumerate(refs[:-1]):
+        refs[-1][m] = ref[...]
+
+
+def packed(*pieces):
+    return pl.pallas_call(
+        pack_body,
+        out_shape=jax.ShapeDtypeStruct((len(pieces),) + pieces[0].shape, pieces[0].dtype),
+        in_specs=[vmem_spec()] * len(pieces),
+        out_specs=vmem_spec(),
+        compiler_params=pltpu.CompilerParams(vmem_limit_bytes=VMEM_LIMIT),
+        cost_estimate=cost_of(0, 4 * len(pieces) * pieces[0].size),
+    )(*pieces)
+
+
+def gradient_body(planes, ids, mine, other, beside_mine, beside_other, pair_a, pair_b, target_a, target_b, *refs):
     send, keep, whole, total = refs[:4]
     plane, side, core = ids[0], ids[1], ids[2]
     rows = mine.shape[1]
@@ -131,7 +171,8 @@
             other_at = pl.multiple_of((block + 1 - core) * rows, rows)
             source = (mine, other)[far]
             target_ref[pl.ds(own_at, rows), :] = source[m].astype(target_ref.dtype)
-            target_ref[pl.ds(other_at, rows), :] = beside[far * planes + m].astype(target_ref.dtype)
+            source = (beside_mine, beside_other)[far]
+            target_ref[pl.ds(other_at, rows), :] = source[m].astype(target_ref.dtype)
     if target_ref is not whole:
         whole[...] = target_ref[...].astype(BF)
     width = whole.shape[1] // 3
@@ -322,7 +363,7 @@
     )(ids, *grouped, *whole, *raw)
 
 
-def update_body(planes, ids, rate, mine, other, flipped, norms, q, win, gates, *refs):
+def update_body(planes, ids, rate, mine, side_in, core_in, diag_in, flipped, norms, q, win, gates, *refs):
     outs, (grads, gated) = refs[:-2], refs[-2:]
     plane, side, core = ids[0], ids[1], ids[2]
     part = mine.shape[1]
@@ -330,8 +371,8 @@
         for far in range(2):
             base = ((side if far == 0 else 1 - side) * planes + (plane ^ m)) * part
             where = pl.ds(pl.multiple_of(base, part), part)
-            grads[core, where, :] = mine[far * planes + m]
-            grads[1 - core, where, :] = other[far * planes + m]
+            grads[core, where, :] = (mine, side_in)[far][m]
+            grads[1 - core, where, :] = (core_in, diag_in)[far][m]
     width = flipped.shape[0] // 3
     half = width // 2
     turned = []
@@ -442,9 +483,9 @@
     pair_0, pair_1, target = prepared(keys, values, token_rates)
     beside_0 = swapped(pair_0, 1)
     target_beside = swapped(target, 1)
-    mine_w = jnp.stack([local] + arrived)
+    mine_w = packed(local, *arrived)
     other_w = swapped(after(mine_w, beside_0, target_beside), 2)
-    beside_w = swapped(jnp.concatenate([mine_w, other_w], 0), 1)
+    beside_w = [swapped(w, 1) for w in (mine_w, other_w)]
 
     pieces = 2 * planes
     part = -(-3 * half // (16 * pieces)) * 16
@@ -453,7 +494,7 @@
         scratch.append(pltpu.VMEM((depth, 3 * width), F32))
     send, keep, whole = call(
         functools.partial(gradient_body, planes),
-        (ids, mine_w, other_w, beside_w, pair_0, beside_0, target, target_beside),
+        (ids, mine_w, other_w, *beside_w, pair_0, beside_0, target, target_beside),
         (
             jax.ShapeDtypeStruct((planes * part, depth), BF),
             jax.ShapeDtypeStruct((planes * part, depth), F32),
@@ -477,16 +518,15 @@
         jax.ShapeDtypeStruct((part, depth), BF),
         cost=cost_of(0, planes * part * depth * 3),
     )
-    stacked = jnp.stack([total] + [swapped(total, 4 * m) for m in range(1, planes)])
-    side_grad = jnp.concatenate([stacked, swapped(stacked, 2)], 0)
-    core_grad = swapped(side_grad, 1)
+    plane_grad = packed(total, *[swapped(total, 4 * m) for m in range(1, planes)])
+    side_grad = swapped(plane_grad, 2)
+    grads = [plane_grad, side_grad] + [swapped(v, 1) for v in (plane_grad, side_grad)]
 
     ring = [(i, (i + reach) % count) for i in everyone]
-    far_0 = sent(after(pair_0, mine_w), ring)
-    pair_1, far_0, _ = lax.optimization_barrier((pair_1, far_0, send))
-    far_1 = sent(pair_1, ring)
-    near_0 = swapped(picked(ids, pair_0, far_0), 2)
-    near_1 = swapped(picked(ids, pair_1, far_1), 2)
+    far_0 = sent(pair_0, ring)
+    far_1 = sent(after(pair_1, mine_w), ring)
+    near_0 = swapped(picked(ids, pair_0, after(far_0, got)), 2)
+    near_1 = swapped(picked(ids, pair_1, after(far_1, total)), 2)
     beside_1, far_beside_0, far_beside_1 = (swapped(v, 1) for v in (pair_1, far_0, far_1))
     diag_0, diag_1 = (swapped(v, 1) for v in (near_0, near_1))
 
@@ -542,8 +582,7 @@
         in_specs=[
             pl.BlockSpec(memory_space=pltpu.SMEM),
             pl.BlockSpec(memory_space=pltpu.SMEM),
-            full(side_grad.shape),
-            full(core_grad.shape),
+            *[full(v.shape) for v in grads],
             full(flipped.shape),
             full(norms.shape),
             pl.BlockSpec((None, rows, depth), lambda i: (1, 0, 0)),
@@ -557,7 +596,7 @@
         ],
         compiler_params=pltpu.CompilerParams(vmem_limit_bytes=VMEM_LIMIT),
         cost_estimate=cost_of(3e9, 4e6),
-    )(ids, fast_rate, side_grad, core_grad, flipped, norms, queries, window_second, gates)
+    )(ids, fast_rate, *grads, flipped, norms, queries, window_second, gates)
     return finished(ids, 1, gated_second, norm_gain, done)
 
 

time: 159 us -> 91.5 us (0.58)
  Pallas kernels: 87.5 us -> 22.6 us
  waiting for transfers between devices: 32.6 us -> 41.6 us
  local copies, waits for them, and re-layouts: 10.2 us -> 4.38 us
  starting transfers between devices: 25.2 us -> 21.4 us
  other arithmetic: 1.76 us -> 0.08 us
    pallas_call x1, Pallas kernels: 34.5 us -> 0.43 us  [prepared(): pl.pallas_call(prepare_body, out_shape=(pair, pair, jax.ShapeDtypeStruct(...]
    pallas_call x2, Pallas kernels: 35.3 us -> 3.96 us  [picked(): pl.pallas_call(pick_body, out_shape=jax.ShapeDtypeStruct(own.shape, own.d...]
    ppermute x25 -> x27, waiting for transfers between devices: 28.3 us -> 34.2 us  [swapped(): return lax.ppermute(value, axis, [(i, i ^ mask) for i in range(count)])]
    unnamed x43 -> x22, local copies, waits for them, and re-layouts: 9.47 us -> 4.38 us
    ppermute x2, waiting for transfers between devices: 4.36 us -> 7.39 us  [sent(): return lax.ppermute(value, axis, pairs)]
    ppermute x25 -> x27, starting transfers between devices: 24.2 us -> 21.4 us  [swapped(): return lax.ppermute(value, axis, [(i, i ^ mask) for i in range(count)])]
    another operation x2 -> x0, other arithmetic: 1.68 us -> none  [the longest x1 0.85 us: shards(): jnp.stack([total] + [swapped(total, 4 * m) for m in range(1, planes)])]
  transfers between devices with their start and end apart: 27 -> 29, of which waited for: 6 -> 13; matrix products, arithmetic and copies ran while one was open for 6% -> 0% of each run, Pallas kernels for 54% -> 23%
where the time goes in v4:
time: 91.5 us; the launch traced here: 91.2 us
  waiting for transfers between devices  41.6 us (45%)
  Pallas kernels  22.6 us (25%)
  starting transfers between devices  21.4 us (23%)
  local copies, waits for them, and re-layouts  4.38 us (5%)
  between operations  1.05 us (1%)
    ppermute x27, waiting for transfers between devices, swapped(): return lax.ppermute(value, axis, [(i, i ^ mask) for i in range(count)])  34.2 us
    ppermute x27, starting transfers between devices, swapped(): return lax.ppermute(value, axis, [(i, i ^ mask) for i in range(count)])  21.4 us
    pallas_call x2, Pallas kernels, group_call(): pl.pallas_call(body, grid=(1,), out_shape=outs, in_specs=[pl.BlockSpec(me...  7.53 us
    ppermute x2, waiting for transfers between devices, sent(): return lax.ppermute(value, axis, pairs)  7.39 us
    unnamed x22, local copies, waits for them, and re-layouts  4.38 us
    pallas_call x4, Pallas kernels, call(): pl.pallas_call(body, out_shape=outs, in_specs=[pl.BlockSpec(memory_space=...  4.09 us
    pallas_call x2, Pallas kernels, picked(): pl.pallas_call(pick_body, out_shape=jax.ShapeDtypeStruct(own.shape, own.d...  3.96 us
    pallas_call x1, Pallas kernels, shards(): pl.pallas_call(functools.partial(update_body, planes), grid=(1,), out_sha...  3.82 us
  transfers between devices with their start and end apart: 29, of which 13 were waited for; matrix products, arithmetic and copies ran while one was open for 0% of the time, Pallas kernels for 23%

profile of v4, /device:TPU:0, one launch (start us, length us, event | category | flops | bytes accessed | tf_op | source)
XLA Modules:
  0.0 91.2 jit_solution(7158865255363681724)
XLA Ops:
  0.0 1.0 %copy-done = bf16[2,256,512]{2,1,0:T(8,128)(2,1)S(1)} copy-done((bf16[2,256,512]{2,1,0:T(8,128)(2,1)S(1)}, bf16[2,256,512]{2,1,0:T(8,128)(2,1)}, u32[]{:S(2)}) %copy-start) | copy-done | bytes 524312
  1.0 1.0 %copy-done.2 = bf16[2,256,512]{2,1,0:T(8,128)(2,1)S(1)} copy-done((bf16[2,256,512]{2,1,0:T(8,128)(2,1)S(1)}, bf16[2,256,512]{2,1,0:T(8,128)(2,1)}, u32[]{:S(2)}) %copy-start.2) | copy-done | bytes 524312
  2.1 0.7 copy-done.9
  2.8 0.4 shard_map.83
  3.2 0.5 collective-permute-start.3
  3.7 0.1 collective-permute-start.4
  3.8 3.0 %collective-permute-start = (bf16[32,768]{1,0:T(8,128)(2,1)}, bf16[32,768]{1,0:T(8,128)(2,1)S(1)}, u32[]{:S(2)}, u32[]{:S(2)}) collective-permute-start(bf16[32,768]{1,0:T(8,128)(2,1)} %bitcast.7), channel_id=1, source_target_pairs={{0,8},{2,10},{4,12},{6,14},{8,0},{10,2},{12,4},{14,6},{16,24},{18,... | collective-permute-start | bytes 147464 | tf_op jit(solution)/shard_map/ppermute | solution.py:33
  6.8 2.6 %collective-permute-start.1 = (bf16[32,768]{1,0:T(8,128)(2,1)}, bf16[32,768]{1,0:T(8,128)(2,1)S(1)}, u32[]{:S(2)}, u32[]{:S(2)}) collective-permute-start(bf16[32,768]{1,0:T(8,128)(2,1)} %bitcast.8), channel_id=1, source_target_pairs={{0,16},{2,18},{4,20},{6,22},{8,24},{10,26},{12,28},{14,30},{16,0},... | collective-permute-start | bytes 147464 | tf_op jit(solution)/shard_map/ppermute | solution.py:33
  9.4 3.5 %collective-permute-done.1.refs_2_ = bf16[32,768]{1,0:T(8,128)(2,1)S(1)} collective-permute-done((bf16[32,768]{1,0:T(8,128)(2,1)}, bf16[32,768]{1,0:T(8,128)(2,1)S(1)}, u32[]{:S(2)}, u32[]{:S(2)}) %collective-permute-start.1) | collective-permute-done | bytes 49184 | tf_op jit(solution)/shard_map/ppermute | solution.py:33
  12.9 2.6 %collective-permute-done.2.refs_3_ = bf16[32,768]{1,0:T(8,128)(2,1)S(1)} collective-permute-done((bf16[32,768]{1,0:T(8,128)(2,1)}, bf16[32,768]{1,0:T(8,128)(2,1)S(1)}, u32[]{:S(2)}, u32[]{:S(2)}) %collective-permute-start.2) | collective-permute-done | bytes 49184 | tf_op jit(solution)/shard_map/ppermute | solution.py:33
  15.5 0.8 copy-done.7
  16.3 0.0 collective-permute-done.3.pair_b.refs_2_
  16.3 1.6 %collective-permute-start.5 = (bf16[4,32,768]{2,1,0:T(8,128)(2,1)S(1)}, bf16[4,32,768]{2,1,0:T(8,128)(2,1)S(1)}, u32[]{:S(2)}, u32[]{:S(2)}) collective-permute-start(bf16[4,32,768]{2,1,0:T(8,128)(2,1)S(1)} %shard_map.82.mine), channel_id=1, source_target_pairs={{0,4},{2,6},{4,0},{6,2},{8,12},{10,14},{12,8},{14,10},{16,20},{18,... | collective-permute-start | bytes 589832 | tf_op jit(solution)/shard_map/ppermute | solution.py:33
  17.9 4.2 %collective-permute-done.5.other = bf16[4,32,768]{2,1,0:T(8,128)(2,1)S(1)} collective-permute-done((bf16[4,32,768]{2,1,0:T(8,128)(2,1)S(1)}, bf16[4,32,768]{2,1,0:T(8,128)(2,1)S(1)}, u32[]{:S(2)}, u32[]{:S(2)}) %collective-permute-start.5) | collective-permute-done | bytes 196640 | tf_op jit(solution)/shard_map/ppermute | solution.py:33
  22.1 0.0 collective-permute-start.7
  22.1 0.1 pad_add_fusion.ids
  22.1 1.5 %collective-permute-done.7.beside_other = bf16[4,32,768]{2,1,0:T(8,128)(2,1)} collective-permute-done((bf16[4,32,768]{2,1,0:T(8,128)(2,1)S(1)}, bf16[4,32,768]{2,1,0:T(8,128)(2,1)}, u32[]{:S(2)}, u32[]{:S(2)}) %collective-permute-start.7) | collective-permute-done | bytes 196640 | tf_op jit(solution)/shard_map/ppermute | solution.py:33
  23.6 2.0 %shard_map.84 = (bf16[192,512]{1,0:T(8,128)(2,1)S(1)}, f32[192,512]{1,0:T(8,128)S(1)}, bf16[512,768]{1,0:T(8,128)(2,1)S(1)}) custom-call(s32[4]{0:T(128)S(1)} %pad_add_fusion.ids, bf16[4,32,768]{2,1,0:T(8,128)(2,1)S(1)} %shard_map.82.mine, bf16[4,32,768]{2,1,0:T(8,128)(2,1)S(1)} %collective-permute-done.5.other, ...), custom_call_target="tpu_custom_call" | custom-call | flops 402653184 | bytes 2097152 | tf_op jit(solution)/shard_map/pallas_call | solution.py:41
  25.6 1.6 %collective-permute-start.8 = (bf16[192,512]{1,0:T(8,128)(2,1)S(1)}, bf16[192,512]{1,0:T(8,128)(2,1)S(1)}, u32[]{:S(2)}, u32[]{:S(2)}) collective-permute-start(bf16[192,512]{1,0:T(8,128)(2,1)S(1)} %get-tuple-element.29), channel_id=1, source_target_pairs={{0,4},{2,6},{4,0},{6,2},{8,12},{10,14},{12,8},{14,10},{16,20},{18,... | collective-permute-start | bytes 589832 | tf_op jit(solution)/shard_map/ppermute | solution.py:33
  27.2 7.4 %collective-permute-done.18.far.refs_0_ = bf16[2,256,512]{2,1,0:T(8,128)(2,1)S(1)} collective-permute-done((bf16[2,256,512]{2,1,0:T(8,128)(2,1)S(1)}, bf16[2,256,512]{2,1,0:T(8,128)(2,1)S(1)}, u32[]{:S(2)}, u32[]{:S(2)}) %collective-permute-start.18) | collective-permute-done | bytes 524320 | tf_op jit(solution)/shard_map/ppermute | solution.py:464
  34.5 0.0 collective-permute-done.8.got
  34.5 2.0 %shard_map.89 = bf16[2,256,512]{2,1,0:T(8,128)(2,1)S(1)} custom-call(s32[4]{0:T(128)S(1)} %pad_add_fusion.ids, bf16[2,256,512]{2,1,0:T(8,128)(2,1)S(1)} %get-tuple-element.25.pair_a.own, bf16[2,256,512]{2,1,0:T(8,128)(2,1)S(1)} %collective-permute-done.18.far.refs_0_), custom_call_target="tpu_custom_call" | custom-call | bytes 1048576 | tf_op jit(solution)/shard_map/pallas_call | solution.py:131
  36.5 0.6 collective-permute-start.20
  37.1 0.6 shard_map.85
  37.7 0.0 copy-start.1
  37.8 0.0 copy-start.3
  37.8 0.0 copy-start.4
  37.8 0.0 copy-start.6
  37.8 0.1 collective-permute-start.10
  37.9 1.5 %collective-permute-start.11 = (bf16[48,512]{1,0:T(8,128)(2,1)S(1)}, bf16[48,512]{1,0:T(8,128)(2,1)S(1)}, u32[]{:S(2)}, u32[]{:S(2)}) collective-permute-start(bf16[48,512]{1,0:T(8,128)(2,1)S(1)} %get-tuple-element.33), channel_id=1, source_target_pairs={{0,24},{2,26},{4,28},{6,30},{8,16},{10,18},{12,20},{14,22},{16,8},... | collective-permute-start | bytes 147464 | tf_op jit(solution)/shard_map/ppermute | solution.py:33
  39.4 1.9 %collective-permute-start.9 = (bf16[48,512]{1,0:T(8,128)(2,1)S(1)}, bf16[48,512]{1,0:T(8,128)(2,1)S(1)}, u32[]{:S(2)}, u32[]{:S(2)}) collective-permute-start(bf16[48,512]{1,0:T(8,128)(2,1)S(1)} %get-tuple-element.31), channel_id=1, source_target_pairs={{0,8},{2,10},{4,12},{6,14},{8,0},{10,2},{12,4},{14,6},{16,24},{18,... | collective-permute-start | bytes 147464 | tf_op jit(solution)/shard_map/ppermute | solution.py:33
  41.4 4.9 %collective-permute-done.10.refs_1_ = bf16[48,512]{1,0:T(8,128)(2,1)S(1)} collective-permute-done((bf16[48,512]{1,0:T(8,128)(2,1)S(1)}, bf16[48,512]{1,0:T(8,128)(2,1)S(1)}, u32[]{:S(2)}, u32[]{:S(2)}) %collective-permute-start.10) | collective-permute-done | bytes 49184 | tf_op jit(solution)/shard_map/ppermute | solution.py:33
  46.2 0.0 collective-permute-done.11.refs_2_
  46.2 0.2 collective-permute-done.9.refs_0_
  46.4 0.6 shard_map.86.refs_0_
  47.0 2.0 %shard_map.90 = bf16[2,256,512]{2,1,0:T(8,128)(2,1)S(1)} custom-call(s32[4]{0:T(128)S(1)} %pad_add_fusion.ids, bf16[2,256,512]{2,1,0:T(8,128)(2,1)S(1)} %get-tuple-element.38.own, bf16[2,256,512]{2,1,0:T(8,128)(2,1)S(1)} %collective-permute-done.19.far.refs_1_), custom_call_target="tpu_custom_call" | custom-call | bytes 1048576 | tf_op jit(solution)/shard_map/pallas_call | solution.py:131
  49.0 0.8 collective-permute-start.21
  49.8 0.0 collective-permute-start.23
  49.8 0.0 collective-permute-done.20.refs_2_.refs_1_
  49.8 0.5 collective-permute-start.25
  50.3 1.1 %collective-permute-start.12 = (bf16[48,512]{1,0:T(8,128)(2,1)S(1)}, bf16[48,512]{1,0:T(8,128)(2,1)S(1)}, u32[]{:S(2)}, u32[]{:S(2)}) collective-permute-start(bf16[48,512]{1,0:T(8,128)(2,1)S(1)} %shard_map.86.refs_0_), channel_id=1, source_target_pairs={{0,8},{2,10},{4,12},{6,14},{8,0},{10,2},{12,4},{14,6},{16,24},{18,... | collective-permute-start | bytes 147464 | tf_op jit(solution)/shard_map/ppermute | solution.py:33
  51.4 0.7 collective-permute-start.13
  52.1 2.3 %collective-permute-done.12.refs_1_ = bf16[48,512]{1,0:T(8,128)(2,1)S(1)} collective-permute-done((bf16[48,512]{1,0:T(8,128)(2,1)S(1)}, bf16[48,512]{1,0:T(8,128)(2,1)S(1)}, u32[]{:S(2)}, u32[]{:S(2)}) %collective-permute-start.12) | collective-permute-done | bytes 49184 | tf_op jit(solution)/shard_map/ppermute | solution.py:33
  54.4 1.8 %collective-permute-start.14 = (bf16[48,512]{1,0:T(8,128)(2,1)S(1)}, bf16[48,512]{1,0:T(8,128)(2,1)S(1)}, u32[]{:S(2)}, u32[]{:S(2)}) collective-permute-start(bf16[48,512]{1,0:T(8,128)(2,1)S(1)} %shard_map.86.refs_0_), channel_id=1, source_target_pairs={{0,24},{2,26},{4,28},{6,30},{8,16},{10,18},{12,20},{14,22},{16,8},... | collective-permute-start | bytes 147464 | tf_op jit(solution)/shard_map/ppermute | solution.py:33
  56.2 0.8 collective-permute-done.13.refs_2_
  57.0 0.0 collective-permute-start.22
  57.0 3.3 %collective-permute-done.14.refs_3_ = bf16[48,512]{1,0:T(8,128)(2,1)S(1)} collective-permute-done((bf16[48,512]{1,0:T(8,128)(2,1)S(1)}, bf16[48,512]{1,0:T(8,128)(2,1)S(1)}, u32[]{:S(2)}, u32[]{:S(2)}) %collective-permute-start.14) | collective-permute-done | bytes 49184 | tf_op jit(solution)/shard_map/ppermute | solution.py:33
  60.3 0.0 collective-permute-start.24
  60.3 2.3 %collective-permute-done.21.refs_3_ = bf16[2,256,512]{2,1,0:T(8,128)(2,1)S(1)} collective-permute-done((bf16[2,256,512]{2,1,0:T(8,128)(2,1)S(1)}, bf16[2,256,512]{2,1,0:T(8,128)(2,1)S(1)}, u32[]{:S(2)}, u32[]{:S(2)}) %collective-permute-start.21) | collective-permute-done | bytes 524320 | tf_op jit(solution)/shard_map/ppermute | solution.py:33
  62.6 0.0 collective-permute-start.26
  62.6 0.4 collective-permute-start.15
  63.6 1.0 %shard_map.88 = (f32[768,512]{1,0:T(8,128)S(1)}, f32[768,1]{1,0:T(8,128)S(1)}) custom-call(s32[4]{0:T(128)S(1)} %pad_add_fusion.ids, bf16[512,768]{1,0:T(8,128)(2,1)S(1)} %get-tuple-element.34.whole), custom_call_target="tpu_custom_call" | custom-call | bytes 3145728 | tf_op jit(solution)/shard_map/pallas_call | solution.py:41
  64.6 5.4 %collective-permute-done.15.side_in = bf16[4,48,512]{2,1,0:T(8,128)(2,1)S(1)} collective-permute-done((bf16[4,48,512]{2,1,0:T(8,128)(2,1)S(1)}, bf16[4,48,512]{2,1,0:T(8,128)(2,1)S(1)}, u32[]{:S(2)}, u32[]{:S(2)}) %collective-permute-start.15) | collective-permute-done | bytes 196640 | tf_op jit(solution)/shard_map/ppermute | solution.py:33
  70.0 0.5 collective-permute-start.17
  70.5 3.9 %shard_map.93 = (bf16[128,512]{1,0:T(8,128)(2,1)S(1)}, bf16[128,512]{1,0:T(8,128)(2,1)S(1)}) custom-call(s32[4]{0:T(128)S(1)} %pad_add_fusion.ids, bf16[2,256,512]{2,1,0:T(8,128)(2,1)S(1)} %copy-done.4, bf16[2,256,512]{2,1,0:T(8,128)(2,1)S(1)} %copy-done.1, bf16[2,256,512]{2,1,0:T(8,128)(2,1)S(1)} %copy-done.3, bf16[2,256,512]{2,1,0:T(8,128)(2,1)S(1)} %copy-done.6, ...), custom_call_target="tpu_custom_call" | custom-call | flops 1342177280 | bytes 3932160 | tf_op jit(solution)/shard_map/pallas_call | solution.py:350
  74.5 1.6 %collective-permute-start.28 = (bf16[128,512]{1,0:T(8,128)(2,1)S(1)}, bf16[128,512]{1,0:T(8,128)(2,1)S(1)}, u32[]{:S(2)}, u32[]{:S(2)}) collective-permute-start(bf16[128,512]{1,0:T(8,128)(2,1)S(1)} %get-tuple-element.44), channel_id=1, source_target_pairs={{0,1},{1,0},{2,3},{3,2},{4,5},{5,4},{6,7},{7,6},{8,9},{9,8},{10,11... | collective-permute-start | bytes 393224 | tf_op jit(solution)/shard_map/ppermute | solution.py:33
  76.0 0.8 copy-done.10
  76.8 3.7 %shard_map.91.win = f32[256,512]{1,0:T(8,128)S(1)} custom-call(s32[4]{0:T(128)S(1)} %pad_add_fusion.ids, bf16[2,256,512]{2,1,0:T(8,128)(2,1)S(1)} %copy-done.4, bf16[2,256,512]{2,1,0:T(8,128)(2,1)S(1)} %copy-done.1, bf16[2,256,512]{2,1,0:T(8,128)(2,1)S(1)} %copy-done.3, bf16[2,256,512]{2,1,0:T(8,128)(2,1)S(1)} %collective-permute-done.18.far.refs_0_, ...), custom_call_target="tpu_custom_call" | custom-call | flops 1342177280 | bytes 3932160 | tf_op jit(solution)/shard_map/pallas_call | solution.py:350
  80.5 0.0 copy-start.8
  80.5 3.8 %shard_map.92 = (bf16[128,512]{1,0:T(8,128)(2,1)S(1)}, bf16[128,512]{1,0:T(8,128)(2,1)S(1)}) custom-call(s32[4]{0:T(128)S(1)} %pad_add_fusion.ids, f32[1]{0:T(128)S(6)} %copy.11.rate, bf16[4,48,512]{2,1,0:T(8,128)(2,1)S(1)} %shard_map.87.mine, bf16[4,48,512]{2,1,0:T(8,128)(2,1)S(1)} %collective-permute-done.15.side_in, ...), custom_call_target="tpu_custom_call" | custom-call | flops 3000000000 | bytes 4000000 | tf_op jit(solution)/shard_map/pallas_call | solution.py:578
  84.3 0.6 collective-permute-start.27
  84.9 1.4 %shard_map.94.refs_0_ = bf16[2,128,1024]{2,1,0:T(8,128)(2,1)} custom-call(s32[4]{0:T(128)S(1)} %pad_add_fusion.ids, bf16[128,512]{1,0:T(8,128)(2,1)S(1)} %get-tuple-element.43.own, bf16[128,512]{1,0:T(8,128)(2,1)S(1)} %collective-permute-done.28.got, f32[1,1024]{1,0:T(1,128)S(1)} %bitcast.11), custom_call_target="tpu_custom_call" | custom-call | bytes 524288 | tf_op jit(solution)/shard_map/pallas_call | solution.py:437
  86.3 3.3 %collective-permute-done.27.got = bf16[128,512]{1,0:T(8,128)(2,1)S(1)} collective-permute-done((bf16[128,512]{1,0:T(8,128)(2,1)S(1)}, bf16[128,512]{1,0:T(8,128)(2,1)S(1)}, u32[]{:S(2)}, u32[]{:S(2)}) %collective-permute-start.27) | collective-permute-done | bytes 131104 | tf_op jit(solution)/shard_map/ppermute | solution.py:33
  89.6 1.4 %shard_map.95 = bf16[2,128,1024]{2,1,0:T(8,128)(2,1)} custom-call(s32[4]{0:T(128)S(1)} %pad_add_fusion.ids, bf16[128,512]{1,0:T(8,128)(2,1)S(1)} %get-tuple-element.41.own, bf16[128,512]{1,0:T(8,128)(2,1)S(1)} %collective-permute-done.27.got, f32[1,1024]{1,0:T(1,128)S(1)} %bitcast.12, ...), custom_call_target="tpu_custom_call", output_to_operand_aliasing={{}: (4, {})} | custom-call | bytes 524288 | tf_op jit(solution)/shard_map/pallas_call | solution.py:437
  (31 shorter events, 0.1 us)
Async XLA Ops:
  0.0 1.0 %copy-start = (bf16[2,256,512]{2,1,0:T(8,128)(2,1)S(1)}, bf16[2,256,512]{2,1,0:T(8,128)(2,1)}, u32[]{:S(2)}) copy-start(bf16[2,256,512]{2,1,0:T(8,128)(2,1)} %k_own.3) | copy-start | bytes 1572868
  1.0 1.0 %copy-start.2 = (bf16[2,256,512]{2,1,0:T(8,128)(2,1)S(1)}, bf16[2,256,512]{2,1,0:T(8,128)(2,1)}, u32[]{:S(2)}) copy-start(bf16[2,256,512]{2,1,0:T(8,128)(2,1)} %v_own.3) | copy-start | bytes 1572868
  2.1 0.7 copy-start.9
  3.2 13.1 %collective-permute-start.3 = (bf16[2,256,512]{2,1,0:T(8,128)(2,1)S(1)}, bf16[2,256,512]{2,1,0:T(8,128)(2,1)S(1)}, u32[]{:S(2)}, u32[]{:S(2)}) collective-permute-start(bf16[2,256,512]{2,1,0:T(8,128)(2,1)S(1)} %get-tuple-element.25.pair_a.own), channel_id=1, source_target_pairs={{0,2},{2,0},{4,6},{6,4},{8,10},{10,8},{12,14},{14,12},{16,18},{18,... | collective-permute-start | bytes 1572872 | tf_op jit(solution)/shard_map/ppermute | solution.py:33
  3.7 12.6 %collective-permute-start.4 = (bf16[256,512]{1,0:T(8,128)(2,1)S(1)}, bf16[256,512]{1,0:T(8,128)(2,1)S(1)}, u32[]{:S(2)}, u32[]{:S(2)}) collective-permute-start(bf16[256,512]{1,0:T(8,128)(2,1)S(1)} %get-tuple-element.26.target_a), channel_id=1, source_target_pairs={{0,2},{2,0},{4,6},{6,4},{8,10},{10,8},{12,14},{14,12},{16,18},{18,... | collective-permute-start | bytes 786440 | tf_op jit(solution)/shard_map/ppermute | solution.py:33
  3.8 5.6 %collective-permute-start = (bf16[32,768]{1,0:T(8,128)(2,1)}, bf16[32,768]{1,0:T(8,128)(2,1)S(1)}, u32[]{:S(2)}, u32[]{:S(2)}) collective-permute-start(bf16[32,768]{1,0:T(8,128)(2,1)} %bitcast.7), channel_id=1, source_target_pairs={{0,8},{2,10},{4,12},{6,14},{8,0},{10,2},{12,4},{14,6},{16,24},{18,... | collective-permute-start | bytes 147464 | tf_op jit(solution)/shard_map/ppermute | solution.py:33
  6.8 6.1 %collective-permute-start.1 = (bf16[32,768]{1,0:T(8,128)(2,1)}, bf16[32,768]{1,0:T(8,128)(2,1)S(1)}, u32[]{:S(2)}, u32[]{:S(2)}) collective-permute-start(bf16[32,768]{1,0:T(8,128)(2,1)} %bitcast.8), channel_id=1, source_target_pairs={{0,16},{2,18},{4,20},{6,22},{8,24},{10,26},{12,28},{14,30},{16,0},... | collective-permute-start | bytes 147464 | tf_op jit(solution)/shard_map/ppermute | solution.py:33
  9.4 6.1 %collective-permute-start.2 = (bf16[32,768]{1,0:T(8,128)(2,1)}, bf16[32,768]{1,0:T(8,128)(2,1)S(1)}, u32[]{:S(2)}, u32[]{:S(2)}) collective-permute-start(bf16[32,768]{1,0:T(8,128)(2,1)} %bitcast.9), channel_id=1, source_target_pairs={{0,24},{2,26},{4,28},{6,30},{8,16},{10,18},{12,20},{14,22},{16,8},... | collective-permute-start | bytes 147464 | tf_op jit(solution)/shard_map/ppermute | solution.py:33
  15.5 0.8 copy-start.7
  16.3 5.7 %collective-permute-start.5 = (bf16[4,32,768]{2,1,0:T(8,128)(2,1)S(1)}, bf16[4,32,768]{2,1,0:T(8,128)(2,1)S(1)}, u32[]{:S(2)}, u32[]{:S(2)}) collective-permute-start(bf16[4,32,768]{2,1,0:T(8,128)(2,1)S(1)} %shard_map.82.mine), channel_id=1, source_target_pairs={{0,4},{2,6},{4,0},{6,2},{8,12},{10,14},{12,8},{14,10},{16,20},{18,... | collective-permute-start | bytes 589832 | tf_op jit(solution)/shard_map/ppermute | solution.py:33
  17.9 16.7 %collective-permute-start.18 = (bf16[2,256,512]{2,1,0:T(8,128)(2,1)S(1)}, bf16[2,256,512]{2,1,0:T(8,128)(2,1)S(1)}, u32[]{:S(2)}, u32[]{:S(2)}) collective-permute-start(bf16[2,256,512]{2,1,0:T(8,128)(2,1)S(1)} %get-tuple-element.25.pair_a.own), channel_id=1, source_target_pairs={{0,8},{2,10},{4,12},{6,14},{8,16},{10,18},{12,20},{14,22},{16,24},... | collective-permute-start | bytes 1572872 | tf_op jit(solution)/shard_map/ppermute | solution.py:464
  17.9 4.3 %collective-permute-start.6 = (bf16[4,32,768]{2,1,0:T(8,128)(2,1)S(1)}, bf16[4,32,768]{2,1,0:T(8,128)(2,1)}, u32[]{:S(2)}, u32[]{:S(2)}) collective-permute-start(bf16[4,32,768]{2,1,0:T(8,128)(2,1)S(1)} %shard_map.82.mine), channel_id=1, source_target_pairs={{0,2},{2,0},{4,6},{6,4},{8,10},{10,8},{12,14},{14,12},{16,18},{18,... | collective-permute-start | bytes 589832 | tf_op jit(solution)/shard_map/ppermute | solution.py:33
  22.1 1.6 %collective-permute-start.7 = (bf16[4,32,768]{2,1,0:T(8,128)(2,1)S(1)}, bf16[4,32,768]{2,1,0:T(8,128)(2,1)}, u32[]{:S(2)}, u32[]{:S(2)}) collective-permute-start(bf16[4,32,768]{2,1,0:T(8,128)(2,1)S(1)} %collective-permute-done.5.other), channel_id=1, source_target_pairs={{0,2},{2,0},{4,6},{6,4},{8,10},{10,8},{12,14},{14,12},{16,18},{18,... | collective-permute-start | bytes 589832 | tf_op jit(solution)/shard_map/ppermute | solution.py:33
  22.1 24.9 %collective-permute-start.19 = (bf16[2,256,512]{2,1,0:T(8,128)(2,1)S(1)}, bf16[2,256,512]{2,1,0:T(8,128)(2,1)S(1)}, u32[]{:S(2)}, u32[]{:S(2)}) collective-permute-start(bf16[2,256,512]{2,1,0:T(8,128)(2,1)S(1)} %get-tuple-element.38.own), channel_id=1, source_target_pairs={{0,8},{2,10},{4,12},{6,14},{8,16},{10,18},{12,20},{14,22},{16,24},... | collective-permute-start | bytes 1572872 | tf_op jit(solution)/shard_map/ppermute | solution.py:464
  25.6 8.9 %collective-permute-start.8 = (bf16[192,512]{1,0:T(8,128)(2,1)S(1)}, bf16[192,512]{1,0:T(8,128)(2,1)S(1)}, u32[]{:S(2)}, u32[]{:S(2)}) collective-permute-start(bf16[192,512]{1,0:T(8,128)(2,1)S(1)} %get-tuple-element.29), channel_id=1, source_target_pairs={{0,4},{2,6},{4,0},{6,2},{8,12},{10,14},{12,8},{14,10},{16,20},{18,... | collective-permute-start | bytes 589832 | tf_op jit(solution)/shard_map/ppermute | solution.py:33
  36.5 13.3 %collective-permute-start.20 = (bf16[2,256,512]{2,1,0:T(8,128)(2,1)S(1)}, bf16[2,256,512]{2,1,0:T(8,128)(2,1)S(1)}, u32[]{:S(2)}, u32[]{:S(2)}) collective-permute-start(bf16[2,256,512]{2,1,0:T(8,128)(2,1)S(1)} %shard_map.89), channel_id=1, source_target_pairs={{0,4},{2,6},{4,0},{6,2},{8,12},{10,14},{12,8},{14,10},{16,20},{18,... | collective-permute-start | bytes 1572872 | tf_op jit(solution)/shard_map/ppermute | solution.py:33
  37.7 32.8 %copy-start.1 = (bf16[2,256,512]{2,1,0:T(8,128)(2,1)S(1)}, bf16[2,256,512]{2,1,0:T(8,128)(2,1)}, u32[]{:S(2)}) copy-start(bf16[2,256,512]{2,1,0:T(8,128)(2,1)} %k_own.3) | copy-start | bytes 1572868
  37.8 32.8 %copy-start.3 = (bf16[2,256,512]{2,1,0:T(8,128)(2,1)S(1)}, bf16[2,256,512]{2,1,0:T(8,128)(2,1)}, u32[]{:S(2)}) copy-start(bf16[2,256,512]{2,1,0:T(8,128)(2,1)} %v_own.3) | copy-start | bytes 1572868
  37.8 32.8 %copy-start.4 = (bf16[2,256,512]{2,1,0:T(8,128)(2,1)S(1)}, bf16[2,256,512]{2,1,0:T(8,128)(2,1)}, u32[]{:S(2)}) copy-start(bf16[2,256,512]{2,1,0:T(8,128)(2,1)} %q.5) | copy-start | bytes 1572868
  37.8 32.8 %copy-start.6 = (bf16[2,256,512]{2,1,0:T(8,128)(2,1)S(1)}, bf16[2,256,512]{2,1,0:T(8,128)(2,1)}, u32[]{:S(2)}) copy-start(bf16[2,256,512]{2,1,0:T(8,128)(2,1)} %gates.3) | copy-start | bytes 1572868
  37.8 8.4 %collective-permute-start.10 = (bf16[48,512]{1,0:T(8,128)(2,1)S(1)}, bf16[48,512]{1,0:T(8,128)(2,1)S(1)}, u32[]{:S(2)}, u32[]{:S(2)}) collective-permute-start(bf16[48,512]{1,0:T(8,128)(2,1)S(1)} %get-tuple-element.32), channel_id=1, source_target_pairs={{0,16},{2,18},{4,20},{6,22},{8,24},{10,26},{12,28},{14,30},{16,0},... | collective-permute-start | bytes 147464 | tf_op jit(solution)/shard_map/ppermute | solution.py:33
  37.9 8.4 %collective-permute-start.11 = (bf16[48,512]{1,0:T(8,128)(2,1)S(1)}, bf16[48,512]{1,0:T(8,128)(2,1)S(1)}, u32[]{:S(2)}, u32[]{:S(2)}) collective-permute-start(bf16[48,512]{1,0:T(8,128)(2,1)S(1)} %get-tuple-element.33), channel_id=1, source_target_pairs={{0,24},{2,26},{4,28},{6,30},{8,16},{10,18},{12,20},{14,22},{16,8},... | collective-permute-start | bytes 147464 | tf_op jit(solution)/shard_map/ppermute | solution.py:33
  39.4 7.0 %collective-permute-start.9 = (bf16[48,512]{1,0:T(8,128)(2,1)S(1)}, bf16[48,512]{1,0:T(8,128)(2,1)S(1)}, u32[]{:S(2)}, u32[]{:S(2)}) collective-permute-start(bf16[48,512]{1,0:T(8,128)(2,1)S(1)} %get-tuple-element.31), channel_id=1, source_target_pairs={{0,8},{2,10},{4,12},{6,14},{8,0},{10,2},{12,4},{14,6},{16,24},{18,... | collective-permute-start | bytes 147464 | tf_op jit(solution)/shard_map/ppermute | solution.py:33
  49.0 13.6 %collective-permute-start.21 = (bf16[2,256,512]{2,1,0:T(8,128)(2,1)S(1)}, bf16[2,256,512]{2,1,0:T(8,128)(2,1)S(1)}, u32[]{:S(2)}, u32[]{:S(2)}) collective-permute-start(bf16[2,256,512]{2,1,0:T(8,128)(2,1)S(1)} %shard_map.90), channel_id=1, source_target_pairs={{0,4},{2,6},{4,0},{6,2},{8,12},{10,14},{12,8},{14,10},{16,20},{18,... | collective-permute-start | bytes 1572872 | tf_op jit(solution)/shard_map/ppermute | solution.py:33
  49.8 12.8 %collective-permute-start.23 = (bf16[2,256,512]{2,1,0:T(8,128)(2,1)S(1)}, bf16[2,256,512]{2,1,0:T(8,128)(2,1)S(1)}, u32[]{:S(2)}, u32[]{:S(2)}) collective-permute-start(bf16[2,256,512]{2,1,0:T(8,128)(2,1)S(1)} %collective-permute-done.18.far.refs_0_), channel_id=1, source_target_pairs={{0,2},{2,0},{4,6},{6,4},{8,10},{10,8},{12,14},{14,12},{16,18},{18,... | collective-permute-start | bytes 1572872 | tf_op jit(solution)/shard_map/ppermute | solution.py:33
  49.8 20.2 %collective-permute-start.25 = (bf16[2,256,512]{2,1,0:T(8,128)(2,1)S(1)}, bf16[2,256,512]{2,1,0:T(8,128)(2,1)S(1)}, u32[]{:S(2)}, u32[]{:S(2)}) collective-permute-start(bf16[2,256,512]{2,1,0:T(8,128)(2,1)S(1)} %collective-permute-done.20.refs_2_.refs_1_), channel_id=1, source_target_pairs={{0,2},{2,0},{4,6},{6,4},{8,10},{10,8},{12,14},{14,12},{16,18},{18,... | collective-permute-start | bytes 1572872 | tf_op jit(solution)/shard_map/ppermute | solution.py:33
  50.3 4.1 %collective-permute-start.12 = (bf16[48,512]{1,0:T(8,128)(2,1)S(1)}, bf16[48,512]{1,0:T(8,128)(2,1)S(1)}, u32[]{:S(2)}, u32[]{:S(2)}) collective-permute-start(bf16[48,512]{1,0:T(8,128)(2,1)S(1)} %shard_map.86.refs_0_), channel_id=1, source_target_pairs={{0,8},{2,10},{4,12},{6,14},{8,0},{10,2},{12,4},{14,6},{16,24},{18,... | collective-permute-start | bytes 147464 | tf_op jit(solution)/shard_map/ppermute | solution.py:33
  51.4 5.6 %collective-permute-start.13 = (bf16[48,512]{1,0:T(8,128)(2,1)S(1)}, bf16[48,512]{1,0:T(8,128)(2,1)S(1)}, u32[]{:S(2)}, u32[]{:S(2)}) collective-permute-start(bf16[48,512]{1,0:T(8,128)(2,1)S(1)} %shard_map.86.refs_0_), channel_id=1, source_target_pairs={{0,16},{2,18},{4,20},{6,22},{8,24},{10,26},{12,28},{14,30},{16,0},... | collective-permute-start | bytes 147464 | tf_op jit(solution)/shard_map/ppermute | solution.py:33
  54.4 5.9 %collective-permute-start.14 = (bf16[48,512]{1,0:T(8,128)(2,1)S(1)}, bf16[48,512]{1,0:T(8,128)(2,1)S(1)}, u32[]{:S(2)}, u32[]{:S(2)}) collective-permute-start(bf16[48,512]{1,0:T(8,128)(2,1)S(1)} %shard_map.86.refs_0_), channel_id=1, source_target_pairs={{0,24},{2,26},{4,28},{6,30},{8,16},{10,18},{12,20},{14,22},{16,8},... | collective-permute-start | bytes 147464 | tf_op jit(solution)/shard_map/ppermute | solution.py:33
  57.0 17.4 %collective-permute-start.22 = (bf16[2,256,512]{2,1,0:T(8,128)(2,1)S(1)}, bf16[2,256,512]{2,1,0:T(8,128)(2,1)S(1)}, u32[]{:S(2)}, u32[]{:S(2)}) collective-permute-start(bf16[2,256,512]{2,1,0:T(8,128)(2,1)S(1)} %get-tuple-element.38.own), channel_id=1, source_target_pairs={{0,2},{2,0},{4,6},{6,4},{8,10},{10,8},{12,14},{14,12},{16,18},{18,... | collective-permute-start | bytes 1572872 | tf_op jit(solution)/shard_map/ppermute | solution.py:33
  60.3 15.7 %collective-permute-start.24 = (bf16[2,256,512]{2,1,0:T(8,128)(2,1)S(1)}, bf16[2,256,512]{2,1,0:T(8,128)(2,1)S(1)}, u32[]{:S(2)}, u32[]{:S(2)}) collective-permute-start(bf16[2,256,512]{2,1,0:T(8,128)(2,1)S(1)} %collective-permute-done.19.far.refs_1_), channel_id=1, source_target_pairs={{0,2},{2,0},{4,6},{6,4},{8,10},{10,8},{12,14},{14,12},{16,18},{18,... | collective-permute-start | bytes 1572872 | tf_op jit(solution)/shard_map/ppermute | solution.py:33
  62.6 13.4 %collective-permute-start.26 = (bf16[2,256,512]{2,1,0:T(8,128)(2,1)S(1)}, bf16[2,256,512]{2,1,0:T(8,128)(2,1)S(1)}, u32[]{:S(2)}, u32[]{:S(2)}) collective-permute-start(bf16[2,256,512]{2,1,0:T(8,128)(2,1)S(1)} %collective-permute-done.21.refs_3_), channel_id=1, source_target_pairs={{0,2},{2,0},{4,6},{6,4},{8,10},{10,8},{12,14},{14,12},{16,18},{18,... | collective-permute-start | bytes 1572872 | tf_op jit(solution)/shard_map/ppermute | solution.py:33
  62.6 7.4 %collective-permute-start.15 = (bf16[4,48,512]{2,1,0:T(8,128)(2,1)S(1)}, bf16[4,48,512]{2,1,0:T(8,128)(2,1)S(1)}, u32[]{:S(2)}, u32[]{:S(2)}) collective-permute-start(bf16[4,48,512]{2,1,0:T(8,128)(2,1)S(1)} %shard_map.87.mine), channel_id=1, source_target_pairs={{0,4},{2,6},{4,0},{6,2},{8,12},{10,14},{12,8},{14,10},{16,20},{18,... | collective-permute-start | bytes 589832 | tf_op jit(solution)/shard_map/ppermute | solution.py:33
  70.0 10.5 %collective-permute-start.16 = (bf16[4,48,512]{2,1,0:T(8,128)(2,1)S(1)}, bf16[4,48,512]{2,1,0:T(8,128)(2,1)S(1)}, u32[]{:S(2)}, u32[]{:S(2)}) collective-permute-start(bf16[4,48,512]{2,1,0:T(8,128)(2,1)S(1)} %shard_map.87.mine), channel_id=1, source_target_pairs={{0,2},{2,0},{4,6},{6,4},{8,10},{10,8},{12,14},{14,12},{16,18},{18,... | collective-permute-start | bytes 589832 | tf_op jit(solution)/shard_map/ppermute | solution.py:33
  70.0 4.4 %copy-start.5 = (bf16[2,256,512]{2,1,0:T(8,128)(2,1)}, bf16[2,256,512]{2,1,0:T(8,128)(2,1)S(1)}, u32[]{:S(2)}) copy-start(bf16[2,256,512]{2,1,0:T(8,128)(2,1)S(1)} %collective-permute-done.25.refs_7_.refs_4_) | copy-start | bytes 1572868
  70.0 10.5 %collective-permute-start.17 = (bf16[4,48,512]{2,1,0:T(8,128)(2,1)S(1)}, bf16[4,48,512]{2,1,0:T(8,128)(2,1)S(1)}, u32[]{:S(2)}, u32[]{:S(2)}) collective-permute-start(bf16[4,48,512]{2,1,0:T(8,128)(2,1)S(1)} %collective-permute-done.15.side_in), channel_id=1, source_target_pairs={{0,2},{2,0},{4,6},{6,4},{8,10},{10,8},{12,14},{14,12},{16,18},{18,... | collective-permute-start | bytes 589832 | tf_op jit(solution)/shard_map/ppermute | solution.py:33
  74.5 10.5 %collective-permute-start.28 = (bf16[128,512]{1,0:T(8,128)(2,1)S(1)}, bf16[128,512]{1,0:T(8,128)(2,1)S(1)}, u32[]{:S(2)}, u32[]{:S(2)}) collective-permute-start(bf16[128,512]{1,0:T(8,128)(2,1)S(1)} %get-tuple-element.44), channel_id=1, source_target_pairs={{0,1},{1,0},{2,3},{3,2},{4,5},{5,4},{6,7},{7,6},{8,9},{9,8},{10,11... | collective-permute-start | bytes 393224 | tf_op jit(solution)/shard_map/ppermute | solution.py:33
  76.0 0.8 copy-start.10
  80.5 4.4 %copy-start.8 = (f32[1024]{0:T(1024)S(1)}, f32[1024]{0:T(1024)}, u32[]{:S(2)}) copy-start(f32[1024]{0:T(1024)} %param.15) | copy-start | bytes 12292
  84.3 5.3 %collective-permute-start.27 = (bf16[128,512]{1,0:T(8,128)(2,1)S(1)}, bf16[128,512]{1,0:T(8,128)(2,1)S(1)}, u32[]{:S(2)}, u32[]{:S(2)}) collective-permute-start(bf16[128,512]{1,0:T(8,128)(2,1)S(1)} %get-tuple-element.42), channel_id=1, source_target_pairs={{0,1},{1,0},{2,3},{3,2},{4,5},{5,4},{6,7},{7,6},{8,9},{9,8},{10,11... | collective-permute-start | bytes 393224 | tf_op jit(solution)/shard_map/ppermute | solution.py:33

commit v5 on v3

v5 whole, which is shorter than its diff:
```python
import functools

import jax
import jax.numpy as jnp
from jax import lax
from jax.experimental import pallas as pl
from jax.experimental.pallas import tpu as pltpu
from jax.sharding import PartitionSpec as P

WIN = 1024
A_COEF = 3.4445
B_COEF = -4.775
C_COEF = 2.0315
BF = jnp.bfloat16
F32 = jnp.float32
VMEM_LIMIT = 32 * 1024 * 1024


def dot_nn(a, b):
    return lax.dot_general(a, b, (((1,), (0,)), ((), ())), preferred_element_type=F32)


def dot_nt(a, b):
    return lax.dot_general(a, b, (((1,), (1,)), ((), ())), preferred_element_type=F32)


def dot_tn(a, b):
    return lax.dot_general(a, b, (((0,), (0,)), ((), ())), preferred_element_type=F32)


def swapped(value, mask, axis="ctx"):
    count = lax.axis_size(axis)
    return lax.ppermute(value, axis, [(i, i ^ mask) for i in range(count)])


def vmem_spec():
    return pl.BlockSpec(memory_space=pltpu.VMEM)


def call(body, args, outs, scratch=(), cost=None):
    return pl.pallas_call(
        body,
        out_shape=outs,
        in_specs=[pl.BlockSpec(memory_space=pltpu.SMEM)] + [vmem_spec()] * (len(args) - 1),
        out_specs=jax.tree.map(lambda _: vmem_spec(), outs),
        scratch_shapes=list(scratch),
        compiler_params=pltpu.CompilerParams(vmem_limit_bytes=VMEM_LIMIT),
        cost_estimate=cost,
    )(*args)


def cost_of(flops, moved):
    return pl.CostEstimate(flops=int(flops), bytes_accessed=int(moved), transcendentals=0)


def silu(v):
    return v / (1.0 + jnp.exp(-v))


def hold_body(keys, values, rates, held_keys, held_values, held_rates):
    held_keys[...] = keys[...]
    held_values[...] = values[...]
    held_rates[...] = rates[...]


def held(keys, values, rates):
    def block(a):
        return pl.BlockSpec((1,) + a.shape[1:], lambda i: (i, 0, 0))

    specs = (block(keys), block(values), pl.BlockSpec(rates.shape, lambda i: (0, 0)))
    return pl.pallas_call(
        hold_body,
        grid=(2,),
        out_shape=tuple(jax.ShapeDtypeStruct(a.shape, a.dtype) for a in (keys, values, rates)),
        in_specs=list(specs),
        out_specs=specs,
        compiler_params=pltpu.CompilerParams(vmem_limit_bytes=VMEM_LIMIT),
        cost_estimate=cost_of(0, keys.size * 8),
    )(keys, values, rates)


def pick_body(ids, own, far, out):
    out[...] = jnp.where(ids[1] == 0, own[...], far[...])


def picked(ids, own, far):
    return call(
        pick_body,
        (ids, own, far),
        jax.ShapeDtypeStruct(own.shape, own.dtype),
        cost=cost_of(0, own.size * 4),
    )


def pack_body(*refs):
    for m, ref in enumerate(refs[:-1]):
        refs[-1][m] = ref[...]


def packed(*pieces):
    return pl.pallas_call(
        pack_body,
        out_shape=jax.ShapeDtypeStruct((len(pieces),) + pieces[0].shape, pieces[0].dtype),
        in_specs=[vmem_spec()] * len(pieces),
        out_specs=vmem_spec(),
        compiler_params=pltpu.CompilerParams(vmem_limit_bytes=VMEM_LIMIT),
        cost_estimate=cost_of(0, 4 * len(pieces) * pieces[0].size),
    )(*pieces)


def gradient_body(planes, ids, mine, other, beside_mine, beside_other, *refs):
    (keys, values, rates, keys_in, values_in, rates_in), refs = refs[:6], refs[6:]
    send, keep, whole, total = refs[:4]
    plane, side, core = ids[0], ids[1], ids[2]
    rows = mine.shape[1]
    target_ref = refs[4] if len(refs) > 4 else whole
    for m in range(planes):
        holder = 1 - core if m == 0 else core
        for far in range(2):
            block = ((plane ^ m) * 2 + (side if far == 0 else 1 - side)) * 2
            for source, at in (((mine, other)[far], holder), ((beside_mine, beside_other)[far], 1 - holder)):
                where = pl.ds(pl.multiple_of((block + at) * rows, rows), rows)
                target_ref[where, :] = source[m].astype(target_ref.dtype)
    if target_ref is not whole:
        whole[...] = target_ref[...].astype(BF)
    width = whole.shape[1] // 3
    half = width // 2
    parts = [
        whole[:, pl.ds(pl.multiple_of(b * width + core * half, half), half)] for b in range(3)
    ]
    gate_up_w = jnp.concatenate(parts[:2], 1)
    out_w = parts[2]
    first = None
    for key_ref, value_ref, rate in ((keys, values, rates), (keys_in, values_in, rates_in)):
        key_rows = key_ref[0]
        column = jnp.broadcast_to(rate[...], (128, rate.shape[1])).T[:, :1]
        target = (-column * value_ref[0].astype(F32)).astype(BF)
        gate_up = dot_nn(key_rows, gate_up_w)
        g, u = gate_up[:, :half], gate_up[:, half:]
        dh = dot_nn(target, out_w)
        s = 1.0 / (1.0 + jnp.exp(-g))
        gs = g * s
        hidden = (gs * u).astype(BF)
        dg = dh * u * s * (1.0 + g * (1.0 - s))
        du = dh * gs
        joined = jnp.concatenate([dg, du], 1).astype(BF)
        in_grad = dot_tn(joined, key_rows)
        out_grad = dot_tn(hidden, target)
        first = (in_grad, out_grad) if first is None else (first[0] + in_grad, first[1] + out_grad)
    total[: 2 * half, :] = first[0]
    total[2 * half : 3 * half, :] = first[1]
    if total.shape[0] > 3 * half:
        total[3 * half :, :] = jnp.zeros((total.shape[0] - 3 * half, total.shape[1]), F32)
    part = send.shape[0]
    send[...] = total[pl.ds(pl.multiple_of((1 - side) * part, part), part), :].astype(BF)
    keep[...] = total[pl.ds(pl.multiple_of(side * part, part), part), :]


def side_sum_body(planes, ids, keep, got, *refs):
    outs, total = refs[:planes], refs[planes]
    plane = ids[0]
    total[...] = keep[...] + got[...].astype(F32)
    part = outs[0].shape[0]
    for m in range(planes):
        rows = total[pl.ds(pl.multiple_of((plane ^ m) * part, part), part), :]
        outs[m][...] = rows.astype(outs[m].dtype)


def plane_sum_body(ids, own, *refs):
    total = own[...]
    for ref in refs[:-1]:
        total = total + ref[...].astype(F32)
    refs[-1][...] = total.astype(BF)


def weights_body(ids, whole, flipped, norms):
    width = whole.shape[1] // 3
    for b in range(3):
        cols = slice(b * width, (b + 1) * width)
        turned = whole[:, cols].astype(F32).T
        flipped[cols, :] = turned
        norms[cols, :] = jnp.sqrt(jnp.sum(turned * turned, 1, keepdims=True))


def blocks_of(ids, group, own, far, near, beside, far_beside, diag):
    plane, side, core = ids[0], ids[1], ids[2]
    moved = group if group == 0 else jnp.where(plane == 0, 0, group)
    crossed = group if group == 0 else jnp.where((plane == 0) & (side == 0), 0, group)
    return [
        own[group],
        far[moved],
        near[crossed],
        jnp.where(core == 1, beside[group], far_beside[moved]),
        diag[crossed],
    ]


def scores_body(ids, queries, *refs):
    key_refs, whole, (weights, totals, fast) = refs[:6], refs[6], refs[7:]
    plane, side, core = ids[0], ids[1], ids[2]
    later = (plane > 0).astype(jnp.int32)
    side_live, core_live = jnp.maximum(later, side), jnp.maximum(later, core)
    rows, depth = queries.shape[1:]
    scale = depth**-0.5
    row = lax.broadcasted_iota(jnp.int32, (rows, rows), 0)
    col = lax.broadcasted_iota(jnp.int32, (rows, rows), 1)
    for group in range(2):
        q = queries[group]
        scores = []
        lives = [None, later, side_live, core_live, side_live]
        for slot, keys in enumerate(blocks_of(ids, group, *key_refs)):
            s = dot_nt(q, keys) * scale
            allowed = {0: col <= row, 1: col > row}.get(slot)
            if group == 0 and slot:
                alive = jnp.full((rows, rows), lives[slot], jnp.int32) != 0
                allowed = alive if allowed is None else allowed & alive
            scores.append(s if allowed is None else jnp.where(allowed, s, -1e30))
        top = jnp.max(scores[0], -1, keepdims=True)
        for s in scores[1:]:
            top = jnp.maximum(top, jnp.max(s, -1, keepdims=True))
        total = None
        for slot, s in enumerate(scores):
            e = jnp.exp(s - top)
            t = jnp.sum(e, -1, keepdims=True)
            total = t if total is None else total + t
            weights[group, slot] = e.astype(BF)
        totals[group] = total
    width = whole.shape[1] // 3
    gate_up = dot_nn(queries[0], whole[:, : 2 * width])
    hidden = (silu(gate_up[:, :width]) * gate_up[:, width:]).astype(BF)
    fast[...] = dot_nt(hidden, whole[:, 2 * width :])


def mix_body(ids, *refs):
    value_refs, (weights, totals, fast, gates), refs = refs[:6], refs[6:10], refs[10:]
    win, outs, gated = refs[0], refs[1:-1], refs[-1]
    for group in range(2):
        out = None
        for slot, values in enumerate(blocks_of(ids, group, *value_refs)):
            o = dot_nn(weights[group, slot], values)
            out = o if out is None else out + o
        out = out / totals[group]
        if group == 0:
            gate = gates[0].astype(F32)
            spread(ids, ((out + fast[...]) * silu(gate)).astype(BF), outs, gated)
        else:
            win[...] = out


def spread(ids, value, outs, held):
    if len(outs) == 1:
        outs[0][...] = value
        return
    held[...] = value
    rows = outs[0].shape[0]
    outs[0][...] = held[pl.ds(pl.multiple_of(ids[3] * rows, rows), rows), :]
    outs[1][...] = held[pl.ds(pl.multiple_of((1 - ids[3]) * rows, rows), rows), :]


def update_body(planes, ids, rate, mine, side_in, core_in, diag_in, flipped, norms, q, win, gates, *refs):
    outs, (grads, gated) = refs[:-2], refs[-2:]
    plane, side, core = ids[0], ids[1], ids[2]
    part = mine.shape[1]
    for m in range(planes):
        for far in range(2):
            base = ((side if far == 0 else 1 - side) * planes + (plane ^ m)) * part
            where = pl.ds(pl.multiple_of(base, part), part)
            grads[core, where, :] = (mine, side_in)[far][m]
            grads[1 - core, where, :] = (core_in, diag_in)[far][m]
    width = flipped.shape[0] // 3
    half = width // 2
    turned = []
    for b in range(3):
        block = jnp.concatenate(
            [grads[0, b * half : (b + 1) * half, :], grads[1, b * half : (b + 1) * half, :]], 0
        ).astype(F32)
        length = jnp.sqrt(jnp.sum(block * block, keepdims=True))
        turned.append((block / (length + 1e-06)).astype(BF))
    for _ in range(3):
        grams = [dot_nt(y, y) for y in turned]
        lows = [a.astype(BF) for a in grams]
        squares = [dot_nn(a, a) for a in lows]
        mixers = [(B_COEF * a + C_COEF * s).astype(BF) for a, s in zip(grams, squares)]
        turned = [
            (A_COEF * y.astype(F32) + dot_nn(b, y)).astype(BF) for b, y in zip(mixers, turned)
        ]
    fresh = []
    for b in range(3):
        cols = slice(b * width, (b + 1) * width)
        moved = flipped[cols, :] - rate[0] * turned[b].astype(F32)
        length = jnp.sqrt(jnp.sum(moved * moved, 1, keepdims=True))
        fresh.append((moved * (norms[cols, :] / (length + 1e-06))).astype(BF))
    x = q[...]
    g = dot_nt(x, fresh[0])
    u = dot_nt(x, fresh[1])
    hidden = (silu(g) * u).astype(BF)
    fast = dot_nn(hidden, fresh[2])
    gate = gates[...].astype(F32)
    spread(ids, ((win[...] + fast) * silu(gate)).astype(BF), outs, gated)


def norm_body(group, ids, own, got, gain, *refs):
    out, held, sems = refs[-3:]
    head = ids[3]
    rows, depth = own.shape
    chunk = rows // 4
    copies = []
    for c in range(4):
        at = slice(c * chunk, (c + 1) * chunk)
        a = own[at, :].astype(F32)
        b = got[at, :].astype(F32)
        low = jnp.where(head == 0, a, b)
        high = jnp.where(head == 0, b, a)
        square = jnp.sum(a * a, -1, keepdims=True) + jnp.sum(b * b, -1, keepdims=True)
        inv = lax.rsqrt(square / (2 * depth) + 1e-06)
        held[at, :depth] = (low * inv * gain[:, :depth]).astype(BF)
        held[at, depth:] = (high * inv * gain[:, depth:]).astype(BF)
        copies.append(pltpu.make_async_copy(held.at[at], out.at[group, at], sems.at[c]))
        copies[-1].start()
    for copy in copies:
        copy.wait()


def finished(ids, group, gated, norm_gain, before):
    total = norm_gain.shape[0]
    if len(gated) == 2:
        own, away = gated
        got = swapped(away, 1, "head")
        rows, depth = own.shape
        earlier = () if before is None else (before,)
        return pl.pallas_call(
            functools.partial(norm_body, group),
            out_shape=jax.ShapeDtypeStruct((2, rows, total), BF),
            in_specs=[
                pl.BlockSpec(memory_space=pltpu.SMEM),
                vmem_spec(),
                vmem_spec(),
                vmem_spec(),
                *([pl.BlockSpec(memory_space=pl.ANY)] * len(earlier)),
            ],
            out_specs=pl.BlockSpec(memory_space=pl.ANY),
            scratch_shapes=[pltpu.VMEM((rows, total), BF), pltpu.SemaphoreType.DMA((4,))],
            input_output_aliases={4: 0} if earlier else {},
            compiler_params=pltpu.CompilerParams(vmem_limit_bytes=VMEM_LIMIT),
            cost_estimate=cost_of(0, 4 * rows * total),
        )(ids, own, got, norm_gain[None, :], *earlier)
    wide = lax.all_to_all(gated[0], "head", split_axis=0, concat_axis=1, tiled=True).astype(F32)
    inv = lax.rsqrt(jnp.mean(wide * wide, -1, keepdims=True) + 1e-06)
    done = (wide * inv * norm_gain).astype(BF)[None]
    return done if before is None else jnp.concatenate([before, done], 0)


def after(value, *needed):
    return lax.optimization_barrier((value,) + needed)[0]


def sent(value, pairs, axis="ctx"):
    return lax.ppermute(value, axis, pairs)


def shards(queries, keys, values, gates, token_rates, fast_init, fast_rate, norm_gain):
    count = lax.axis_size("ctx")
    heads = lax.axis_size("head")
    rows, depth = queries.shape[1], queries.shape[2]
    reach = (WIN - 1) // rows + 1
    planes = count // reach
    if reach != 4 or WIN % rows or planes * reach != count or planes & (planes - 1):
        raise ValueError("unsupported shapes")
    position = lax.axis_index("ctx")
    plane, side, core = position // 4, (position // 2) % 2, position % 2
    ids = jnp.stack([plane, side, core, lax.axis_index("head")]).astype(jnp.int32)
    width = fast_init.shape[2] // 3
    half = width // 2
    everyone = range(count)
    local = fast_init[0]
    local_in = swapped(local, 1)
    arrived = [swapped(after(local, local_in) if m == 1 else local, 4 * m) for m in range(1, planes)]
    rates = token_rates.reshape(1, rows)
    keys_in, values_in, rates_in = (swapped(v, 1) for v in (keys, values, rates))
    mine_w = packed(local_in, *arrived)
    other_w = swapped(mine_w, 2)
    own_keys, own_values, own_rates = held(keys, values, rates)
    beside_w = [swapped(mine_w, 1), swapped(after(other_w, own_keys), 1)]

    pieces = 2 * planes
    part = -(-3 * half // (16 * pieces)) * 16
    scratch = [pltpu.VMEM((pieces * part, depth), F32)]
    if local.shape[0] % 16:
        scratch.append(pltpu.VMEM((depth, 3 * width), F32))
    send, keep, whole = call(
        functools.partial(gradient_body, planes),
        (ids, mine_w, other_w, *beside_w)
        + (own_keys, own_values, own_rates, keys_in, values_in, rates_in),
        (
            jax.ShapeDtypeStruct((planes * part, depth), BF),
            jax.ShapeDtypeStruct((planes * part, depth), F32),
            jax.ShapeDtypeStruct((depth, 3 * width), BF),
        ),
        scratch=scratch,
        cost=cost_of(2 * 2 * rows * depth * half * 6, 4 * rows * depth * 4),
    )
    got = swapped(send, 2)

    flipped, norms = call(
        weights_body,
        (ids, whole),
        (
            jax.ShapeDtypeStruct((3 * width, depth), F32),
            jax.ShapeDtypeStruct((3 * width, 1), F32),
        ),
        cost=cost_of(0, depth * width * 3 * 8),
    )
    parts = call(
        functools.partial(side_sum_body, planes),
        (ids, after(keep, flipped), got),
        tuple(jax.ShapeDtypeStruct((part, depth), F32 if m == 0 else BF) for m in range(planes)),
        scratch=(pltpu.VMEM((planes * part, depth), F32),),
        cost=cost_of(0, planes * part * depth * 8),
    )
    partial = [swapped(parts[m], 4 * m) for m in range(1, planes)]
    ring = [(i, (i + reach) % count) for i in everyone]
    far_keys = sent(after(keys, *arrived), ring)
    far_values = sent(after(values, send), ring)
    near_keys = swapped(picked(ids, own_keys, after(far_keys, got)), 2)
    pick_values = picked(ids, own_values, after(far_values, parts[0]))
    near_values = swapped(after(pick_values, *partial), 2)

    total = call(
        plane_sum_body,
        (ids, after(parts[0], pick_values), *partial),
        jax.ShapeDtypeStruct((part, depth), BF),
        cost=cost_of(0, planes * part * depth * 3),
    )
    far_keys_in = swapped(after(far_keys, total), 1)
    near_keys_in = swapped(after(near_keys, total), 1)
    all_keys = [own_keys, far_keys, near_keys, keys_in, far_keys_in, near_keys_in]
    planes_grad = [
        swapped(total if m < planes - 1 else after(total, far_keys_in, near_keys_in), 4 * m)
        for m in range(1, planes)
    ]

    if heads == 2:
        split = (jax.ShapeDtypeStruct((rows // 2, depth), BF),) * 2
    else:
        split = (jax.ShapeDtypeStruct((rows, depth), BF),)
    attn_cost = cost_of(6 * rows * depth * 10 * rows, rows * depth * 40)
    weights, totals, fast_first = call(
        scores_body,
        (ids, queries, *all_keys, whole),
        (
            jax.ShapeDtypeStruct((2, reach + 1, rows, rows), BF),
            jax.ShapeDtypeStruct((2, rows, 1), F32),
            jax.ShapeDtypeStruct((rows, depth), F32),
        ),
        cost=attn_cost,
    )
    plane_grad = packed(after(total, totals), *planes_grad)
    far_values_in = swapped(after(far_values, plane_grad), 1)
    near_values_in = swapped(after(near_values, plane_grad), 1)
    all_values = [own_values, far_values, near_values, values_in, far_values_in, near_values_in]
    window_second, *gated_first = call(
        mix_body,
        (ids, *all_values, weights, totals, fast_first, gates),
        (jax.ShapeDtypeStruct((rows, depth), F32), *split),
        scratch=(pltpu.VMEM((rows, depth), BF),),
        cost=attn_cost,
    )
    side_grad = swapped(plane_grad, 2)
    beside_grad = [swapped(plane_grad, 1), swapped(after(side_grad, window_second), 1)]
    grads = [plane_grad, side_grad, *beside_grad]
    done = finished(ids, 0, gated_first, norm_gain, None)

    def full(shape):
        return pl.BlockSpec(shape, lambda i, nd=len(shape): (0,) * nd)

    gated_second = pl.pallas_call(
        functools.partial(update_body, planes),
        grid=(1,),
        out_shape=split,
        in_specs=[
            pl.BlockSpec(memory_space=pltpu.SMEM),
            pl.BlockSpec(memory_space=pltpu.SMEM),
            *[full(v.shape) for v in grads],
            full(flipped.shape),
            full(norms.shape),
            pl.BlockSpec((None, rows, depth), lambda i: (1, 0, 0)),
            full((rows, depth)),
            pl.BlockSpec((None, rows, depth), lambda i: (1, 0, 0)),
        ],
        out_specs=tuple(full(s.shape) for s in split),
        scratch_shapes=[
            pltpu.VMEM((2, pieces * part, depth), BF),
            pltpu.VMEM((rows, depth), BF),
        ],
        compiler_params=pltpu.CompilerParams(vmem_limit_bytes=VMEM_LIMIT),
        cost_estimate=cost_of(3e9, 4e6),
    )(ids, fast_rate, *grads, flipped, norms, queries, window_second, gates)
    return finished(ids, 1, gated_second, norm_gain, done)


def solution(mesh):
    placed = (
        P(None, "ctx", "head"),
        P(None, "ctx", "head"),
        P(None, "ctx", "head"),
        P(None, "ctx", "head"),
        P("ctx", "head"),
        P("head", "ctx", None),
        P("head"),
        P(),
    )
    return jax.shard_map(
        shards,
        mesh=mesh,
        in_specs=placed,
        out_specs=P(None, ("ctx", "head"), None),
        check_vma=False,
    )
```

time: 159 us -> 78.1 us (0.49)
  Pallas kernels: 87.5 us -> 15.7 us
  local copies, waits for them, and re-layouts: 10.2 us -> 2.81 us
  other arithmetic: 1.76 us -> 0.08 us
    pallas_call x5 -> x3, Pallas kernels: 77.3 us -> 0.12 us  [the longest x1 0.1 us: held(): pl.pallas_call(hold_body, grid=(2,), out_shape=tuple((jax.ShapeDtypeStruc...]
    unnamed x43 -> x14, local copies, waits for them, and re-layouts: 9.47 us -> 2.81 us
    pallas_call x4 -> x8, Pallas kernels: 3.59 us -> 9.02 us  [call(): pl.pallas_call(body, out_shape=outs, in_specs=[pl.BlockSpec(memory_space=...]
    ppermute x25 -> x28, waiting for transfers between devices: 28.3 us -> 25.1 us  [swapped(): return lax.ppermute(value, axis, [(i, i ^ mask) for i in range(count)])]
    ppermute x2, waiting for transfers between devices: 4.36 us -> 6.84 us  [sent(): return lax.ppermute(value, axis, pairs)]
    another operation x2 -> x0, other arithmetic: 1.68 us -> none  [the longest x1 0.85 us: shards(): jnp.stack([total] + [swapped(total, 4 * m) for m in range(1, planes)])]
    ppermute x25 -> x28, starting transfers between devices: 24.2 us -> 24.9 us  [swapped(): return lax.ppermute(value, axis, [(i, i ^ mask) for i in range(count)])]
  transfers between devices with their start and end apart: 27 -> 30, of which waited for: 6 -> 19; matrix products, arithmetic and copies ran while one was open for 6% -> 0% of each run, Pallas kernels for 54% -> 18%
where the time goes in v5:
time: 78.1 us; the launch traced here: 77.8 us
  waiting for transfers between devices  32 us (41%)
  starting transfers between devices  26.4 us (34%)
  Pallas kernels  15.7 us (20%)
  local copies, waits for them, and re-layouts  2.81 us (4%)
  between operations  0.81 us (1%)
    ppermute x28, waiting for transfers between devices, swapped(): return lax.ppermute(value, axis, [(i, i ^ mask) for i in range(count)])  25.1 us
    ppermute x28, starting transfers between devices, swapped(): return lax.ppermute(value, axis, [(i, i ^ mask) for i in range(count)])  24.9 us
    pallas_call x8, Pallas kernels, call(): pl.pallas_call(body, out_shape=outs, in_specs=[pl.BlockSpec(memory_space=...  9.02 us
    ppermute x2, waiting for transfers between devices, sent(): return lax.ppermute(value, axis, pairs)  6.84 us
    pallas_call x1, Pallas kernels, shards(): pl.pallas_call(functools.partial(update_body, planes), grid=(1,), out_sha...  3.84 us
    unnamed x14, local copies, waits for them, and re-layouts  2.81 us
    pallas_call x2, Pallas kernels, finished(): pl.pallas_call(functools.partial(norm_body, group), out_shape=jax.ShapeDt...  2.76 us
  transfers between devices with their start and end apart: 30, of which 19 were waited for; matrix products, arithmetic and copies ran while one was open for 0% of the time, Pallas kernels for 18%

profile of v5, /device:TPU:0, one launch (start us, length us, event | category | flops | bytes accessed | tf_op | source)
XLA Modules:
  0.0 77.8 jit_solution(6048952393934979362)
XLA Ops:
  0.0 0.5 collective-permute-start.7
  0.5 0.1 collective-permute-start.8
  0.5 0.5 collective-permute-start
  1.0 3.6 %collective-permute-start.2 = (bf16[32,768]{1,0:T(8,128)(2,1)}, bf16[32,768]{1,0:T(8,128)(2,1)S(1)}, u32[]{:S(2)}, u32[]{:S(2)}) collective-permute-start(bf16[32,768]{1,0:T(8,128)(2,1)} %bitcast.12), channel_id=1, source_target_pairs={{0,16},{2,18},{4,20},{6,22},{8,24},{10,26},{12,28},{14,30},{16,0},... | collective-permute-start | bytes 147464 | tf_op jit(solution)/shard_map/ppermute | solution.py:33
  4.6 1.3 %collective-permute-start.3 = (bf16[32,768]{1,0:T(8,128)(2,1)}, bf16[32,768]{1,0:T(8,128)(2,1)S(1)}, u32[]{:S(2)}, u32[]{:S(2)}) collective-permute-start(bf16[32,768]{1,0:T(8,128)(2,1)} %bitcast.13), channel_id=1, source_target_pairs={{0,24},{2,26},{4,28},{6,30},{8,16},{10,18},{12,20},{14,22},{16,8},... | collective-permute-start | bytes 147464 | tf_op jit(solution)/shard_map/ppermute | solution.py:33
  5.9 0.2 collective-permute-start.1
  6.1 1.0 %collective-permute-done.2.refs_2_ = bf16[32,768]{1,0:T(8,128)(2,1)S(1)} collective-permute-done((bf16[32,768]{1,0:T(8,128)(2,1)}, bf16[32,768]{1,0:T(8,128)(2,1)S(1)}, u32[]{:S(2)}, u32[]{:S(2)}) %collective-permute-start.2) | collective-permute-done | bytes 49184 | tf_op jit(solution)/shard_map/ppermute | solution.py:33
  7.2 3.8 %collective-permute-done.3.refs_3_ = bf16[32,768]{1,0:T(8,128)(2,1)S(1)} collective-permute-done((bf16[32,768]{1,0:T(8,128)(2,1)}, bf16[32,768]{1,0:T(8,128)(2,1)S(1)}, u32[]{:S(2)}, u32[]{:S(2)}) %collective-permute-start.3) | collective-permute-done | bytes 49184 | tf_op jit(solution)/shard_map/ppermute | solution.py:33
  11.0 0.1 collective-permute-done.1.refs_1_
  11.1 1.6 %collective-permute-start.4 = (bf16[4,32,768]{2,1,0:T(8,128)(2,1)S(1)}, bf16[4,32,768]{2,1,0:T(8,128)(2,1)S(1)}, u32[]{:S(2)}, u32[]{:S(2)}) collective-permute-start(bf16[4,32,768]{2,1,0:T(8,128)(2,1)S(1)} %shard_map.82.mine), channel_id=1, source_target_pairs={{0,4},{2,6},{4,0},{6,2},{8,12},{10,14},{12,8},{14,10},{16,20},{18,... | collective-permute-start | bytes 589832 | tf_op jit(solution)/shard_map/ppermute | solution.py:33
  12.6 0.2 collective-permute-start.15
  12.8 0.0 collective-permute-start.9
  12.8 1.1 %copy-done = bf16[2,256,512]{2,1,0:T(8,128)(2,1)S(1)} copy-done((bf16[2,256,512]{2,1,0:T(8,128)(2,1)S(1)}, bf16[2,256,512]{2,1,0:T(8,128)(2,1)}, u32[]{:S(2)}) %copy-start) | copy-done | bytes 524312
  13.9 1.0 %copy-done.1 = bf16[2,256,512]{2,1,0:T(8,128)(2,1)S(1)} copy-done((bf16[2,256,512]{2,1,0:T(8,128)(2,1)S(1)}, bf16[2,256,512]{2,1,0:T(8,128)(2,1)}, u32[]{:S(2)}) %copy-start.1) | copy-done | bytes 524312
  15.0 0.7 copy-done.4
  15.6 0.1 shard_map.83
  15.7 0.0 copy-start.2
  15.7 1.1 %collective-permute-done.4.other = bf16[4,32,768]{2,1,0:T(8,128)(2,1)S(1)} collective-permute-done((bf16[4,32,768]{2,1,0:T(8,128)(2,1)S(1)}, bf16[4,32,768]{2,1,0:T(8,128)(2,1)S(1)}, u32[]{:S(2)}, u32[]{:S(2)}) %collective-permute-start.4) | collective-permute-done | bytes 196640 | tf_op jit(solution)/shard_map/ppermute | solution.py:33
  16.8 0.5 collective-permute-start.6
  17.3 0.1 pad_add_fusion.ids
  17.4 1.0 %collective-permute-done.5.beside_mine = bf16[4,32,768]{2,1,0:T(8,128)(2,1)} collective-permute-done((bf16[4,32,768]{2,1,0:T(8,128)(2,1)S(1)}, bf16[4,32,768]{2,1,0:T(8,128)(2,1)}, u32[]{:S(2)}, u32[]{:S(2)}) %collective-permute-start.5) | collective-permute-done | bytes 196640 | tf_op jit(solution)/shard_map/ppermute | solution.py:33
  18.4 0.3 collective-permute-done.6.beside_other
  18.7 0.0 collective-permute-done.7.refs_3_
  18.7 2.2 %shard_map.84 = (bf16[192,512]{1,0:T(8,128)(2,1)S(1)}, f32[192,512]{1,0:T(8,128)S(1)}, bf16[512,768]{1,0:T(8,128)(2,1)S(1)}) custom-call(s32[4]{0:T(128)S(1)} %pad_add_fusion.ids, bf16[4,32,768]{2,1,0:T(8,128)(2,1)S(1)} %shard_map.82.mine, bf16[4,32,768]{2,1,0:T(8,128)(2,1)S(1)} %collective-permute-done.4.other, ...), custom_call_target="tpu_custom_call" | custom-call | flops 402653184 | bytes 2097152 | tf_op jit(solution)/shard_map/pallas_call | solution.py:41
  20.9 1.6 %collective-permute-start.10 = (bf16[192,512]{1,0:T(8,128)(2,1)S(1)}, bf16[192,512]{1,0:T(8,128)(2,1)S(1)}, u32[]{:S(2)}, u32[]{:S(2)}) collective-permute-start(bf16[192,512]{1,0:T(8,128)(2,1)S(1)} %get-tuple-element.50), channel_id=1, source_target_pairs={{0,4},{2,6},{4,0},{6,2},{8,12},{10,14},{12,8},{14,10},{16,20},{18,... | collective-permute-start | bytes 589832 | tf_op jit(solution)/shard_map/ppermute | solution.py:33
  22.4 1.3 %collective-permute-start.11 = (bf16[2,256,512]{2,1,0:T(8,128)(2,1)S(1)}, bf16[2,256,512]{2,1,0:T(8,128)(2,1)S(1)}, u32[]{:S(2)}, u32[]{:S(2)}) collective-permute-start(bf16[2,256,512]{2,1,0:T(8,128)(2,1)S(1)} %copy-done.2), channel_id=1, source_target_pairs={{0,8},{2,10},{4,12},{6,14},{8,16},{10,18},{12,20},{14,22},{16,24},... | collective-permute-start | bytes 1572872 | tf_op jit(solution)/shard_map/ppermute | solution.py:358
  23.7 4.0 %collective-permute-done.15.far.refs_1_ = bf16[2,256,512]{2,1,0:T(8,128)(2,1)S(1)} collective-permute-done((bf16[2,256,512]{2,1,0:T(8,128)(2,1)}, bf16[2,256,512]{2,1,0:T(8,128)(2,1)S(1)}, u32[]{:S(2)}, u32[]{:S(2)}) %collective-permute-start.15) | collective-permute-done | bytes 524320 | tf_op jit(solution)/shard_map/ppermute | solution.py:358
  27.7 0.3 collective-permute-done.10.got
  28.0 0.6 shard_map.89
  28.6 1.6 %collective-permute-start.16 = (bf16[2,256,512]{2,1,0:T(8,128)(2,1)S(1)}, bf16[2,256,512]{2,1,0:T(8,128)(2,1)S(1)}, u32[]{:S(2)}, u32[]{:S(2)}) collective-permute-start(bf16[2,256,512]{2,1,0:T(8,128)(2,1)S(1)} %shard_map.89), channel_id=1, source_target_pairs={{0,4},{2,6},{4,0},{6,2},{8,12},{10,14},{12,8},{14,10},{16,20},{18,... | collective-permute-start | bytes 1572872 | tf_op jit(solution)/shard_map/ppermute | solution.py:33
  30.1 0.9 %shard_map.85 = (f32[768,512]{1,0:T(8,128)S(1)}, f32[768,1]{1,0:T(8,128)S(1)}) custom-call(s32[4]{0:T(128)S(1)} %pad_add_fusion.ids, bf16[512,768]{1,0:T(8,128)(2,1)S(1)} %get-tuple-element.47.whole.refs_6_), custom_call_target="tpu_custom_call" | custom-call | bytes 3145728 | tf_op jit(solution)/shard_map/pallas_call | solution.py:41
  31.1 0.6 shard_map.86
  31.7 1.4 %collective-permute-start.12 = (bf16[48,512]{1,0:T(8,128)(2,1)S(1)}, bf16[48,512]{1,0:T(8,128)(2,1)S(1)}, u32[]{:S(2)}, u32[]{:S(2)}) collective-permute-start(bf16[48,512]{1,0:T(8,128)(2,1)S(1)} %get-tuple-element.55), channel_id=1, source_target_pairs={{0,8},{2,10},{4,12},{6,14},{8,0},{10,2},{12,4},{14,6},{16,24},{18,... | collective-permute-start | bytes 147464 | tf_op jit(solution)/shard_map/ppermute | solution.py:33
  33.1 3.2 %collective-permute-start.13 = (bf16[48,512]{1,0:T(8,128)(2,1)S(1)}, bf16[48,512]{1,0:T(8,128)(2,1)S(1)}, u32[]{:S(2)}, u32[]{:S(2)}) collective-permute-start(bf16[48,512]{1,0:T(8,128)(2,1)S(1)} %get-tuple-element.56), channel_id=1, source_target_pairs={{0,16},{2,18},{4,20},{6,22},{8,24},{10,26},{12,28},{14,30},{16,0},... | collective-permute-start | bytes 147464 | tf_op jit(solution)/shard_map/ppermute | solution.py:33
  36.3 0.1 collective-permute-start.14
  36.4 2.9 %collective-permute-done.11.far.refs_1_ = bf16[2,256,512]{2,1,0:T(8,128)(2,1)S(1)} collective-permute-done((bf16[2,256,512]{2,1,0:T(8,128)(2,1)S(1)}, bf16[2,256,512]{2,1,0:T(8,128)(2,1)S(1)}, u32[]{:S(2)}, u32[]{:S(2)}) %collective-permute-start.11) | collective-permute-done | bytes 524320 | tf_op jit(solution)/shard_map/ppermute | solution.py:358
  39.3 0.6 shard_map.87
  39.9 1.2 %collective-permute-done.12.refs_0_ = bf16[48,512]{1,0:T(8,128)(2,1)S(1)} collective-permute-done((bf16[48,512]{1,0:T(8,128)(2,1)S(1)}, bf16[48,512]{1,0:T(8,128)(2,1)S(1)}, u32[]{:S(2)}, u32[]{:S(2)}) %collective-permute-start.12) | collective-permute-done | bytes 49184 | tf_op jit(solution)/shard_map/ppermute | solution.py:33
  41.1 0.4 collective-permute-done.13.refs_1_
  41.5 0.8 collective-permute-done.14.refs_2_
  42.2 0.6 shard_map.88.refs_0_
  42.8 0.0 copy-start.6
  42.8 0.1 collective-permute-start.17
  42.9 0.5 collective-permute-start.18
  43.4 0.5 collective-permute-start.24
  43.9 1.3 %collective-permute-start.19 = (bf16[48,512]{1,0:T(8,128)(2,1)S(1)}, bf16[48,512]{1,0:T(8,128)(2,1)S(1)}, u32[]{:S(2)}, u32[]{:S(2)}) collective-permute-start(bf16[48,512]{1,0:T(8,128)(2,1)S(1)} %shard_map.88.refs_0_), channel_id=1, source_target_pairs={{0,8},{2,10},{4,12},{6,14},{8,0},{10,2},{12,4},{14,6},{16,24},{18,... | collective-permute-start | bytes 147464 | tf_op jit(solution)/shard_map/ppermute | solution.py:33
  45.2 2.7 %collective-permute-start.20 = (bf16[48,512]{1,0:T(8,128)(2,1)S(1)}, bf16[48,512]{1,0:T(8,128)(2,1)S(1)}, u32[]{:S(2)}, u32[]{:S(2)}) collective-permute-start(bf16[48,512]{1,0:T(8,128)(2,1)S(1)} %shard_map.88.refs_0_), channel_id=1, source_target_pairs={{0,16},{2,18},{4,20},{6,22},{8,24},{10,26},{12,28},{14,30},{16,0},... | collective-permute-start | bytes 147464 | tf_op jit(solution)/shard_map/ppermute | solution.py:33
  47.9 0.4 collective-permute-start.21
  48.3 2.0 %shard_map.90 = (bf16[2,5,256,256]{3,2,1,0:T(8,128)(2,1)S(1)}, f32[2,256,1]{2,1,0:T(8,128)S(1)}, f32[256,512]{1,0:T(8,128)S(1)}) custom-call(s32[4]{0:T(128)S(1)} %pad_add_fusion.ids, bf16[2,256,512]{2,1,0:T(8,128)(2,1)S(1)} %copy-done.5, bf16[2,256,512]{2,1,0:T(8,128)(2,1)S(1)} %get-tuple-element.42.refs_0_.own, ...), custom_call_target="tpu_custom_call" | custom-call | flops 2013265920 | bytes 5242880 | tf_op jit(solution)/shard_map/pallas_call | solution.py:41
  50.4 0.8 %collective-permute-done.20.refs_2_ = bf16[48,512]{1,0:T(8,128)(2,1)S(1)} collective-permute-done((bf16[48,512]{1,0:T(8,128)(2,1)S(1)}, bf16[48,512]{1,0:T(8,128)(2,1)S(1)}, u32[]{:S(2)}, u32[]{:S(2)}) %collective-permute-start.20) | collective-permute-done | bytes 49184 | tf_op jit(solution)/shard_map/ppermute | solution.py:33
  51.2 2.6 %collective-permute-done.21.refs_3_ = bf16[48,512]{1,0:T(8,128)(2,1)S(1)} collective-permute-done((bf16[48,512]{1,0:T(8,128)(2,1)S(1)}, bf16[48,512]{1,0:T(8,128)(2,1)S(1)}, u32[]{:S(2)}, u32[]{:S(2)}) %collective-permute-start.21) | collective-permute-done | bytes 49184 | tf_op jit(solution)/shard_map/ppermute | solution.py:33
  53.8 3.5 %collective-permute-done.24.refs_2_ = bf16[2,256,512]{2,1,0:T(8,128)(2,1)S(1)} collective-permute-done((bf16[2,256,512]{2,1,0:T(8,128)(2,1)S(1)}, bf16[2,256,512]{2,1,0:T(8,128)(2,1)S(1)}, u32[]{:S(2)}, u32[]{:S(2)}) %collective-permute-start.24) | collective-permute-done | bytes 524320 | tf_op jit(solution)/shard_map/ppermute | solution.py:33
  57.3 0.5 collective-permute-start.25
  57.8 0.5 collective-permute-start.22
  58.4 0.9 %collective-permute-done.26.refs_5_ = bf16[2,256,512]{2,1,0:T(8,128)(2,1)S(1)} collective-permute-done((bf16[2,256,512]{2,1,0:T(8,128)(2,1)S(1)}, bf16[2,256,512]{2,1,0:T(8,128)(2,1)S(1)}, u32[]{:S(2)}, u32[]{:S(2)}) %collective-permute-start.26) | collective-permute-done | bytes 524320 | tf_op jit(solution)/shard_map/ppermute | solution.py:33
  59.2 0.7 collective-permute-done.25.refs_4_
  60.0 1.5 %shard_map.92 = (f32[256,512]{1,0:T(8,128)S(1)}, bf16[128,512]{1,0:T(8,128)(2,1)S(1)}, bf16[128,512]{1,0:T(8,128)(2,1)S(1)}) custom-call(s32[4]{0:T(128)S(1)} %pad_add_fusion.ids, bf16[2,256,512]{2,1,0:T(8,128)(2,1)S(1)} %get-tuple-element.44.refs_1_.own.refs_0_, bf16[2,256,512]{2,1,0:T(8,128)(2,1)S(1)} %collective-permute-done.11.far.refs_1_, ...), custom_call_target="tpu_custom_call" | custom-call | flops 2013265920 | bytes 5242880 | tf_op jit(solution)/shard_map/pallas_call | solution.py:41
  61.5 3.2 %collective-permute-done.22.side_in = bf16[4,48,512]{2,1,0:T(8,128)(2,1)S(1)} collective-permute-done((bf16[4,48,512]{2,1,0:T(8,128)(2,1)S(1)}, bf16[4,48,512]{2,1,0:T(8,128)(2,1)S(1)}, u32[]{:S(2)}, u32[]{:S(2)}) %collective-permute-start.22) | collective-permute-done | bytes 196640 | tf_op jit(solution)/shard_map/ppermute | solution.py:33
  65.3 1.6 %collective-permute-start.29 = (bf16[128,512]{1,0:T(8,128)(2,1)S(1)}, bf16[128,512]{1,0:T(8,128)(2,1)S(1)}, u32[]{:S(2)}, u32[]{:S(2)}) collective-permute-start(bf16[128,512]{1,0:T(8,128)(2,1)S(1)} %get-tuple-element.76), channel_id=1, source_target_pairs={{0,1},{1,0},{2,3},{3,2},{4,5},{5,4},{6,7},{7,6},{8,9},{9,8},{10,11... | collective-permute-start | bytes 393224 | tf_op jit(solution)/shard_map/ppermute | solution.py:33
  66.9 3.8 %shard_map.93 = (bf16[128,512]{1,0:T(8,128)(2,1)S(1)}, bf16[128,512]{1,0:T(8,128)(2,1)S(1)}) custom-call(s32[4]{0:T(128)S(1)} %pad_add_fusion.ids, f32[1]{0:T(128)S(6)} %copy.11.rate, bf16[4,48,512]{2,1,0:T(8,128)(2,1)S(1)} %shard_map.91.mine, bf16[4,48,512]{2,1,0:T(8,128)(2,1)S(1)} %collective-permute-done.22.side_in, ...), custom_call_target="tpu_custom_call" | custom-call | flops 3000000000 | bytes 4000000 | tf_op jit(solution)/shard_map/pallas_call | solution.py:476
  70.7 0.8 collective-permute-start.28
  71.5 1.4 %shard_map.94.refs_0_ = bf16[2,128,1024]{2,1,0:T(8,128)(2,1)} custom-call(s32[4]{0:T(128)S(1)} %pad_add_fusion.ids, bf16[128,512]{1,0:T(8,128)(2,1)S(1)} %get-tuple-element.75.own, bf16[128,512]{1,0:T(8,128)(2,1)S(1)} %collective-permute-done.29.got, f32[1,1024]{1,0:T(1,128)S(1)} %bitcast.7), custom_call_target="tpu_custom_call" | custom-call | bytes 524288 | tf_op jit(solution)/shard_map/pallas_call | solution.py:331
  72.9 3.5 %collective-permute-done.28.got = bf16[128,512]{1,0:T(8,128)(2,1)S(1)} collective-permute-done((bf16[128,512]{1,0:T(8,128)(2,1)S(1)}, bf16[128,512]{1,0:T(8,128)(2,1)S(1)}, u32[]{:S(2)}, u32[]{:S(2)}) %collective-permute-start.28) | collective-permute-done | bytes 131104 | tf_op jit(solution)/shard_map/ppermute | solution.py:33
  76.4 1.4 %shard_map.95 = bf16[2,128,1024]{2,1,0:T(8,128)(2,1)} custom-call(s32[4]{0:T(128)S(1)} %pad_add_fusion.ids, bf16[128,512]{1,0:T(8,128)(2,1)S(1)} %get-tuple-element.73.own, bf16[128,512]{1,0:T(8,128)(2,1)S(1)} %collective-permute-done.28.got, f32[1,1024]{1,0:T(1,128)S(1)} %bitcast.8, ...), custom_call_target="tpu_custom_call", output_to_operand_aliasing={{}: (4, {})} | custom-call | bytes 524288 | tf_op jit(solution)/shard_map/pallas_call | solution.py:331
  (25 shorter events, 0.1 us)
Async XLA Ops:
  0.0 18.7 %collective-permute-start.7 = (bf16[2,256,512]{2,1,0:T(8,128)(2,1)}, bf16[2,256,512]{2,1,0:T(8,128)(2,1)S(1)}, u32[]{:S(2)}, u32[]{:S(2)}) collective-permute-start(bf16[2,256,512]{2,1,0:T(8,128)(2,1)} %keys.1), channel_id=1, source_target_pairs={{0,2},{2,0},{4,6},{6,4},{8,10},{10,8},{12,14},{14,12},{16,18},{18,... | collective-permute-start | bytes 1572872 | tf_op jit(solution)/shard_map/ppermute | solution.py:33
  0.5 18.2 %collective-permute-start.8 = (bf16[2,256,512]{2,1,0:T(8,128)(2,1)}, bf16[2,256,512]{2,1,0:T(8,128)(2,1)S(1)}, u32[]{:S(2)}, u32[]{:S(2)}) collective-permute-start(bf16[2,256,512]{2,1,0:T(8,128)(2,1)} %values.1), channel_id=1, source_target_pairs={{0,2},{2,0},{4,6},{6,4},{8,10},{10,8},{12,14},{14,12},{16,18},{18,... | collective-permute-start | bytes 1572872 | tf_op jit(solution)/shard_map/ppermute | solution.py:33
  0.5 5.4 %collective-permute-start = (bf16[32,768]{1,0:T(8,128)(2,1)}, bf16[32,768]{1,0:T(8,128)(2,1)S(1)}, u32[]{:S(2)}, u32[]{:S(2)}) collective-permute-start(bf16[32,768]{1,0:T(8,128)(2,1)} %bitcast.11), channel_id=1, source_target_pairs={{0,2},{2,0},{4,6},{6,4},{8,10},{10,8},{12,14},{14,12},{16,18},{18,... | collective-permute-start | bytes 147464 | tf_op jit(solution)/shard_map/ppermute | solution.py:33
  1.0 6.2 %collective-permute-start.2 = (bf16[32,768]{1,0:T(8,128)(2,1)}, bf16[32,768]{1,0:T(8,128)(2,1)S(1)}, u32[]{:S(2)}, u32[]{:S(2)}) collective-permute-start(bf16[32,768]{1,0:T(8,128)(2,1)} %bitcast.12), channel_id=1, source_target_pairs={{0,16},{2,18},{4,20},{6,22},{8,24},{10,26},{12,28},{14,30},{16,0},... | collective-permute-start | bytes 147464 | tf_op jit(solution)/shard_map/ppermute | solution.py:33
  4.6 6.4 %collective-permute-start.3 = (bf16[32,768]{1,0:T(8,128)(2,1)}, bf16[32,768]{1,0:T(8,128)(2,1)S(1)}, u32[]{:S(2)}, u32[]{:S(2)}) collective-permute-start(bf16[32,768]{1,0:T(8,128)(2,1)} %bitcast.13), channel_id=1, source_target_pairs={{0,24},{2,26},{4,28},{6,30},{8,16},{10,18},{12,20},{14,22},{16,8},... | collective-permute-start | bytes 147464 | tf_op jit(solution)/shard_map/ppermute | solution.py:33
  5.9 5.2 %collective-permute-start.1 = (bf16[32,768]{1,0:T(8,128)(2,1)}, bf16[32,768]{1,0:T(8,128)(2,1)S(1)}, u32[]{:S(2)}, u32[]{:S(2)}) collective-permute-start(bf16[32,768]{1,0:T(8,128)(2,1)} %bitcast.14), channel_id=1, source_target_pairs={{0,8},{2,10},{4,12},{6,14},{8,0},{10,2},{12,4},{14,6},{16,24},{18,... | collective-permute-start | bytes 147464 | tf_op jit(solution)/shard_map/ppermute | solution.py:33
  11.1 5.7 %collective-permute-start.4 = (bf16[4,32,768]{2,1,0:T(8,128)(2,1)S(1)}, bf16[4,32,768]{2,1,0:T(8,128)(2,1)S(1)}, u32[]{:S(2)}, u32[]{:S(2)}) collective-permute-start(bf16[4,32,768]{2,1,0:T(8,128)(2,1)S(1)} %shard_map.82.mine), channel_id=1, source_target_pairs={{0,4},{2,6},{4,0},{6,2},{8,12},{10,14},{12,8},{14,10},{16,20},{18,... | collective-permute-start | bytes 589832 | tf_op jit(solution)/shard_map/ppermute | solution.py:33
  12.6 15.1 %collective-permute-start.15 = (bf16[2,256,512]{2,1,0:T(8,128)(2,1)}, bf16[2,256,512]{2,1,0:T(8,128)(2,1)S(1)}, u32[]{:S(2)}, u32[]{:S(2)}) collective-permute-start(bf16[2,256,512]{2,1,0:T(8,128)(2,1)} %keys.1), channel_id=1, source_target_pairs={{0,8},{2,10},{4,12},{6,14},{8,16},{10,18},{12,20},{14,22},{16,24},... | collective-permute-start | bytes 1572872 | tf_op jit(solution)/shard_map/ppermute | solution.py:358
  12.8 4.0 %collective-permute-start.9 = (f32[1,256]{1,0:T(1,128)}, f32[1,256]{1,0:T(1,128)S(1)}, u32[]{:S(2)}, u32[]{:S(2)}) collective-permute-start(f32[1,256]{1,0:T(1,128)} %bitcast.9), channel_id=1, source_target_pairs={{0,2},{2,0},{4,6},{6,4},{8,10},{10,8},{12,14},{14,12},{16,18},{18,... | collective-permute-start | bytes 3080 | tf_op jit(solution)/shard_map/ppermute | solution.py:33
  12.8 1.1 %copy-start = (bf16[2,256,512]{2,1,0:T(8,128)(2,1)S(1)}, bf16[2,256,512]{2,1,0:T(8,128)(2,1)}, u32[]{:S(2)}) copy-start(bf16[2,256,512]{2,1,0:T(8,128)(2,1)} %keys.1) | copy-start | bytes 1572868
  13.9 1.0 %copy-start.1 = (bf16[2,256,512]{2,1,0:T(8,128)(2,1)S(1)}, bf16[2,256,512]{2,1,0:T(8,128)(2,1)}, u32[]{:S(2)}) copy-start(bf16[2,256,512]{2,1,0:T(8,128)(2,1)} %values.1) | copy-start | bytes 1572868
  15.0 0.7 copy-start.4
  15.7 6.7 %copy-start.2 = (bf16[2,256,512]{2,1,0:T(8,128)(2,1)S(1)}, bf16[2,256,512]{2,1,0:T(8,128)(2,1)}, u32[]{:S(2)}) copy-start(bf16[2,256,512]{2,1,0:T(8,128)(2,1)} %values.1) | copy-start | bytes 1572868
  16.8 1.6 %collective-permute-start.5 = (bf16[4,32,768]{2,1,0:T(8,128)(2,1)S(1)}, bf16[4,32,768]{2,1,0:T(8,128)(2,1)}, u32[]{:S(2)}, u32[]{:S(2)}) collective-permute-start(bf16[4,32,768]{2,1,0:T(8,128)(2,1)S(1)} %shard_map.82.mine), channel_id=1, source_target_pairs={{0,2},{2,0},{4,6},{6,4},{8,10},{10,8},{12,14},{14,12},{16,18},{18,... | collective-permute-start | bytes 589832 | tf_op jit(solution)/shard_map/ppermute | solution.py:33
  16.8 1.8 %collective-permute-start.6 = (bf16[4,32,768]{2,1,0:T(8,128)(2,1)S(1)}, bf16[4,32,768]{2,1,0:T(8,128)(2,1)}, u32[]{:S(2)}, u32[]{:S(2)}) collective-permute-start(bf16[4,32,768]{2,1,0:T(8,128)(2,1)S(1)} %collective-permute-done.4.other), channel_id=1, source_target_pairs={{0,2},{2,0},{4,6},{6,4},{8,10},{10,8},{12,14},{14,12},{16,18},{18,... | collective-permute-start | bytes 589832 | tf_op jit(solution)/shard_map/ppermute | solution.py:33
  20.9 7.1 %collective-permute-start.10 = (bf16[192,512]{1,0:T(8,128)(2,1)S(1)}, bf16[192,512]{1,0:T(8,128)(2,1)S(1)}, u32[]{:S(2)}, u32[]{:S(2)}) collective-permute-start(bf16[192,512]{1,0:T(8,128)(2,1)S(1)} %get-tuple-element.50), channel_id=1, source_target_pairs={{0,4},{2,6},{4,0},{6,2},{8,12},{10,14},{12,8},{14,10},{16,20},{18,... | collective-permute-start | bytes 589832 | tf_op jit(solution)/shard_map/ppermute | solution.py:33
  22.4 16.8 %collective-permute-start.11 = (bf16[2,256,512]{2,1,0:T(8,128)(2,1)S(1)}, bf16[2,256,512]{2,1,0:T(8,128)(2,1)S(1)}, u32[]{:S(2)}, u32[]{:S(2)}) collective-permute-start(bf16[2,256,512]{2,1,0:T(8,128)(2,1)S(1)} %copy-done.2), channel_id=1, source_target_pairs={{0,8},{2,10},{4,12},{6,14},{8,16},{10,18},{12,20},{14,22},{16,24},... | collective-permute-start | bytes 1572872 | tf_op jit(solution)/shard_map/ppermute | solution.py:358
  28.6 14.3 %collective-permute-start.16 = (bf16[2,256,512]{2,1,0:T(8,128)(2,1)S(1)}, bf16[2,256,512]{2,1,0:T(8,128)(2,1)S(1)}, u32[]{:S(2)}, u32[]{:S(2)}) collective-permute-start(bf16[2,256,512]{2,1,0:T(8,128)(2,1)S(1)} %shard_map.89), channel_id=1, source_target_pairs={{0,4},{2,6},{4,0},{6,2},{8,12},{10,14},{12,8},{14,10},{16,20},{18,... | collective-permute-start | bytes 1572872 | tf_op jit(solution)/shard_map/ppermute | solution.py:33
  30.1 18.2 %copy-start.5 = (bf16[2,256,512]{2,1,0:T(8,128)(2,1)S(1)}, bf16[2,256,512]{2,1,0:T(8,128)(2,1)}, u32[]{:S(2)}) copy-start(bf16[2,256,512]{2,1,0:T(8,128)(2,1)} %q.1) | copy-start | bytes 1572868
  31.7 9.4 %collective-permute-start.12 = (bf16[48,512]{1,0:T(8,128)(2,1)S(1)}, bf16[48,512]{1,0:T(8,128)(2,1)S(1)}, u32[]{:S(2)}, u32[]{:S(2)}) collective-permute-start(bf16[48,512]{1,0:T(8,128)(2,1)S(1)} %get-tuple-element.55), channel_id=1, source_target_pairs={{0,8},{2,10},{4,12},{6,14},{8,0},{10,2},{12,4},{14,6},{16,24},{18,... | collective-permute-start | bytes 147464 | tf_op jit(solution)/shard_map/ppermute | solution.py:33
  33.1 8.4 %collective-permute-start.13 = (bf16[48,512]{1,0:T(8,128)(2,1)S(1)}, bf16[48,512]{1,0:T(8,128)(2,1)S(1)}, u32[]{:S(2)}, u32[]{:S(2)}) collective-permute-start(bf16[48,512]{1,0:T(8,128)(2,1)S(1)} %get-tuple-element.56), channel_id=1, source_target_pairs={{0,16},{2,18},{4,20},{6,22},{8,24},{10,26},{12,28},{14,30},{16,0},... | collective-permute-start | bytes 147464 | tf_op jit(solution)/shard_map/ppermute | solution.py:33
  36.3 5.9 %collective-permute-start.14 = (bf16[48,512]{1,0:T(8,128)(2,1)S(1)}, bf16[48,512]{1,0:T(8,128)(2,1)S(1)}, u32[]{:S(2)}, u32[]{:S(2)}) collective-permute-start(bf16[48,512]{1,0:T(8,128)(2,1)S(1)} %get-tuple-element.57), channel_id=1, source_target_pairs={{0,24},{2,26},{4,28},{6,30},{8,16},{10,18},{12,20},{14,22},{16,8},... | collective-permute-start | bytes 147464 | tf_op jit(solution)/shard_map/ppermute | solution.py:33
  42.8 17.2 %copy-start.6 = (bf16[2,256,512]{2,1,0:T(8,128)(2,1)S(1)}, bf16[2,256,512]{2,1,0:T(8,128)(2,1)}, u32[]{:S(2)}) copy-start(bf16[2,256,512]{2,1,0:T(8,128)(2,1)} %gates.1) | copy-start | bytes 1572868
  42.8 5.1 %collective-permute-start.17 = (bf16[2,256,512]{2,1,0:T(8,128)(2,1)S(1)}, bf16[2,256,512]{2,1,0:T(8,128)(2,1)S(1)}, u32[]{:S(2)}, u32[]{:S(2)}) collective-permute-start(bf16[2,256,512]{2,1,0:T(8,128)(2,1)S(1)} %collective-permute-done.15.far.refs_1_), channel_id=1, source_target_pairs={{0,2},{2,0},{4,6},{6,4},{8,10},{10,8},{12,14},{14,12},{16,18},{18,... | collective-permute-start | bytes 1572872 | tf_op jit(solution)/shard_map/ppermute | solution.py:33
  42.9 5.0 %collective-permute-start.18 = (bf16[2,256,512]{2,1,0:T(8,128)(2,1)S(1)}, bf16[2,256,512]{2,1,0:T(8,128)(2,1)S(1)}, u32[]{:S(2)}, u32[]{:S(2)}) collective-permute-start(bf16[2,256,512]{2,1,0:T(8,128)(2,1)S(1)} %collective-permute-done.16.refs_2_), channel_id=1, source_target_pairs={{0,2},{2,0},{4,6},{6,4},{8,10},{10,8},{12,14},{14,12},{16,18},{18,... | collective-permute-start | bytes 1572872 | tf_op jit(solution)/shard_map/ppermute | solution.py:33
  43.4 13.9 %collective-permute-start.24 = (bf16[2,256,512]{2,1,0:T(8,128)(2,1)S(1)}, bf16[2,256,512]{2,1,0:T(8,128)(2,1)S(1)}, u32[]{:S(2)}, u32[]{:S(2)}) collective-permute-start(bf16[2,256,512]{2,1,0:T(8,128)(2,1)S(1)} %shard_map.87), channel_id=1, source_target_pairs={{0,4},{2,6},{4,0},{6,2},{8,12},{10,14},{12,8},{14,10},{16,20},{18,... | collective-permute-start | bytes 1572872 | tf_op jit(solution)/shard_map/ppermute | solution.py:33
  43.9 6.4 %collective-permute-start.19 = (bf16[48,512]{1,0:T(8,128)(2,1)S(1)}, bf16[48,512]{1,0:T(8,128)(2,1)S(1)}, u32[]{:S(2)}, u32[]{:S(2)}) collective-permute-start(bf16[48,512]{1,0:T(8,128)(2,1)S(1)} %shard_map.88.refs_0_), channel_id=1, source_target_pairs={{0,8},{2,10},{4,12},{6,14},{8,0},{10,2},{12,4},{14,6},{16,24},{18,... | collective-permute-start | bytes 147464 | tf_op jit(solution)/shard_map/ppermute | solution.py:33
  45.2 6.0 %collective-permute-start.20 = (bf16[48,512]{1,0:T(8,128)(2,1)S(1)}, bf16[48,512]{1,0:T(8,128)(2,1)S(1)}, u32[]{:S(2)}, u32[]{:S(2)}) collective-permute-start(bf16[48,512]{1,0:T(8,128)(2,1)S(1)} %shard_map.88.refs_0_), channel_id=1, source_target_pairs={{0,16},{2,18},{4,20},{6,22},{8,24},{10,26},{12,28},{14,30},{16,0},... | collective-permute-start | bytes 147464 | tf_op jit(solution)/shard_map/ppermute | solution.py:33
  47.9 5.9 %collective-permute-start.21 = (bf16[48,512]{1,0:T(8,128)(2,1)S(1)}, bf16[48,512]{1,0:T(8,128)(2,1)S(1)}, u32[]{:S(2)}, u32[]{:S(2)}) collective-permute-start(bf16[48,512]{1,0:T(8,128)(2,1)S(1)} %shard_map.88.refs_0_), channel_id=1, source_target_pairs={{0,24},{2,26},{4,28},{6,30},{8,16},{10,18},{12,20},{14,22},{16,8},... | collective-permute-start | bytes 147464 | tf_op jit(solution)/shard_map/ppermute | solution.py:33
  57.3 1.9 %collective-permute-start.26 = (bf16[2,256,512]{2,1,0:T(8,128)(2,1)S(1)}, bf16[2,256,512]{2,1,0:T(8,128)(2,1)S(1)}, u32[]{:S(2)}, u32[]{:S(2)}) collective-permute-start(bf16[2,256,512]{2,1,0:T(8,128)(2,1)S(1)} %collective-permute-done.24.refs_2_), channel_id=1, source_target_pairs={{0,2},{2,0},{4,6},{6,4},{8,10},{10,8},{12,14},{14,12},{16,18},{18,... | collective-permute-start | bytes 1572872 | tf_op jit(solution)/shard_map/ppermute | solution.py:33
  57.3 2.7 %collective-permute-start.25 = (bf16[2,256,512]{2,1,0:T(8,128)(2,1)S(1)}, bf16[2,256,512]{2,1,0:T(8,128)(2,1)S(1)}, u32[]{:S(2)}, u32[]{:S(2)}) collective-permute-start(bf16[2,256,512]{2,1,0:T(8,128)(2,1)S(1)} %collective-permute-done.11.far.refs_1_), channel_id=1, source_target_pairs={{0,2},{2,0},{4,6},{6,4},{8,10},{10,8},{12,14},{14,12},{16,18},{18,... | collective-permute-start | bytes 1572872 | tf_op jit(solution)/shard_map/ppermute | solution.py:33
  57.8 6.8 %collective-permute-start.22 = (bf16[4,48,512]{2,1,0:T(8,128)(2,1)S(1)}, bf16[4,48,512]{2,1,0:T(8,128)(2,1)S(1)}, u32[]{:S(2)}, u32[]{:S(2)}) collective-permute-start(bf16[4,48,512]{2,1,0:T(8,128)(2,1)S(1)} %shard_map.91.mine), channel_id=1, source_target_pairs={{0,4},{2,6},{4,0},{6,2},{8,12},{10,14},{12,8},{14,10},{16,20},{18,... | collective-permute-start | bytes 589832 | tf_op jit(solution)/shard_map/ppermute | solution.py:33
  58.4 8.5 %collective-permute-start.23 = (bf16[4,48,512]{2,1,0:T(8,128)(2,1)S(1)}, bf16[4,48,512]{2,1,0:T(8,128)(2,1)S(1)}, u32[]{:S(2)}, u32[]{:S(2)}) collective-permute-start(bf16[4,48,512]{2,1,0:T(8,128)(2,1)S(1)} %shard_map.91.mine), channel_id=1, source_target_pairs={{0,2},{2,0},{4,6},{6,4},{8,10},{10,8},{12,14},{14,12},{16,18},{18,... | collective-permute-start | bytes 589832 | tf_op jit(solution)/shard_map/ppermute | solution.py:33
  64.6 2.2 %collective-permute-start.27 = (bf16[4,48,512]{2,1,0:T(8,128)(2,1)S(1)}, bf16[4,48,512]{2,1,0:T(8,128)(2,1)S(1)}, u32[]{:S(2)}, u32[]{:S(2)}) collective-permute-start(bf16[4,48,512]{2,1,0:T(8,128)(2,1)S(1)} %collective-permute-done.22.side_in), channel_id=1, source_target_pairs={{0,2},{2,0},{4,6},{6,4},{8,10},{10,8},{12,14},{14,12},{16,18},{18,... | collective-permute-start | bytes 589832 | tf_op jit(solution)/shard_map/ppermute | solution.py:33
  65.3 6.2 %collective-permute-start.29 = (bf16[128,512]{1,0:T(8,128)(2,1)S(1)}, bf16[128,512]{1,0:T(8,128)(2,1)S(1)}, u32[]{:S(2)}, u32[]{:S(2)}) collective-permute-start(bf16[128,512]{1,0:T(8,128)(2,1)S(1)} %get-tuple-element.76), channel_id=1, source_target_pairs={{0,1},{1,0},{2,3},{3,2},{4,5},{5,4},{6,7},{7,6},{8,9},{9,8},{10,11... | collective-permute-start | bytes 393224 | tf_op jit(solution)/shard_map/ppermute | solution.py:33
  66.9 4.6 %copy-start.3 = (f32[1024]{0:T(1024)S(1)}, f32[1024]{0:T(1024)}, u32[]{:S(2)}) copy-start(f32[1024]{0:T(1024)} %param.15) | copy-start | bytes 12292
  70.7 5.7 %collective-permute-start.28 = (bf16[128,512]{1,0:T(8,128)(2,1)S(1)}, bf16[128,512]{1,0:T(8,128)(2,1)S(1)}, u32[]{:S(2)}, u32[]{:S(2)}) collective-permute-start(bf16[128,512]{1,0:T(8,128)(2,1)S(1)} %get-tuple-element.74), channel_id=1, source_target_pairs={{0,1},{1,0},{2,3},{3,2},{4,5},{5,4},{6,7},{7,6},{8,9},{9,8},{10,11... | collective-permute-start | bytes 393224 | tf_op jit(solution)/shard_map/ppermute | solution.py:33

commit v6 on v5

--- a/solution.py
+++ b/solution.py
@@ -33,6 +33,11 @@
     return lax.ppermute(value, axis, [(i, i ^ mask) for i in range(count)])
 
 
+def place():
+    position = lax.axis_index("ctx")
+    return position >> 2, (position >> 1) & 1, position & 1, lax.axis_index("head")
+
+
 def vmem_spec():
     return pl.BlockSpec(memory_space=pltpu.VMEM)
 
@@ -41,7 +46,7 @@
     return pl.pallas_call(
         body,
         out_shape=outs,
-        in_specs=[pl.BlockSpec(memory_space=pltpu.SMEM)] + [vmem_spec()] * (len(args) - 1),
+        in_specs=[vmem_spec()] * len(args),
         out_specs=jax.tree.map(lambda _: vmem_spec(), outs),
         scratch_shapes=list(scratch),
         compiler_params=pltpu.CompilerParams(vmem_limit_bytes=VMEM_LIMIT),
@@ -53,40 +58,35 @@
     return pl.CostEstimate(flops=int(flops), bytes_accessed=int(moved), transcendentals=0)
 
 
+def sigmoid(v):
+    return 0.5 * jnp.tanh(0.5 * v) + 0.5
+
+
 def silu(v):
-    return v / (1.0 + jnp.exp(-v))
-
-
-def hold_body(keys, values, rates, held_keys, held_values, held_rates):
+    return v * sigmoid(v)
+
+
+def hold_body(keys, values, rates, rate, held_keys, held_values, held_rates, held_rate):
     held_keys[...] = keys[...]
     held_values[...] = values[...]
     held_rates[...] = rates[...]
-
-
-def held(keys, values, rates):
-    def block(a):
-        return pl.BlockSpec((1,) + a.shape[1:], lambda i: (i, 0, 0))
-
-    specs = (block(keys), block(values), pl.BlockSpec(rates.shape, lambda i: (0, 0)))
-    return pl.pallas_call(
-        hold_body,
-        grid=(2,),
-        out_shape=tuple(jax.ShapeDtypeStruct(a.shape, a.dtype) for a in (keys, values, rates)),
-        in_specs=list(specs),
-        out_specs=specs,
-        compiler_params=pltpu.CompilerParams(vmem_limit_bytes=VMEM_LIMIT),
-        cost_estimate=cost_of(0, keys.size * 8),
-    )(keys, values, rates)
-
-
-def pick_body(ids, own, far, out):
-    out[...] = jnp.where(ids[1] == 0, own[...], far[...])
-
-
-def picked(ids, own, far):
+    held_rate[...] = jnp.broadcast_to(rate[...], held_rate.shape)
+
+
+def held(keys, values, rates, rate):
+    outs = tuple(jax.ShapeDtypeStruct(a.shape, a.dtype) for a in (keys, values, rates))
+    outs += (jax.ShapeDtypeStruct((8, 128), rate.dtype),)
+    return call(hold_body, (keys, values, rates, rate), outs)
+
+
+def pick_body(own, far, out):
+    out[...] = jnp.where(place()[1] == 0, own[...], far[...])
+
+
+def picked(own, far):
     return call(
         pick_body,
-        (ids, own, far),
+        (own, far),
         jax.ShapeDtypeStruct(own.shape, own.dtype),
         cost=cost_of(0, own.size * 4),
     )
@@ -108,10 +108,10 @@
     )(*pieces)
 
 
-def gradient_body(planes, ids, mine, other, beside_mine, beside_other, *refs):
+def gradient_body(planes, mine, other, beside_mine, beside_other, *refs):
     (keys, values, rates, keys_in, values_in, rates_in), refs = refs[:6], refs[6:]
     send, keep, whole, total = refs[:4]
-    plane, side, core = ids[0], ids[1], ids[2]
+    plane, side, core, _ = place()
     rows = mine.shape[1]
     target_ref = refs[4] if len(refs) > 4 else whole
     for m in range(planes):
@@ -138,7 +138,7 @@
         gate_up = dot_nn(key_rows, gate_up_w)
         g, u = gate_up[:, :half], gate_up[:, half:]
         dh = dot_nn(target, out_w)
-        s = 1.0 / (1.0 + jnp.exp(-g))
+        s = sigmoid(g)
         gs = g * s
         hidden = (gs * u).astype(BF)
         dg = dh * u * s * (1.0 + g * (1.0 - s))
@@ -156,9 +156,9 @@
     keep[...] = total[pl.ds(pl.multiple_of(side * part, part), part), :]
 
 
-def side_sum_body(planes, ids, keep, got, *refs):
+def side_sum_body(planes, keep, got, *refs):
     outs, total = refs[:planes], refs[planes]
-    plane = ids[0]
+    plane = place()[0]
     total[...] = keep[...] + got[...].astype(F32)
     part = outs[0].shape[0]
     for m in range(planes):
@@ -166,14 +166,14 @@
         outs[m][...] = rows.astype(outs[m].dtype)
 
 
-def plane_sum_body(ids, own, *refs):
+def plane_sum_body(own, *refs):
     total = own[...]
     for ref in refs[:-1]:
         total = total + ref[...].astype(F32)
     refs[-1][...] = total.astype(BF)
 
 
-def weights_body(ids, whole, flipped, norms):
+def weights_body(whole, flipped, norms):
     width = whole.shape[1] // 3
     for b in range(3):
         cols = slice(b * width, (b + 1) * width)
@@ -182,8 +182,8 @@
         norms[cols, :] = jnp.sqrt(jnp.sum(turned * turned, 1, keepdims=True))
 
 
-def blocks_of(ids, group, own, far, near, beside, far_beside, diag):
-    plane, side, core = ids[0], ids[1], ids[2]
+def blocks_of(group, own, far, near, beside, far_beside, diag):
+    plane, side, core, _ = place()
     moved = group if group == 0 else jnp.where(plane == 0, 0, group)
     crossed = group if group == 0 else jnp.where((plane == 0) & (side == 0), 0, group)
     return [
@@ -195,9 +195,9 @@
     ]
 
 
-def scores_body(ids, queries, *refs):
-    key_refs, whole, (weights, totals, fast) = refs[:6], refs[6], refs[7:]
-    plane, side, core = ids[0], ids[1], ids[2]
+def scores_body(queries, *refs):
+    key_refs, whole, (weights, inverses, fast) = refs[:6], refs[6], refs[7:]
+    plane, side, core, _ = place()
     later = (plane > 0).astype(jnp.int32)
     side_live, core_live = jnp.maximum(later, side), jnp.maximum(later, core)
     rows, depth = queries.shape[1:]
@@ -208,7 +208,7 @@
         q = queries[group]
         scores = []
         lives = [None, later, side_live, core_live, side_live]
-        for slot, keys in enumerate(blocks_of(ids, group, *key_refs)):
+        for slot, keys in enumerate(blocks_of(group, *key_refs)):
             s = dot_nt(q, keys) * scale
             allowed = {0: col <= row, 1: col > row}.get(slot)
             if group == 0 and slot:
@@ -224,42 +224,43 @@
             t = jnp.sum(e, -1, keepdims=True)
             total = t if total is None else total + t
             weights[group, slot] = e.astype(BF)
-        totals[group] = total
+        inverses[group] = 1.0 / total
     width = whole.shape[1] // 3
     gate_up = dot_nn(queries[0], whole[:, : 2 * width])
     hidden = (silu(gate_up[:, :width]) * gate_up[:, width:]).astype(BF)
     fast[...] = dot_nt(hidden, whole[:, 2 * width :])
 
 
-def mix_body(ids, *refs):
-    value_refs, (weights, totals, fast, gates), refs = refs[:6], refs[6:10], refs[10:]
-    win, outs, gated = refs[0], refs[1:-1], refs[-1]
-    for group in range(2):
-        out = None
-        for slot, values in enumerate(blocks_of(ids, group, *value_refs)):
-            o = dot_nn(weights[group, slot], values)
-            out = o if out is None else out + o
-        out = out / totals[group]
-        if group == 0:
-            gate = gates[0].astype(F32)
-            spread(ids, ((out + fast[...]) * silu(gate)).astype(BF), outs, gated)
-        else:
-            win[...] = out
-
-
-def spread(ids, value, outs, held):
+def mixed(group, value_refs, weights, inverses):
+    out = None
+    for slot, values in enumerate(blocks_of(group, *value_refs)):
+        o = dot_nn(weights[group, slot], values)
+        out = o if out is None else out + o
+    return out * inverses[group]
+
+
+def mix_body(*refs):
+    value_refs, (weights, inverses, fast, gates), refs = refs[:6], refs[6:10], refs[10:]
+    outs, gated = refs[:-1], refs[-1]
+    win = mixed(0, value_refs, weights, inverses)
+    gate = gates[0].astype(F32)
+    spread(((win + fast[...]) * silu(gate)).astype(BF), outs, gated)
+
+
+def spread(value, outs, held):
     if len(outs) == 1:
         outs[0][...] = value
         return
     held[...] = value
-    rows = outs[0].shape[0]
-    outs[0][...] = held[pl.ds(pl.multiple_of(ids[3] * rows, rows), rows), :]
-    outs[1][...] = held[pl.ds(pl.multiple_of((1 - ids[3]) * rows, rows), rows), :]
-
-
-def update_body(planes, ids, rate, mine, side_in, core_in, diag_in, flipped, norms, q, win, gates, *refs):
-    outs, (grads, gated) = refs[:-2], refs[-2:]
-    plane, side, core = ids[0], ids[1], ids[2]
+    rows, head = outs[0].shape[0], place()[3]
+    outs[0][...] = held[pl.ds(pl.multiple_of(head * rows, rows), rows), :]
+    outs[1][...] = held[pl.ds(pl.multiple_of((1 - head) * rows, rows), rows), :]
+
+
+def update_body(planes, rate, mine, side_in, core_in, diag_in, flipped, norms, *refs):
+    (queries, gates, weights, inverses), refs = refs[:4], refs[4:]
+    value_refs, outs, (grads, gated) = refs[:6], refs[6:-2], refs[-2:]
+    plane, side, core, _ = place()
     part = mine.shape[1]
     for m in range(planes):
         for far in range(2):
@@ -275,7 +276,7 @@
             [grads[0, b * half : (b + 1) * half, :], grads[1, b * half : (b + 1) * half, :]], 0
         ).astype(F32)
         length = jnp.sqrt(jnp.sum(block * block, keepdims=True))
-        turned.append((block / (length + 1e-06)).astype(BF))
+        turned.append((block * (1.0 / (length + 1e-06))).astype(BF))
     for _ in range(3):
         grams = [dot_nt(y, y) for y in turned]
         lows = [a.astype(BF) for a in grams]
@@ -287,21 +288,22 @@
     fresh = []
     for b in range(3):
         cols = slice(b * width, (b + 1) * width)
-        moved = flipped[cols, :] - rate[0] * turned[b].astype(F32)
+        moved = flipped[cols, :] - rate[:1, :1] * turned[b].astype(F32)
         length = jnp.sqrt(jnp.sum(moved * moved, 1, keepdims=True))
         fresh.append((moved * (norms[cols, :] / (length + 1e-06))).astype(BF))
-    x = q[...]
+    win = mixed(1, value_refs, weights, inverses)
+    x = queries[1]
     g = dot_nt(x, fresh[0])
     u = dot_nt(x, fresh[1])
     hidden = (silu(g) * u).astype(BF)
     fast = dot_nn(hidden, fresh[2])
-    gate = gates[...].astype(F32)
-    spread(ids, ((win[...] + fast) * silu(gate)).astype(BF), outs, gated)
-
-
-def norm_body(group, ids, own, got, gain, *refs):
+    gate = gates[1].astype(F32)
+    spread(((win + fast) * silu(gate)).astype(BF), outs, gated)
+
+
+def norm_body(group, own, got, gain, *refs):
     out, held, sems = refs[-3:]
-    head = ids[3]
+    head = place()[3]
     rows, depth = own.shape
     chunk = rows // 4
     copies = []
@@ -321,7 +323,7 @@
         copy.wait()
 
 
-def finished(ids, group, gated, norm_gain, before):
+def finished(group, gated, norm_gain, before):
     total = norm_gain.shape[0]
     if len(gated) == 2:
         own, away = gated
@@ -332,7 +334,6 @@
             functools.partial(norm_body, group),
             out_shape=jax.ShapeDtypeStruct((2, rows, total), BF),
             in_specs=[
-                pl.BlockSpec(memory_space=pltpu.SMEM),
                 vmem_spec(),
                 vmem_spec(),
                 vmem_spec(),
@@ -340,10 +341,10 @@
             ],
             out_specs=pl.BlockSpec(memory_space=pl.ANY),
             scratch_shapes=[pltpu.VMEM((rows, total), BF), pltpu.SemaphoreType.DMA((4,))],
-            input_output_aliases={4: 0} if earlier else {},
+            input_output_aliases={3: 0} if earlier else {},
             compiler_params=pltpu.CompilerParams(vmem_limit_bytes=VMEM_LIMIT),
             cost_estimate=cost_of(0, 4 * rows * total),
-        )(ids, own, got, norm_gain[None, :], *earlier)
+        )(own, got, norm_gain[None, :], *earlier)
     wide = lax.all_to_all(gated[0], "head", split_axis=0, concat_axis=1, tiled=True).astype(F32)
     inv = lax.rsqrt(jnp.mean(wide * wide, -1, keepdims=True) + 1e-06)
     done = (wide * inv * norm_gain).astype(BF)[None]
@@ -366,9 +367,6 @@
     planes = count // reach
     if reach != 4 or WIN % rows or planes * reach != count or planes & (planes - 1):
         raise ValueError("unsupported shapes")
-    position = lax.axis_index("ctx")
-    plane, side, core = position // 4, (position // 2) % 2, position % 2
-    ids = jnp.stack([plane, side, core, lax.axis_index("head")]).astype(jnp.int32)
     width = fast_init.shape[2] // 3
     half = width // 2
     everyone = range(count)
@@ -379,7 +377,7 @@
     keys_in, values_in, rates_in = (swapped(v, 1) for v in (keys, values, rates))
     mine_w = packed(local_in, *arrived)
     other_w = swapped(mine_w, 2)
-    own_keys, own_values, own_rates = held(keys, values, rates)
+    own_keys, own_values, own_rates, own_rate = held(keys, values, rates, fast_rate.reshape(1, 1))
     beside_w = [swapped(mine_w, 1), swapped(after(other_w, own_keys), 1)]
 
     pieces = 2 * planes
@@ -389,7 +387,7 @@
         scratch.append(pltpu.VMEM((depth, 3 * width), F32))
     send, keep, whole = call(
         functools.partial(gradient_body, planes),
-        (ids, mine_w, other_w, *beside_w)
+        (mine_w, other_w, *beside_w)
         + (own_keys, own_values, own_rates, keys_in, values_in, rates_in),
         (
             jax.ShapeDtypeStruct((planes * part, depth), BF),
@@ -403,7 +401,7 @@
 
     flipped, norms = call(
         weights_body,
-        (ids, whole),
+        (whole,),
         (
             jax.ShapeDtypeStruct((3 * width, depth), F32),
             jax.ShapeDtypeStruct((3 * width, 1), F32),
@@ -412,7 +410,7 @@
     )
     parts = call(
         functools.partial(side_sum_body, planes),
-        (ids, after(keep, flipped), got),
+        (keep, got),
         tuple(jax.ShapeDtypeStruct((part, depth), F32 if m == 0 else BF) for m in range(planes)),
         scratch=(pltpu.VMEM((planes * part, depth), F32),),
         cost=cost_of(0, planes * part * depth * 8),
@@ -421,13 +419,13 @@
     ring = [(i, (i + reach) % count) for i in everyone]
     far_keys = sent(after(keys, *arrived), ring)
     far_values = sent(after(values, send), ring)
-    near_keys = swapped(picked(ids, own_keys, after(far_keys, got)), 2)
-    pick_values = picked(ids, own_values, after(far_values, parts[0]))
-    near_values = swapped(after(pick_values, *partial), 2)
+    near_keys = swapped(picked(own_keys, after(far_keys, got)), 2)
+    pick_values = picked(own_values, after(far_values, parts[0]))
+    near_values = swapped(pick_values, 2)
 
     total = call(
         plane_sum_body,
-        (ids, after(parts[0], pick_values), *partial),
+        (after(parts[0], pick_values, flipped), *partial),
         jax.ShapeDtypeStruct((part, depth), BF),
         cost=cost_of(0, planes * part * depth * 3),
     )
@@ -443,10 +441,10 @@
         split = (jax.ShapeDtypeStruct((rows // 2, depth), BF),) * 2
     else:
         split = (jax.ShapeDtypeStruct((rows, depth), BF),)
-    attn_cost = cost_of(6 * rows * depth * 10 * rows, rows * depth * 40)
-    weights, totals, fast_first = call(
+    attn_cost = cost_of(1000, 1000)
+    weights, inverses, fast_first = call(
         scores_body,
-        (ids, queries, *all_keys, whole),
+        (queries, *all_keys, whole),
         (
             jax.ShapeDtypeStruct((2, reach + 1, rows, rows), BF),
             jax.ShapeDtypeStruct((2, rows, 1), F32),
@@ -454,48 +452,30 @@
         ),
         cost=attn_cost,
     )
-    plane_grad = packed(after(total, totals), *planes_grad)
+    plane_grad = packed(after(total, inverses), *planes_grad)
+    side_grad = swapped(plane_grad, 2)
     far_values_in = swapped(after(far_values, plane_grad), 1)
-    near_values_in = swapped(after(near_values, plane_grad), 1)
+    near_values_in = swapped(after(near_values, side_grad), 1)
     all_values = [own_values, far_values, near_values, values_in, far_values_in, near_values_in]
-    window_second, *gated_first = call(
+    gated_first = call(
         mix_body,
-        (ids, *all_values, weights, totals, fast_first, gates),
-        (jax.ShapeDtypeStruct((rows, depth), F32), *split),
+        (*all_values, weights, inverses, fast_first, gates),
+        split,
         scratch=(pltpu.VMEM((rows, depth), BF),),
         cost=attn_cost,
     )
-    side_grad = swapped(plane_grad, 2)
-    beside_grad = [swapped(plane_grad, 1), swapped(after(side_grad, window_second), 1)]
+    beside_grad = [swapped(plane_grad, 1), swapped(side_grad, 1)]
     grads = [plane_grad, side_grad, *beside_grad]
-    done = finished(ids, 0, gated_first, norm_gain, None)
-
-    def full(shape):
-        return pl.BlockSpec(shape, lambda i, nd=len(shape): (0,) * nd)
-
-    gated_second = pl.pallas_call(
+    done = finished(0, gated_first, norm_gain, None)
+
+    gated_second = call(
         functools.partial(update_body, planes),
-        grid=(1,),
-        out_shape=split,
-        in_specs=[
-            pl.BlockSpec(memory_space=pltpu.SMEM),
-            pl.BlockSpec(memory_space=pltpu.SMEM),
-            *[full(v.shape) for v in grads],
-            full(flipped.shape),
-            full(norms.shape),
-            pl.BlockSpec((None, rows, depth), lambda i: (1, 0, 0)),
-            full((rows, depth)),
-            pl.BlockSpec((None, rows, depth), lambda i: (1, 0, 0)),
-        ],
-        out_specs=tuple(full(s.shape) for s in split),
-        scratch_shapes=[
-            pltpu.VMEM((2, pieces * part, depth), BF),
-            pltpu.VMEM((rows, depth), BF),
-        ],
-        compiler_params=pltpu.CompilerParams(vmem_limit_bytes=VMEM_LIMIT),
-        cost_estimate=cost_of(3e9, 4e6),
-    )(ids, fast_rate, *grads, flipped, norms, queries, window_second, gates)
-    return finished(ids, 1, gated_second, norm_gain, done)
+        (own_rate, *grads, flipped, norms, queries, gates, weights, inverses, *all_values),
+        split,
+        scratch=(pltpu.VMEM((2, pieces * part, depth), BF), pltpu.VMEM((rows, depth), BF)),
+        cost=cost_of(3e9, 4e6),
+    )
+    return finished(1, gated_second, norm_gain, done)
 
 
 def solution(mesh):

time: 78.1 us -> 74.7 us (0.956)
  Pallas kernels: 15.7 us -> 10.1 us
  waiting for transfers between devices: 32 us -> 36.1 us
  local copies, waits for them, and re-layouts: 2.81 us -> 1.73 us
    ppermute x2, waiting for transfers between devices: 6.84 us -> 11.7 us  [sent(): return lax.ppermute(value, axis, pairs)]
    pallas_call x10, Pallas kernels: 12.9 us -> 8.44 us  [call(): pl.pallas_call(body, out_shape=outs, in_specs=[vmem_spec()] * len(args),...]
    unnamed x14 -> x10, local copies, waits for them, and re-layouts: 2.81 us -> 1.73 us
    pallas_call x2, Pallas kernels: 2.76 us -> 1.68 us  [finished(): pl.pallas_call(functools.partial(norm_body, group), out_shape=jax.ShapeDt...]
    ppermute x28, waiting for transfers between devices: 25.1 us -> 24.3 us  [swapped(): return lax.ppermute(value, axis, [(i, i ^ mask) for i in range(count)])]
  transfers between devices with their start and end apart: 30 -> 30, of which waited for: 19 -> 16; matrix products, arithmetic and copies ran while one was open for 0% -> 0% of each run, Pallas kernels for 18% -> 12%
where the time goes in v6:
time: 74.7 us; the launch traced here: 74.5 us
  waiting for transfers between devices  36.1 us (48%)
  starting transfers between devices  25.8 us (35%)
  Pallas kernels  10.1 us (14%)
  local copies, waits for them, and re-layouts  1.73 us (2%)
  between operations  0.78 us (1%)
    ppermute x28, waiting for transfers between devices, swapped(): return lax.ppermute(value, axis, [(i, i ^ mask) for i in range(count)])  24.3 us
    ppermute x28, starting transfers between devices, swapped(): return lax.ppermute(value, axis, [(i, i ^ mask) for i in range(count)])  24.2 us
    ppermute x2, waiting for transfers between devices, sent(): return lax.ppermute(value, axis, pairs)  11.7 us
    pallas_call x10, Pallas kernels, call(): pl.pallas_call(body, out_shape=outs, in_specs=[vmem_spec()] * len(args),...  8.44 us
    unnamed x10, local copies, waits for them, and re-layouts  1.73 us
    pallas_call x2, Pallas kernels, finished(): pl.pallas_call(functools.partial(norm_body, group), out_shape=jax.ShapeDt...  1.68 us
    ppermute x2, starting transfers between devices, sent(): return lax.ppermute(value, axis, pairs)  1.53 us
  transfers between devices with their start and end apart: 30, of which 16 were waited for; matrix products, arithmetic and copies ran while one was open for 0% of the time, Pallas kernels for 12%

profile of v6, /device:TPU:0, one launch (start us, length us, event | category | flops | bytes accessed | tf_op | source)
XLA Modules:
  0.0 74.5 jit_solution(15172042424624197477)
XLA Ops:
  0.0 0.5 collective-permute-start.7
  0.5 0.1 collective-permute-start.8
  0.5 0.5 collective-permute-start
  1.0 3.6 %collective-permute-start.2 = (bf16[32,768]{1,0:T(8,128)(2,1)}, bf16[32,768]{1,0:T(8,128)(2,1)S(1)}, u32[]{:S(2)}, u32[]{:S(2)}) collective-permute-start(bf16[32,768]{1,0:T(8,128)(2,1)} %bitcast.10), channel_id=1, source_target_pairs={{0,16},{2,18},{4,20},{6,22},{8,24},{10,26},{12,28},{14,30},{16,0},... | collective-permute-start | bytes 147464 | tf_op jit(solution)/shard_map/ppermute | solution.py:33
  4.6 1.3 %collective-permute-start.3 = (bf16[32,768]{1,0:T(8,128)(2,1)}, bf16[32,768]{1,0:T(8,128)(2,1)S(1)}, u32[]{:S(2)}, u32[]{:S(2)}) collective-permute-start(bf16[32,768]{1,0:T(8,128)(2,1)} %bitcast.11), channel_id=1, source_target_pairs={{0,24},{2,26},{4,28},{6,30},{8,16},{10,18},{12,20},{14,22},{16,8},... | collective-permute-start | bytes 147464 | tf_op jit(solution)/shard_map/ppermute | solution.py:33
  5.9 0.0 collective-permute-done.refs_0_
  5.9 0.2 collective-permute-start.1
  6.1 1.0 %collective-permute-done.2.refs_2_ = bf16[32,768]{1,0:T(8,128)(2,1)S(1)} collective-permute-done((bf16[32,768]{1,0:T(8,128)(2,1)}, bf16[32,768]{1,0:T(8,128)(2,1)S(1)}, u32[]{:S(2)}, u32[]{:S(2)}) %collective-permute-start.2) | collective-permute-done | bytes 49184 | tf_op jit(solution)/shard_map/ppermute | solution.py:33
  7.2 3.8 %collective-permute-done.3.refs_3_ = bf16[32,768]{1,0:T(8,128)(2,1)S(1)} collective-permute-done((bf16[32,768]{1,0:T(8,128)(2,1)}, bf16[32,768]{1,0:T(8,128)(2,1)S(1)}, u32[]{:S(2)}, u32[]{:S(2)}) %collective-permute-start.3) | collective-permute-done | bytes 49184 | tf_op jit(solution)/shard_map/ppermute | solution.py:33
  11.0 0.1 collective-permute-done.1.refs_1_
  11.1 1.6 %collective-permute-start.4 = (bf16[4,32,768]{2,1,0:T(8,128)(2,1)S(1)}, bf16[4,32,768]{2,1,0:T(8,128)(2,1)S(1)}, u32[]{:S(2)}, u32[]{:S(2)}) collective-permute-start(bf16[4,32,768]{2,1,0:T(8,128)(2,1)S(1)} %shard_map.83.mine), channel_id=1, source_target_pairs={{0,4},{2,6},{4,0},{6,2},{8,12},{10,14},{12,8},{14,10},{16,20},{18,... | collective-permute-start | bytes 589832 | tf_op jit(solution)/shard_map/ppermute | solution.py:33
  12.6 0.2 collective-permute-start.15
  13.5 1.0 %copy-done.1 = bf16[2,256,512]{2,1,0:T(8,128)(2,1)S(1)} copy-done((bf16[2,256,512]{2,1,0:T(8,128)(2,1)S(1)}, bf16[2,256,512]{2,1,0:T(8,128)(2,1)}, u32[]{:S(2)}) %copy-start.1) | copy-done | bytes 524312
  14.5 0.7 copy-done.4
  15.2 1.1 %shard_map.82 = (bf16[2,256,512]{2,1,0:T(8,128)(2,1)S(1)}, bf16[2,256,512]{2,1,0:T(8,128)(2,1)S(1)}, f32[1,256]{1,0:T(1,128)S(1)}, f32[8,128]{1,0:T(8,128)S(1)}) custom-call(bf16[2,256,512]{2,1,0:T(8,128)(2,1)S(1)} %copy-done.1, bf16[2,256,512]{2,1,0:T(8,128)(2,1)} %values.1, f32[1,256]{1,0:T(1,128)S(1)} %bitcast.8, f32[1,1]{1,0:T(1,128)} %bitcast.4.rate), custom_call_target="tpu_custom_call" | custom-call | tf_op jit(solution)/shard_map/pallas_call | solution.py:46
  16.3 0.5 collective-permute-done.4.other
  16.8 0.1 collective-permute-start.5
  16.9 0.4 collective-permute-start.6
  17.3 0.9 %collective-permute-done.5.beside_mine = bf16[4,32,768]{2,1,0:T(8,128)(2,1)S(1)} collective-permute-done((bf16[4,32,768]{2,1,0:T(8,128)(2,1)S(1)}, bf16[4,32,768]{2,1,0:T(8,128)(2,1)S(1)}, u32[]{:S(2)}, u32[]{:S(2)}) %collective-permute-start.5) | collective-permute-done | bytes 196640 | tf_op jit(solution)/shard_map/ppermute | solution.py:33
  18.3 0.3 collective-permute-done.6.beside_other
  18.5 0.0 collective-permute-done.8.refs_4_.refs_7_.refs_3_
  18.5 1.2 %shard_map.84 = (bf16[192,512]{1,0:T(8,128)(2,1)S(1)}, f32[192,512]{1,0:T(8,128)S(1)}, bf16[512,768]{1,0:T(8,128)(2,1)S(1)}) custom-call(bf16[4,32,768]{2,1,0:T(8,128)(2,1)S(1)} %shard_map.83.mine, bf16[4,32,768]{2,1,0:T(8,128)(2,1)S(1)} %collective-permute-done.4.other, bf16[4,32,768]{2,1,0:T(8,128)(2,1)S(1)} %collective-permute-done.5.beside_mine, ...), custom_call_target="tpu_custom_call" | custom-call | flops 402653184 | bytes 2097152 | tf_op jit(solution)/shard_map/pallas_call | solution.py:46
  19.7 1.6 %collective-permute-start.10 = (bf16[192,512]{1,0:T(8,128)(2,1)S(1)}, bf16[192,512]{1,0:T(8,128)(2,1)S(1)}, u32[]{:S(2)}, u32[]{:S(2)}) collective-permute-start(bf16[192,512]{1,0:T(8,128)(2,1)S(1)} %get-tuple-element.45), channel_id=1, source_target_pairs={{0,4},{2,6},{4,0},{6,2},{8,12},{10,14},{12,8},{14,10},{16,20},{18,... | collective-permute-start | bytes 589832 | tf_op jit(solution)/shard_map/ppermute | solution.py:33
  21.3 1.3 %collective-permute-start.11 = (bf16[2,256,512]{2,1,0:T(8,128)(2,1)}, bf16[2,256,512]{2,1,0:T(8,128)(2,1)S(1)}, u32[]{:S(2)}, u32[]{:S(2)}) collective-permute-start(bf16[2,256,512]{2,1,0:T(8,128)(2,1)} %values.1), channel_id=1, source_target_pairs={{0,8},{2,10},{4,12},{6,14},{8,16},{10,18},{12,20},{14,22},{16,24},... | collective-permute-start | bytes 1572872 | tf_op jit(solution)/shard_map/ppermute | solution.py:359
  22.6 6.0 %collective-permute-done.15.far.refs_1_ = bf16[2,256,512]{2,1,0:T(8,128)(2,1)S(1)} collective-permute-done((bf16[2,256,512]{2,1,0:T(8,128)(2,1)}, bf16[2,256,512]{2,1,0:T(8,128)(2,1)S(1)}, u32[]{:S(2)}, u32[]{:S(2)}) %collective-permute-start.15) | collective-permute-done | bytes 524320 | tf_op jit(solution)/shard_map/ppermute | solution.py:359
  28.6 0.0 collective-permute-done.10.got
  28.6 0.1 shard_map.89
  28.7 0.6 collective-permute-start.16
  29.3 0.1 shard_map.85
  29.4 0.6 collective-permute-start.12
  29.9 3.2 %collective-permute-start.13 = (bf16[48,512]{1,0:T(8,128)(2,1)S(1)}, bf16[48,512]{1,0:T(8,128)(2,1)S(1)}, u32[]{:S(2)}, u32[]{:S(2)}) collective-permute-start(bf16[48,512]{1,0:T(8,128)(2,1)S(1)} %get-tuple-element.53), channel_id=1, source_target_pairs={{0,16},{2,18},{4,20},{6,22},{8,24},{10,26},{12,28},{14,30},{16,0},... | collective-permute-start | bytes 147464 | tf_op jit(solution)/shard_map/ppermute | solution.py:33
  33.1 0.7 collective-permute-start.14
  33.8 0.4 shard_map.87
  34.3 5.7 %collective-permute-done.11.far.refs_5_.refs_1_ = bf16[2,256,512]{2,1,0:T(8,128)(2,1)S(1)} collective-permute-done((bf16[2,256,512]{2,1,0:T(8,128)(2,1)}, bf16[2,256,512]{2,1,0:T(8,128)(2,1)S(1)}, u32[]{:S(2)}, u32[]{:S(2)}) %collective-permute-start.11) | collective-permute-done | bytes 524320 | tf_op jit(solution)/shard_map/ppermute | solution.py:359
  40.0 0.1 shard_map.86
  40.0 1.3 %collective-permute-done.12.refs_0_ = bf16[48,512]{1,0:T(8,128)(2,1)S(1)} collective-permute-done((bf16[48,512]{1,0:T(8,128)(2,1)S(1)}, bf16[48,512]{1,0:T(8,128)(2,1)S(1)}, u32[]{:S(2)}, u32[]{:S(2)}) %collective-permute-start.12) | collective-permute-done | bytes 49184 | tf_op jit(solution)/shard_map/ppermute | solution.py:33
  41.3 0.7 collective-permute-done.13.refs_1_
  42.0 0.0 copy-start.2
  42.1 0.1 collective-permute-start.17
  42.1 0.0 collective-permute-done.16.refs_2_
  42.1 0.5 collective-permute-start.18
  42.6 0.5 collective-permute-start.25
  43.2 1.5 %collective-permute-start.19 = (bf16[48,512]{1,0:T(8,128)(2,1)S(1)}, bf16[48,512]{1,0:T(8,128)(2,1)S(1)}, u32[]{:S(2)}, u32[]{:S(2)}) collective-permute-start(bf16[48,512]{1,0:T(8,128)(2,1)S(1)} %shard_map.88.refs_0_), channel_id=1, source_target_pairs={{0,8},{2,10},{4,12},{6,14},{8,0},{10,2},{12,4},{14,6},{16,24},{18,... | collective-permute-start | bytes 147464 | tf_op jit(solution)/shard_map/ppermute | solution.py:33
  44.7 1.6 %collective-permute-start.20 = (bf16[48,512]{1,0:T(8,128)(2,1)S(1)}, bf16[48,512]{1,0:T(8,128)(2,1)S(1)}, u32[]{:S(2)}, u32[]{:S(2)}) collective-permute-start(bf16[48,512]{1,0:T(8,128)(2,1)S(1)} %shard_map.88.refs_0_), channel_id=1, source_target_pairs={{0,16},{2,18},{4,20},{6,22},{8,24},{10,26},{12,28},{14,30},{16,0},... | collective-permute-start | bytes 147464 | tf_op jit(solution)/shard_map/ppermute | solution.py:33
  46.3 0.0 collective-permute-done.17.refs_4_
  46.3 0.0 collective-permute-done.18.refs_5_
  46.3 1.3 %collective-permute-start.21 = (bf16[48,512]{1,0:T(8,128)(2,1)S(1)}, bf16[48,512]{1,0:T(8,128)(2,1)S(1)}, u32[]{:S(2)}, u32[]{:S(2)}) collective-permute-start(bf16[48,512]{1,0:T(8,128)(2,1)S(1)} %shard_map.88.refs_0_), channel_id=1, source_target_pairs={{0,24},{2,26},{4,28},{6,30},{8,16},{10,18},{12,20},{14,22},{16,8},... | collective-permute-start | bytes 147464 | tf_op jit(solution)/shard_map/ppermute | solution.py:33
  47.6 1.5 %shard_map.90 = (bf16[2,5,256,256]{3,2,1,0:T(8,128)(2,1)S(1)}, f32[2,256,1]{2,1,0:T(8,128)S(1)}, f32[256,512]{1,0:T(8,128)S(1)}) custom-call(bf16[2,256,512]{2,1,0:T(8,128)(2,1)S(1)} %copy-done, bf16[2,256,512]{2,1,0:T(8,128)(2,1)S(1)} %get-tuple-element.40.refs_0_.own, bf16[2,256,512]{2,1,0:T(8,128)(2,1)S(1)} %collective-permute-done.15.far.refs_1_, ...), custom_call_target="tpu_custom_call" | custom-call | flops 1000 | bytes 1000 | tf_op jit(solution)/shard_map/pallas_call | solution.py:46
  49.1 1.2 %collective-permute-done.20.refs_2_ = bf16[48,512]{1,0:T(8,128)(2,1)S(1)} collective-permute-done((bf16[48,512]{1,0:T(8,128)(2,1)S(1)}, bf16[48,512]{1,0:T(8,128)(2,1)S(1)}, u32[]{:S(2)}, u32[]{:S(2)}) %collective-permute-start.20) | collective-permute-done | bytes 49184 | tf_op jit(solution)/shard_map/ppermute | solution.py:33
  50.3 1.9 %collective-permute-done.21.refs_3_ = bf16[48,512]{1,0:T(8,128)(2,1)S(1)} collective-permute-done((bf16[48,512]{1,0:T(8,128)(2,1)S(1)}, bf16[48,512]{1,0:T(8,128)(2,1)S(1)}, u32[]{:S(2)}, u32[]{:S(2)}) %collective-permute-start.21) | collective-permute-done | bytes 49184 | tf_op jit(solution)/shard_map/ppermute | solution.py:33
  52.2 1.3 %collective-permute-start.22 = (bf16[4,48,512]{2,1,0:T(8,128)(2,1)S(1)}, bf16[4,48,512]{2,1,0:T(8,128)(2,1)S(1)}, u32[]{:S(2)}, u32[]{:S(2)}) collective-permute-start(bf16[4,48,512]{2,1,0:T(8,128)(2,1)S(1)} %shard_map.91.mine), channel_id=1, source_target_pairs={{0,4},{2,6},{4,0},{6,2},{8,12},{10,14},{12,8},{14,10},{16,20},{18,... | collective-permute-start | bytes 589832 | tf_op jit(solution)/shard_map/ppermute | solution.py:33
  53.4 4.0 %collective-permute-done.25.refs_6_.refs_2_ = bf16[2,256,512]{2,1,0:T(8,128)(2,1)S(1)} collective-permute-done((bf16[2,256,512]{2,1,0:T(8,128)(2,1)S(1)}, bf16[2,256,512]{2,1,0:T(8,128)(2,1)S(1)}, u32[]{:S(2)}, u32[]{:S(2)}) %collective-permute-start.25) | collective-permute-done | bytes 524320 | tf_op jit(solution)/shard_map/ppermute | solution.py:33
  57.4 3.3 %collective-permute-done.22.side_in = bf16[4,48,512]{2,1,0:T(8,128)(2,1)S(1)} collective-permute-done((bf16[4,48,512]{2,1,0:T(8,128)(2,1)S(1)}, bf16[4,48,512]{2,1,0:T(8,128)(2,1)S(1)}, u32[]{:S(2)}, u32[]{:S(2)}) %collective-permute-start.22) | collective-permute-done | bytes 196640 | tf_op jit(solution)/shard_map/ppermute | solution.py:33
  60.8 0.0 collective-permute-start.27
  60.8 0.5 collective-permute-start.23
  61.3 0.0 collective-permute-start.24
  61.3 1.4 %collective-permute-done.27.refs_9_.refs_5_ = bf16[2,256,512]{2,1,0:T(8,128)(2,1)S(1)} collective-permute-done((bf16[2,256,512]{2,1,0:T(8,128)(2,1)S(1)}, bf16[2,256,512]{2,1,0:T(8,128)(2,1)S(1)}, u32[]{:S(2)}, u32[]{:S(2)}) %collective-permute-start.27) | collective-permute-done | bytes 524320 | tf_op jit(solution)/shard_map/ppermute | solution.py:33
  62.7 0.6 shard_map.93
  63.3 1.6 %collective-permute-start.29 = (bf16[128,512]{1,0:T(8,128)(2,1)S(1)}, bf16[128,512]{1,0:T(8,128)(2,1)S(1)}, u32[]{:S(2)}, u32[]{:S(2)}) collective-permute-start(bf16[128,512]{1,0:T(8,128)(2,1)S(1)} %get-tuple-element.70), channel_id=1, source_target_pairs={{0,1},{1,0},{2,3},{3,2},{4,5},{5,4},{6,7},{7,6},{8,9},{9,8},{10,11... | collective-permute-start | bytes 393224 | tf_op jit(solution)/shard_map/ppermute | solution.py:33
  64.9 3.5 %shard_map.92 = (bf16[128,512]{1,0:T(8,128)(2,1)S(1)}, bf16[128,512]{1,0:T(8,128)(2,1)S(1)}) custom-call(f32[8,128]{1,0:T(8,128)S(1)} %get-tuple-element.38.rate, bf16[4,48,512]{2,1,0:T(8,128)(2,1)S(1)} %shard_map.91.mine, bf16[4,48,512]{2,1,0:T(8,128)(2,1)S(1)} %collective-permute-done.22.side_in, bf16[4,48,512]{2,1,0:T(8,128)(2,1)S(1)} %collective-permute-done.23.core_in, ...), custom_call_target="tpu_custom_call" | custom-call | flops 3000000000 | bytes 4000000 | tf_op jit(solution)/shard_map/pallas_call | solution.py:46
  68.3 0.6 collective-permute-start.28
  68.9 0.8 %shard_map.94.refs_0_ = bf16[2,128,1024]{2,1,0:T(8,128)(2,1)} custom-call(bf16[128,512]{1,0:T(8,128)(2,1)S(1)} %get-tuple-element.69.own, bf16[128,512]{1,0:T(8,128)(2,1)S(1)} %collective-permute-done.29.got, f32[1,1024]{1,0:T(1,128)S(1)} %bitcast.5), custom_call_target="tpu_custom_call" | custom-call | bytes 524288 | tf_op jit(solution)/shard_map/pallas_call | solution.py:333
  69.7 3.9 %collective-permute-done.28.got = bf16[128,512]{1,0:T(8,128)(2,1)S(1)} collective-permute-done((bf16[128,512]{1,0:T(8,128)(2,1)S(1)}, bf16[128,512]{1,0:T(8,128)(2,1)S(1)}, u32[]{:S(2)}, u32[]{:S(2)}) %collective-permute-start.28) | collective-permute-done | bytes 131104 | tf_op jit(solution)/shard_map/ppermute | solution.py:33
  73.6 0.8 %shard_map.95 = bf16[2,128,1024]{2,1,0:T(8,128)(2,1)} custom-call(bf16[128,512]{1,0:T(8,128)(2,1)S(1)} %get-tuple-element.66.own, bf16[128,512]{1,0:T(8,128)(2,1)S(1)} %collective-permute-done.28.got, f32[1,1024]{1,0:T(1,128)S(1)} %bitcast.6, bf16[2,128,1024]{2,1,0:T(8,128)(2,1)} %shard_map.94.refs_0_), custom_call_target="tpu_custom_call", output_to_operand_aliasing={{}: (3, {})} | custom-call | bytes 524288 | tf_op jit(solution)/shard_map/pallas_call | solution.py:333
  (20 shorter events, 0.1 us)
Async XLA Ops:
  0.0 18.5 %collective-permute-start.7 = (bf16[2,256,512]{2,1,0:T(8,128)(2,1)}, bf16[2,256,512]{2,1,0:T(8,128)(2,1)S(1)}, u32[]{:S(2)}, u32[]{:S(2)}) collective-permute-start(bf16[2,256,512]{2,1,0:T(8,128)(2,1)} %keys.1), channel_id=1, source_target_pairs={{0,2},{2,0},{4,6},{6,4},{8,10},{10,8},{12,14},{14,12},{16,18},{18,... | collective-permute-start | bytes 1572872 | tf_op jit(solution)/shard_map/ppermute | solution.py:33
  0.5 18.1 %collective-permute-start.8 = (bf16[2,256,512]{2,1,0:T(8,128)(2,1)}, bf16[2,256,512]{2,1,0:T(8,128)(2,1)S(1)}, u32[]{:S(2)}, u32[]{:S(2)}) collective-permute-start(bf16[2,256,512]{2,1,0:T(8,128)(2,1)} %values.1), channel_id=1, source_target_pairs={{0,2},{2,0},{4,6},{6,4},{8,10},{10,8},{12,14},{14,12},{16,18},{18,... | collective-permute-start | bytes 1572872 | tf_op jit(solution)/shard_map/ppermute | solution.py:33
  0.5 5.4 %collective-permute-start = (bf16[32,768]{1,0:T(8,128)(2,1)}, bf16[32,768]{1,0:T(8,128)(2,1)S(1)}, u32[]{:S(2)}, u32[]{:S(2)}) collective-permute-start(bf16[32,768]{1,0:T(8,128)(2,1)} %bitcast.9), channel_id=1, source_target_pairs={{0,2},{2,0},{4,6},{6,4},{8,10},{10,8},{12,14},{14,12},{16,18},{18,... | collective-permute-start | bytes 147464 | tf_op jit(solution)/shard_map/ppermute | solution.py:33
  1.0 6.2 %collective-permute-start.2 = (bf16[32,768]{1,0:T(8,128)(2,1)}, bf16[32,768]{1,0:T(8,128)(2,1)S(1)}, u32[]{:S(2)}, u32[]{:S(2)}) collective-permute-start(bf16[32,768]{1,0:T(8,128)(2,1)} %bitcast.10), channel_id=1, source_target_pairs={{0,16},{2,18},{4,20},{6,22},{8,24},{10,26},{12,28},{14,30},{16,0},... | collective-permute-start | bytes 147464 | tf_op jit(solution)/shard_map/ppermute | solution.py:33
  4.6 6.4 %collective-permute-start.3 = (bf16[32,768]{1,0:T(8,128)(2,1)}, bf16[32,768]{1,0:T(8,128)(2,1)S(1)}, u32[]{:S(2)}, u32[]{:S(2)}) collective-permute-start(bf16[32,768]{1,0:T(8,128)(2,1)} %bitcast.11), channel_id=1, source_target_pairs={{0,24},{2,26},{4,28},{6,30},{8,16},{10,18},{12,20},{14,22},{16,8},... | collective-permute-start | bytes 147464 | tf_op jit(solution)/shard_map/ppermute | solution.py:33
  5.9 5.2 %collective-permute-start.1 = (bf16[32,768]{1,0:T(8,128)(2,1)}, bf16[32,768]{1,0:T(8,128)(2,1)S(1)}, u32[]{:S(2)}, u32[]{:S(2)}) collective-permute-start(bf16[32,768]{1,0:T(8,128)(2,1)} %bitcast.12), channel_id=1, source_target_pairs={{0,8},{2,10},{4,12},{6,14},{8,0},{10,2},{12,4},{14,6},{16,24},{18,... | collective-permute-start | bytes 147464 | tf_op jit(solution)/shard_map/ppermute | solution.py:33
  11.1 5.7 %collective-permute-start.4 = (bf16[4,32,768]{2,1,0:T(8,128)(2,1)S(1)}, bf16[4,32,768]{2,1,0:T(8,128)(2,1)S(1)}, u32[]{:S(2)}, u32[]{:S(2)}) collective-permute-start(bf16[4,32,768]{2,1,0:T(8,128)(2,1)S(1)} %shard_map.83.mine), channel_id=1, source_target_pairs={{0,4},{2,6},{4,0},{6,2},{8,12},{10,14},{12,8},{14,10},{16,20},{18,... | collective-permute-start | bytes 589832 | tf_op jit(solution)/shard_map/ppermute | solution.py:33
  12.6 16.0 %collective-permute-start.15 = (bf16[2,256,512]{2,1,0:T(8,128)(2,1)}, bf16[2,256,512]{2,1,0:T(8,128)(2,1)S(1)}, u32[]{:S(2)}, u32[]{:S(2)}) collective-permute-start(bf16[2,256,512]{2,1,0:T(8,128)(2,1)} %keys.1), channel_id=1, source_target_pairs={{0,8},{2,10},{4,12},{6,14},{8,16},{10,18},{12,20},{14,22},{16,24},... | collective-permute-start | bytes 1572872 | tf_op jit(solution)/shard_map/ppermute | solution.py:359
  12.8 4.1 %collective-permute-start.9 = (f32[1,256]{1,0:T(1,128)}, f32[1,256]{1,0:T(1,128)S(1)}, u32[]{:S(2)}, u32[]{:S(2)}) collective-permute-start(f32[1,256]{1,0:T(1,128)} %bitcast.7), channel_id=1, source_target_pairs={{0,2},{2,0},{4,6},{6,4},{8,10},{10,8},{12,14},{14,12},{16,18},{18,... | collective-permute-start | bytes 3080 | tf_op jit(solution)/shard_map/ppermute | solution.py:33
  13.5 1.0 %copy-start.1 = (bf16[2,256,512]{2,1,0:T(8,128)(2,1)S(1)}, bf16[2,256,512]{2,1,0:T(8,128)(2,1)}, u32[]{:S(2)}) copy-start(bf16[2,256,512]{2,1,0:T(8,128)(2,1)} %keys.1) | copy-start | bytes 1572868
  14.5 0.7 copy-start.4
  16.8 1.4 %collective-permute-start.5 = (bf16[4,32,768]{2,1,0:T(8,128)(2,1)S(1)}, bf16[4,32,768]{2,1,0:T(8,128)(2,1)S(1)}, u32[]{:S(2)}, u32[]{:S(2)}) collective-permute-start(bf16[4,32,768]{2,1,0:T(8,128)(2,1)S(1)} %shard_map.83.mine), channel_id=1, source_target_pairs={{0,2},{2,0},{4,6},{6,4},{8,10},{10,8},{12,14},{14,12},{16,18},{18,... | collective-permute-start | bytes 589832 | tf_op jit(solution)/shard_map/ppermute | solution.py:33
  16.9 1.6 %collective-permute-start.6 = (bf16[4,32,768]{2,1,0:T(8,128)(2,1)S(1)}, bf16[4,32,768]{2,1,0:T(8,128)(2,1)S(1)}, u32[]{:S(2)}, u32[]{:S(2)}) collective-permute-start(bf16[4,32,768]{2,1,0:T(8,128)(2,1)S(1)} %collective-permute-done.4.other), channel_id=1, source_target_pairs={{0,2},{2,0},{4,6},{6,4},{8,10},{10,8},{12,14},{14,12},{16,18},{18,... | collective-permute-start | bytes 589832 | tf_op jit(solution)/shard_map/ppermute | solution.py:33
  19.7 8.9 %collective-permute-start.10 = (bf16[192,512]{1,0:T(8,128)(2,1)S(1)}, bf16[192,512]{1,0:T(8,128)(2,1)S(1)}, u32[]{:S(2)}, u32[]{:S(2)}) collective-permute-start(bf16[192,512]{1,0:T(8,128)(2,1)S(1)} %get-tuple-element.45), channel_id=1, source_target_pairs={{0,4},{2,6},{4,0},{6,2},{8,12},{10,14},{12,8},{14,10},{16,20},{18,... | collective-permute-start | bytes 589832 | tf_op jit(solution)/shard_map/ppermute | solution.py:33
  21.3 18.7 %collective-permute-start.11 = (bf16[2,256,512]{2,1,0:T(8,128)(2,1)}, bf16[2,256,512]{2,1,0:T(8,128)(2,1)S(1)}, u32[]{:S(2)}, u32[]{:S(2)}) collective-permute-start(bf16[2,256,512]{2,1,0:T(8,128)(2,1)} %values.1), channel_id=1, source_target_pairs={{0,8},{2,10},{4,12},{6,14},{8,16},{10,18},{12,20},{14,22},{16,24},... | collective-permute-start | bytes 1572872 | tf_op jit(solution)/shard_map/ppermute | solution.py:359
  28.7 13.4 %collective-permute-start.16 = (bf16[2,256,512]{2,1,0:T(8,128)(2,1)S(1)}, bf16[2,256,512]{2,1,0:T(8,128)(2,1)S(1)}, u32[]{:S(2)}, u32[]{:S(2)}) collective-permute-start(bf16[2,256,512]{2,1,0:T(8,128)(2,1)S(1)} %shard_map.89), channel_id=1, source_target_pairs={{0,4},{2,6},{4,0},{6,2},{8,12},{10,14},{12,8},{14,10},{16,20},{18,... | collective-permute-start | bytes 1572872 | tf_op jit(solution)/shard_map/ppermute | solution.py:33
  29.3 18.3 %copy-start = (bf16[2,256,512]{2,1,0:T(8,128)(2,1)S(1)}, bf16[2,256,512]{2,1,0:T(8,128)(2,1)}, u32[]{:S(2)}) copy-start(bf16[2,256,512]{2,1,0:T(8,128)(2,1)} %refs_0_.1) | copy-start | bytes 1572868
  29.4 11.9 %collective-permute-start.12 = (bf16[48,512]{1,0:T(8,128)(2,1)S(1)}, bf16[48,512]{1,0:T(8,128)(2,1)S(1)}, u32[]{:S(2)}, u32[]{:S(2)}) collective-permute-start(bf16[48,512]{1,0:T(8,128)(2,1)S(1)} %get-tuple-element.52), channel_id=1, source_target_pairs={{0,8},{2,10},{4,12},{6,14},{8,0},{10,2},{12,4},{14,6},{16,24},{18,... | collective-permute-start | bytes 147464 | tf_op jit(solution)/shard_map/ppermute | solution.py:33
  29.9 12.1 %collective-permute-start.13 = (bf16[48,512]{1,0:T(8,128)(2,1)S(1)}, bf16[48,512]{1,0:T(8,128)(2,1)S(1)}, u32[]{:S(2)}, u32[]{:S(2)}) collective-permute-start(bf16[48,512]{1,0:T(8,128)(2,1)S(1)} %get-tuple-element.53), channel_id=1, source_target_pairs={{0,16},{2,18},{4,20},{6,22},{8,24},{10,26},{12,28},{14,30},{16,0},... | collective-permute-start | bytes 147464 | tf_op jit(solution)/shard_map/ppermute | solution.py:33
  33.1 8.9 %collective-permute-start.14 = (bf16[48,512]{1,0:T(8,128)(2,1)S(1)}, bf16[48,512]{1,0:T(8,128)(2,1)S(1)}, u32[]{:S(2)}, u32[]{:S(2)}) collective-permute-start(bf16[48,512]{1,0:T(8,128)(2,1)S(1)} %get-tuple-element.54), channel_id=1, source_target_pairs={{0,24},{2,26},{4,28},{6,30},{8,16},{10,18},{12,20},{14,22},{16,8},... | collective-permute-start | bytes 147464 | tf_op jit(solution)/shard_map/ppermute | solution.py:33
  42.0 20.6 %copy-start.2 = (bf16[2,256,512]{2,1,0:T(8,128)(2,1)S(1)}, bf16[2,256,512]{2,1,0:T(8,128)(2,1)}, u32[]{:S(2)}) copy-start(bf16[2,256,512]{2,1,0:T(8,128)(2,1)} %refs_9_.1) | copy-start | bytes 1572868
  42.1 4.2 %collective-permute-start.17 = (bf16[2,256,512]{2,1,0:T(8,128)(2,1)S(1)}, bf16[2,256,512]{2,1,0:T(8,128)(2,1)S(1)}, u32[]{:S(2)}, u32[]{:S(2)}) collective-permute-start(bf16[2,256,512]{2,1,0:T(8,128)(2,1)S(1)} %collective-permute-done.15.far.refs_1_), channel_id=1, source_target_pairs={{0,2},{2,0},{4,6},{6,4},{8,10},{10,8},{12,14},{14,12},{16,18},{18,... | collective-permute-start | bytes 1572872 | tf_op jit(solution)/shard_map/ppermute | solution.py:33
  42.1 4.1 %collective-permute-start.18 = (bf16[2,256,512]{2,1,0:T(8,128)(2,1)S(1)}, bf16[2,256,512]{2,1,0:T(8,128)(2,1)S(1)}, u32[]{:S(2)}, u32[]{:S(2)}) collective-permute-start(bf16[2,256,512]{2,1,0:T(8,128)(2,1)S(1)} %collective-permute-done.16.refs_2_), channel_id=1, source_target_pairs={{0,2},{2,0},{4,6},{6,4},{8,10},{10,8},{12,14},{14,12},{16,18},{18,... | collective-permute-start | bytes 1572872 | tf_op jit(solution)/shard_map/ppermute | solution.py:33
  42.6 14.8 %collective-permute-start.25 = (bf16[2,256,512]{2,1,0:T(8,128)(2,1)S(1)}, bf16[2,256,512]{2,1,0:T(8,128)(2,1)S(1)}, u32[]{:S(2)}, u32[]{:S(2)}) collective-permute-start(bf16[2,256,512]{2,1,0:T(8,128)(2,1)S(1)} %shard_map.86), channel_id=1, source_target_pairs={{0,4},{2,6},{4,0},{6,2},{8,12},{10,14},{12,8},{14,10},{16,20},{18,... | collective-permute-start | bytes 1572872 | tf_op jit(solution)/shard_map/ppermute | solution.py:33
  43.2 5.9 %collective-permute-start.19 = (bf16[48,512]{1,0:T(8,128)(2,1)S(1)}, bf16[48,512]{1,0:T(8,128)(2,1)S(1)}, u32[]{:S(2)}, u32[]{:S(2)}) collective-permute-start(bf16[48,512]{1,0:T(8,128)(2,1)S(1)} %shard_map.88.refs_0_), channel_id=1, source_target_pairs={{0,8},{2,10},{4,12},{6,14},{8,0},{10,2},{12,4},{14,6},{16,24},{18,... | collective-permute-start | bytes 147464 | tf_op jit(solution)/shard_map/ppermute | solution.py:33
  44.7 5.6 %collective-permute-start.20 = (bf16[48,512]{1,0:T(8,128)(2,1)S(1)}, bf16[48,512]{1,0:T(8,128)(2,1)S(1)}, u32[]{:S(2)}, u32[]{:S(2)}) collective-permute-start(bf16[48,512]{1,0:T(8,128)(2,1)S(1)} %shard_map.88.refs_0_), channel_id=1, source_target_pairs={{0,16},{2,18},{4,20},{6,22},{8,24},{10,26},{12,28},{14,30},{16,0},... | collective-permute-start | bytes 147464 | tf_op jit(solution)/shard_map/ppermute | solution.py:33
  46.3 5.9 %collective-permute-start.21 = (bf16[48,512]{1,0:T(8,128)(2,1)S(1)}, bf16[48,512]{1,0:T(8,128)(2,1)S(1)}, u32[]{:S(2)}, u32[]{:S(2)}) collective-permute-start(bf16[48,512]{1,0:T(8,128)(2,1)S(1)} %shard_map.88.refs_0_), channel_id=1, source_target_pairs={{0,24},{2,26},{4,28},{6,30},{8,16},{10,18},{12,20},{14,22},{16,8},... | collective-permute-start | bytes 147464 | tf_op jit(solution)/shard_map/ppermute | solution.py:33
  52.2 8.6 %collective-permute-start.22 = (bf16[4,48,512]{2,1,0:T(8,128)(2,1)S(1)}, bf16[4,48,512]{2,1,0:T(8,128)(2,1)S(1)}, u32[]{:S(2)}, u32[]{:S(2)}) collective-permute-start(bf16[4,48,512]{2,1,0:T(8,128)(2,1)S(1)} %shard_map.91.mine), channel_id=1, source_target_pairs={{0,4},{2,6},{4,0},{6,2},{8,12},{10,14},{12,8},{14,10},{16,20},{18,... | collective-permute-start | bytes 589832 | tf_op jit(solution)/shard_map/ppermute | solution.py:33
  53.4 7.8 %collective-permute-start.26 = (bf16[2,256,512]{2,1,0:T(8,128)(2,1)S(1)}, bf16[2,256,512]{2,1,0:T(8,128)(2,1)S(1)}, u32[]{:S(2)}, u32[]{:S(2)}) collective-permute-start(bf16[2,256,512]{2,1,0:T(8,128)(2,1)S(1)} %collective-permute-done.11.far.refs_5_.refs_1_), channel_id=1, source_target_pairs={{0,2},{2,0},{4,6},{6,4},{8,10},{10,8},{12,14},{14,12},{16,18},{18,... | collective-permute-start | bytes 1572872 | tf_op jit(solution)/shard_map/ppermute | solution.py:33
  60.8 1.9 %collective-permute-start.27 = (bf16[2,256,512]{2,1,0:T(8,128)(2,1)S(1)}, bf16[2,256,512]{2,1,0:T(8,128)(2,1)S(1)}, u32[]{:S(2)}, u32[]{:S(2)}) collective-permute-start(bf16[2,256,512]{2,1,0:T(8,128)(2,1)S(1)} %collective-permute-done.25.refs_6_.refs_2_), channel_id=1, source_target_pairs={{0,2},{2,0},{4,6},{6,4},{8,10},{10,8},{12,14},{14,12},{16,18},{18,... | collective-permute-start | bytes 1572872 | tf_op jit(solution)/shard_map/ppermute | solution.py:33
  60.8 4.1 %collective-permute-start.23 = (bf16[4,48,512]{2,1,0:T(8,128)(2,1)S(1)}, bf16[4,48,512]{2,1,0:T(8,128)(2,1)S(1)}, u32[]{:S(2)}, u32[]{:S(2)}) collective-permute-start(bf16[4,48,512]{2,1,0:T(8,128)(2,1)S(1)} %shard_map.91.mine), channel_id=1, source_target_pairs={{0,2},{2,0},{4,6},{6,4},{8,10},{10,8},{12,14},{14,12},{16,18},{18,... | collective-permute-start | bytes 589832 | tf_op jit(solution)/shard_map/ppermute | solution.py:33
  61.3 3.6 %collective-permute-start.24 = (bf16[4,48,512]{2,1,0:T(8,128)(2,1)S(1)}, bf16[4,48,512]{2,1,0:T(8,128)(2,1)S(1)}, u32[]{:S(2)}, u32[]{:S(2)}) collective-permute-start(bf16[4,48,512]{2,1,0:T(8,128)(2,1)S(1)} %collective-permute-done.22.side_in), channel_id=1, source_target_pairs={{0,2},{2,0},{4,6},{6,4},{8,10},{10,8},{12,14},{14,12},{16,18},{18,... | collective-permute-start | bytes 589832 | tf_op jit(solution)/shard_map/ppermute | solution.py:33
  63.3 5.6 %collective-permute-start.29 = (bf16[128,512]{1,0:T(8,128)(2,1)S(1)}, bf16[128,512]{1,0:T(8,128)(2,1)S(1)}, u32[]{:S(2)}, u32[]{:S(2)}) collective-permute-start(bf16[128,512]{1,0:T(8,128)(2,1)S(1)} %get-tuple-element.70), channel_id=1, source_target_pairs={{0,1},{1,0},{2,3},{3,2},{4,5},{5,4},{6,7},{7,6},{8,9},{9,8},{10,11... | collective-permute-start | bytes 393224 | tf_op jit(solution)/shard_map/ppermute | solution.py:33
  64.9 4.0 %copy-start.3 = (f32[1024]{0:T(1024)S(1)}, f32[1024]{0:T(1024)}, u32[]{:S(2)}) copy-start(f32[1024]{0:T(1024)} %param.15) | copy-start | bytes 12292
  68.3 5.3 %collective-permute-start.28 = (bf16[128,512]{1,0:T(8,128)(2,1)S(1)}, bf16[128,512]{1,0:T(8,128)(2,1)S(1)}, u32[]{:S(2)}, u32[]{:S(2)}) collective-permute-start(bf16[128,512]{1,0:T(8,128)(2,1)S(1)} %get-tuple-element.67), channel_id=1, source_target_pairs={{0,1},{1,0},{2,3},{3,2},{4,5},{5,4},{6,7},{7,6},{8,9},{9,8},{10,11... | collective-permute-start | bytes 393224 | tf_op jit(solution)/shard_map/ppermute | solution.py:33

commit v7 on v6

--- a/solution.py
+++ b/solution.py
@@ -93,11 +93,13 @@
 
 
 def pack_body(*refs):
-    for m, ref in enumerate(refs[:-1]):
+    first, *others, second = refs[:-1]
+    for m, ref in enumerate((first, second, *others)):
         refs[-1][m] = ref[...]
 
 
-def packed(*pieces):
+def packed(first, second, *others):
+    pieces = (first, *others, second)
     return pl.pallas_call(
         pack_body,
         out_shape=jax.ShapeDtypeStruct((len(pieces),) + pieces[0].shape, pieces[0].dtype),
@@ -425,7 +427,7 @@
 
     total = call(
         plane_sum_body,
-        (after(parts[0], pick_values, flipped), *partial),
+        (after(parts[0], pick_values, flipped), *partial[1:], partial[0]),
         jax.ShapeDtypeStruct((part, depth), BF),
         cost=cost_of(0, planes * part * depth * 3),
     )
@@ -433,7 +435,7 @@
     near_keys_in = swapped(after(near_keys, total), 1)
     all_keys = [own_keys, far_keys, near_keys, keys_in, far_keys_in, near_keys_in]
     planes_grad = [
-        swapped(total if m < planes - 1 else after(total, far_keys_in, near_keys_in), 4 * m)
+        swapped(total, 4 * m)
         for m in range(1, planes)
     ]
 

time: 74.7 us -> 74.7 us (level)
  starting transfers between devices: 25.8 us -> 24.8 us
  waiting for transfers between devices: 36.1 us -> 37 us
    ppermute x28, starting transfers between devices: 24.2 us -> 23.3 us  [swapped(): return lax.ppermute(value, axis, [(i, i ^ mask) for i in range(count)])]
where the time goes in v7:
time: 74.7 us; the launch traced here: 74.5 us
  waiting for transfers between devices  37 us (50%)
  starting transfers between devices  24.8 us (33%)
  Pallas kernels  10.1 us (14%)
  local copies, waits for them, and re-layouts  1.73 us (2%)
  between operations  0.79 us (1%)
    ppermute x28, waiting for transfers between devices, swapped(): return lax.ppermute(value, axis, [(i, i ^ mask) for i in range(count)])  24.5 us
    ppermute x28, starting transfers between devices, swapped(): return lax.ppermute(value, axis, [(i, i ^ mask) for i in range(count)])  23.3 us
    ppermute x2, waiting for transfers between devices, sent(): return lax.ppermute(value, axis, pairs)  12.4 us
    pallas_call x10, Pallas kernels, call(): pl.pallas_call(body, out_shape=outs, in_specs=[vmem_spec()] * len(args),...  8.44 us
    unnamed x10, local copies, waits for them, and re-layouts  1.73 us
    pallas_call x2, Pallas kernels, finished(): pl.pallas_call(functools.partial(norm_body, group), out_shape=jax.ShapeDt...  1.68 us
    ppermute x2, starting transfers between devices, sent(): return lax.ppermute(value, axis, pairs)  1.53 us
  transfers between devices with their start and end apart: 30, of which 16 were waited for; matrix products, arithmetic and copies ran while one was open for 0% of the time, Pallas kernels for 12%

profile of v7, /device:TPU:0, one launch (start us, length us, event | category | flops | bytes accessed | tf_op | source)
XLA Modules:
  0.0 74.5 jit_solution(7372820920843458773)
XLA Ops:
  0.0 0.5 collective-permute-start.7
  0.5 0.1 collective-permute-start.8
  0.5 0.5 collective-permute-start
  1.0 3.6 %collective-permute-start.1 = (bf16[32,768]{1,0:T(8,128)(2,1)}, bf16[32,768]{1,0:T(8,128)(2,1)S(1)}, u32[]{:S(2)}, u32[]{:S(2)}) collective-permute-start(bf16[32,768]{1,0:T(8,128)(2,1)} %bitcast.10), channel_id=1, source_target_pairs={{0,16},{2,18},{4,20},{6,22},{8,24},{10,26},{12,28},{14,30},{16,0},... | collective-permute-start | bytes 147464 | tf_op jit(solution)/shard_map/ppermute | solution.py:33
  4.6 1.3 %collective-permute-start.2 = (bf16[32,768]{1,0:T(8,128)(2,1)}, bf16[32,768]{1,0:T(8,128)(2,1)S(1)}, u32[]{:S(2)}, u32[]{:S(2)}) collective-permute-start(bf16[32,768]{1,0:T(8,128)(2,1)} %bitcast.11), channel_id=1, source_target_pairs={{0,24},{2,26},{4,28},{6,30},{8,16},{10,18},{12,20},{14,22},{16,8},... | collective-permute-start | bytes 147464 | tf_op jit(solution)/shard_map/ppermute | solution.py:33
  5.9 0.2 collective-permute-start.3
  6.1 1.0 %collective-permute-done.1.refs_1_ = bf16[32,768]{1,0:T(8,128)(2,1)S(1)} collective-permute-done((bf16[32,768]{1,0:T(8,128)(2,1)}, bf16[32,768]{1,0:T(8,128)(2,1)S(1)}, u32[]{:S(2)}, u32[]{:S(2)}) %collective-permute-start.1) | collective-permute-done | bytes 49184 | tf_op jit(solution)/shard_map/ppermute | solution.py:33
  7.2 3.8 %collective-permute-done.2.refs_2_ = bf16[32,768]{1,0:T(8,128)(2,1)S(1)} collective-permute-done((bf16[32,768]{1,0:T(8,128)(2,1)}, bf16[32,768]{1,0:T(8,128)(2,1)S(1)}, u32[]{:S(2)}, u32[]{:S(2)}) %collective-permute-start.2) | collective-permute-done | bytes 49184 | tf_op jit(solution)/shard_map/ppermute | solution.py:33
  11.0 0.1 collective-permute-done.3.refs_3_
  11.1 1.6 %collective-permute-start.4 = (bf16[4,32,768]{2,1,0:T(8,128)(2,1)S(1)}, bf16[4,32,768]{2,1,0:T(8,128)(2,1)S(1)}, u32[]{:S(2)}, u32[]{:S(2)}) collective-permute-start(bf16[4,32,768]{2,1,0:T(8,128)(2,1)S(1)} %shard_map.83.mine), channel_id=1, source_target_pairs={{0,4},{2,6},{4,0},{6,2},{8,12},{10,14},{12,8},{14,10},{16,20},{18,... | collective-permute-start | bytes 589832 | tf_op jit(solution)/shard_map/ppermute | solution.py:33
  12.6 0.2 collective-permute-start.15
  12.8 0.0 collective-permute-start.9
  13.5 1.0 %copy-done.1 = bf16[2,256,512]{2,1,0:T(8,128)(2,1)S(1)} copy-done((bf16[2,256,512]{2,1,0:T(8,128)(2,1)S(1)}, bf16[2,256,512]{2,1,0:T(8,128)(2,1)}, u32[]{:S(2)}) %copy-start.1) | copy-done | bytes 524312
  14.5 0.7 copy-done.4
  15.2 1.1 %shard_map.82 = (bf16[2,256,512]{2,1,0:T(8,128)(2,1)S(1)}, bf16[2,256,512]{2,1,0:T(8,128)(2,1)S(1)}, f32[1,256]{1,0:T(1,128)S(1)}, f32[8,128]{1,0:T(8,128)S(1)}) custom-call(bf16[2,256,512]{2,1,0:T(8,128)(2,1)S(1)} %copy-done.1, bf16[2,256,512]{2,1,0:T(8,128)(2,1)} %values.1, f32[1,256]{1,0:T(1,128)S(1)} %bitcast.8, f32[1,1]{1,0:T(1,128)} %bitcast.4.rate), custom_call_target="tpu_custom_call" | custom-call | tf_op jit(solution)/shard_map/pallas_call | solution.py:46
  16.3 0.5 collective-permute-done.4.other
  16.8 0.1 collective-permute-start.5
  16.9 0.0 collective-permute-done.9.refs_5_
  16.9 0.4 collective-permute-start.6
  17.3 0.9 %collective-permute-done.5.beside_mine = bf16[4,32,768]{2,1,0:T(8,128)(2,1)S(1)} collective-permute-done((bf16[4,32,768]{2,1,0:T(8,128)(2,1)S(1)}, bf16[4,32,768]{2,1,0:T(8,128)(2,1)S(1)}, u32[]{:S(2)}, u32[]{:S(2)}) %collective-permute-start.5) | collective-permute-done | bytes 196640 | tf_op jit(solution)/shard_map/ppermute | solution.py:33
  18.3 0.3 collective-permute-done.6.beside_other
  18.5 0.0 collective-permute-done.7.refs_3_
  18.5 0.0 collective-permute-done.8.refs_4_.refs_7_.refs_3_
  18.5 1.2 %shard_map.84 = (bf16[192,512]{1,0:T(8,128)(2,1)S(1)}, f32[192,512]{1,0:T(8,128)S(1)}, bf16[512,768]{1,0:T(8,128)(2,1)S(1)}) custom-call(bf16[4,32,768]{2,1,0:T(8,128)(2,1)S(1)} %shard_map.83.mine, bf16[4,32,768]{2,1,0:T(8,128)(2,1)S(1)} %collective-permute-done.4.other, bf16[4,32,768]{2,1,0:T(8,128)(2,1)S(1)} %collective-permute-done.5.beside_mine, ...), custom_call_target="tpu_custom_call" | custom-call | flops 402653184 | bytes 2097152 | tf_op jit(solution)/shard_map/pallas_call | solution.py:46
  19.7 1.6 %collective-permute-start.10 = (bf16[192,512]{1,0:T(8,128)(2,1)S(1)}, bf16[192,512]{1,0:T(8,128)(2,1)S(1)}, u32[]{:S(2)}, u32[]{:S(2)}) collective-permute-start(bf16[192,512]{1,0:T(8,128)(2,1)S(1)} %get-tuple-element.44), channel_id=1, source_target_pairs={{0,4},{2,6},{4,0},{6,2},{8,12},{10,14},{12,8},{14,10},{16,20},{18,... | collective-permute-start | bytes 589832 | tf_op jit(solution)/shard_map/ppermute | solution.py:33
  21.3 1.3 %collective-permute-start.11 = (bf16[2,256,512]{2,1,0:T(8,128)(2,1)}, bf16[2,256,512]{2,1,0:T(8,128)(2,1)S(1)}, u32[]{:S(2)}, u32[]{:S(2)}) collective-permute-start(bf16[2,256,512]{2,1,0:T(8,128)(2,1)} %values.1), channel_id=1, source_target_pairs={{0,8},{2,10},{4,12},{6,14},{8,16},{10,18},{12,20},{14,22},{16,24},... | collective-permute-start | bytes 1572872 | tf_op jit(solution)/shard_map/ppermute | solution.py:361
  22.6 6.0 %collective-permute-done.15.far.refs_1_ = bf16[2,256,512]{2,1,0:T(8,128)(2,1)S(1)} collective-permute-done((bf16[2,256,512]{2,1,0:T(8,128)(2,1)}, bf16[2,256,512]{2,1,0:T(8,128)(2,1)S(1)}, u32[]{:S(2)}, u32[]{:S(2)}) %collective-permute-start.15) | collective-permute-done | bytes 524320 | tf_op jit(solution)/shard_map/ppermute | solution.py:361
  28.6 0.1 shard_map.89
  28.7 0.6 collective-permute-start.16
  29.3 0.1 shard_map.85
  29.4 2.4 %collective-permute-start.12 = (bf16[48,512]{1,0:T(8,128)(2,1)S(1)}, bf16[48,512]{1,0:T(8,128)(2,1)S(1)}, u32[]{:S(2)}, u32[]{:S(2)}) collective-permute-start(bf16[48,512]{1,0:T(8,128)(2,1)S(1)} %get-tuple-element.51), channel_id=1, source_target_pairs={{0,16},{2,18},{4,20},{6,22},{8,24},{10,26},{12,28},{14,30},{16,0},... | collective-permute-start | bytes 147464 | tf_op jit(solution)/shard_map/ppermute | solution.py:33
  31.7 0.9 %collective-permute-start.13 = (bf16[48,512]{1,0:T(8,128)(2,1)S(1)}, bf16[48,512]{1,0:T(8,128)(2,1)S(1)}, u32[]{:S(2)}, u32[]{:S(2)}) collective-permute-start(bf16[48,512]{1,0:T(8,128)(2,1)S(1)} %get-tuple-element.52), channel_id=1, source_target_pairs={{0,24},{2,26},{4,28},{6,30},{8,16},{10,18},{12,20},{14,22},{16,8},... | collective-permute-start | bytes 147464 | tf_op jit(solution)/shard_map/ppermute | solution.py:33
  32.7 0.5 collective-permute-start.14
  33.1 0.4 shard_map.87
  33.6 6.4 %collective-permute-done.11.far.refs_5_.refs_1_ = bf16[2,256,512]{2,1,0:T(8,128)(2,1)S(1)} collective-permute-done((bf16[2,256,512]{2,1,0:T(8,128)(2,1)}, bf16[2,256,512]{2,1,0:T(8,128)(2,1)S(1)}, u32[]{:S(2)}, u32[]{:S(2)}) %collective-permute-start.11) | collective-permute-done | bytes 524320 | tf_op jit(solution)/shard_map/ppermute | solution.py:361
  40.0 0.1 shard_map.86
  40.1 2.0 %collective-permute-done.12.refs_0_ = bf16[48,512]{1,0:T(8,128)(2,1)S(1)} collective-permute-done((bf16[48,512]{1,0:T(8,128)(2,1)S(1)}, bf16[48,512]{1,0:T(8,128)(2,1)S(1)}, u32[]{:S(2)}, u32[]{:S(2)}) %collective-permute-start.12) | collective-permute-done | bytes 49184 | tf_op jit(solution)/shard_map/ppermute | solution.py:33
  42.0 0.0 collective-permute-done.13.refs_1_
  42.0 0.0 collective-permute-done.14.refs_2_
  42.0 0.0 copy-start.2
  42.1 0.1 collective-permute-start.17
  42.1 0.0 collective-permute-done.16.refs_2_
  42.2 0.5 collective-permute-start.18
  42.6 0.5 collective-permute-start.25
  43.2 1.8 %collective-permute-start.19 = (bf16[48,512]{1,0:T(8,128)(2,1)S(1)}, bf16[48,512]{1,0:T(8,128)(2,1)S(1)}, u32[]{:S(2)}, u32[]{:S(2)}) collective-permute-start(bf16[48,512]{1,0:T(8,128)(2,1)S(1)} %shard_map.88.refs_0_), channel_id=1, source_target_pairs={{0,16},{2,18},{4,20},{6,22},{8,24},{10,26},{12,28},{14,30},{16,0},... | collective-permute-start | bytes 147464 | tf_op jit(solution)/shard_map/ppermute | solution.py:33
  45.0 2.0 %collective-permute-start.20 = (bf16[48,512]{1,0:T(8,128)(2,1)S(1)}, bf16[48,512]{1,0:T(8,128)(2,1)S(1)}, u32[]{:S(2)}, u32[]{:S(2)}) collective-permute-start(bf16[48,512]{1,0:T(8,128)(2,1)S(1)} %shard_map.88.refs_0_), channel_id=1, source_target_pairs={{0,24},{2,26},{4,28},{6,30},{8,16},{10,18},{12,20},{14,22},{16,8},... | collective-permute-start | bytes 147464 | tf_op jit(solution)/shard_map/ppermute | solution.py:33
  47.1 0.0 collective-permute-done.18.refs_5_
  47.1 1.5 %shard_map.90 = (bf16[2,5,256,256]{3,2,1,0:T(8,128)(2,1)S(1)}, f32[2,256,1]{2,1,0:T(8,128)S(1)}, f32[256,512]{1,0:T(8,128)S(1)}) custom-call(bf16[2,256,512]{2,1,0:T(8,128)(2,1)S(1)} %copy-done, bf16[2,256,512]{2,1,0:T(8,128)(2,1)S(1)} %get-tuple-element.39.refs_0_.own, bf16[2,256,512]{2,1,0:T(8,128)(2,1)S(1)} %collective-permute-done.15.far.refs_1_, ...), custom_call_target="tpu_custom_call" | custom-call | flops 1000 | bytes 1000 | tf_op jit(solution)/shard_map/pallas_call | solution.py:46
  48.6 1.3 %collective-permute-done.19.refs_1_ = bf16[48,512]{1,0:T(8,128)(2,1)S(1)} collective-permute-done((bf16[48,512]{1,0:T(8,128)(2,1)S(1)}, bf16[48,512]{1,0:T(8,128)(2,1)S(1)}, u32[]{:S(2)}, u32[]{:S(2)}) %collective-permute-start.19) | collective-permute-done | bytes 49184 | tf_op jit(solution)/shard_map/ppermute | solution.py:33
  49.9 1.2 %collective-permute-done.20.refs_2_ = bf16[48,512]{1,0:T(8,128)(2,1)S(1)} collective-permute-done((bf16[48,512]{1,0:T(8,128)(2,1)S(1)}, bf16[48,512]{1,0:T(8,128)(2,1)S(1)}, u32[]{:S(2)}, u32[]{:S(2)}) %collective-permute-start.20) | collective-permute-done | bytes 49184 | tf_op jit(solution)/shard_map/ppermute | solution.py:33
  51.1 0.5 collective-permute-done.21.refs_3_
  51.6 1.5 %collective-permute-start.22 = (bf16[4,48,512]{2,1,0:T(8,128)(2,1)S(1)}, bf16[4,48,512]{2,1,0:T(8,128)(2,1)S(1)}, u32[]{:S(2)}, u32[]{:S(2)}) collective-permute-start(bf16[4,48,512]{2,1,0:T(8,128)(2,1)S(1)} %shard_map.91.mine), channel_id=1, source_target_pairs={{0,4},{2,6},{4,0},{6,2},{8,12},{10,14},{12,8},{14,10},{16,20},{18,... | collective-permute-start | bytes 589832 | tf_op jit(solution)/shard_map/ppermute | solution.py:33
  53.1 4.3 %collective-permute-done.25.refs_6_.refs_2_ = bf16[2,256,512]{2,1,0:T(8,128)(2,1)S(1)} collective-permute-done((bf16[2,256,512]{2,1,0:T(8,128)(2,1)S(1)}, bf16[2,256,512]{2,1,0:T(8,128)(2,1)S(1)}, u32[]{:S(2)}, u32[]{:S(2)}) %collective-permute-start.25) | collective-permute-done | bytes 524320 | tf_op jit(solution)/shard_map/ppermute | solution.py:33
  57.4 3.3 %collective-permute-done.22.side_in = bf16[4,48,512]{2,1,0:T(8,128)(2,1)S(1)} collective-permute-done((bf16[4,48,512]{2,1,0:T(8,128)(2,1)S(1)}, bf16[4,48,512]{2,1,0:T(8,128)(2,1)S(1)}, u32[]{:S(2)}, u32[]{:S(2)}) %collective-permute-start.22) | collective-permute-done | bytes 196640 | tf_op jit(solution)/shard_map/ppermute | solution.py:33
  60.8 0.5 collective-permute-start.23
  61.3 0.0 collective-permute-start.24
  61.3 1.4 %collective-permute-done.27.refs_9_.refs_5_ = bf16[2,256,512]{2,1,0:T(8,128)(2,1)S(1)} collective-permute-done((bf16[2,256,512]{2,1,0:T(8,128)(2,1)S(1)}, bf16[2,256,512]{2,1,0:T(8,128)(2,1)S(1)}, u32[]{:S(2)}, u32[]{:S(2)}) %collective-permute-start.27) | collective-permute-done | bytes 524320 | tf_op jit(solution)/shard_map/ppermute | solution.py:33
  62.7 0.6 shard_map.93
  63.3 1.6 %collective-permute-start.29 = (bf16[128,512]{1,0:T(8,128)(2,1)S(1)}, bf16[128,512]{1,0:T(8,128)(2,1)S(1)}, u32[]{:S(2)}, u32[]{:S(2)}) collective-permute-start(bf16[128,512]{1,0:T(8,128)(2,1)S(1)} %get-tuple-element.68), channel_id=1, source_target_pairs={{0,1},{1,0},{2,3},{3,2},{4,5},{5,4},{6,7},{7,6},{8,9},{9,8},{10,11... | collective-permute-start | bytes 393224 | tf_op jit(solution)/shard_map/ppermute | solution.py:33
  64.9 3.4 %shard_map.92 = (bf16[128,512]{1,0:T(8,128)(2,1)S(1)}, bf16[128,512]{1,0:T(8,128)(2,1)S(1)}) custom-call(f32[8,128]{1,0:T(8,128)S(1)} %get-tuple-element.37.rate, bf16[4,48,512]{2,1,0:T(8,128)(2,1)S(1)} %shard_map.91.mine, bf16[4,48,512]{2,1,0:T(8,128)(2,1)S(1)} %collective-permute-done.22.side_in, bf16[4,48,512]{2,1,0:T(8,128)(2,1)S(1)} %collective-permute-done.23.core_in, ...), custom_call_target="tpu_custom_call" | custom-call | flops 3000000000 | bytes 4000000 | tf_op jit(solution)/shard_map/pallas_call | solution.py:46
  68.3 0.6 collective-permute-start.28
  68.9 0.8 %shard_map.94.refs_0_ = bf16[2,128,1024]{2,1,0:T(8,128)(2,1)} custom-call(bf16[128,512]{1,0:T(8,128)(2,1)S(1)} %get-tuple-element.67.own, bf16[128,512]{1,0:T(8,128)(2,1)S(1)} %collective-permute-done.29.got, f32[1,1024]{1,0:T(1,128)S(1)} %bitcast.5), custom_call_target="tpu_custom_call" | custom-call | bytes 524288 | tf_op jit(solution)/shard_map/pallas_call | solution.py:335
  69.7 3.9 %collective-permute-done.28.got = bf16[128,512]{1,0:T(8,128)(2,1)S(1)} collective-permute-done((bf16[128,512]{1,0:T(8,128)(2,1)S(1)}, bf16[128,512]{1,0:T(8,128)(2,1)S(1)}, u32[]{:S(2)}, u32[]{:S(2)}) %collective-permute-start.28) | collective-permute-done | bytes 131104 | tf_op jit(solution)/shard_map/ppermute | solution.py:33
  73.6 0.8 %shard_map.95 = bf16[2,128,1024]{2,1,0:T(8,128)(2,1)} custom-call(bf16[128,512]{1,0:T(8,128)(2,1)S(1)} %get-tuple-element.64.own, bf16[128,512]{1,0:T(8,128)(2,1)S(1)} %collective-permute-done.28.got, f32[1,1024]{1,0:T(1,128)S(1)} %bitcast.6, bf16[2,128,1024]{2,1,0:T(8,128)(2,1)} %shard_map.94.refs_0_), custom_call_target="tpu_custom_call", output_to_operand_aliasing={{}: (3, {})} | custom-call | bytes 524288 | tf_op jit(solution)/shard_map/pallas_call | solution.py:335
  (20 shorter events, 0.1 us)
Async XLA Ops:
  0.0 18.5 %collective-permute-start.7 = (bf16[2,256,512]{2,1,0:T(8,128)(2,1)}, bf16[2,256,512]{2,1,0:T(8,128)(2,1)S(1)}, u32[]{:S(2)}, u32[]{:S(2)}) collective-permute-start(bf16[2,256,512]{2,1,0:T(8,128)(2,1)} %keys.1), channel_id=1, source_target_pairs={{0,2},{2,0},{4,6},{6,4},{8,10},{10,8},{12,14},{14,12},{16,18},{18,... | collective-permute-start | bytes 1572872 | tf_op jit(solution)/shard_map/ppermute | solution.py:33
  0.5 18.1 %collective-permute-start.8 = (bf16[2,256,512]{2,1,0:T(8,128)(2,1)}, bf16[2,256,512]{2,1,0:T(8,128)(2,1)S(1)}, u32[]{:S(2)}, u32[]{:S(2)}) collective-permute-start(bf16[2,256,512]{2,1,0:T(8,128)(2,1)} %values.1), channel_id=1, source_target_pairs={{0,2},{2,0},{4,6},{6,4},{8,10},{10,8},{12,14},{14,12},{16,18},{18,... | collective-permute-start | bytes 1572872 | tf_op jit(solution)/shard_map/ppermute | solution.py:33
  0.5 5.4 %collective-permute-start = (bf16[32,768]{1,0:T(8,128)(2,1)}, bf16[32,768]{1,0:T(8,128)(2,1)S(1)}, u32[]{:S(2)}, u32[]{:S(2)}) collective-permute-start(bf16[32,768]{1,0:T(8,128)(2,1)} %bitcast.9), channel_id=1, source_target_pairs={{0,2},{2,0},{4,6},{6,4},{8,10},{10,8},{12,14},{14,12},{16,18},{18,... | collective-permute-start | bytes 147464 | tf_op jit(solution)/shard_map/ppermute | solution.py:33
  1.0 6.2 %collective-permute-start.1 = (bf16[32,768]{1,0:T(8,128)(2,1)}, bf16[32,768]{1,0:T(8,128)(2,1)S(1)}, u32[]{:S(2)}, u32[]{:S(2)}) collective-permute-start(bf16[32,768]{1,0:T(8,128)(2,1)} %bitcast.10), channel_id=1, source_target_pairs={{0,16},{2,18},{4,20},{6,22},{8,24},{10,26},{12,28},{14,30},{16,0},... | collective-permute-start | bytes 147464 | tf_op jit(solution)/shard_map/ppermute | solution.py:33
  4.6 6.4 %collective-permute-start.2 = (bf16[32,768]{1,0:T(8,128)(2,1)}, bf16[32,768]{1,0:T(8,128)(2,1)S(1)}, u32[]{:S(2)}, u32[]{:S(2)}) collective-permute-start(bf16[32,768]{1,0:T(8,128)(2,1)} %bitcast.11), channel_id=1, source_target_pairs={{0,24},{2,26},{4,28},{6,30},{8,16},{10,18},{12,20},{14,22},{16,8},... | collective-permute-start | bytes 147464 | tf_op jit(solution)/shard_map/ppermute | solution.py:33
  5.9 5.2 %collective-permute-start.3 = (bf16[32,768]{1,0:T(8,128)(2,1)}, bf16[32,768]{1,0:T(8,128)(2,1)S(1)}, u32[]{:S(2)}, u32[]{:S(2)}) collective-permute-start(bf16[32,768]{1,0:T(8,128)(2,1)} %bitcast.12), channel_id=1, source_target_pairs={{0,8},{2,10},{4,12},{6,14},{8,0},{10,2},{12,4},{14,6},{16,24},{18,... | collective-permute-start | bytes 147464 | tf_op jit(solution)/shard_map/ppermute | solution.py:33
  11.1 5.7 %collective-permute-start.4 = (bf16[4,32,768]{2,1,0:T(8,128)(2,1)S(1)}, bf16[4,32,768]{2,1,0:T(8,128)(2,1)S(1)}, u32[]{:S(2)}, u32[]{:S(2)}) collective-permute-start(bf16[4,32,768]{2,1,0:T(8,128)(2,1)S(1)} %shard_map.83.mine), channel_id=1, source_target_pairs={{0,4},{2,6},{4,0},{6,2},{8,12},{10,14},{12,8},{14,10},{16,20},{18,... | collective-permute-start | bytes 589832 | tf_op jit(solution)/shard_map/ppermute | solution.py:33
  12.6 16.0 %collective-permute-start.15 = (bf16[2,256,512]{2,1,0:T(8,128)(2,1)}, bf16[2,256,512]{2,1,0:T(8,128)(2,1)S(1)}, u32[]{:S(2)}, u32[]{:S(2)}) collective-permute-start(bf16[2,256,512]{2,1,0:T(8,128)(2,1)} %keys.1), channel_id=1, source_target_pairs={{0,8},{2,10},{4,12},{6,14},{8,16},{10,18},{12,20},{14,22},{16,24},... | collective-permute-start | bytes 1572872 | tf_op jit(solution)/shard_map/ppermute | solution.py:361
  12.8 4.1 %collective-permute-start.9 = (f32[1,256]{1,0:T(1,128)}, f32[1,256]{1,0:T(1,128)S(1)}, u32[]{:S(2)}, u32[]{:S(2)}) collective-permute-start(f32[1,256]{1,0:T(1,128)} %bitcast.7), channel_id=1, source_target_pairs={{0,2},{2,0},{4,6},{6,4},{8,10},{10,8},{12,14},{14,12},{16,18},{18,... | collective-permute-start | bytes 3080 | tf_op jit(solution)/shard_map/ppermute | solution.py:33
  13.5 1.0 %copy-start.1 = (bf16[2,256,512]{2,1,0:T(8,128)(2,1)S(1)}, bf16[2,256,512]{2,1,0:T(8,128)(2,1)}, u32[]{:S(2)}) copy-start(bf16[2,256,512]{2,1,0:T(8,128)(2,1)} %keys.1) | copy-start | bytes 1572868
  14.5 0.7 copy-start.4
  16.8 1.4 %collective-permute-start.5 = (bf16[4,32,768]{2,1,0:T(8,128)(2,1)S(1)}, bf16[4,32,768]{2,1,0:T(8,128)(2,1)S(1)}, u32[]{:S(2)}, u32[]{:S(2)}) collective-permute-start(bf16[4,32,768]{2,1,0:T(8,128)(2,1)S(1)} %shard_map.83.mine), channel_id=1, source_target_pairs={{0,2},{2,0},{4,6},{6,4},{8,10},{10,8},{12,14},{14,12},{16,18},{18,... | collective-permute-start | bytes 589832 | tf_op jit(solution)/shard_map/ppermute | solution.py:33
  16.9 1.6 %collective-permute-start.6 = (bf16[4,32,768]{2,1,0:T(8,128)(2,1)S(1)}, bf16[4,32,768]{2,1,0:T(8,128)(2,1)S(1)}, u32[]{:S(2)}, u32[]{:S(2)}) collective-permute-start(bf16[4,32,768]{2,1,0:T(8,128)(2,1)S(1)} %collective-permute-done.4.other), channel_id=1, source_target_pairs={{0,2},{2,0},{4,6},{6,4},{8,10},{10,8},{12,14},{14,12},{16,18},{18,... | collective-permute-start | bytes 589832 | tf_op jit(solution)/shard_map/ppermute | solution.py:33
  19.7 8.9 %collective-permute-start.10 = (bf16[192,512]{1,0:T(8,128)(2,1)S(1)}, bf16[192,512]{1,0:T(8,128)(2,1)S(1)}, u32[]{:S(2)}, u32[]{:S(2)}) collective-permute-start(bf16[192,512]{1,0:T(8,128)(2,1)S(1)} %get-tuple-element.44), channel_id=1, source_target_pairs={{0,4},{2,6},{4,0},{6,2},{8,12},{10,14},{12,8},{14,10},{16,20},{18,... | collective-permute-start | bytes 589832 | tf_op jit(solution)/shard_map/ppermute | solution.py:33
  21.3 18.7 %collective-permute-start.11 = (bf16[2,256,512]{2,1,0:T(8,128)(2,1)}, bf16[2,256,512]{2,1,0:T(8,128)(2,1)S(1)}, u32[]{:S(2)}, u32[]{:S(2)}) collective-permute-start(bf16[2,256,512]{2,1,0:T(8,128)(2,1)} %values.1), channel_id=1, source_target_pairs={{0,8},{2,10},{4,12},{6,14},{8,16},{10,18},{12,20},{14,22},{16,24},... | collective-permute-start | bytes 1572872 | tf_op jit(solution)/shard_map/ppermute | solution.py:361
  28.7 13.4 %collective-permute-start.16 = (bf16[2,256,512]{2,1,0:T(8,128)(2,1)S(1)}, bf16[2,256,512]{2,1,0:T(8,128)(2,1)S(1)}, u32[]{:S(2)}, u32[]{:S(2)}) collective-permute-start(bf16[2,256,512]{2,1,0:T(8,128)(2,1)S(1)} %shard_map.89), channel_id=1, source_target_pairs={{0,4},{2,6},{4,0},{6,2},{8,12},{10,14},{12,8},{14,10},{16,20},{18,... | collective-permute-start | bytes 1572872 | tf_op jit(solution)/shard_map/ppermute | solution.py:33
  29.3 17.8 %copy-start = (bf16[2,256,512]{2,1,0:T(8,128)(2,1)S(1)}, bf16[2,256,512]{2,1,0:T(8,128)(2,1)}, u32[]{:S(2)}) copy-start(bf16[2,256,512]{2,1,0:T(8,128)(2,1)} %refs_0_.1) | copy-start | bytes 1572868
  29.4 12.6 %collective-permute-start.12 = (bf16[48,512]{1,0:T(8,128)(2,1)S(1)}, bf16[48,512]{1,0:T(8,128)(2,1)S(1)}, u32[]{:S(2)}, u32[]{:S(2)}) collective-permute-start(bf16[48,512]{1,0:T(8,128)(2,1)S(1)} %get-tuple-element.51), channel_id=1, source_target_pairs={{0,16},{2,18},{4,20},{6,22},{8,24},{10,26},{12,28},{14,30},{16,0},... | collective-permute-start | bytes 147464 | tf_op jit(solution)/shard_map/ppermute | solution.py:33
  31.7 10.3 %collective-permute-start.13 = (bf16[48,512]{1,0:T(8,128)(2,1)S(1)}, bf16[48,512]{1,0:T(8,128)(2,1)S(1)}, u32[]{:S(2)}, u32[]{:S(2)}) collective-permute-start(bf16[48,512]{1,0:T(8,128)(2,1)S(1)} %get-tuple-element.52), channel_id=1, source_target_pairs={{0,24},{2,26},{4,28},{6,30},{8,16},{10,18},{12,20},{14,22},{16,8},... | collective-permute-start | bytes 147464 | tf_op jit(solution)/shard_map/ppermute | solution.py:33
  32.7 9.4 %collective-permute-start.14 = (bf16[48,512]{1,0:T(8,128)(2,1)S(1)}, bf16[48,512]{1,0:T(8,128)(2,1)S(1)}, u32[]{:S(2)}, u32[]{:S(2)}) collective-permute-start(bf16[48,512]{1,0:T(8,128)(2,1)S(1)} %get-tuple-element.53), channel_id=1, source_target_pairs={{0,8},{2,10},{4,12},{6,14},{8,0},{10,2},{12,4},{14,6},{16,24},{18,... | collective-permute-start | bytes 147464 | tf_op jit(solution)/shard_map/ppermute | solution.py:33
  42.0 20.6 %copy-start.2 = (bf16[2,256,512]{2,1,0:T(8,128)(2,1)S(1)}, bf16[2,256,512]{2,1,0:T(8,128)(2,1)}, u32[]{:S(2)}) copy-start(bf16[2,256,512]{2,1,0:T(8,128)(2,1)} %refs_9_.1) | copy-start | bytes 1572868
  42.1 5.0 %collective-permute-start.17 = (bf16[2,256,512]{2,1,0:T(8,128)(2,1)S(1)}, bf16[2,256,512]{2,1,0:T(8,128)(2,1)S(1)}, u32[]{:S(2)}, u32[]{:S(2)}) collective-permute-start(bf16[2,256,512]{2,1,0:T(8,128)(2,1)S(1)} %collective-permute-done.15.far.refs_1_), channel_id=1, source_target_pairs={{0,2},{2,0},{4,6},{6,4},{8,10},{10,8},{12,14},{14,12},{16,18},{18,... | collective-permute-start | bytes 1572872 | tf_op jit(solution)/shard_map/ppermute | solution.py:33
  42.2 4.9 %collective-permute-start.18 = (bf16[2,256,512]{2,1,0:T(8,128)(2,1)S(1)}, bf16[2,256,512]{2,1,0:T(8,128)(2,1)S(1)}, u32[]{:S(2)}, u32[]{:S(2)}) collective-permute-start(bf16[2,256,512]{2,1,0:T(8,128)(2,1)S(1)} %collective-permute-done.16.refs_2_), channel_id=1, source_target_pairs={{0,2},{2,0},{4,6},{6,4},{8,10},{10,8},{12,14},{14,12},{16,18},{18,... | collective-permute-start | bytes 1572872 | tf_op jit(solution)/shard_map/ppermute | solution.py:33
  42.6 14.8 %collective-permute-start.25 = (bf16[2,256,512]{2,1,0:T(8,128)(2,1)S(1)}, bf16[2,256,512]{2,1,0:T(8,128)(2,1)S(1)}, u32[]{:S(2)}, u32[]{:S(2)}) collective-permute-start(bf16[2,256,512]{2,1,0:T(8,128)(2,1)S(1)} %shard_map.86), channel_id=1, source_target_pairs={{0,4},{2,6},{4,0},{6,2},{8,12},{10,14},{12,8},{14,10},{16,20},{18,... | collective-permute-start | bytes 1572872 | tf_op jit(solution)/shard_map/ppermute | solution.py:33
  43.2 6.7 %collective-permute-start.19 = (bf16[48,512]{1,0:T(8,128)(2,1)S(1)}, bf16[48,512]{1,0:T(8,128)(2,1)S(1)}, u32[]{:S(2)}, u32[]{:S(2)}) collective-permute-start(bf16[48,512]{1,0:T(8,128)(2,1)S(1)} %shard_map.88.refs_0_), channel_id=1, source_target_pairs={{0,16},{2,18},{4,20},{6,22},{8,24},{10,26},{12,28},{14,30},{16,0},... | collective-permute-start | bytes 147464 | tf_op jit(solution)/shard_map/ppermute | solution.py:33
  45.0 6.0 %collective-permute-start.20 = (bf16[48,512]{1,0:T(8,128)(2,1)S(1)}, bf16[48,512]{1,0:T(8,128)(2,1)S(1)}, u32[]{:S(2)}, u32[]{:S(2)}) collective-permute-start(bf16[48,512]{1,0:T(8,128)(2,1)S(1)} %shard_map.88.refs_0_), channel_id=1, source_target_pairs={{0,24},{2,26},{4,28},{6,30},{8,16},{10,18},{12,20},{14,22},{16,8},... | collective-permute-start | bytes 147464 | tf_op jit(solution)/shard_map/ppermute | solution.py:33
  47.1 4.5 %collective-permute-start.21 = (bf16[48,512]{1,0:T(8,128)(2,1)S(1)}, bf16[48,512]{1,0:T(8,128)(2,1)S(1)}, u32[]{:S(2)}, u32[]{:S(2)}) collective-permute-start(bf16[48,512]{1,0:T(8,128)(2,1)S(1)} %shard_map.88.refs_0_), channel_id=1, source_target_pairs={{0,8},{2,10},{4,12},{6,14},{8,0},{10,2},{12,4},{14,6},{16,24},{18,... | collective-permute-start | bytes 147464 | tf_op jit(solution)/shard_map/ppermute | solution.py:33
  51.6 9.2 %collective-permute-start.22 = (bf16[4,48,512]{2,1,0:T(8,128)(2,1)S(1)}, bf16[4,48,512]{2,1,0:T(8,128)(2,1)S(1)}, u32[]{:S(2)}, u32[]{:S(2)}) collective-permute-start(bf16[4,48,512]{2,1,0:T(8,128)(2,1)S(1)} %shard_map.91.mine), channel_id=1, source_target_pairs={{0,4},{2,6},{4,0},{6,2},{8,12},{10,14},{12,8},{14,10},{16,20},{18,... | collective-permute-start | bytes 589832 | tf_op jit(solution)/shard_map/ppermute | solution.py:33
  53.1 8.2 %collective-permute-start.26 = (bf16[2,256,512]{2,1,0:T(8,128)(2,1)S(1)}, bf16[2,256,512]{2,1,0:T(8,128)(2,1)S(1)}, u32[]{:S(2)}, u32[]{:S(2)}) collective-permute-start(bf16[2,256,512]{2,1,0:T(8,128)(2,1)S(1)} %collective-permute-done.11.far.refs_5_.refs_1_), channel_id=1, source_target_pairs={{0,2},{2,0},{4,6},{6,4},{8,10},{10,8},{12,14},{14,12},{16,18},{18,... | collective-permute-start | bytes 1572872 | tf_op jit(solution)/shard_map/ppermute | solution.py:33
  60.8 1.9 %collective-permute-start.27 = (bf16[2,256,512]{2,1,0:T(8,128)(2,1)S(1)}, bf16[2,256,512]{2,1,0:T(8,128)(2,1)S(1)}, u32[]{:S(2)}, u32[]{:S(2)}) collective-permute-start(bf16[2,256,512]{2,1,0:T(8,128)(2,1)S(1)} %collective-permute-done.25.refs_6_.refs_2_), channel_id=1, source_target_pairs={{0,2},{2,0},{4,6},{6,4},{8,10},{10,8},{12,14},{14,12},{16,18},{18,... | collective-permute-start | bytes 1572872 | tf_op jit(solution)/shard_map/ppermute | solution.py:33
  60.8 4.1 %collective-permute-start.23 = (bf16[4,48,512]{2,1,0:T(8,128)(2,1)S(1)}, bf16[4,48,512]{2,1,0:T(8,128)(2,1)S(1)}, u32[]{:S(2)}, u32[]{:S(2)}) collective-permute-start(bf16[4,48,512]{2,1,0:T(8,128)(2,1)S(1)} %shard_map.91.mine), channel_id=1, source_target_pairs={{0,2},{2,0},{4,6},{6,4},{8,10},{10,8},{12,14},{14,12},{16,18},{18,... | collective-permute-start | bytes 589832 | tf_op jit(solution)/shard_map/ppermute | solution.py:33
  61.3 3.6 %collective-permute-start.24 = (bf16[4,48,512]{2,1,0:T(8,128)(2,1)S(1)}, bf16[4,48,512]{2,1,0:T(8,128)(2,1)S(1)}, u32[]{:S(2)}, u32[]{:S(2)}) collective-permute-start(bf16[4,48,512]{2,1,0:T(8,128)(2,1)S(1)} %collective-permute-done.22.side_in), channel_id=1, source_target_pairs={{0,2},{2,0},{4,6},{6,4},{8,10},{10,8},{12,14},{14,12},{16,18},{18,... | collective-permute-start | bytes 589832 | tf_op jit(solution)/shard_map/ppermute | solution.py:33
  63.3 5.6 %collective-permute-start.29 = (bf16[128,512]{1,0:T(8,128)(2,1)S(1)}, bf16[128,512]{1,0:T(8,128)(2,1)S(1)}, u32[]{:S(2)}, u32[]{:S(2)}) collective-permute-start(bf16[128,512]{1,0:T(8,128)(2,1)S(1)} %get-tuple-element.68), channel_id=1, source_target_pairs={{0,1},{1,0},{2,3},{3,2},{4,5},{5,4},{6,7},{7,6},{8,9},{9,8},{10,11... | collective-permute-start | bytes 393224 | tf_op jit(solution)/shard_map/ppermute | solution.py:33
  64.9 4.0 %copy-start.3 = (f32[1024]{0:T(1024)S(1)}, f32[1024]{0:T(1024)}, u32[]{:S(2)}) copy-start(f32[1024]{0:T(1024)} %param.15) | copy-start | bytes 12292
  68.3 5.3 %collective-permute-start.28 = (bf16[128,512]{1,0:T(8,128)(2,1)S(1)}, bf16[128,512]{1,0:T(8,128)(2,1)S(1)}, u32[]{:S(2)}, u32[]{:S(2)}) collective-permute-start(bf16[128,512]{1,0:T(8,128)(2,1)S(1)} %get-tuple-element.65), channel_id=1, source_target_pairs={{0,1},{1,0},{2,3},{3,2},{4,5},{5,4},{6,7},{7,6},{8,9},{9,8},{10,11... | collective-permute-start | bytes 393224 | tf_op jit(solution)/shard_map/ppermute | solution.py:33

commit v8 on v7

--- a/solution.py
+++ b/solution.py
@@ -279,26 +279,31 @@
         ).astype(F32)
         length = jnp.sqrt(jnp.sum(block * block, keepdims=True))
         turned.append((block * (1.0 / (length + 1e-06))).astype(BF))
-    for _ in range(3):
-        grams = [dot_nt(y, y) for y in turned]
+    def step(ys):
+        grams = [dot_nt(y, y) for y in ys]
         lows = [a.astype(BF) for a in grams]
         squares = [dot_nn(a, a) for a in lows]
         mixers = [(B_COEF * a + C_COEF * s).astype(BF) for a, s in zip(grams, squares)]
-        turned = [
-            (A_COEF * y.astype(F32) + dot_nn(b, y)).astype(BF) for b, y in zip(mixers, turned)
-        ]
-    fresh = []
-    for b in range(3):
+        return [(A_COEF * y.astype(F32) + dot_nn(b, y)).astype(BF) for b, y in zip(mixers, ys)]
+
+    def renewed(b, y):
         cols = slice(b * width, (b + 1) * width)
-        moved = flipped[cols, :] - rate[:1, :1] * turned[b].astype(F32)
+        moved = flipped[cols, :] - rate[:1, :1] * y.astype(F32)
         length = jnp.sqrt(jnp.sum(moved * moved, 1, keepdims=True))
-        fresh.append((moved * (norms[cols, :] / (length + 1e-06))).astype(BF))
+        return (moved * (norms[cols, :] / (length + 1e-06))).astype(BF)
+
+    gate_up, last = step(turned[:2]), turned[2:]
+    for _ in range(2):
+        *gate_up, behind = step(gate_up + last)
+        last = [behind]
+    gate_w, up_w = renewed(0, gate_up[0]), renewed(1, gate_up[1])
+    x = queries[1]
+    g = dot_nt(x, gate_w)
+    u = dot_nt(x, up_w)
+    out_w = renewed(2, step(last)[0])
     win = mixed(1, value_refs, weights, inverses)
-    x = queries[1]
-    g = dot_nt(x, fresh[0])
-    u = dot_nt(x, fresh[1])
     hidden = (silu(g) * u).astype(BF)
-    fast = dot_nn(hidden, fresh[2])
+    fast = dot_nn(hidden, out_w)
     gate = gates[1].astype(F32)
     spread(((win + fast) * silu(gate)).astype(BF), outs, gated)
 

time: 74.7 us -> 75.2 us (level)
  transfers between devices with their start and end apart: 30 -> 30, of which waited for: 16 -> 16; matrix products, arithmetic and copies ran while one was open for 0% -> 0% of each run, Pallas kernels for 12% -> 13%
where the time goes in v8:
time: 75.2 us; the launch traced here: 75 us
  waiting for transfers between devices  37 us (49%)
  starting transfers between devices  24.8 us (33%)
  Pallas kernels  10.6 us (14%)
  local copies, waits for them, and re-layouts  1.73 us (2%)
  between operations  0.79 us (1%)
    ppermute x28, waiting for transfers between devices, swapped(): return lax.ppermute(value, axis, [(i, i ^ mask) for i in range(count)])  24.5 us
    ppermute x28, starting transfers between devices, swapped(): return lax.ppermute(value, axis, [(i, i ^ mask) for i in range(count)])  23.3 us
    ppermute x2, waiting for transfers between devices, sent(): return lax.ppermute(value, axis, pairs)  12.4 us
    pallas_call x10, Pallas kernels, call(): pl.pallas_call(body, out_shape=outs, in_specs=[vmem_spec()] * len(args),...  8.94 us
    unnamed x10, local copies, waits for them, and re-layouts  1.73 us
    pallas_call x2, Pallas kernels, finished(): pl.pallas_call(functools.partial(norm_body, group), out_shape=jax.ShapeDt...  1.68 us
    ppermute x2, starting transfers between devices, sent(): return lax.ppermute(value, axis, pairs)  1.53 us
  transfers between devices with their start and end apart: 30, of which 16 were waited for; matrix products, arithmetic and copies ran while one was open for 0% of the time, Pallas kernels for 13%

profile of v8, /device:TPU:0, one launch (start us, length us, event | category | flops | bytes accessed | tf_op | source)
XLA Modules:
  0.0 75.0 jit_solution(11053904822996736420)
XLA Ops:
  0.0 0.5 collective-permute-start.7
  0.5 0.1 collective-permute-start.8
  0.5 0.5 collective-permute-start
  1.0 3.6 %collective-permute-start.1 = (bf16[32,768]{1,0:T(8,128)(2,1)}, bf16[32,768]{1,0:T(8,128)(2,1)S(1)}, u32[]{:S(2)}, u32[]{:S(2)}) collective-permute-start(bf16[32,768]{1,0:T(8,128)(2,1)} %bitcast.10), channel_id=1, source_target_pairs={{0,16},{2,18},{4,20},{6,22},{8,24},{10,26},{12,28},{14,30},{16,0},... | collective-permute-start | bytes 147464 | tf_op jit(solution)/shard_map/ppermute | solution.py:33
  4.6 1.3 %collective-permute-start.2 = (bf16[32,768]{1,0:T(8,128)(2,1)}, bf16[32,768]{1,0:T(8,128)(2,1)S(1)}, u32[]{:S(2)}, u32[]{:S(2)}) collective-permute-start(bf16[32,768]{1,0:T(8,128)(2,1)} %bitcast.11), channel_id=1, source_target_pairs={{0,24},{2,26},{4,28},{6,30},{8,16},{10,18},{12,20},{14,22},{16,8},... | collective-permute-start | bytes 147464 | tf_op jit(solution)/shard_map/ppermute | solution.py:33
  5.9 0.0 collective-permute-done.refs_0_
  5.9 0.2 collective-permute-start.3
  6.1 1.0 %collective-permute-done.1.refs_1_ = bf16[32,768]{1,0:T(8,128)(2,1)S(1)} collective-permute-done((bf16[32,768]{1,0:T(8,128)(2,1)}, bf16[32,768]{1,0:T(8,128)(2,1)S(1)}, u32[]{:S(2)}, u32[]{:S(2)}) %collective-permute-start.1) | collective-permute-done | bytes 49184 | tf_op jit(solution)/shard_map/ppermute | solution.py:33
  7.2 3.8 %collective-permute-done.2.refs_2_ = bf16[32,768]{1,0:T(8,128)(2,1)S(1)} collective-permute-done((bf16[32,768]{1,0:T(8,128)(2,1)}, bf16[32,768]{1,0:T(8,128)(2,1)S(1)}, u32[]{:S(2)}, u32[]{:S(2)}) %collective-permute-start.2) | collective-permute-done | bytes 49184 | tf_op jit(solution)/shard_map/ppermute | solution.py:33
  11.0 0.1 collective-permute-done.3.refs_3_
  11.1 1.6 %collective-permute-start.4 = (bf16[4,32,768]{2,1,0:T(8,128)(2,1)S(1)}, bf16[4,32,768]{2,1,0:T(8,128)(2,1)S(1)}, u32[]{:S(2)}, u32[]{:S(2)}) collective-permute-start(bf16[4,32,768]{2,1,0:T(8,128)(2,1)S(1)} %shard_map.83.mine), channel_id=1, source_target_pairs={{0,4},{2,6},{4,0},{6,2},{8,12},{10,14},{12,8},{14,10},{16,20},{18,... | collective-permute-start | bytes 589832 | tf_op jit(solution)/shard_map/ppermute | solution.py:33
  12.6 0.2 collective-permute-start.15
  12.8 0.0 collective-permute-start.9
  13.5 1.0 %copy-done.1 = bf16[2,256,512]{2,1,0:T(8,128)(2,1)S(1)} copy-done((bf16[2,256,512]{2,1,0:T(8,128)(2,1)S(1)}, bf16[2,256,512]{2,1,0:T(8,128)(2,1)}, u32[]{:S(2)}) %copy-start.1) | copy-done | bytes 524312
  14.5 0.7 copy-done.4
  15.2 1.1 %shard_map.82 = (bf16[2,256,512]{2,1,0:T(8,128)(2,1)S(1)}, bf16[2,256,512]{2,1,0:T(8,128)(2,1)S(1)}, f32[1,256]{1,0:T(1,128)S(1)}, f32[8,128]{1,0:T(8,128)S(1)}) custom-call(bf16[2,256,512]{2,1,0:T(8,128)(2,1)S(1)} %copy-done.1, bf16[2,256,512]{2,1,0:T(8,128)(2,1)} %values.1, f32[1,256]{1,0:T(1,128)S(1)} %bitcast.8, f32[1,1]{1,0:T(1,128)} %bitcast.4.rate), custom_call_target="tpu_custom_call" | custom-call | tf_op jit(solution)/shard_map/pallas_call | solution.py:46
  16.3 0.5 collective-permute-done.4.other
  16.8 0.1 collective-permute-start.5
  16.9 0.4 collective-permute-start.6
  17.3 0.9 %collective-permute-done.5.beside_mine = bf16[4,32,768]{2,1,0:T(8,128)(2,1)S(1)} collective-permute-done((bf16[4,32,768]{2,1,0:T(8,128)(2,1)S(1)}, bf16[4,32,768]{2,1,0:T(8,128)(2,1)S(1)}, u32[]{:S(2)}, u32[]{:S(2)}) %collective-permute-start.5) | collective-permute-done | bytes 196640 | tf_op jit(solution)/shard_map/ppermute | solution.py:33
  18.3 0.3 collective-permute-done.6.beside_other
  18.5 1.2 %shard_map.84 = (bf16[192,512]{1,0:T(8,128)(2,1)S(1)}, f32[192,512]{1,0:T(8,128)S(1)}, bf16[512,768]{1,0:T(8,128)(2,1)S(1)}) custom-call(bf16[4,32,768]{2,1,0:T(8,128)(2,1)S(1)} %shard_map.83.mine, bf16[4,32,768]{2,1,0:T(8,128)(2,1)S(1)} %collective-permute-done.4.other, bf16[4,32,768]{2,1,0:T(8,128)(2,1)S(1)} %collective-permute-done.5.beside_mine, ...), custom_call_target="tpu_custom_call" | custom-call | flops 402653184 | bytes 2097152 | tf_op jit(solution)/shard_map/pallas_call | solution.py:46
  19.7 1.6 %collective-permute-start.10 = (bf16[192,512]{1,0:T(8,128)(2,1)S(1)}, bf16[192,512]{1,0:T(8,128)(2,1)S(1)}, u32[]{:S(2)}, u32[]{:S(2)}) collective-permute-start(bf16[192,512]{1,0:T(8,128)(2,1)S(1)} %get-tuple-element.44), channel_id=1, source_target_pairs={{0,4},{2,6},{4,0},{6,2},{8,12},{10,14},{12,8},{14,10},{16,20},{18,... | collective-permute-start | bytes 589832 | tf_op jit(solution)/shard_map/ppermute | solution.py:33
  21.3 1.3 %collective-permute-start.11 = (bf16[2,256,512]{2,1,0:T(8,128)(2,1)}, bf16[2,256,512]{2,1,0:T(8,128)(2,1)S(1)}, u32[]{:S(2)}, u32[]{:S(2)}) collective-permute-start(bf16[2,256,512]{2,1,0:T(8,128)(2,1)} %values.1), channel_id=1, source_target_pairs={{0,8},{2,10},{4,12},{6,14},{8,16},{10,18},{12,20},{14,22},{16,24},... | collective-permute-start | bytes 1572872 | tf_op jit(solution)/shard_map/ppermute | solution.py:366
  22.6 6.0 %collective-permute-done.15.far.refs_1_ = bf16[2,256,512]{2,1,0:T(8,128)(2,1)S(1)} collective-permute-done((bf16[2,256,512]{2,1,0:T(8,128)(2,1)}, bf16[2,256,512]{2,1,0:T(8,128)(2,1)S(1)}, u32[]{:S(2)}, u32[]{:S(2)}) %collective-permute-start.15) | collective-permute-done | bytes 524320 | tf_op jit(solution)/shard_map/ppermute | solution.py:366
  28.6 0.0 collective-permute-done.10.got
  28.6 0.1 shard_map.89
  28.7 0.6 collective-permute-start.16
  29.3 0.1 shard_map.85
  29.4 2.4 %collective-permute-start.12 = (bf16[48,512]{1,0:T(8,128)(2,1)S(1)}, bf16[48,512]{1,0:T(8,128)(2,1)S(1)}, u32[]{:S(2)}, u32[]{:S(2)}) collective-permute-start(bf16[48,512]{1,0:T(8,128)(2,1)S(1)} %get-tuple-element.51), channel_id=1, source_target_pairs={{0,16},{2,18},{4,20},{6,22},{8,24},{10,26},{12,28},{14,30},{16,0},... | collective-permute-start | bytes 147464 | tf_op jit(solution)/shard_map/ppermute | solution.py:33
  31.7 0.9 %collective-permute-start.13 = (bf16[48,512]{1,0:T(8,128)(2,1)S(1)}, bf16[48,512]{1,0:T(8,128)(2,1)S(1)}, u32[]{:S(2)}, u32[]{:S(2)}) collective-permute-start(bf16[48,512]{1,0:T(8,128)(2,1)S(1)} %get-tuple-element.52), channel_id=1, source_target_pairs={{0,24},{2,26},{4,28},{6,30},{8,16},{10,18},{12,20},{14,22},{16,8},... | collective-permute-start | bytes 147464 | tf_op jit(solution)/shard_map/ppermute | solution.py:33
  32.7 0.5 collective-permute-start.14
  33.1 0.4 shard_map.87
  33.6 6.4 %collective-permute-done.11.far.refs_5_.refs_1_ = bf16[2,256,512]{2,1,0:T(8,128)(2,1)S(1)} collective-permute-done((bf16[2,256,512]{2,1,0:T(8,128)(2,1)}, bf16[2,256,512]{2,1,0:T(8,128)(2,1)S(1)}, u32[]{:S(2)}, u32[]{:S(2)}) %collective-permute-start.11) | collective-permute-done | bytes 524320 | tf_op jit(solution)/shard_map/ppermute | solution.py:366
  40.0 0.1 shard_map.86
  40.1 2.0 %collective-permute-done.12.refs_0_ = bf16[48,512]{1,0:T(8,128)(2,1)S(1)} collective-permute-done((bf16[48,512]{1,0:T(8,128)(2,1)S(1)}, bf16[48,512]{1,0:T(8,128)(2,1)S(1)}, u32[]{:S(2)}, u32[]{:S(2)}) %collective-permute-start.12) | collective-permute-done | bytes 49184 | tf_op jit(solution)/shard_map/ppermute | solution.py:33
  42.0 0.0 copy-start.2
  42.1 0.1 collective-permute-start.17
  42.2 0.5 collective-permute-start.18
  42.6 0.5 collective-permute-start.25
  43.2 1.8 %collective-permute-start.19 = (bf16[48,512]{1,0:T(8,128)(2,1)S(1)}, bf16[48,512]{1,0:T(8,128)(2,1)S(1)}, u32[]{:S(2)}, u32[]{:S(2)}) collective-permute-start(bf16[48,512]{1,0:T(8,128)(2,1)S(1)} %shard_map.88.refs_0_), channel_id=1, source_target_pairs={{0,16},{2,18},{4,20},{6,22},{8,24},{10,26},{12,28},{14,30},{16,0},... | collective-permute-start | bytes 147464 | tf_op jit(solution)/shard_map/ppermute | solution.py:33
  45.0 2.0 %collective-permute-start.20 = (bf16[48,512]{1,0:T(8,128)(2,1)S(1)}, bf16[48,512]{1,0:T(8,128)(2,1)S(1)}, u32[]{:S(2)}, u32[]{:S(2)}) collective-permute-start(bf16[48,512]{1,0:T(8,128)(2,1)S(1)} %shard_map.88.refs_0_), channel_id=1, source_target_pairs={{0,24},{2,26},{4,28},{6,30},{8,16},{10,18},{12,20},{14,22},{16,8},... | collective-permute-start | bytes 147464 | tf_op jit(solution)/shard_map/ppermute | solution.py:33
  47.1 0.0 collective-permute-done.17.refs_4_
  47.1 0.0 collective-permute-start.21
  47.1 0.0 collective-permute-done.18.refs_5_
  47.1 1.5 %shard_map.90 = (bf16[2,5,256,256]{3,2,1,0:T(8,128)(2,1)S(1)}, f32[2,256,1]{2,1,0:T(8,128)S(1)}, f32[256,512]{1,0:T(8,128)S(1)}) custom-call(bf16[2,256,512]{2,1,0:T(8,128)(2,1)S(1)} %copy-done, bf16[2,256,512]{2,1,0:T(8,128)(2,1)S(1)} %get-tuple-element.39.refs_0_.own, bf16[2,256,512]{2,1,0:T(8,128)(2,1)S(1)} %collective-permute-done.15.far.refs_1_, ...), custom_call_target="tpu_custom_call" | custom-call | flops 1000 | bytes 1000 | tf_op jit(solution)/shard_map/pallas_call | solution.py:46
  48.6 1.3 %collective-permute-done.19.refs_1_ = bf16[48,512]{1,0:T(8,128)(2,1)S(1)} collective-permute-done((bf16[48,512]{1,0:T(8,128)(2,1)S(1)}, bf16[48,512]{1,0:T(8,128)(2,1)S(1)}, u32[]{:S(2)}, u32[]{:S(2)}) %collective-permute-start.19) | collective-permute-done | bytes 49184 | tf_op jit(solution)/shard_map/ppermute | solution.py:33
  49.9 1.2 %collective-permute-done.20.refs_2_ = bf16[48,512]{1,0:T(8,128)(2,1)S(1)} collective-permute-done((bf16[48,512]{1,0:T(8,128)(2,1)S(1)}, bf16[48,512]{1,0:T(8,128)(2,1)S(1)}, u32[]{:S(2)}, u32[]{:S(2)}) %collective-permute-start.20) | collective-permute-done | bytes 49184 | tf_op jit(solution)/shard_map/ppermute | solution.py:33
  51.1 0.5 collective-permute-done.21.refs_3_
  51.6 1.5 %collective-permute-start.22 = (bf16[4,48,512]{2,1,0:T(8,128)(2,1)S(1)}, bf16[4,48,512]{2,1,0:T(8,128)(2,1)S(1)}, u32[]{:S(2)}, u32[]{:S(2)}) collective-permute-start(bf16[4,48,512]{2,1,0:T(8,128)(2,1)S(1)} %shard_map.91.mine), channel_id=1, source_target_pairs={{0,4},{2,6},{4,0},{6,2},{8,12},{10,14},{12,8},{14,10},{16,20},{18,... | collective-permute-start | bytes 589832 | tf_op jit(solution)/shard_map/ppermute | solution.py:33
  53.1 4.3 %collective-permute-done.25.refs_6_.refs_2_ = bf16[2,256,512]{2,1,0:T(8,128)(2,1)S(1)} collective-permute-done((bf16[2,256,512]{2,1,0:T(8,128)(2,1)S(1)}, bf16[2,256,512]{2,1,0:T(8,128)(2,1)S(1)}, u32[]{:S(2)}, u32[]{:S(2)}) %collective-permute-start.25) | collective-permute-done | bytes 524320 | tf_op jit(solution)/shard_map/ppermute | solution.py:33
  57.4 3.3 %collective-permute-done.22.side_in = bf16[4,48,512]{2,1,0:T(8,128)(2,1)S(1)} collective-permute-done((bf16[4,48,512]{2,1,0:T(8,128)(2,1)S(1)}, bf16[4,48,512]{2,1,0:T(8,128)(2,1)S(1)}, u32[]{:S(2)}, u32[]{:S(2)}) %collective-permute-start.22) | collective-permute-done | bytes 196640 | tf_op jit(solution)/shard_map/ppermute | solution.py:33
  60.8 0.5 collective-permute-start.23
  61.3 0.0 collective-permute-start.24
  61.3 1.4 %collective-permute-done.27.refs_9_.refs_5_ = bf16[2,256,512]{2,1,0:T(8,128)(2,1)S(1)} collective-permute-done((bf16[2,256,512]{2,1,0:T(8,128)(2,1)S(1)}, bf16[2,256,512]{2,1,0:T(8,128)(2,1)S(1)}, u32[]{:S(2)}, u32[]{:S(2)}) %collective-permute-start.27) | collective-permute-done | bytes 524320 | tf_op jit(solution)/shard_map/ppermute | solution.py:33
  62.7 0.6 shard_map.93
  63.3 1.6 %collective-permute-start.29 = (bf16[128,512]{1,0:T(8,128)(2,1)S(1)}, bf16[128,512]{1,0:T(8,128)(2,1)S(1)}, u32[]{:S(2)}, u32[]{:S(2)}) collective-permute-start(bf16[128,512]{1,0:T(8,128)(2,1)S(1)} %get-tuple-element.68), channel_id=1, source_target_pairs={{0,1},{1,0},{2,3},{3,2},{4,5},{5,4},{6,7},{7,6},{8,9},{9,8},{10,11... | collective-permute-start | bytes 393224 | tf_op jit(solution)/shard_map/ppermute | solution.py:33
  64.9 0.0 collective-permute-done.23.core_in
  64.9 0.0 collective-permute-done.24.diag_in
  64.9 3.9 %shard_map.92 = (bf16[128,512]{1,0:T(8,128)(2,1)S(1)}, bf16[128,512]{1,0:T(8,128)(2,1)S(1)}) custom-call(f32[8,128]{1,0:T(8,128)S(1)} %get-tuple-element.37.rate, bf16[4,48,512]{2,1,0:T(8,128)(2,1)S(1)} %shard_map.91.mine, bf16[4,48,512]{2,1,0:T(8,128)(2,1)S(1)} %collective-permute-done.22.side_in, bf16[4,48,512]{2,1,0:T(8,128)(2,1)S(1)} %collective-permute-done.23.core_in, ...), custom_call_target="tpu_custom_call" | custom-call | flops 3000000000 | bytes 4000000 | tf_op jit(solution)/shard_map/pallas_call | solution.py:46
  68.8 0.6 collective-permute-start.28
  69.4 0.8 %shard_map.94.refs_0_ = bf16[2,128,1024]{2,1,0:T(8,128)(2,1)} custom-call(bf16[128,512]{1,0:T(8,128)(2,1)S(1)} %get-tuple-element.67.own, bf16[128,512]{1,0:T(8,128)(2,1)S(1)} %collective-permute-done.29.got, f32[1,1024]{1,0:T(1,128)S(1)} %bitcast.5), custom_call_target="tpu_custom_call" | custom-call | bytes 524288 | tf_op jit(solution)/shard_map/pallas_call | solution.py:340
  70.2 3.9 %collective-permute-done.28.got = bf16[128,512]{1,0:T(8,128)(2,1)S(1)} collective-permute-done((bf16[128,512]{1,0:T(8,128)(2,1)S(1)}, bf16[128,512]{1,0:T(8,128)(2,1)S(1)}, u32[]{:S(2)}, u32[]{:S(2)}) %collective-permute-start.28) | collective-permute-done | bytes 131104 | tf_op jit(solution)/shard_map/ppermute | solution.py:33
  74.1 0.8 %shard_map.95 = bf16[2,128,1024]{2,1,0:T(8,128)(2,1)} custom-call(bf16[128,512]{1,0:T(8,128)(2,1)S(1)} %get-tuple-element.64.own, bf16[128,512]{1,0:T(8,128)(2,1)S(1)} %collective-permute-done.28.got, f32[1,1024]{1,0:T(1,128)S(1)} %bitcast.6, bf16[2,128,1024]{2,1,0:T(8,128)(2,1)} %shard_map.94.refs_0_), custom_call_target="tpu_custom_call", output_to_operand_aliasing={{}: (3, {})} | custom-call | bytes 524288 | tf_op jit(solution)/shard_map/pallas_call | solution.py:340
  (20 shorter events, 0.1 us)
Async XLA Ops:
  0.0 18.5 %collective-permute-start.7 = (bf16[2,256,512]{2,1,0:T(8,128)(2,1)}, bf16[2,256,512]{2,1,0:T(8,128)(2,1)S(1)}, u32[]{:S(2)}, u32[]{:S(2)}) collective-permute-start(bf16[2,256,512]{2,1,0:T(8,128)(2,1)} %keys.1), channel_id=1, source_target_pairs={{0,2},{2,0},{4,6},{6,4},{8,10},{10,8},{12,14},{14,12},{16,18},{18,... | collective-permute-start | bytes 1572872 | tf_op jit(solution)/shard_map/ppermute | solution.py:33
  0.5 18.1 %collective-permute-start.8 = (bf16[2,256,512]{2,1,0:T(8,128)(2,1)}, bf16[2,256,512]{2,1,0:T(8,128)(2,1)S(1)}, u32[]{:S(2)}, u32[]{:S(2)}) collective-permute-start(bf16[2,256,512]{2,1,0:T(8,128)(2,1)} %values.1), channel_id=1, source_target_pairs={{0,2},{2,0},{4,6},{6,4},{8,10},{10,8},{12,14},{14,12},{16,18},{18,... | collective-permute-start | bytes 1572872 | tf_op jit(solution)/shard_map/ppermute | solution.py:33
  0.5 5.4 %collective-permute-start = (bf16[32,768]{1,0:T(8,128)(2,1)}, bf16[32,768]{1,0:T(8,128)(2,1)S(1)}, u32[]{:S(2)}, u32[]{:S(2)}) collective-permute-start(bf16[32,768]{1,0:T(8,128)(2,1)} %bitcast.9), channel_id=1, source_target_pairs={{0,2},{2,0},{4,6},{6,4},{8,10},{10,8},{12,14},{14,12},{16,18},{18,... | collective-permute-start | bytes 147464 | tf_op jit(solution)/shard_map/ppermute | solution.py:33
  1.0 6.2 %collective-permute-start.1 = (bf16[32,768]{1,0:T(8,128)(2,1)}, bf16[32,768]{1,0:T(8,128)(2,1)S(1)}, u32[]{:S(2)}, u32[]{:S(2)}) collective-permute-start(bf16[32,768]{1,0:T(8,128)(2,1)} %bitcast.10), channel_id=1, source_target_pairs={{0,16},{2,18},{4,20},{6,22},{8,24},{10,26},{12,28},{14,30},{16,0},... | collective-permute-start | bytes 147464 | tf_op jit(solution)/shard_map/ppermute | solution.py:33
  4.6 6.4 %collective-permute-start.2 = (bf16[32,768]{1,0:T(8,128)(2,1)}, bf16[32,768]{1,0:T(8,128)(2,1)S(1)}, u32[]{:S(2)}, u32[]{:S(2)}) collective-permute-start(bf16[32,768]{1,0:T(8,128)(2,1)} %bitcast.11), channel_id=1, source_target_pairs={{0,24},{2,26},{4,28},{6,30},{8,16},{10,18},{12,20},{14,22},{16,8},... | collective-permute-start | bytes 147464 | tf_op jit(solution)/shard_map/ppermute | solution.py:33
  5.9 5.2 %collective-permute-start.3 = (bf16[32,768]{1,0:T(8,128)(2,1)}, bf16[32,768]{1,0:T(8,128)(2,1)S(1)}, u32[]{:S(2)}, u32[]{:S(2)}) collective-permute-start(bf16[32,768]{1,0:T(8,128)(2,1)} %bitcast.12), channel_id=1, source_target_pairs={{0,8},{2,10},{4,12},{6,14},{8,0},{10,2},{12,4},{14,6},{16,24},{18,... | collective-permute-start | bytes 147464 | tf_op jit(solution)/shard_map/ppermute | solution.py:33
  11.1 5.7 %collective-permute-start.4 = (bf16[4,32,768]{2,1,0:T(8,128)(2,1)S(1)}, bf16[4,32,768]{2,1,0:T(8,128)(2,1)S(1)}, u32[]{:S(2)}, u32[]{:S(2)}) collective-permute-start(bf16[4,32,768]{2,1,0:T(8,128)(2,1)S(1)} %shard_map.83.mine), channel_id=1, source_target_pairs={{0,4},{2,6},{4,0},{6,2},{8,12},{10,14},{12,8},{14,10},{16,20},{18,... | collective-permute-start | bytes 589832 | tf_op jit(solution)/shard_map/ppermute | solution.py:33
  12.6 16.0 %collective-permute-start.15 = (bf16[2,256,512]{2,1,0:T(8,128)(2,1)}, bf16[2,256,512]{2,1,0:T(8,128)(2,1)S(1)}, u32[]{:S(2)}, u32[]{:S(2)}) collective-permute-start(bf16[2,256,512]{2,1,0:T(8,128)(2,1)} %keys.1), channel_id=1, source_target_pairs={{0,8},{2,10},{4,12},{6,14},{8,16},{10,18},{12,20},{14,22},{16,24},... | collective-permute-start | bytes 1572872 | tf_op jit(solution)/shard_map/ppermute | solution.py:366
  12.8 4.1 %collective-permute-start.9 = (f32[1,256]{1,0:T(1,128)}, f32[1,256]{1,0:T(1,128)S(1)}, u32[]{:S(2)}, u32[]{:S(2)}) collective-permute-start(f32[1,256]{1,0:T(1,128)} %bitcast.7), channel_id=1, source_target_pairs={{0,2},{2,0},{4,6},{6,4},{8,10},{10,8},{12,14},{14,12},{16,18},{18,... | collective-permute-start | bytes 3080 | tf_op jit(solution)/shard_map/ppermute | solution.py:33
  13.5 1.0 %copy-start.1 = (bf16[2,256,512]{2,1,0:T(8,128)(2,1)S(1)}, bf16[2,256,512]{2,1,0:T(8,128)(2,1)}, u32[]{:S(2)}) copy-start(bf16[2,256,512]{2,1,0:T(8,128)(2,1)} %keys.1) | copy-start | bytes 1572868
  14.5 0.7 copy-start.4
  16.8 1.4 %collective-permute-start.5 = (bf16[4,32,768]{2,1,0:T(8,128)(2,1)S(1)}, bf16[4,32,768]{2,1,0:T(8,128)(2,1)S(1)}, u32[]{:S(2)}, u32[]{:S(2)}) collective-permute-start(bf16[4,32,768]{2,1,0:T(8,128)(2,1)S(1)} %shard_map.83.mine), channel_id=1, source_target_pairs={{0,2},{2,0},{4,6},{6,4},{8,10},{10,8},{12,14},{14,12},{16,18},{18,... | collective-permute-start | bytes 589832 | tf_op jit(solution)/shard_map/ppermute | solution.py:33
  16.9 1.6 %collective-permute-start.6 = (bf16[4,32,768]{2,1,0:T(8,128)(2,1)S(1)}, bf16[4,32,768]{2,1,0:T(8,128)(2,1)S(1)}, u32[]{:S(2)}, u32[]{:S(2)}) collective-permute-start(bf16[4,32,768]{2,1,0:T(8,128)(2,1)S(1)} %collective-permute-done.4.other), channel_id=1, source_target_pairs={{0,2},{2,0},{4,6},{6,4},{8,10},{10,8},{12,14},{14,12},{16,18},{18,... | collective-permute-start | bytes 589832 | tf_op jit(solution)/shard_map/ppermute | solution.py:33
  19.7 8.9 %collective-permute-start.10 = (bf16[192,512]{1,0:T(8,128)(2,1)S(1)}, bf16[192,512]{1,0:T(8,128)(2,1)S(1)}, u32[]{:S(2)}, u32[]{:S(2)}) collective-permute-start(bf16[192,512]{1,0:T(8,128)(2,1)S(1)} %get-tuple-element.44), channel_id=1, source_target_pairs={{0,4},{2,6},{4,0},{6,2},{8,12},{10,14},{12,8},{14,10},{16,20},{18,... | collective-permute-start | bytes 589832 | tf_op jit(solution)/shard_map/ppermute | solution.py:33
  21.3 18.7 %collective-permute-start.11 = (bf16[2,256,512]{2,1,0:T(8,128)(2,1)}, bf16[2,256,512]{2,1,0:T(8,128)(2,1)S(1)}, u32[]{:S(2)}, u32[]{:S(2)}) collective-permute-start(bf16[2,256,512]{2,1,0:T(8,128)(2,1)} %values.1), channel_id=1, source_target_pairs={{0,8},{2,10},{4,12},{6,14},{8,16},{10,18},{12,20},{14,22},{16,24},... | collective-permute-start | bytes 1572872 | tf_op jit(solution)/shard_map/ppermute | solution.py:366
  28.7 13.4 %collective-permute-start.16 = (bf16[2,256,512]{2,1,0:T(8,128)(2,1)S(1)}, bf16[2,256,512]{2,1,0:T(8,128)(2,1)S(1)}, u32[]{:S(2)}, u32[]{:S(2)}) collective-permute-start(bf16[2,256,512]{2,1,0:T(8,128)(2,1)S(1)} %shard_map.89), channel_id=1, source_target_pairs={{0,4},{2,6},{4,0},{6,2},{8,12},{10,14},{12,8},{14,10},{16,20},{18,... | collective-permute-start | bytes 1572872 | tf_op jit(solution)/shard_map/ppermute | solution.py:33
  29.3 17.8 %copy-start = (bf16[2,256,512]{2,1,0:T(8,128)(2,1)S(1)}, bf16[2,256,512]{2,1,0:T(8,128)(2,1)}, u32[]{:S(2)}) copy-start(bf16[2,256,512]{2,1,0:T(8,128)(2,1)} %refs_0_.1) | copy-start | bytes 1572868
  29.4 12.6 %collective-permute-start.12 = (bf16[48,512]{1,0:T(8,128)(2,1)S(1)}, bf16[48,512]{1,0:T(8,128)(2,1)S(1)}, u32[]{:S(2)}, u32[]{:S(2)}) collective-permute-start(bf16[48,512]{1,0:T(8,128)(2,1)S(1)} %get-tuple-element.51), channel_id=1, source_target_pairs={{0,16},{2,18},{4,20},{6,22},{8,24},{10,26},{12,28},{14,30},{16,0},... | collective-permute-start | bytes 147464 | tf_op jit(solution)/shard_map/ppermute | solution.py:33
  31.7 10.3 %collective-permute-start.13 = (bf16[48,512]{1,0:T(8,128)(2,1)S(1)}, bf16[48,512]{1,0:T(8,128)(2,1)S(1)}, u32[]{:S(2)}, u32[]{:S(2)}) collective-permute-start(bf16[48,512]{1,0:T(8,128)(2,1)S(1)} %get-tuple-element.52), channel_id=1, source_target_pairs={{0,24},{2,26},{4,28},{6,30},{8,16},{10,18},{12,20},{14,22},{16,8},... | collective-permute-start | bytes 147464 | tf_op jit(solution)/shard_map/ppermute | solution.py:33
  32.7 9.4 %collective-permute-start.14 = (bf16[48,512]{1,0:T(8,128)(2,1)S(1)}, bf16[48,512]{1,0:T(8,128)(2,1)S(1)}, u32[]{:S(2)}, u32[]{:S(2)}) collective-permute-start(bf16[48,512]{1,0:T(8,128)(2,1)S(1)} %get-tuple-element.53), channel_id=1, source_target_pairs={{0,8},{2,10},{4,12},{6,14},{8,0},{10,2},{12,4},{14,6},{16,24},{18,... | collective-permute-start | bytes 147464 | tf_op jit(solution)/shard_map/ppermute | solution.py:33
  42.0 20.6 %copy-start.2 = (bf16[2,256,512]{2,1,0:T(8,128)(2,1)S(1)}, bf16[2,256,512]{2,1,0:T(8,128)(2,1)}, u32[]{:S(2)}) copy-start(bf16[2,256,512]{2,1,0:T(8,128)(2,1)} %refs_9_.1) | copy-start | bytes 1572868
  42.1 5.0 %collective-permute-start.17 = (bf16[2,256,512]{2,1,0:T(8,128)(2,1)S(1)}, bf16[2,256,512]{2,1,0:T(8,128)(2,1)S(1)}, u32[]{:S(2)}, u32[]{:S(2)}) collective-permute-start(bf16[2,256,512]{2,1,0:T(8,128)(2,1)S(1)} %collective-permute-done.15.far.refs_1_), channel_id=1, source_target_pairs={{0,2},{2,0},{4,6},{6,4},{8,10},{10,8},{12,14},{14,12},{16,18},{18,... | collective-permute-start | bytes 1572872 | tf_op jit(solution)/shard_map/ppermute | solution.py:33
  42.2 4.9 %collective-permute-start.18 = (bf16[2,256,512]{2,1,0:T(8,128)(2,1)S(1)}, bf16[2,256,512]{2,1,0:T(8,128)(2,1)S(1)}, u32[]{:S(2)}, u32[]{:S(2)}) collective-permute-start(bf16[2,256,512]{2,1,0:T(8,128)(2,1)S(1)} %collective-permute-done.16.refs_2_), channel_id=1, source_target_pairs={{0,2},{2,0},{4,6},{6,4},{8,10},{10,8},{12,14},{14,12},{16,18},{18,... | collective-permute-start | bytes 1572872 | tf_op jit(solution)/shard_map/ppermute | solution.py:33
  42.6 14.8 %collective-permute-start.25 = (bf16[2,256,512]{2,1,0:T(8,128)(2,1)S(1)}, bf16[2,256,512]{2,1,0:T(8,128)(2,1)S(1)}, u32[]{:S(2)}, u32[]{:S(2)}) collective-permute-start(bf16[2,256,512]{2,1,0:T(8,128)(2,1)S(1)} %shard_map.86), channel_id=1, source_target_pairs={{0,4},{2,6},{4,0},{6,2},{8,12},{10,14},{12,8},{14,10},{16,20},{18,... | collective-permute-start | bytes 1572872 | tf_op jit(solution)/shard_map/ppermute | solution.py:33
  43.2 6.7 %collective-permute-start.19 = (bf16[48,512]{1,0:T(8,128)(2,1)S(1)}, bf16[48,512]{1,0:T(8,128)(2,1)S(1)}, u32[]{:S(2)}, u32[]{:S(2)}) collective-permute-start(bf16[48,512]{1,0:T(8,128)(2,1)S(1)} %shard_map.88.refs_0_), channel_id=1, source_target_pairs={{0,16},{2,18},{4,20},{6,22},{8,24},{10,26},{12,28},{14,30},{16,0},... | collective-permute-start | bytes 147464 | tf_op jit(solution)/shard_map/ppermute | solution.py:33
  45.0 6.0 %collective-permute-start.20 = (bf16[48,512]{1,0:T(8,128)(2,1)S(1)}, bf16[48,512]{1,0:T(8,128)(2,1)S(1)}, u32[]{:S(2)}, u32[]{:S(2)}) collective-permute-start(bf16[48,512]{1,0:T(8,128)(2,1)S(1)} %shard_map.88.refs_0_), channel_id=1, source_target_pairs={{0,24},{2,26},{4,28},{6,30},{8,16},{10,18},{12,20},{14,22},{16,8},... | collective-permute-start | bytes 147464 | tf_op jit(solution)/shard_map/ppermute | solution.py:33
  47.1 4.5 %collective-permute-start.21 = (bf16[48,512]{1,0:T(8,128)(2,1)S(1)}, bf16[48,512]{1,0:T(8,128)(2,1)S(1)}, u32[]{:S(2)}, u32[]{:S(2)}) collective-permute-start(bf16[48,512]{1,0:T(8,128)(2,1)S(1)} %shard_map.88.refs_0_), channel_id=1, source_target_pairs={{0,8},{2,10},{4,12},{6,14},{8,0},{10,2},{12,4},{14,6},{16,24},{18,... | collective-permute-start | bytes 147464 | tf_op jit(solution)/shard_map/ppermute | solution.py:33
  51.6 9.2 %collective-permute-start.22 = (bf16[4,48,512]{2,1,0:T(8,128)(2,1)S(1)}, bf16[4,48,512]{2,1,0:T(8,128)(2,1)S(1)}, u32[]{:S(2)}, u32[]{:S(2)}) collective-permute-start(bf16[4,48,512]{2,1,0:T(8,128)(2,1)S(1)} %shard_map.91.mine), channel_id=1, source_target_pairs={{0,4},{2,6},{4,0},{6,2},{8,12},{10,14},{12,8},{14,10},{16,20},{18,... | collective-permute-start | bytes 589832 | tf_op jit(solution)/shard_map/ppermute | solution.py:33
  53.1 8.2 %collective-permute-start.26 = (bf16[2,256,512]{2,1,0:T(8,128)(2,1)S(1)}, bf16[2,256,512]{2,1,0:T(8,128)(2,1)S(1)}, u32[]{:S(2)}, u32[]{:S(2)}) collective-permute-start(bf16[2,256,512]{2,1,0:T(8,128)(2,1)S(1)} %collective-permute-done.11.far.refs_5_.refs_1_), channel_id=1, source_target_pairs={{0,2},{2,0},{4,6},{6,4},{8,10},{10,8},{12,14},{14,12},{16,18},{18,... | collective-permute-start | bytes 1572872 | tf_op jit(solution)/shard_map/ppermute | solution.py:33
  60.8 1.9 %collective-permute-start.27 = (bf16[2,256,512]{2,1,0:T(8,128)(2,1)S(1)}, bf16[2,256,512]{2,1,0:T(8,128)(2,1)S(1)}, u32[]{:S(2)}, u32[]{:S(2)}) collective-permute-start(bf16[2,256,512]{2,1,0:T(8,128)(2,1)S(1)} %collective-permute-done.25.refs_6_.refs_2_), channel_id=1, source_target_pairs={{0,2},{2,0},{4,6},{6,4},{8,10},{10,8},{12,14},{14,12},{16,18},{18,... | collective-permute-start | bytes 1572872 | tf_op jit(solution)/shard_map/ppermute | solution.py:33
  60.8 4.1 %collective-permute-start.23 = (bf16[4,48,512]{2,1,0:T(8,128)(2,1)S(1)}, bf16[4,48,512]{2,1,0:T(8,128)(2,1)S(1)}, u32[]{:S(2)}, u32[]{:S(2)}) collective-permute-start(bf16[4,48,512]{2,1,0:T(8,128)(2,1)S(1)} %shard_map.91.mine), channel_id=1, source_target_pairs={{0,2},{2,0},{4,6},{6,4},{8,10},{10,8},{12,14},{14,12},{16,18},{18,... | collective-permute-start | bytes 589832 | tf_op jit(solution)/shard_map/ppermute | solution.py:33
  61.3 3.6 %collective-permute-start.24 = (bf16[4,48,512]{2,1,0:T(8,128)(2,1)S(1)}, bf16[4,48,512]{2,1,0:T(8,128)(2,1)S(1)}, u32[]{:S(2)}, u32[]{:S(2)}) collective-permute-start(bf16[4,48,512]{2,1,0:T(8,128)(2,1)S(1)} %collective-permute-done.22.side_in), channel_id=1, source_target_pairs={{0,2},{2,0},{4,6},{6,4},{8,10},{10,8},{12,14},{14,12},{16,18},{18,... | collective-permute-start | bytes 589832 | tf_op jit(solution)/shard_map/ppermute | solution.py:33
  63.3 6.1 %collective-permute-start.29 = (bf16[128,512]{1,0:T(8,128)(2,1)S(1)}, bf16[128,512]{1,0:T(8,128)(2,1)S(1)}, u32[]{:S(2)}, u32[]{:S(2)}) collective-permute-start(bf16[128,512]{1,0:T(8,128)(2,1)S(1)} %get-tuple-element.68), channel_id=1, source_target_pairs={{0,1},{1,0},{2,3},{3,2},{4,5},{5,4},{6,7},{7,6},{8,9},{9,8},{10,11... | collective-permute-start | bytes 393224 | tf_op jit(solution)/shard_map/ppermute | solution.py:33
  64.9 4.5 %copy-start.3 = (f32[1024]{0:T(1024)S(1)}, f32[1024]{0:T(1024)}, u32[]{:S(2)}) copy-start(f32[1024]{0:T(1024)} %param.15) | copy-start | bytes 12292
  68.8 5.3 %collective-permute-start.28 = (bf16[128,512]{1,0:T(8,128)(2,1)S(1)}, bf16[128,512]{1,0:T(8,128)(2,1)S(1)}, u32[]{:S(2)}, u32[]{:S(2)}) collective-permute-start(bf16[128,512]{1,0:T(8,128)(2,1)S(1)} %get-tuple-element.65), channel_id=1, source_target_pairs={{0,1},{1,0},{2,3},{3,2},{4,5},{5,4},{6,7},{7,6},{8,9},{9,8},{10,11... | collective-permute-start | bytes 393224 | tf_op jit(solution)/shard_map/ppermute | solution.py:33

commit v9 on v7

--- a/solution.py
+++ b/solution.py
@@ -420,7 +420,7 @@
     partial = [swapped(parts[m], 4 * m) for m in range(1, planes)]
     ring = [(i, (i + reach) % count) for i in everyone]
     far_keys = sent(after(keys, *arrived), ring)
-    far_values = sent(after(values, send), ring)
+    far_values = sent(after(values, other_w), ring)
     near_keys = swapped(picked(own_keys, after(far_keys, got)), 2)
     pick_values = picked(own_values, after(far_values, parts[0]))
     near_values = swapped(pick_values, 2)

time: 74.7 us -> 74.7 us (level)
  no operation moved by 1% of the time
where the time goes in v9:
time: 74.7 us; the launch traced here: 74.5 us
  waiting for transfers between devices  37 us (50%)
  starting transfers between devices  24.8 us (33%)
  Pallas kernels  10.1 us (14%)
  local copies, waits for them, and re-layouts  1.73 us (2%)
  between operations  0.79 us (1%)
    ppermute x28, waiting for transfers between devices, swapped(): return lax.ppermute(value, axis, [(i, i ^ mask) for i in range(count)])  24.5 us
    ppermute x28, starting transfers between devices, swapped(): return lax.ppermute(value, axis, [(i, i ^ mask) for i in range(count)])  23.3 us
    ppermute x2, waiting for transfers between devices, sent(): return lax.ppermute(value, axis, pairs)  12.4 us
    pallas_call x10, Pallas kernels, call(): pl.pallas_call(body, out_shape=outs, in_specs=[vmem_spec()] * len(args),...  8.44 us
    unnamed x10, local copies, waits for them, and re-layouts  1.73 us
    pallas_call x2, Pallas kernels, finished(): pl.pallas_call(functools.partial(norm_body, group), out_shape=jax.ShapeDt...  1.68 us
    ppermute x2, starting transfers between devices, sent(): return lax.ppermute(value, axis, pairs)  1.53 us
  transfers between devices with their start and end apart: 30, of which 16 were waited for; matrix products, arithmetic and copies ran while one was open for 0% of the time, Pallas kernels for 12%

profile of v9, /device:TPU:0, one launch (start us, length us, event | category | flops | bytes accessed | tf_op | source)
XLA Modules:
  0.0 74.5 jit_solution(7372820920843458773)
XLA Ops:
  0.0 0.5 collective-permute-start.7
  0.5 0.1 collective-permute-start.8
  0.5 0.5 collective-permute-start
  1.0 3.6 %collective-permute-start.1 = (bf16[32,768]{1,0:T(8,128)(2,1)}, bf16[32,768]{1,0:T(8,128)(2,1)S(1)}, u32[]{:S(2)}, u32[]{:S(2)}) collective-permute-start(bf16[32,768]{1,0:T(8,128)(2,1)} %bitcast.10), channel_id=1, source_target_pairs={{0,16},{2,18},{4,20},{6,22},{8,24},{10,26},{12,28},{14,30},{16,0},... | collective-permute-start | bytes 147464 | tf_op jit(solution)/shard_map/ppermute | solution.py:33
  4.6 1.3 %collective-permute-start.2 = (bf16[32,768]{1,0:T(8,128)(2,1)}, bf16[32,768]{1,0:T(8,128)(2,1)S(1)}, u32[]{:S(2)}, u32[]{:S(2)}) collective-permute-start(bf16[32,768]{1,0:T(8,128)(2,1)} %bitcast.11), channel_id=1, source_target_pairs={{0,24},{2,26},{4,28},{6,30},{8,16},{10,18},{12,20},{14,22},{16,8},... | collective-permute-start | bytes 147464 | tf_op jit(solution)/shard_map/ppermute | solution.py:33
  5.9 0.2 collective-permute-start.3
  6.1 1.0 %collective-permute-done.1.refs_1_ = bf16[32,768]{1,0:T(8,128)(2,1)S(1)} collective-permute-done((bf16[32,768]{1,0:T(8,128)(2,1)}, bf16[32,768]{1,0:T(8,128)(2,1)S(1)}, u32[]{:S(2)}, u32[]{:S(2)}) %collective-permute-start.1) | collective-permute-done | bytes 49184 | tf_op jit(solution)/shard_map/ppermute | solution.py:33
  7.2 3.8 %collective-permute-done.2.refs_2_ = bf16[32,768]{1,0:T(8,128)(2,1)S(1)} collective-permute-done((bf16[32,768]{1,0:T(8,128)(2,1)}, bf16[32,768]{1,0:T(8,128)(2,1)S(1)}, u32[]{:S(2)}, u32[]{:S(2)}) %collective-permute-start.2) | collective-permute-done | bytes 49184 | tf_op jit(solution)/shard_map/ppermute | solution.py:33
  11.0 0.1 collective-permute-done.3.refs_3_
  11.1 1.6 %collective-permute-start.4 = (bf16[4,32,768]{2,1,0:T(8,128)(2,1)S(1)}, bf16[4,32,768]{2,1,0:T(8,128)(2,1)S(1)}, u32[]{:S(2)}, u32[]{:S(2)}) collective-permute-start(bf16[4,32,768]{2,1,0:T(8,128)(2,1)S(1)} %shard_map.83.mine), channel_id=1, source_target_pairs={{0,4},{2,6},{4,0},{6,2},{8,12},{10,14},{12,8},{14,10},{16,20},{18,... | collective-permute-start | bytes 589832 | tf_op jit(solution)/shard_map/ppermute | solution.py:33
  12.6 0.2 collective-permute-start.15
  12.8 0.0 collective-permute-start.9
  13.5 1.0 %copy-done.1 = bf16[2,256,512]{2,1,0:T(8,128)(2,1)S(1)} copy-done((bf16[2,256,512]{2,1,0:T(8,128)(2,1)S(1)}, bf16[2,256,512]{2,1,0:T(8,128)(2,1)}, u32[]{:S(2)}) %copy-start.1) | copy-done | bytes 524312
  14.5 0.7 copy-done.4
  15.2 1.1 %shard_map.82 = (bf16[2,256,512]{2,1,0:T(8,128)(2,1)S(1)}, bf16[2,256,512]{2,1,0:T(8,128)(2,1)S(1)}, f32[1,256]{1,0:T(1,128)S(1)}, f32[8,128]{1,0:T(8,128)S(1)}) custom-call(bf16[2,256,512]{2,1,0:T(8,128)(2,1)S(1)} %copy-done.1, bf16[2,256,512]{2,1,0:T(8,128)(2,1)} %values.1, f32[1,256]{1,0:T(1,128)S(1)} %bitcast.8, f32[1,1]{1,0:T(1,128)} %bitcast.4.rate), custom_call_target="tpu_custom_call" | custom-call | tf_op jit(solution)/shard_map/pallas_call | solution.py:46
  16.3 0.5 collective-permute-done.4.other
  16.8 0.1 collective-permute-start.5
  16.9 0.0 collective-permute-done.9.refs_5_
  16.9 0.4 collective-permute-start.6
  17.3 0.9 %collective-permute-done.5.beside_mine = bf16[4,32,768]{2,1,0:T(8,128)(2,1)S(1)} collective-permute-done((bf16[4,32,768]{2,1,0:T(8,128)(2,1)S(1)}, bf16[4,32,768]{2,1,0:T(8,128)(2,1)S(1)}, u32[]{:S(2)}, u32[]{:S(2)}) %collective-permute-start.5) | collective-permute-done | bytes 196640 | tf_op jit(solution)/shard_map/ppermute | solution.py:33
  18.3 0.3 collective-permute-done.6.beside_other
  18.5 0.0 collective-permute-done.7.refs_3_
  18.5 0.0 collective-permute-done.8.refs_4_.refs_7_.refs_3_
  18.5 1.2 %shard_map.84 = (bf16[192,512]{1,0:T(8,128)(2,1)S(1)}, f32[192,512]{1,0:T(8,128)S(1)}, bf16[512,768]{1,0:T(8,128)(2,1)S(1)}) custom-call(bf16[4,32,768]{2,1,0:T(8,128)(2,1)S(1)} %shard_map.83.mine, bf16[4,32,768]{2,1,0:T(8,128)(2,1)S(1)} %collective-permute-done.4.other, bf16[4,32,768]{2,1,0:T(8,128)(2,1)S(1)} %collective-permute-done.5.beside_mine, ...), custom_call_target="tpu_custom_call" | custom-call | flops 402653184 | bytes 2097152 | tf_op jit(solution)/shard_map/pallas_call | solution.py:46
  19.7 1.6 %collective-permute-start.10 = (bf16[192,512]{1,0:T(8,128)(2,1)S(1)}, bf16[192,512]{1,0:T(8,128)(2,1)S(1)}, u32[]{:S(2)}, u32[]{:S(2)}) collective-permute-start(bf16[192,512]{1,0:T(8,128)(2,1)S(1)} %get-tuple-element.44), channel_id=1, source_target_pairs={{0,4},{2,6},{4,0},{6,2},{8,12},{10,14},{12,8},{14,10},{16,20},{18,... | collective-permute-start | bytes 589832 | tf_op jit(solution)/shard_map/ppermute | solution.py:33
  21.3 1.3 %collective-permute-start.11 = (bf16[2,256,512]{2,1,0:T(8,128)(2,1)}, bf16[2,256,512]{2,1,0:T(8,128)(2,1)S(1)}, u32[]{:S(2)}, u32[]{:S(2)}) collective-permute-start(bf16[2,256,512]{2,1,0:T(8,128)(2,1)} %values.1), channel_id=1, source_target_pairs={{0,8},{2,10},{4,12},{6,14},{8,16},{10,18},{12,20},{14,22},{16,24},... | collective-permute-start | bytes 1572872 | tf_op jit(solution)/shard_map/ppermute | solution.py:361
  22.6 6.0 %collective-permute-done.15.far.refs_1_ = bf16[2,256,512]{2,1,0:T(8,128)(2,1)S(1)} collective-permute-done((bf16[2,256,512]{2,1,0:T(8,128)(2,1)}, bf16[2,256,512]{2,1,0:T(8,128)(2,1)S(1)}, u32[]{:S(2)}, u32[]{:S(2)}) %collective-permute-start.15) | collective-permute-done | bytes 524320 | tf_op jit(solution)/shard_map/ppermute | solution.py:361
  28.6 0.1 shard_map.89
  28.7 0.6 collective-permute-start.16
  29.3 0.1 shard_map.85
  29.4 2.4 %collective-permute-start.12 = (bf16[48,512]{1,0:T(8,128)(2,1)S(1)}, bf16[48,512]{1,0:T(8,128)(2,1)S(1)}, u32[]{:S(2)}, u32[]{:S(2)}) collective-permute-start(bf16[48,512]{1,0:T(8,128)(2,1)S(1)} %get-tuple-element.51), channel_id=1, source_target_pairs={{0,16},{2,18},{4,20},{6,22},{8,24},{10,26},{12,28},{14,30},{16,0},... | collective-permute-start | bytes 147464 | tf_op jit(solution)/shard_map/ppermute | solution.py:33
  31.7 0.9 %collective-permute-start.13 = (bf16[48,512]{1,0:T(8,128)(2,1)S(1)}, bf16[48,512]{1,0:T(8,128)(2,1)S(1)}, u32[]{:S(2)}, u32[]{:S(2)}) collective-permute-start(bf16[48,512]{1,0:T(8,128)(2,1)S(1)} %get-tuple-element.52), channel_id=1, source_target_pairs={{0,24},{2,26},{4,28},{6,30},{8,16},{10,18},{12,20},{14,22},{16,8},... | collective-permute-start | bytes 147464 | tf_op jit(solution)/shard_map/ppermute | solution.py:33
  32.7 0.5 collective-permute-start.14
  33.1 0.4 shard_map.87
  33.6 6.4 %collective-permute-done.11.far.refs_5_.refs_1_ = bf16[2,256,512]{2,1,0:T(8,128)(2,1)S(1)} collective-permute-done((bf16[2,256,512]{2,1,0:T(8,128)(2,1)}, bf16[2,256,512]{2,1,0:T(8,128)(2,1)S(1)}, u32[]{:S(2)}, u32[]{:S(2)}) %collective-permute-start.11) | collective-permute-done | bytes 524320 | tf_op jit(solution)/shard_map/ppermute | solution.py:361
  40.0 0.1 shard_map.86
  40.1 2.0 %collective-permute-done.12.refs_0_ = bf16[48,512]{1,0:T(8,128)(2,1)S(1)} collective-permute-done((bf16[48,512]{1,0:T(8,128)(2,1)S(1)}, bf16[48,512]{1,0:T(8,128)(2,1)S(1)}, u32[]{:S(2)}, u32[]{:S(2)}) %collective-permute-start.12) | collective-permute-done | bytes 49184 | tf_op jit(solution)/shard_map/ppermute | solution.py:33
  42.0 0.0 collective-permute-done.13.refs_1_
  42.0 0.0 collective-permute-done.14.refs_2_
  42.0 0.0 copy-start.2
  42.1 0.1 collective-permute-start.17
  42.1 0.0 collective-permute-done.16.refs_2_
  42.2 0.5 collective-permute-start.18
  42.6 0.5 collective-permute-start.25
  43.2 1.8 %collective-permute-start.19 = (bf16[48,512]{1,0:T(8,128)(2,1)S(1)}, bf16[48,512]{1,0:T(8,128)(2,1)S(1)}, u32[]{:S(2)}, u32[]{:S(2)}) collective-permute-start(bf16[48,512]{1,0:T(8,128)(2,1)S(1)} %shard_map.88.refs_0_), channel_id=1, source_target_pairs={{0,16},{2,18},{4,20},{6,22},{8,24},{10,26},{12,28},{14,30},{16,0},... | collective-permute-start | bytes 147464 | tf_op jit(solution)/shard_map/ppermute | solution.py:33
  45.0 2.0 %collective-permute-start.20 = (bf16[48,512]{1,0:T(8,128)(2,1)S(1)}, bf16[48,512]{1,0:T(8,128)(2,1)S(1)}, u32[]{:S(2)}, u32[]{:S(2)}) collective-permute-start(bf16[48,512]{1,0:T(8,128)(2,1)S(1)} %shard_map.88.refs_0_), channel_id=1, source_target_pairs={{0,24},{2,26},{4,28},{6,30},{8,16},{10,18},{12,20},{14,22},{16,8},... | collective-permute-start | bytes 147464 | tf_op jit(solution)/shard_map/ppermute | solution.py:33
  47.1 0.0 collective-permute-done.18.refs_5_
  47.1 1.5 %shard_map.90 = (bf16[2,5,256,256]{3,2,1,0:T(8,128)(2,1)S(1)}, f32[2,256,1]{2,1,0:T(8,128)S(1)}, f32[256,512]{1,0:T(8,128)S(1)}) custom-call(bf16[2,256,512]{2,1,0:T(8,128)(2,1)S(1)} %copy-done, bf16[2,256,512]{2,1,0:T(8,128)(2,1)S(1)} %get-tuple-element.39.refs_0_.own, bf16[2,256,512]{2,1,0:T(8,128)(2,1)S(1)} %collective-permute-done.15.far.refs_1_, ...), custom_call_target="tpu_custom_call" | custom-call | flops 1000 | bytes 1000 | tf_op jit(solution)/shard_map/pallas_call | solution.py:46
  48.6 1.3 %collective-permute-done.19.refs_1_ = bf16[48,512]{1,0:T(8,128)(2,1)S(1)} collective-permute-done((bf16[48,512]{1,0:T(8,128)(2,1)S(1)}, bf16[48,512]{1,0:T(8,128)(2,1)S(1)}, u32[]{:S(2)}, u32[]{:S(2)}) %collective-permute-start.19) | collective-permute-done | bytes 49184 | tf_op jit(solution)/shard_map/ppermute | solution.py:33
  49.9 1.2 %collective-permute-done.20.refs_2_ = bf16[48,512]{1,0:T(8,128)(2,1)S(1)} collective-permute-done((bf16[48,512]{1,0:T(8,128)(2,1)S(1)}, bf16[48,512]{1,0:T(8,128)(2,1)S(1)}, u32[]{:S(2)}, u32[]{:S(2)}) %collective-permute-start.20) | collective-permute-done | bytes 49184 | tf_op jit(solution)/shard_map/ppermute | solution.py:33
  51.1 0.5 collective-permute-done.21.refs_3_
  51.6 1.5 %collective-permute-start.22 = (bf16[4,48,512]{2,1,0:T(8,128)(2,1)S(1)}, bf16[4,48,512]{2,1,0:T(8,128)(2,1)S(1)}, u32[]{:S(2)}, u32[]{:S(2)}) collective-permute-start(bf16[4,48,512]{2,1,0:T(8,128)(2,1)S(1)} %shard_map.91.mine), channel_id=1, source_target_pairs={{0,4},{2,6},{4,0},{6,2},{8,12},{10,14},{12,8},{14,10},{16,20},{18,... | collective-permute-start | bytes 589832 | tf_op jit(solution)/shard_map/ppermute | solution.py:33
  53.1 4.3 %collective-permute-done.25.refs_6_.refs_2_ = bf16[2,256,512]{2,1,0:T(8,128)(2,1)S(1)} collective-permute-done((bf16[2,256,512]{2,1,0:T(8,128)(2,1)S(1)}, bf16[2,256,512]{2,1,0:T(8,128)(2,1)S(1)}, u32[]{:S(2)}, u32[]{:S(2)}) %collective-permute-start.25) | collective-permute-done | bytes 524320 | tf_op jit(solution)/shard_map/ppermute | solution.py:33
  57.4 3.3 %collective-permute-done.22.side_in = bf16[4,48,512]{2,1,0:T(8,128)(2,1)S(1)} collective-permute-done((bf16[4,48,512]{2,1,0:T(8,128)(2,1)S(1)}, bf16[4,48,512]{2,1,0:T(8,128)(2,1)S(1)}, u32[]{:S(2)}, u32[]{:S(2)}) %collective-permute-start.22) | collective-permute-done | bytes 196640 | tf_op jit(solution)/shard_map/ppermute | solution.py:33
  60.8 0.5 collective-permute-start.23
  61.3 0.0 collective-permute-start.24
  61.3 1.4 %collective-permute-done.27.refs_9_.refs_5_ = bf16[2,256,512]{2,1,0:T(8,128)(2,1)S(1)} collective-permute-done((bf16[2,256,512]{2,1,0:T(8,128)(2,1)S(1)}, bf16[2,256,512]{2,1,0:T(8,128)(2,1)S(1)}, u32[]{:S(2)}, u32[]{:S(2)}) %collective-permute-start.27) | collective-permute-done | bytes 524320 | tf_op jit(solution)/shard_map/ppermute | solution.py:33
  62.7 0.6 shard_map.93
  63.3 1.6 %collective-permute-start.29 = (bf16[128,512]{1,0:T(8,128)(2,1)S(1)}, bf16[128,512]{1,0:T(8,128)(2,1)S(1)}, u32[]{:S(2)}, u32[]{:S(2)}) collective-permute-start(bf16[128,512]{1,0:T(8,128)(2,1)S(1)} %get-tuple-element.68), channel_id=1, source_target_pairs={{0,1},{1,0},{2,3},{3,2},{4,5},{5,4},{6,7},{7,6},{8,9},{9,8},{10,11... | collective-permute-start | bytes 393224 | tf_op jit(solution)/shard_map/ppermute | solution.py:33
  64.9 3.4 %shard_map.92 = (bf16[128,512]{1,0:T(8,128)(2,1)S(1)}, bf16[128,512]{1,0:T(8,128)(2,1)S(1)}) custom-call(f32[8,128]{1,0:T(8,128)S(1)} %get-tuple-element.37.rate, bf16[4,48,512]{2,1,0:T(8,128)(2,1)S(1)} %shard_map.91.mine, bf16[4,48,512]{2,1,0:T(8,128)(2,1)S(1)} %collective-permute-done.22.side_in, bf16[4,48,512]{2,1,0:T(8,128)(2,1)S(1)} %collective-permute-done.23.core_in, ...), custom_call_target="tpu_custom_call" | custom-call | flops 3000000000 | bytes 4000000 | tf_op jit(solution)/shard_map/pallas_call | solution.py:46
  68.3 0.6 collective-permute-start.28
  68.9 0.8 %shard_map.94.refs_0_ = bf16[2,128,1024]{2,1,0:T(8,128)(2,1)} custom-call(bf16[128,512]{1,0:T(8,128)(2,1)S(1)} %get-tuple-element.67.own, bf16[128,512]{1,0:T(8,128)(2,1)S(1)} %collective-permute-done.29.got, f32[1,1024]{1,0:T(1,128)S(1)} %bitcast.5), custom_call_target="tpu_custom_call" | custom-call | bytes 524288 | tf_op jit(solution)/shard_map/pallas_call | solution.py:335
  69.7 3.9 %collective-permute-done.28.got = bf16[128,512]{1,0:T(8,128)(2,1)S(1)} collective-permute-done((bf16[128,512]{1,0:T(8,128)(2,1)S(1)}, bf16[128,512]{1,0:T(8,128)(2,1)S(1)}, u32[]{:S(2)}, u32[]{:S(2)}) %collective-permute-start.28) | collective-permute-done | bytes 131104 | tf_op jit(solution)/shard_map/ppermute | solution.py:33
  73.6 0.8 %shard_map.95 = bf16[2,128,1024]{2,1,0:T(8,128)(2,1)} custom-call(bf16[128,512]{1,0:T(8,128)(2,1)S(1)} %get-tuple-element.64.own, bf16[128,512]{1,0:T(8,128)(2,1)S(1)} %collective-permute-done.28.got, f32[1,1024]{1,0:T(1,128)S(1)} %bitcast.6, bf16[2,128,1024]{2,1,0:T(8,128)(2,1)} %shard_map.94.refs_0_), custom_call_target="tpu_custom_call", output_to_operand_aliasing={{}: (3, {})} | custom-call | bytes 524288 | tf_op jit(solution)/shard_map/pallas_call | solution.py:335
  (20 shorter events, 0.1 us)
Async XLA Ops:
  0.0 18.5 %collective-permute-start.7 = (bf16[2,256,512]{2,1,0:T(8,128)(2,1)}, bf16[2,256,512]{2,1,0:T(8,128)(2,1)S(1)}, u32[]{:S(2)}, u32[]{:S(2)}) collective-permute-start(bf16[2,256,512]{2,1,0:T(8,128)(2,1)} %keys.1), channel_id=1, source_target_pairs={{0,2},{2,0},{4,6},{6,4},{8,10},{10,8},{12,14},{14,12},{16,18},{18,... | collective-permute-start | bytes 1572872 | tf_op jit(solution)/shard_map/ppermute | solution.py:33
  0.5 18.1 %collective-permute-start.8 = (bf16[2,256,512]{2,1,0:T(8,128)(2,1)}, bf16[2,256,512]{2,1,0:T(8,128)(2,1)S(1)}, u32[]{:S(2)}, u32[]{:S(2)}) collective-permute-start(bf16[2,256,512]{2,1,0:T(8,128)(2,1)} %values.1), channel_id=1, source_target_pairs={{0,2},{2,0},{4,6},{6,4},{8,10},{10,8},{12,14},{14,12},{16,18},{18,... | collective-permute-start | bytes 1572872 | tf_op jit(solution)/shard_map/ppermute | solution.py:33
  0.5 5.4 %collective-permute-start = (bf16[32,768]{1,0:T(8,128)(2,1)}, bf16[32,768]{1,0:T(8,128)(2,1)S(1)}, u32[]{:S(2)}, u32[]{:S(2)}) collective-permute-start(bf16[32,768]{1,0:T(8,128)(2,1)} %bitcast.9), channel_id=1, source_target_pairs={{0,2},{2,0},{4,6},{6,4},{8,10},{10,8},{12,14},{14,12},{16,18},{18,... | collective-permute-start | bytes 147464 | tf_op jit(solution)/shard_map/ppermute | solution.py:33
  1.0 6.2 %collective-permute-start.1 = (bf16[32,768]{1,0:T(8,128)(2,1)}, bf16[32,768]{1,0:T(8,128)(2,1)S(1)}, u32[]{:S(2)}, u32[]{:S(2)}) collective-permute-start(bf16[32,768]{1,0:T(8,128)(2,1)} %bitcast.10), channel_id=1, source_target_pairs={{0,16},{2,18},{4,20},{6,22},{8,24},{10,26},{12,28},{14,30},{16,0},... | collective-permute-start | bytes 147464 | tf_op jit(solution)/shard_map/ppermute | solution.py:33
  4.6 6.4 %collective-permute-start.2 = (bf16[32,768]{1,0:T(8,128)(2,1)}, bf16[32,768]{1,0:T(8,128)(2,1)S(1)}, u32[]{:S(2)}, u32[]{:S(2)}) collective-permute-start(bf16[32,768]{1,0:T(8,128)(2,1)} %bitcast.11), channel_id=1, source_target_pairs={{0,24},{2,26},{4,28},{6,30},{8,16},{10,18},{12,20},{14,22},{16,8},... | collective-permute-start | bytes 147464 | tf_op jit(solution)/shard_map/ppermute | solution.py:33
  5.9 5.2 %collective-permute-start.3 = (bf16[32,768]{1,0:T(8,128)(2,1)}, bf16[32,768]{1,0:T(8,128)(2,1)S(1)}, u32[]{:S(2)}, u32[]{:S(2)}) collective-permute-start(bf16[32,768]{1,0:T(8,128)(2,1)} %bitcast.12), channel_id=1, source_target_pairs={{0,8},{2,10},{4,12},{6,14},{8,0},{10,2},{12,4},{14,6},{16,24},{18,... | collective-permute-start | bytes 147464 | tf_op jit(solution)/shard_map/ppermute | solution.py:33
  11.1 5.7 %collective-permute-start.4 = (bf16[4,32,768]{2,1,0:T(8,128)(2,1)S(1)}, bf16[4,32,768]{2,1,0:T(8,128)(2,1)S(1)}, u32[]{:S(2)}, u32[]{:S(2)}) collective-permute-start(bf16[4,32,768]{2,1,0:T(8,128)(2,1)S(1)} %shard_map.83.mine), channel_id=1, source_target_pairs={{0,4},{2,6},{4,0},{6,2},{8,12},{10,14},{12,8},{14,10},{16,20},{18,... | collective-permute-start | bytes 589832 | tf_op jit(solution)/shard_map/ppermute | solution.py:33
  12.6 16.0 %collective-permute-start.15 = (bf16[2,256,512]{2,1,0:T(8,128)(2,1)}, bf16[2,256,512]{2,1,0:T(8,128)(2,1)S(1)}, u32[]{:S(2)}, u32[]{:S(2)}) collective-permute-start(bf16[2,256,512]{2,1,0:T(8,128)(2,1)} %keys.1), channel_id=1, source_target_pairs={{0,8},{2,10},{4,12},{6,14},{8,16},{10,18},{12,20},{14,22},{16,24},... | collective-permute-start | bytes 1572872 | tf_op jit(solution)/shard_map/ppermute | solution.py:361
  12.8 4.1 %collective-permute-start.9 = (f32[1,256]{1,0:T(1,128)}, f32[1,256]{1,0:T(1,128)S(1)}, u32[]{:S(2)}, u32[]{:S(2)}) collective-permute-start(f32[1,256]{1,0:T(1,128)} %bitcast.7), channel_id=1, source_target_pairs={{0,2},{2,0},{4,6},{6,4},{8,10},{10,8},{12,14},{14,12},{16,18},{18,... | collective-permute-start | bytes 3080 | tf_op jit(solution)/shard_map/ppermute | solution.py:33
  13.5 1.0 %copy-start.1 = (bf16[2,256,512]{2,1,0:T(8,128)(2,1)S(1)}, bf16[2,256,512]{2,1,0:T(8,128)(2,1)}, u32[]{:S(2)}) copy-start(bf16[2,256,512]{2,1,0:T(8,128)(2,1)} %keys.1) | copy-start | bytes 1572868
  14.5 0.7 copy-start.4
  16.8 1.4 %collective-permute-start.5 = (bf16[4,32,768]{2,1,0:T(8,128)(2,1)S(1)}, bf16[4,32,768]{2,1,0:T(8,128)(2,1)S(1)}, u32[]{:S(2)}, u32[]{:S(2)}) collective-permute-start(bf16[4,32,768]{2,1,0:T(8,128)(2,1)S(1)} %shard_map.83.mine), channel_id=1, source_target_pairs={{0,2},{2,0},{4,6},{6,4},{8,10},{10,8},{12,14},{14,12},{16,18},{18,... | collective-permute-start | bytes 589832 | tf_op jit(solution)/shard_map/ppermute | solution.py:33
  16.9 1.6 %collective-permute-start.6 = (bf16[4,32,768]{2,1,0:T(8,128)(2,1)S(1)}, bf16[4,32,768]{2,1,0:T(8,128)(2,1)S(1)}, u32[]{:S(2)}, u32[]{:S(2)}) collective-permute-start(bf16[4,32,768]{2,1,0:T(8,128)(2,1)S(1)} %collective-permute-done.4.other), channel_id=1, source_target_pairs={{0,2},{2,0},{4,6},{6,4},{8,10},{10,8},{12,14},{14,12},{16,18},{18,... | collective-permute-start | bytes 589832 | tf_op jit(solution)/shard_map/ppermute | solution.py:33
  19.7 8.9 %collective-permute-start.10 = (bf16[192,512]{1,0:T(8,128)(2,1)S(1)}, bf16[192,512]{1,0:T(8,128)(2,1)S(1)}, u32[]{:S(2)}, u32[]{:S(2)}) collective-permute-start(bf16[192,512]{1,0:T(8,128)(2,1)S(1)} %get-tuple-element.44), channel_id=1, source_target_pairs={{0,4},{2,6},{4,0},{6,2},{8,12},{10,14},{12,8},{14,10},{16,20},{18,... | collective-permute-start | bytes 589832 | tf_op jit(solution)/shard_map/ppermute | solution.py:33
  21.3 18.7 %collective-permute-start.11 = (bf16[2,256,512]{2,1,0:T(8,128)(2,1)}, bf16[2,256,512]{2,1,0:T(8,128)(2,1)S(1)}, u32[]{:S(2)}, u32[]{:S(2)}) collective-permute-start(bf16[2,256,512]{2,1,0:T(8,128)(2,1)} %values.1), channel_id=1, source_target_pairs={{0,8},{2,10},{4,12},{6,14},{8,16},{10,18},{12,20},{14,22},{16,24},... | collective-permute-start | bytes 1572872 | tf_op jit(solution)/shard_map/ppermute | solution.py:361
  28.7 13.4 %collective-permute-start.16 = (bf16[2,256,512]{2,1,0:T(8,128)(2,1)S(1)}, bf16[2,256,512]{2,1,0:T(8,128)(2,1)S(1)}, u32[]{:S(2)}, u32[]{:S(2)}) collective-permute-start(bf16[2,256,512]{2,1,0:T(8,128)(2,1)S(1)} %shard_map.89), channel_id=1, source_target_pairs={{0,4},{2,6},{4,0},{6,2},{8,12},{10,14},{12,8},{14,10},{16,20},{18,... | collective-permute-start | bytes 1572872 | tf_op jit(solution)/shard_map/ppermute | solution.py:33
  29.3 17.8 %copy-start = (bf16[2,256,512]{2,1,0:T(8,128)(2,1)S(1)}, bf16[2,256,512]{2,1,0:T(8,128)(2,1)}, u32[]{:S(2)}) copy-start(bf16[2,256,512]{2,1,0:T(8,128)(2,1)} %refs_0_.1) | copy-start | bytes 1572868
  29.4 12.6 %collective-permute-start.12 = (bf16[48,512]{1,0:T(8,128)(2,1)S(1)}, bf16[48,512]{1,0:T(8,128)(2,1)S(1)}, u32[]{:S(2)}, u32[]{:S(2)}) collective-permute-start(bf16[48,512]{1,0:T(8,128)(2,1)S(1)} %get-tuple-element.51), channel_id=1, source_target_pairs={{0,16},{2,18},{4,20},{6,22},{8,24},{10,26},{12,28},{14,30},{16,0},... | collective-permute-start | bytes 147464 | tf_op jit(solution)/shard_map/ppermute | solution.py:33
  31.7 10.3 %collective-permute-start.13 = (bf16[48,512]{1,0:T(8,128)(2,1)S(1)}, bf16[48,512]{1,0:T(8,128)(2,1)S(1)}, u32[]{:S(2)}, u32[]{:S(2)}) collective-permute-start(bf16[48,512]{1,0:T(8,128)(2,1)S(1)} %get-tuple-element.52), channel_id=1, source_target_pairs={{0,24},{2,26},{4,28},{6,30},{8,16},{10,18},{12,20},{14,22},{16,8},... | collective-permute-start | bytes 147464 | tf_op jit(solution)/shard_map/ppermute | solution.py:33
  32.7 9.4 %collective-permute-start.14 = (bf16[48,512]{1,0:T(8,128)(2,1)S(1)}, bf16[48,512]{1,0:T(8,128)(2,1)S(1)}, u32[]{:S(2)}, u32[]{:S(2)}) collective-permute-start(bf16[48,512]{1,0:T(8,128)(2,1)S(1)} %get-tuple-element.53), channel_id=1, source_target_pairs={{0,8},{2,10},{4,12},{6,14},{8,0},{10,2},{12,4},{14,6},{16,24},{18,... | collective-permute-start | bytes 147464 | tf_op jit(solution)/shard_map/ppermute | solution.py:33
  42.0 20.6 %copy-start.2 = (bf16[2,256,512]{2,1,0:T(8,128)(2,1)S(1)}, bf16[2,256,512]{2,1,0:T(8,128)(2,1)}, u32[]{:S(2)}) copy-start(bf16[2,256,512]{2,1,0:T(8,128)(2,1)} %refs_9_.1) | copy-start | bytes 1572868
  42.1 5.0 %collective-permute-start.17 = (bf16[2,256,512]{2,1,0:T(8,128)(2,1)S(1)}, bf16[2,256,512]{2,1,0:T(8,128)(2,1)S(1)}, u32[]{:S(2)}, u32[]{:S(2)}) collective-permute-start(bf16[2,256,512]{2,1,0:T(8,128)(2,1)S(1)} %collective-permute-done.15.far.refs_1_), channel_id=1, source_target_pairs={{0,2},{2,0},{4,6},{6,4},{8,10},{10,8},{12,14},{14,12},{16,18},{18,... | collective-permute-start | bytes 1572872 | tf_op jit(solution)/shard_map/ppermute | solution.py:33
  42.2 4.9 %collective-permute-start.18 = (bf16[2,256,512]{2,1,0:T(8,128)(2,1)S(1)}, bf16[2,256,512]{2,1,0:T(8,128)(2,1)S(1)}, u32[]{:S(2)}, u32[]{:S(2)}) collective-permute-start(bf16[2,256,512]{2,1,0:T(8,128)(2,1)S(1)} %collective-permute-done.16.refs_2_), channel_id=1, source_target_pairs={{0,2},{2,0},{4,6},{6,4},{8,10},{10,8},{12,14},{14,12},{16,18},{18,... | collective-permute-start | bytes 1572872 | tf_op jit(solution)/shard_map/ppermute | solution.py:33
  42.6 14.8 %collective-permute-start.25 = (bf16[2,256,512]{2,1,0:T(8,128)(2,1)S(1)}, bf16[2,256,512]{2,1,0:T(8,128)(2,1)S(1)}, u32[]{:S(2)}, u32[]{:S(2)}) collective-permute-start(bf16[2,256,512]{2,1,0:T(8,128)(2,1)S(1)} %shard_map.86), channel_id=1, source_target_pairs={{0,4},{2,6},{4,0},{6,2},{8,12},{10,14},{12,8},{14,10},{16,20},{18,... | collective-permute-start | bytes 1572872 | tf_op jit(solution)/shard_map/ppermute | solution.py:33
  43.2 6.7 %collective-permute-start.19 = (bf16[48,512]{1,0:T(8,128)(2,1)S(1)}, bf16[48,512]{1,0:T(8,128)(2,1)S(1)}, u32[]{:S(2)}, u32[]{:S(2)}) collective-permute-start(bf16[48,512]{1,0:T(8,128)(2,1)S(1)} %shard_map.88.refs_0_), channel_id=1, source_target_pairs={{0,16},{2,18},{4,20},{6,22},{8,24},{10,26},{12,28},{14,30},{16,0},... | collective-permute-start | bytes 147464 | tf_op jit(solution)/shard_map/ppermute | solution.py:33
  45.0 6.0 %collective-permute-start.20 = (bf16[48,512]{1,0:T(8,128)(2,1)S(1)}, bf16[48,512]{1,0:T(8,128)(2,1)S(1)}, u32[]{:S(2)}, u32[]{:S(2)}) collective-permute-start(bf16[48,512]{1,0:T(8,128)(2,1)S(1)} %shard_map.88.refs_0_), channel_id=1, source_target_pairs={{0,24},{2,26},{4,28},{6,30},{8,16},{10,18},{12,20},{14,22},{16,8},... | collective-permute-start | bytes 147464 | tf_op jit(solution)/shard_map/ppermute | solution.py:33
  47.1 4.5 %collective-permute-start.21 = (bf16[48,512]{1,0:T(8,128)(2,1)S(1)}, bf16[48,512]{1,0:T(8,128)(2,1)S(1)}, u32[]{:S(2)}, u32[]{:S(2)}) collective-permute-start(bf16[48,512]{1,0:T(8,128)(2,1)S(1)} %shard_map.88.refs_0_), channel_id=1, source_target_pairs={{0,8},{2,10},{4,12},{6,14},{8,0},{10,2},{12,4},{14,6},{16,24},{18,... | collective-permute-start | bytes 147464 | tf_op jit(solution)/shard_map/ppermute | solution.py:33
  51.6 9.2 %collective-permute-start.22 = (bf16[4,48,512]{2,1,0:T(8,128)(2,1)S(1)}, bf16[4,48,512]{2,1,0:T(8,128)(2,1)S(1)}, u32[]{:S(2)}, u32[]{:S(2)}) collective-permute-start(bf16[4,48,512]{2,1,0:T(8,128)(2,1)S(1)} %shard_map.91.mine), channel_id=1, source_target_pairs={{0,4},{2,6},{4,0},{6,2},{8,12},{10,14},{12,8},{14,10},{16,20},{18,... | collective-permute-start | bytes 589832 | tf_op jit(solution)/shard_map/ppermute | solution.py:33
  53.1 8.2 %collective-permute-start.26 = (bf16[2,256,512]{2,1,0:T(8,128)(2,1)S(1)}, bf16[2,256,512]{2,1,0:T(8,128)(2,1)S(1)}, u32[]{:S(2)}, u32[]{:S(2)}) collective-permute-start(bf16[2,256,512]{2,1,0:T(8,128)(2,1)S(1)} %collective-permute-done.11.far.refs_5_.refs_1_), channel_id=1, source_target_pairs={{0,2},{2,0},{4,6},{6,4},{8,10},{10,8},{12,14},{14,12},{16,18},{18,... | collective-permute-start | bytes 1572872 | tf_op jit(solution)/shard_map/ppermute | solution.py:33
  60.8 1.9 %collective-permute-start.27 = (bf16[2,256,512]{2,1,0:T(8,128)(2,1)S(1)}, bf16[2,256,512]{2,1,0:T(8,128)(2,1)S(1)}, u32[]{:S(2)}, u32[]{:S(2)}) collective-permute-start(bf16[2,256,512]{2,1,0:T(8,128)(2,1)S(1)} %collective-permute-done.25.refs_6_.refs_2_), channel_id=1, source_target_pairs={{0,2},{2,0},{4,6},{6,4},{8,10},{10,8},{12,14},{14,12},{16,18},{18,... | collective-permute-start | bytes 1572872 | tf_op jit(solution)/shard_map/ppermute | solution.py:33
  60.8 4.1 %collective-permute-start.23 = (bf16[4,48,512]{2,1,0:T(8,128)(2,1)S(1)}, bf16[4,48,512]{2,1,0:T(8,128)(2,1)S(1)}, u32[]{:S(2)}, u32[]{:S(2)}) collective-permute-start(bf16[4,48,512]{2,1,0:T(8,128)(2,1)S(1)} %shard_map.91.mine), channel_id=1, source_target_pairs={{0,2},{2,0},{4,6},{6,4},{8,10},{10,8},{12,14},{14,12},{16,18},{18,... | collective-permute-start | bytes 589832 | tf_op jit(solution)/shard_map/ppermute | solution.py:33
  61.3 3.6 %collective-permute-start.24 = (bf16[4,48,512]{2,1,0:T(8,128)(2,1)S(1)}, bf16[4,48,512]{2,1,0:T(8,128)(2,1)S(1)}, u32[]{:S(2)}, u32[]{:S(2)}) collective-permute-start(bf16[4,48,512]{2,1,0:T(8,128)(2,1)S(1)} %collective-permute-done.22.side_in), channel_id=1, source_target_pairs={{0,2},{2,0},{4,6},{6,4},{8,10},{10,8},{12,14},{14,12},{16,18},{18,... | collective-permute-start | bytes 589832 | tf_op jit(solution)/shard_map/ppermute | solution.py:33
  63.3 5.6 %collective-permute-start.29 = (bf16[128,512]{1,0:T(8,128)(2,1)S(1)}, bf16[128,512]{1,0:T(8,128)(2,1)S(1)}, u32[]{:S(2)}, u32[]{:S(2)}) collective-permute-start(bf16[128,512]{1,0:T(8,128)(2,1)S(1)} %get-tuple-element.68), channel_id=1, source_target_pairs={{0,1},{1,0},{2,3},{3,2},{4,5},{5,4},{6,7},{7,6},{8,9},{9,8},{10,11... | collective-permute-start | bytes 393224 | tf_op jit(solution)/shard_map/ppermute | solution.py:33
  64.9 4.0 %copy-start.3 = (f32[1024]{0:T(1024)S(1)}, f32[1024]{0:T(1024)}, u32[]{:S(2)}) copy-start(f32[1024]{0:T(1024)} %param.15) | copy-start | bytes 12292
  68.3 5.3 %collective-permute-start.28 = (bf16[128,512]{1,0:T(8,128)(2,1)S(1)}, bf16[128,512]{1,0:T(8,128)(2,1)S(1)}, u32[]{:S(2)}, u32[]{:S(2)}) collective-permute-start(bf16[128,512]{1,0:T(8,128)(2,1)S(1)} %get-tuple-element.65), channel_id=1, source_target_pairs={{0,1},{1,0},{2,3},{3,2},{4,5},{5,4},{6,7},{7,6},{8,9},{9,8},{10,11... | collective-permute-start | bytes 393224 | tf_op jit(solution)/shard_map/ppermute | solution.py:33
